TPU v7x, 128 devices: a whole 4x4x4 slice. The times are simulated.
128 devices in a mesh: dp: 8 (over x, core), mp: 16 (over y, z).
Axes of the slice: x: 4, y: 4, z: 4, core: 2. Of those that a mesh axis runs over, the one named last changes fastest.
Arguments:
- attention: bfloat16 [2048, 8192], P('dp', 'mp'), may hold values from -6 to 6
- out_proj: bfloat16 [8192, 8192], P('mp'), may hold values from -0.0625 to 0.0625
- residual: bfloat16 [2048, 8192], P('dp', 'mp')
- final_gain: float32 [8192], P('mp'), may hold values from 0.1 to 1.9
- adapter_weight: bfloat16 [8192, 3072], P('mp'), may hold values from -0.0625 to 0.0625
- token_slot: int32 [2048], P('dp'), may hold values from 0 to 127, as said below
- block_owner: int32 [16], replicated, may hold values from 0 to 7, as said below
- student_hidden: bfloat16 [8, 128, 4, 3072], P('dp', 'mp'), may hold values from -6 to 6
- cotangent: bfloat16 [8, 128, 4, 3072], P('dp', 'mp'), may hold values from -1.25 to 1.25
- student_gain: float32 [3072], replicated, may hold values from 0.1 to 1.9
- gate_weight: bfloat16 [3072, 8192], P(None, 'mp'), may hold values from -0.109375 to 0.109375
- up_weight: bfloat16 [3072, 8192], P(None, 'mp'), may hold values from -0.109375 to 0.109375
- down_weight: bfloat16 [3072, 8192], P(None, 'mp'), may hold values from -0.0625 to 0.0625
Outputs:
- student_out: bfloat16 [8, 128, 4, 3072], P('dp', 'mp')
- adapter_grad: float32 [8192, 3072], P('mp', 'dp')
Inputs may be any that keep to these rules, and one draw needn't show every extreme that they name: `token_slot`: within each aligned block of 128 teacher tokens the slot never falls, and the block's last token has slot 127. `block_owner`: every dp index owns 2 blocks, except one that owns 2 * 2 and one that owns none; which ones varies.
All inputs are finite; a program needn't handle non-finite values.
Results may differ from a plain program's by a relative error of at most 0.03.
Values may be sent and summed in bfloat16 or wider, within the bound.
No kernel may reach another device: no remote copies, remote signals or barrier semaphores. Data moves between devices by JAX's collectives and lax.ppermute only.
A program may use at most 384 MiB of HBM per device.

v0:
```python
import jax
import jax.numpy as jnp
from jax import lax
from jax.sharding import PartitionSpec as P

BLK = 128


epsilon = 1e-06


def silu_slope(preact):
    sigma = jax.nn.sigmoid(preact)
    return sigma * (1.0 + preact * (1.0 - sigma))


def times_rows(left, right):
    return lax.dot_general(
        left, right, (((left.ndim - 1,), (1,)), ((), ())), preferred_element_type=jnp.float32
    )


def on_device(
    attention,
    out_proj,
    residual,
    final_gain,
    adapter_weight,
    token_slot,
    block_owner,
    student_hidden,
    cotangent,
    student_gain,
    gate_weight,
    up_weight,
    down_weight,
):
    tokens_here = attention.shape[0]
    width_here = attention.shape[1]
    width_full = out_proj.shape[1]
    student_width = adapter_weight.shape[1]
    block_len = BLK
    blocks_here = tokens_here // block_len
    groups_mp = lax.axis_size("mp")
    groups_dp = lax.axis_size("dp")
    row_piece = block_len // groups_mp
    slot_count = student_hidden.shape[2]
    my_index = lax.axis_index("dp")
    partial_heads = jnp.dot(attention, out_proj, preferred_element_type=jnp.float32)
    summed = lax.psum_scatter(
        partial_heads.astype(jnp.bfloat16), "mp", scatter_dimension=1, tiled=True
    ).astype(jnp.float32)
    hidden = residual.astype(jnp.float32) + summed
    squares = lax.psum(jnp.sum(hidden * hidden, axis=1), "mp")
    inverse_rms = lax.rsqrt(squares / width_full + epsilon)
    normed = (hidden * inverse_rms[:, None] * final_gain).astype(jnp.bfloat16)
    slots_block = token_slot.reshape(blocks_here, block_len)
    onehot = slots_block[:, None, :] == jnp.arange(block_len, dtype=jnp.int32)[None, :, None]
    counts = jnp.sum(onehot.astype(jnp.float32), axis=2)
    pooled_sum = jnp.einsum(
        "krt,ktd->rkd",
        onehot.astype(jnp.bfloat16),
        normed.reshape(blocks_here, block_len, width_here),
        preferred_element_type=jnp.float32,
    )
    pooled = (pooled_sum / jnp.maximum(counts, 1.0).T[:, :, None]).astype(jnp.bfloat16)
    full_proj = lax.psum(
        jnp.einsum(
            "rkd,de->rke", pooled, adapter_weight, preferred_element_type=jnp.float32
        ).astype(jnp.bfloat16),
        "mp",
    ).astype(jnp.float32)
    my_rows = lax.dynamic_slice_in_dim(full_proj, lax.axis_index("mp") * row_piece, row_piece, 0)
    projected = my_rows.astype(jnp.bfloat16)
    sender_owner = lax.dynamic_slice_in_dim(block_owner, my_index * blocks_here, blocks_here)
    dest_mask = sender_owner[None, :] == jnp.arange(groups_dp, dtype=jnp.int32)[:, None]
    outgoing = jnp.where(
        dest_mask[None, :, :, None], projected[:, None, :, :], jnp.zeros((), jnp.bfloat16)
    )
    incoming = lax.all_to_all(outgoing, "dp", split_axis=1, concat_axis=1, tiled=True)
    received = incoming.reshape(row_piece, groups_dp * blocks_here, student_width)
    owned = block_owner == my_index
    owned_int = owned.astype(jnp.int32)
    ranks = jnp.cumsum(owned_int) - owned_int
    select = owned[None, :] & (ranks[None, :] == jnp.arange(slot_count, dtype=jnp.int32)[:, None])
    live = jnp.any(select, axis=1)
    select_half = select.astype(jnp.bfloat16)
    placed = jnp.einsum("cb,rbe->rce", select_half, received, preferred_element_type=jnp.float32)
    state = student_hidden[0].astype(jnp.float32) + placed
    inverse_student = lax.rsqrt(jnp.mean(state * state, axis=-1, keepdims=True) + epsilon)
    normed_student = (state * inverse_student * student_gain).astype(jnp.bfloat16)
    live_mask = live[None, :, None]
    grad_out = jnp.where(live_mask, cotangent[0], jnp.zeros((), jnp.bfloat16))
    section = lax.all_gather(normed_student, "mp", axis=0, tiled=True)
    gate_val = jnp.einsum("rce,ef->rcf", section, gate_weight, preferred_element_type=jnp.float32)
    up_val = jnp.einsum("rce,ef->rcf", section, up_weight, preferred_element_type=jnp.float32)
    gate_up_all = jnp.stack([gate_val, up_val])
    gate_all = gate_up_all[0]
    up_all = gate_up_all[1]
    act = (jax.nn.silu(gate_all) * up_all).astype(jnp.bfloat16)
    section = act
    output = lax.psum_scatter(
        times_rows(section, down_weight).astype(jnp.bfloat16), "mp", scatter_dimension=0, tiled=True
    ).astype(jnp.float32)
    grad_hidden = jnp.einsum(
        "rce,ef->rcf",
        lax.all_gather(grad_out, "mp", axis=0, tiled=True),
        down_weight,
        preferred_element_type=jnp.float32,
    )
    gate_val = gate_all
    up_val = up_all
    grad_gate = (grad_hidden * up_val * silu_slope(gate_val)).astype(jnp.bfloat16)
    grad_up = (grad_hidden * jax.nn.silu(gate_val)).astype(jnp.bfloat16)
    grads_all = jnp.stack([grad_gate, grad_up])
    section = grads_all
    grad_norm = lax.psum_scatter(
        (times_rows(section[0], gate_weight) + times_rows(section[1], up_weight)).astype(
            jnp.bfloat16
        ),
        "mp",
        scatter_dimension=0,
        tiled=True,
    ).astype(jnp.float32)
    student_out = jnp.where(live_mask, state + output, 0.0).astype(jnp.bfloat16)
    gained = student_gain * grad_norm
    grad_state = grad_out.astype(jnp.float32) + inverse_student * gained
    grad_state = grad_state - state * inverse_student**3 * jnp.mean(
        gained * state, axis=-1, keepdims=True
    )
    grad_proj = jnp.where(live_mask, grad_state, 0.0).astype(jnp.bfloat16)
    returning = jnp.einsum(
        "cb,rce->rbe", select_half, grad_proj, preferred_element_type=jnp.float32
    ).astype(jnp.bfloat16)
    returning = returning.reshape(row_piece, groups_dp, blocks_here, student_width)
    came_back = lax.all_to_all(returning, "dp", split_axis=1, concat_axis=1, tiled=True)
    grad_rows = jnp.einsum(
        "ok,roke->rke",
        dest_mask.astype(jnp.bfloat16),
        came_back,
        preferred_element_type=jnp.float32,
    ).astype(jnp.bfloat16)
    grad_local = jnp.einsum(
        "rkd,rke->de",
        pooled,
        lax.all_gather(grad_rows, "mp", axis=0, tiled=True),
        preferred_element_type=jnp.float32,
    )
    adapter_grad = lax.psum_scatter(
        grad_local.astype(jnp.bfloat16), "dp", scatter_dimension=1, tiled=True
    ).astype(jnp.float32)
    return (student_out[None], adapter_grad)


def solution(mesh):
    return jax.shard_map(
        on_device,
        mesh=mesh,
        in_specs=(
            P("dp", "mp"),
            P("mp", None),
            P("dp", "mp"),
            P("mp"),
            P("mp", None),
            P("dp"),
            P(),
            P("dp", "mp", None, None),
            P("dp", "mp", None, None),
            P(),
            P(None, "mp"),
            P(None, "mp"),
            P(None, "mp"),
        ),
        out_specs=(P("dp", "mp", None, None), P("mp", "dp")),
        check_vma=False,
    )
```

profile of v0, /device:TPU:0, one launch (start us, length us, event | category | flops | bytes accessed | tf_op | source)
XLA Modules:
  0.0 587.8 jit_solution(16093144323272335550)
XLA Ops:
  7.2 7.9 %convolution_convert_fusion = bf16[256,8192]{1,0:T(8,128)(2,1)} fusion(bf16[256,512]{1,0:T(8,128)(2,1)} %param.13, bf16[512,8192]{1,0:T(8,128)(2,1)} %param.14), kind=kOutput, calls=%fused_computation | convolution fusion | flops 2149580800 | bytes 12845056 | tf_op jit(solution)/shard_map/dot_general | solution.py:49
  15.9 79.7 %reduce-scatter.5.cloned.1.call-done = bf16[256,512]{1,0:T(8,128)(2,1)} async-done(((bf16[256,8192]{1,0:T(8,128)(2,1)}), bf16[256,512]{1,0:T(8,128)(2,1)}) %reduce-scatter.5.cloned.1.call-update) | async-done | bytes 262160 | tf_op jit(solution)/shard_map/reduce_scatter | solution.py:50
  95.6 1.1 multiply_reduce_fusion
  96.7 38.1 %psum.14 = f32[256]{0:T(256)S(1)} all-reduce(f32[256]{0:T(256)S(1)} %multiply_reduce_fusion), channel_id=1, replica_groups=mesh['dp'=8,'mp'=16] {'mp'}, use_global_device_ids=true, to_apply=%region_4.0 | all-reduce | flops 256 | bytes 2048 | tf_op jit(solution)/shard_map/psum | solution.py:54
  134.9 1.1 multiply_convert_fusion.6
  137.0 4.1 convolution_convert_fusion.2
  143.7 82.5 %all-reduce.6.cloned.1.call-done = bf16[128,2,3072]{2,0,1:T(8,128)(2,1)} async-done(((bf16[128,2,3072]{2,0,1:T(8,128)(2,1)}), bf16[128,2,3072]{2,0,1:T(8,128)(2,1)}) %all-reduce.6.cloned.1.call-update) | async-done | bytes 1572880 | tf_op jit(solution)/shard_map/psum | solution.py:67
  228.0 17.3 %all_to_all.10 = bf16[8,8,2,3072]{3,2,0,1:T(2,128)(2,1)S(1)} all-to-all(bf16[8,8,2,3072]{3,2,0,1:T(2,128)(2,1)S(1)} %broadcast_select_fusion), channel_id=1, replica_groups=mesh['dp'=8,'mp'=16] {'dp'}, dimensions={1} | all-to-all | bytes 1572864 | tf_op jit(solution)/shard_map/all_to_all | solution.py:80
  245.3 1.5 copy.39
  246.8 3.0 reshape.92
  249.7 1.5 multiply_reduce_fusion.2
  253.0 23.0 %all-gather.6.cloned.1.call-done = bf16[128,4,3072]{2,1,0:T(4,128)(2,1)} async-done(((bf16[8,4,3072]{2,1,0:T(4,128)(2,1)}), bf16[128,4,3072]{2,1,0:T(4,128)(2,1)}) %all-gather.6.cloned.1.call-update) | async-done | bytes 3145744 | tf_op jit(solution)/shard_map/all_gather | solution.py:107
  276.0 4.7 fusion.2
  280.7 45.1 %all-gather.4.cloned.1.call-done = bf16[128,4,3072]{2,1,0:T(4,128)(2,1)} async-done(((bf16[8,4,3072]{2,1,0:T(4,128)(2,1)}), bf16[128,4,3072]{2,1,0:T(4,128)(2,1)}) %all-gather.4.cloned.1.call-update) | async-done | bytes 3145744 | tf_op jit(solution)/shard_map/all_gather | solution.py:94
  325.8 4.8 fusion.10
  330.6 1.8 fusion.6
  332.4 1.9 convolution_convert_fusion.1
  334.6 2.0 fusion.8
  336.6 1.9 add_convert_fusion
  338.5 4.1 copy.44
  342.6 4.3 copy.42
  348.8 119.7 %all-reduce.8.cloned.1.call-done = (bf16[128,4,3072]{2,1,0:T(4,128)(2,1)}, bf16[128,4,3072]{2,1,0:T(4,128)(2,1)}) async-done(((bf16[128,4,3072]{2,1,0:T(4,128)(2,1)}, bf16[128,4,3072]{2,1,0:T(4,128)(2,1)}), (bf16[128,4,3072]{2,1,0:T(4,128)(2,1)}, bf16[128,4,3072]{2,1,0:T(4,128)(2,1)})) %all-reduce.8.cloned.1.call-update) | async-done | bytes 6291472
  468.5 2.0 multiply_reduce_fusion.1
  470.6 1.4 fusion
  472.3 1.5 copy.45
  473.8 4.3 all-to-all-start.1
  478.2 13.0 %all-to-all-done.1 = bf16[8,8,2,3072]{3,2,0,1:T(2,128)(2,1)S(1)} async-done(((bf16[8,8,2,3072]{3,2,0,1:T(2,128)(2,1)}), bf16[8,8,2,3072]{3,2,0,1:T(2,128)(2,1)S(1)}, u32[]{:S(2)}, u32[]{:S(2)}) %all-to-all-start.1) | async-done | bytes 786464 | tf_op jit(solution)/shard_map/all_to_all | solution.py:136
  492.9 42.1 %all-gather.8.cloned.1.call-done = bf16[128,2,3072]{2,0,1:T(8,128)(2,1)} async-done(((bf16[8,2,3072]{2,0,1:T(8,128)(2,1)}), bf16[128,2,3072]{2,0,1:T(8,128)(2,1)}) %all-gather.8.cloned.1.call-update) | async-done | bytes 1572880 | tf_op jit(solution)/shard_map/all_gather | solution.py:146
  535.0 4.0 bitcast_convert_fusion
  539.0 4.8 copy.51
  543.8 35.0 %reduce-scatter.7.cloned.1.call-done = bf16[384,512]{1,0:T(8,128)(2,1)} async-done(((bf16[3072,512]{1,0:T(8,128)(2,1)}), bf16[384,512]{1,0:T(8,128)(2,1)}) %reduce-scatter.7.cloned.1.call-update) | async-done | bytes 393232
  578.8 1.2 copy.52
  (87 shorter events, 12.4 us)
Async XLA Ops:
  7.2 268.8 %copy-start = (bf16[3072,512]{1,0:T(8,128)(2,1)S(1)}, bf16[3072,512]{1,0:T(8,128)(2,1)}, u32[]{:S(2)}) copy-start(bf16[3072,512]{1,0:T(8,128)(2,1)} %param.25) | copy-start | bytes 9437188
  7.2 88.4 %reduce-scatter.5.cloned.1.call-start = ((), (), s32[]{:S(2)}) async-start(), calls=%async_computation.4 | async-start | bytes 4456448 | tf_op jit(solution)/shard_map/reduce_scatter | solution.py:50
  15.1 0.7 copy-start.18
  15.1 80.5 %copy-start.7 = (bf16[256,512]{1,0:T(8,128)(2,1)S(1)}, bf16[256,512]{1,0:T(8,128)(2,1)}, u32[]{:S(2)}) copy-start(bf16[256,512]{1,0:T(8,128)(2,1)} %param.15) | copy-start | bytes 786436
  15.2 119.7 %copy-start.13 = (f32[512]{0:T(512)S(1)}, f32[512]{0:T(512)}, u32[]{:S(2)}) copy-start(f32[512]{0:T(512)} %param.16) | copy-start | bytes 6148
  15.2 211.1 %all-reduce.6.cloned.1.call-start = ((), (), s32[]{:S(2)}) async-start(), calls=%async_computation.5 | async-start | bytes 3145728 | tf_op jit(solution)/shard_map/psum | solution.py:67
  136.2 0.7 copy-start.5
  137.0 4.2 copy-start.21
  137.0 5.2 copy-start.8
  141.1 134.9 %all-gather.6.cloned.1.call-start = ((), (), s32[]{:S(2)}) async-start(), calls=%async_computation.7 | async-start | bytes 3342336 | tf_op jit(solution)/shard_map/all_gather | solution.py:107
  141.2 108.5 %copy-start.16 = (pred[16]{0:T(512)(128)(4,1)}, pred[16]{0:T(512)(128)(4,1)S(1)}, u32[]{:S(2)}) copy-start(pred[16]{0:T(512)(128)(4,1)S(1)} %get-tuple-element.5) | copy-start | bytes 52
  141.5 105.3 %copy-start.19 = (s32[16]{0:T(128)}, s32[16]{0:T(128)S(1)}, u32[]{:S(2)}) copy-start(s32[16]{0:T(128)S(1)} %convert_subtract_fusion) | copy-start | bytes 196
  141.6 0.6 copy-start.14
  143.0 182.8 %all-gather.4.cloned.1.call-start = ((), (), s32[]{:S(2)}) async-start(), calls=%async_computation.6 | async-start | bytes 3342336 | tf_op jit(solution)/shard_map/all_gather | solution.py:94
  228.0 23.9 %copy-start.10 = (f32[3072]{0:T(1024)S(1)}, f32[3072]{0:T(1024)}, u32[]{:S(2)}) copy-start(f32[3072]{0:T(1024)} %param.22) | copy-start | bytes 36868
  252.7 215.8 %all-reduce.8.cloned.1.call-start = ((), (), s32[]{:S(2)}) async-start(), calls=%async_computation.10 | async-start | bytes 12582912
  325.8 4.8 copy-start.3
  325.8 4.8 copy-start.22
  332.4 1.9 copy-start.2
  332.4 2.2 copy-start.4
  346.9 0.7 copy-start.23
  346.9 121.6 %copy-start.15 = (pred[4]{0:T(512)(128)(4,1)S(1)}, pred[4]{0:T(512)(128)(4,1)}, u32[]{:S(2)}) copy-start(pred[4]{0:T(512)(128)(4,1)} %copy-done.14) | copy-start | bytes 16
  346.9 123.6 %copy-start.9 = (bf16[1,8,4,3072]{3,2,1,0:T(4,128)(2,1)S(1)}, bf16[1,8,4,3072]{3,2,1,0:T(4,128)(2,1)}, u32[]{:S(2)}) copy-start(bf16[1,8,4,3072]{3,2,1,0:T(4,128)(2,1)} %param.21) | copy-start | bytes 589828
  346.9 123.6 %copy-start.11 = (f32[8,4]{1,0:T(8,128)S(1)}, f32[8,4]{1,0:T(8,128)}, u32[]{:S(2)}) copy-start(f32[8,4]{1,0:T(8,128)} %get-tuple-element.8) | copy-start | bytes 388
  347.0 123.6 %copy-start.17 = (pred[16]{0:T(512)(128)(4,1)S(1)}, pred[16]{0:T(512)(128)(4,1)}, u32[]{:S(2)}) copy-start(pred[16]{0:T(512)(128)(4,1)} %copy-done.16) | copy-start | bytes 52
  347.0 123.6 %copy-start.20 = (s32[16]{0:T(128)S(1)}, s32[16]{0:T(128)}, u32[]{:S(2)}) copy-start(s32[16]{0:T(128)} %copy-done.19) | copy-start | bytes 196
  470.5 7.5 %copy-start.12 = (pred[8,2,1,1]{1,0,2,3:T(8,128)(4,1)S(1)}, pred[8,2,1,1]{1,0,2,3:T(8,128)(4,1)}, u32[]{:S(2)}) copy-start(pred[8,2,1,1]{1,0,2,3:T(8,128)(4,1)} %get-tuple-element.10) | copy-start | bytes 52
  472.0 63.0 %copy-start.6 = (bf16[128,2,512]{0,2,1:T(8,128)(2,1)S(1)}, bf16[128,2,512]{0,2,1:T(8,128)(2,1)}, u32[]{:S(2)}) copy-start(bf16[128,2,512]{0,2,1:T(8,128)(2,1)} %copy-done.5) | copy-start | bytes 786436
  473.8 17.4 %all-to-all-start.1 = ((bf16[8,8,2,3072]{3,2,0,1:T(2,128)(2,1)}), bf16[8,8,2,3072]{3,2,0,1:T(2,128)(2,1)S(1)}, u32[]{:S(2)}, u32[]{:S(2)}) async-start(bf16[8,8,2,3072]{3,2,0,1:T(2,128)(2,1)} %copy.45), calls=%async_computation.2 | async-start | bytes 1572864 | tf_op jit(solution)/shard_map/all_to_all | solution.py:136
  478.0 56.9 %all-gather.8.cloned.1.call-start = ((), (), s32[]{:S(2)}) async-start(), calls=%async_computation.8 | async-start | bytes 1671168 | tf_op jit(solution)/shard_map/all_gather | solution.py:146
  492.8 86.0 %reduce-scatter.7.cloned.1.call-start = ((), (), s32[]{:S(2)}) async-start(), calls=%async_computation.9 | async-start | bytes 3538944
  539.0 42.0 %copy-start.1 = (bf16[3072,512]{1,0:T(8,128)(2,1)S(1)}, bf16[3072,512]{1,0:T(8,128)(2,1)}, u32[]{:S(2)}) copy-start(bf16[3072,512]{1,0:T(8,128)(2,1)} %param.25) | copy-start | bytes 9437188
Sparse Core Ops, SparseCore 0:
  15.3 80.2 reduce-scatter.4
  141.2 84.9 all-reduce.5
  228.7 47.2 all-gather.5
  278.9 46.8 all-gather.3
  347.1 121.3 all-reduce.7
  493.0 41.9 all-gather.7
  544.0 34.8 reduce-scatter.6
where the time goes:
time: 588 us
  waiting for transfers between devices  440 us (75%)
  blocking collectives  55.4 us (9%)
  matrix products  37.3 us (6%)
  local copies, waits for them, and re-layouts  25.2 us (4%)
  between operations  15.1 us (3%)
  other arithmetic  9.97 us (2%)
    unnamed x9, waiting for transfers between devices  155 us
    psum x1, waiting for transfers between devices, on_device(): lax.psum(jnp.einsum('rkd,de->rke', pooled, adapter_weight, preferred_elem...  82.5 us
    reduce_scatter x1, waiting for transfers between devices, on_device(): lax.psum_scatter(partial_heads.astype(jnp.bfloat16), 'mp', scatter_dimens...  79.7 us
    all_gather x1, waiting for transfers between devices, on_device(): section = lax.all_gather(normed_student, 'mp', axis=0, tiled=True)  45.1 us
    all_gather x1, waiting for transfers between devices, on_device(): lax.all_gather(grad_rows, 'mp', axis=0, tiled=True)  42.1 us
    psum x1, blocking collectives, on_device(): squares = lax.psum(jnp.sum(hidden * hidden, axis=1), 'mp')  38.1 us
    all_gather x1, waiting for transfers between devices, on_device(): lax.all_gather(grad_out, 'mp', axis=0, tiled=True)  23 us
    all_to_all x1, blocking collectives, on_device(): lax.all_to_all(outgoing, 'dp', split_axis=1, concat_axis=1, tiled=True)  17.3 us
  transfers between devices with their start and end apart: 8, of which 8 were waited for; matrix products, arithmetic and copies ran while one was open for 3% of the time, Pallas kernels for 0%

commit v1 on v0

v1 whole, which is shorter than its diff:
```python
import jax
import jax.numpy as jnp
from jax import lax
from jax.experimental import pallas as pl
from jax.experimental.pallas import tpu as pltpu
from jax.sharding import PartitionSpec as P

BLK = 128
epsilon = 1e-06
half = jnp.bfloat16
full = jnp.float32


def exchange(pieces, axis):
    return lax.all_to_all(pieces, axis, split_axis=0, concat_axis=0, tiled=True)


def share(piece, axis):
    size = lax.axis_size(axis)
    return exchange(jnp.broadcast_to(piece[None], (size,) + piece.shape), axis)


def three_parts(value):
    first = lax.reduce_precision(value, 8, 7)
    rest = value - first
    second = lax.reduce_precision(rest, 8, 7)
    return jnp.stack([first, second, rest - second]).astype(half)


def times_rows(left, right):
    return lax.dot_general(left, right, (((1,), (1,)), ((), ())), preferred_element_type=full)


def piece_kernel(left, right, out):
    out[0] = jnp.dot(left[...], right[...], preferred_element_type=full).astype(out.dtype)


def product_in_pieces(left, right, pieces):
    rows, depth = left.shape
    width = right.shape[1] // pieces
    return pl.pallas_call(
        piece_kernel,
        grid=(pieces,),
        in_specs=[
            pl.BlockSpec((rows, depth), lambda i: (0, 0)),
            pl.BlockSpec((depth, width), lambda i: (0, i)),
        ],
        out_specs=pl.BlockSpec((1, rows, width), lambda i: (i, 0, 0)),
        out_shape=jax.ShapeDtypeStruct((pieces, rows, width), half),
        compiler_params=pltpu.CompilerParams(vmem_limit_bytes=16 * 1024 * 1024),
        cost_estimate=pl.CostEstimate(
            flops=2 * rows * depth * width * pieces,
            bytes_accessed=2 * (depth + rows) * width * pieces,
            transcendentals=0,
        ),
    )(left, right)


def on_device(
    attention,
    out_proj,
    residual,
    final_gain,
    adapter_weight,
    token_slot,
    block_owner,
    student_hidden,
    cotangent,
    student_gain,
    gate_weight,
    up_weight,
    down_weight,
):
    tokens, width_here = attention.shape
    width_full = out_proj.shape[1]
    student_width = adapter_weight.shape[1]
    blocks = tokens // BLK
    n_mp = lax.axis_size("mp")
    n_dp = lax.axis_size("dp")
    dp = lax.axis_index("dp")
    mp = lax.axis_index("mp")
    slots = student_hidden.shape[2]
    rows = BLK // n_mp
    groups = n_mp // blocks
    cols = student_width // groups
    out_cols = student_width // n_dp
    mine_rows = blocks * rows

    owned = block_owner[None, :] == jnp.arange(n_dp, dtype=jnp.int32)[:, None]
    ranks = jnp.sum(jnp.where(owned, jnp.cumsum(owned.astype(jnp.int32), axis=1) - 1, 0), axis=0)
    place = block_owner * slots + ranks
    my_place = lax.dynamic_slice_in_dim(place, dp * blocks, blocks)

    def fetch(array):
        by_slot = jnp.swapaxes(array[0], 0, 1)
        everyone = lax.all_gather(by_slot, "dp", axis=0, tiled=True)
        return jnp.stack(
            [lax.dynamic_index_in_dim(everyone, my_place[k], 0, False) for k in range(blocks)]
        )

    sh_rows = fetch(student_hidden)
    dy_rows = fetch(cotangent).reshape(mine_rows, student_width)
    dy = lax.all_gather(dy_rows, "mp", axis=0, tiled=True)

    terms = product_in_pieces(attention, out_proj, n_mp)
    hidden = residual.astype(full) + jnp.sum(exchange(terms, "mp").astype(full), axis=0)
    squares = jnp.sum(hidden * hidden, axis=1)
    gained_hidden = hidden * final_gain
    parts = jnp.einsum(
        "ktd,dce->kcte",
        gained_hidden.astype(half).reshape(blocks, BLK, width_here),
        adapter_weight.reshape(width_here, groups, cols),
        preferred_element_type=full,
    ).astype(half)
    sh_parts = jnp.swapaxes(sh_rows.reshape(blocks, rows, groups, cols), 1, 2)
    sq_parts = jnp.zeros((8, cols), half).at[:3, :tokens].set(three_parts(squares))
    message = jnp.concatenate(
        [
            parts,
            sh_parts,
            jnp.broadcast_to(sq_parts[None, None], (blocks, groups) + sq_parts.shape),
        ],
        axis=2,
    )
    message = exchange(message.reshape(n_mp, BLK + rows + 8, cols), "mp")
    token_proj = jnp.sum(message[:, :BLK].astype(full), axis=0)
    sh_here = message[:, BLK : BLK + rows].reshape(BLK, cols)
    squares_all = jnp.sum(message[:, BLK + rows : BLK + rows + 3].astype(full), axis=(0, 1))[:tokens]
    inverse_rms = lax.rsqrt(squares_all / width_full + epsilon)

    slots_block = token_slot.reshape(blocks, BLK)
    onehot = slots_block[:, None, :] == jnp.arange(BLK, dtype=jnp.int32)[None, :, None]
    counts = jnp.maximum(jnp.sum(onehot.astype(full), axis=2), 1.0)
    onehot = onehot.astype(half)
    my_block = mp // groups
    inv_block = lax.dynamic_index_in_dim(inverse_rms.reshape(blocks, BLK), my_block, 0, False)
    onehot_block = lax.dynamic_index_in_dim(onehot, my_block, 0, False)
    counts_block = lax.dynamic_index_in_dim(counts, my_block, 0, False)
    placed = jnp.dot(
        onehot_block, (token_proj * inv_block[:, None]).astype(half), preferred_element_type=full
    )
    placed = (placed / counts_block[:, None]).astype(half).astype(full)
    state_here = (sh_here.astype(full) + placed).astype(half)
    state = share(state_here, "mp")
    state = state.reshape(blocks, groups, n_mp, rows, cols)
    state = jnp.transpose(state, (2, 0, 3, 1, 4)).reshape(tokens, student_width)

    normed = (gained_hidden * inverse_rms[:, None]).astype(half).reshape(blocks, BLK, width_here)
    pooled = jnp.einsum("krt,ktd->krd", onehot, normed, preferred_element_type=full)
    pooled = (pooled / counts[:, :, None]).astype(half)
    pooled = jnp.swapaxes(pooled.reshape(blocks, n_mp, rows, width_here), 0, 1)
    pooled_all = lax.all_gather(pooled.reshape(1, n_mp, mine_rows, width_here), "dp", axis=0, tiled=True)
    pooled_all = jnp.swapaxes(pooled_all, 0, 1).reshape(n_dp * tokens, width_here)

    wide = state.astype(full)
    inverse = lax.rsqrt(jnp.mean(wide * wide, axis=-1, keepdims=True) + epsilon)
    normed_student = (wide * inverse * student_gain).astype(half)
    dh = jnp.dot(dy, down_weight, preferred_element_type=full)
    gate = jnp.dot(normed_student, gate_weight, preferred_element_type=full)
    up = jnp.dot(normed_student, up_weight, preferred_element_type=full)
    sigma = jax.nn.sigmoid(gate)
    silu = gate * sigma
    act = (silu * up).astype(half)
    grad_gate = (dh * up * sigma * (1.0 + gate * (1.0 - sigma))).astype(half)
    grad_up = (dh * silu).astype(half)
    dn = (times_rows(grad_gate, gate_weight) + times_rows(grad_up, up_weight)).astype(half)
    output = times_rows(act, down_weight).astype(half)
    both = jnp.stack(
        [
            dn.reshape(n_mp, mine_rows, student_width),
            output.reshape(n_mp, mine_rows, student_width),
        ],
        axis=1,
    )
    both = jnp.sum(exchange(both, "mp").astype(full), axis=0)
    state_rows = lax.dynamic_slice_in_dim(state, mp * mine_rows, mine_rows, 0).astype(full)
    inv_rows = lax.dynamic_slice_in_dim(inverse, mp * mine_rows, mine_rows, 0)
    gained = student_gain * both[0]
    dx = dy_rows.astype(full) + inv_rows * gained
    dx = dx - state_rows * inv_rows**3 * jnp.mean(gained * state_rows, axis=-1, keepdims=True)
    dproj = jnp.swapaxes(dx.astype(half).reshape(mine_rows, n_dp, out_cols), 0, 1)
    dproj = share(exchange(dproj, "dp"), "mp")
    adapter_grad = lax.dot_general(
        pooled_all,
        dproj.reshape(n_dp * tokens, out_cols),
        (((0,), (0,)), ((), ())),
        preferred_element_type=full,
    )

    out_rows = (state_rows + both[1]).astype(half)
    back = lax.all_gather(
        out_rows.reshape(blocks, rows, student_width), "dp", axis=0, tiled=True
    )
    mine = block_owner == dp
    picks = []
    for slot in range(slots):
        chosen = mine & (ranks == slot)
        index = jnp.sum(jnp.where(chosen, jnp.arange(chosen.shape[0], dtype=jnp.int32), 0))
        piece = lax.dynamic_index_in_dim(back, index, 0, False)
        picks.append(jnp.where(jnp.any(chosen), piece, jnp.zeros((), half)))
    student_out = jnp.stack(picks, axis=1)
    return (student_out[None], adapter_grad)


def solution(mesh):
    return jax.shard_map(
        on_device,
        mesh=mesh,
        in_specs=(
            P("dp", "mp"),
            P("mp", None),
            P("dp", "mp"),
            P("mp"),
            P("mp", None),
            P("dp"),
            P(),
            P("dp", "mp", None, None),
            P("dp", "mp", None, None),
            P(),
            P(None, "mp"),
            P(None, "mp"),
            P(None, "mp"),
        ),
        out_specs=(P("dp", "mp", None, None), P("mp", "dp")),
        check_vma=False,
    )
```

time: 588 us -> 295 us (0.50)
  waiting for transfers between devices: 440 us -> 142 us
  blocking collectives: 55.4 us -> 23.2 us
  starting transfers between devices: 4.72 us -> 34.4 us
  matrix products: 37.3 us -> 17.5 us
  other arithmetic: 9.97 us -> 23 us
  between operations: 15.1 us -> 25.3 us
    unnamed x9 -> x4, waiting for transfers between devices: 155 us -> 0.08 us
    psum x1 -> x0, waiting for transfers between devices: 82.5 us -> none  [on_device(): lax.psum(jnp.einsum('rkd,de->rke', pooled, adapter_weight, preferred_elem...]
    reduce_scatter x1 -> x0, waiting for transfers between devices: 79.7 us -> none  [on_device(): lax.psum_scatter(partial_heads.astype(jnp.bfloat16), 'mp', scatter_dimens...]
    all_to_all x1 -> x5, waiting for transfers between devices: 13 us -> 89.8 us  [exchange(): return lax.all_to_all(pieces, axis, split_axis=0, concat_axis=0, tiled=True)]
    all_gather x3 -> x4, waiting for transfers between devices: 110 us -> 51.9 us  [the longest x2 26.5 us: fetch(): everyone = lax.all_gather(by_slot, 'dp', axis=0, tiled=True)]
    psum x1 -> x0, blocking collectives: 38.1 us -> none  [on_device(): squares = lax.psum(jnp.sum(hidden * hidden, axis=1), 'mp')]
    all_to_all x1 -> x5, starting transfers between devices: 4.25 us -> 34.3 us  [exchange(): return lax.all_to_all(pieces, axis, split_axis=0, concat_axis=0, tiled=True)]
    dot_general x13 -> x10, matrix products: 37.3 us -> 17.5 us  [the longest x1 4.2 us: on_device(): lax.dot_general(pooled_all, dproj.reshape(n_dp * tokens, out_cols), (((0,...]
  transfers between devices with their start and end apart: 8 -> 9, of which waited for: 8 -> 6; matrix products, arithmetic and copies ran while one was open for 3% -> 9% of each run, Pallas kernels for 0% -> 2%
where the time goes in v1:
time: 295 us; the launch traced here: 293 us
  waiting for transfers between devices  142 us (48%)
  starting transfers between devices  34.4 us (12%)
  between operations  25.3 us (9%)
  blocking collectives  23.2 us (8%)
  other arithmetic  23 us (8%)
  local copies, waits for them, and re-layouts  22.2 us (8%)
  matrix products  17.5 us (6%)
  Pallas kernels  5.55 us (2%)
    all_to_all x5, waiting for transfers between devices, exchange(): return lax.all_to_all(pieces, axis, split_axis=0, concat_axis=0, tiled=True)  89.8 us
    all_to_all x5, starting transfers between devices, exchange(): return lax.all_to_all(pieces, axis, split_axis=0, concat_axis=0, tiled=True)  34.3 us
    all_gather x2, waiting for transfers between devices, fetch(): everyone = lax.all_gather(by_slot, 'dp', axis=0, tiled=True)  26.5 us
    all_gather x1, waiting for transfers between devices, on_device(): dy = lax.all_gather(dy_rows, 'mp', axis=0, tiled=True)  25.3 us
    unnamed x45, local copies, waits for them, and re-layouts  13.4 us
    all_gather x1, blocking collectives, on_device(): lax.all_gather(out_rows.reshape(blocks, rows, student_width), 'dp', axis=...  13.4 us
    all_to_all x1, blocking collectives, exchange(): return lax.all_to_all(pieces, axis, split_axis=0, concat_axis=0, tiled=True)  9.85 us
  transfers between devices with their start and end apart: 9, of which 6 were waited for; matrix products, arithmetic and copies ran while one was open for 9% of the time, Pallas kernels for 2%

profile of v1, /device:TPU:0, one launch (start us, length us, event | category | flops | bytes accessed | tf_op | source)
XLA Modules:
  0.0 293.0 jit_solution(7246233596216023558)
XLA Ops:
  7.2 1.8 copy.78
  9.1 3.4 %copy-done.2 = bf16[512,8192]{1,0:T(8,128)(2,1)S(1)} copy-done((bf16[512,8192]{1,0:T(8,128)(2,1)S(1)}, bf16[512,8192]{1,0:T(8,128)(2,1)}, u32[]{:S(2)}) %copy-start.2) | copy-done | bytes 8388632
  13.4 5.6 %shard_map.140 = bf16[16,256,512]{2,1,0:T(8,128)(2,1)S(1)} custom-call(bf16[256,512]{1,0:T(8,128)(2,1)S(1)} %copy-done.3, bf16[512,8192]{1,0:T(8,128)(2,1)S(1)} %copy-done.2), custom_call_target="tpu_custom_call" | custom-call | flops 2147483648 | bytes 12582912 | tf_op jit(solution)/shard_map/pallas_call | solution.py:41
  19.0 2.0 copy-done.1
  20.9 8.3 %all-to-all-start = ((bf16[16,256,512]{2,1,0:T(8,128)(2,1)}), bf16[16,256,512]{2,1,0:T(8,128)(2,1)}, u32[]{:S(2)}, u32[]{:S(2)}) async-start(bf16[16,256,512]{2,1,0:T(8,128)(2,1)} %copy-done.1), calls=%async_computation | async-start | bytes 8388608 | tf_op jit(solution)/shard_map/all_to_all | solution.py:15
  29.3 1.7 copy.77
  37.4 26.5 %all-gather.7.cloned.1.call-done = bf16[32,8,3072]{2,1,0:T(8,128)(2,1)} async-done(((bf16[4,8,3072]{2,1,0:T(8,128)(2,1)}), bf16[32,8,3072]{2,1,0:T(8,128)(2,1)}) %all-gather.7.cloned.1.call-update) | async-done | bytes 1572880 | tf_op jit(solution)/shard_map/all_gather | solution.py:96
  65.5 26.7 %all-to-all-done = bf16[16,256,512]{2,1,0:T(8,128)(2,1)} async-done(((bf16[16,256,512]{2,1,0:T(8,128)(2,1)}), bf16[16,256,512]{2,1,0:T(8,128)(2,1)}, u32[]{:S(2)}, u32[]{:S(2)}) %all-to-all-start) | async-done | bytes 4194336 | tf_op jit(solution)/shard_map/all_to_all | solution.py:15
  92.2 3.0 %convert_reduce_fusion = f32[256,512]{1,0:T(8,128)S(1)} fusion(bf16[16,256,512]{2,1,0:T(8,128)(2,1)} %all-to-all-done), kind=kLoop, calls=%fused_computation | loop fusion | flops 4063232 | bytes 4718592 | tf_op jit(solution)/shard_map/reduce_sum | solution.py:106
  96.5 1.4 pad_maximum_fusion.1
  97.9 10.2 %all-to-all-start.1 = ((bf16[16,144,384]{2,1,0:T(8,128)(2,1)}), bf16[16,144,384]{2,1,0:T(8,128)(2,1)}, u32[]{:S(2)}, u32[]{:S(2)}) async-start(bf16[16,144,384]{2,1,0:T(8,128)(2,1)} %bitcast.131), calls=%async_computation.1 | async-start | bytes 3538944 | tf_op jit(solution)/shard_map/all_to_all | solution.py:15
  109.5 22.9 %all-to-all-done.1 = bf16[16,144,384]{2,1,0:T(8,128)(2,1)} async-done(((bf16[16,144,384]{2,1,0:T(8,128)(2,1)}), bf16[16,144,384]{2,1,0:T(8,128)(2,1)}, u32[]{:S(2)}, u32[]{:S(2)}) %all-to-all-start.1) | async-done | bytes 1769504 | tf_op jit(solution)/shard_map/all_to_all | solution.py:15
  134.0 1.6 convert_reduce_fusion.2
  135.6 1.1 fusion.15
  136.8 1.4 broadcast_in_dim.24
  138.1 4.9 %all-to-all-start.2 = ((bf16[16,128,384]{2,1,0:T(8,128)(2,1)}), bf16[16,128,384]{2,1,0:T(8,128)(2,1)}, u32[]{:S(2)}, u32[]{:S(2)}) async-start(bf16[16,128,384]{2,1,0:T(8,128)(2,1)} %broadcast_in_dim.24), calls=%async_computation.2 | async-start | bytes 3145728 | tf_op jit(solution)/shard_map/all_to_all | solution.py:15
  143.0 25.3 %all-gather.9.cloned.1.call-done = bf16[256,3072]{1,0:T(8,128)(2,1)} async-done(((bf16[16,3072]{1,0:T(8,128)(2,1)}), bf16[256,3072]{1,0:T(8,128)(2,1)}) %all-gather.9.cloned.1.call-update) | async-done | bytes 1572880 | tf_op jit(solution)/shard_map/all_gather | solution.py:103
  168.3 3.2 %fusion.59 = f32[256,512]{1,0:T(8,128)} fusion(bf16[256,3072]{1,0:T(8,128)(2,1)} %all-gather.9.cloned.1.call-done, bf16[3072,512]{1,0:T(8,128)(2,1)S(1)} %copy-done), kind=kOutput, calls=%fused_computation.125 | convolution fusion | flops 805306368 | bytes 5242880 | tf_op jit(solution)/shard_map/dot_general | solution.py:158
  171.5 2.9 copy.50
  174.4 1.8 multiply_reduce_fusion
  176.2 1.5 copy.63
  178.0 3.5 %fusion.17 = f32[256,512]{1,0:T(8,128)S(1)} fusion(bf16[3072,512]{1,0:T(8,128)(2,1)} %param.25, bf16[256,3072]{1,0:T(8,128)(2,1)} %bitcast.134, f32[3072]{0:T(1024)S(1)} %copy-done.11, f32[256]{0:T(256)S(1)} %rsqrt.28), kind=kOutput, calls=%fused_computation.35 | convolution fusion | flops 808452096 | bytes 5256192 | tf_op jit(solution)/shard_map/dot_general | solution.py:159
  187.0 2.0 pad_maximum_fusion
  189.0 6.5 %all-to-all-start.3 = ((bf16[16,2,16,3072]{3,2,1,0:T(8,128)(2,1)}), bf16[16,2,16,3072]{3,2,1,0:T(8,128)(2,1)}, u32[]{:S(2)}, u32[]{:S(2)}) async-start(bf16[16,2,16,3072]{3,2,1,0:T(8,128)(2,1)} %pad_maximum_fusion), calls=%async_computation.3 | async-start | bytes 6291456 | tf_op jit(solution)/shard_map/all_to_all | solution.py:15
  197.8 40.2 %all-to-all-done.3 = bf16[16,2,16,3072]{3,2,1,0:T(8,128)(2,1)} async-done(((bf16[16,2,16,3072]{3,2,1,0:T(8,128)(2,1)}), bf16[16,2,16,3072]{3,2,1,0:T(8,128)(2,1)}, u32[]{:S(2)}, u32[]{:S(2)}) %all-to-all-start.3) | async-done | bytes 3145760 | tf_op jit(solution)/shard_map/all_to_all | solution.py:15
  238.0 2.5 convert_reduce_fusion.1
  242.6 9.9 %all_to_all.30 = bf16[8,16,384]{2,1,0:T(8,128)(2,1)S(1)} all-to-all(bf16[8,16,384]{2,1,0:T(8,128)(2,1)S(1)} %copy.58), channel_id=1, replica_groups=mesh['dp'=8,'mp'=16] {'dp'}, dimensions={0} | all-to-all | bytes 196608 | tf_op jit(solution)/shard_map/all_to_all | solution.py:15
  252.5 1.4 broadcast_in_dim.27
  253.8 4.4 %all-to-all-start.5 = ((bf16[16,8,16,384]{3,2,1,0:T(8,128)(2,1)}), bf16[16,8,16,384]{3,2,1,0:T(8,128)(2,1)}, u32[]{:S(2)}, u32[]{:S(2)}) async-start(bf16[16,8,16,384]{3,2,1,0:T(8,128)(2,1)} %broadcast_in_dim.27), calls=%async_computation.5 | async-start | bytes 3145728 | tf_op jit(solution)/shard_map/all_to_all | solution.py:15
  265.3 13.4 %all_gather.18 = bf16[16,8,3072]{2,1,0:T(8,128)(2,1)S(1)} all-gather(bf16[2,8,3072]{2,1,0:T(8,128)(2,1)S(1)} %get-tuple-element.32), channel_id=1, replica_groups=mesh['dp'=8,'mp'=16] {'dp'}, dimensions={0}, use_global_device_ids=true | all-gather | bytes 884736 | tf_op jit(solution)/shard_map/all_gather | solution.py:191
  278.7 2.6 select_bitcast_fusion.3
  282.2 4.2 %fusion.7 = f32[512,384]{1,0:T(8,128)} fusion(bf16[16,8,16,384]{3,2,1,0:T(8,128)(2,1)} %all-to-all-done.5, bf16[8,16,16,512]{3,2,0,1:T(8,128)(2,1)} %all-gather.11.cloned.1.call-done), kind=kOutput, calls=%fused_computation.17 | convolution fusion | flops 805306368 | bytes 4456448 | tf_op jit(solution)/shard_map/dot_general | solution.py:183
  (92 shorter events, 20.1 us)
Async XLA Ops:
  7.2 161.2 %copy-start = (bf16[3072,512]{1,0:T(8,128)(2,1)S(1)}, bf16[3072,512]{1,0:T(8,128)(2,1)}, u32[]{:S(2)}) copy-start(bf16[3072,512]{1,0:T(8,128)(2,1)} %param.27) | copy-start | bytes 9437188
  7.2 30.2 %all-gather.5.cloned.1.call-start = ((), (), s32[]{:S(2)}) async-start(), calls=%async_computation.6 | async-start | bytes 1769472 | tf_op jit(solution)/shard_map/all_gather | solution.py:96
  9.1 3.4 %copy-start.2 = (bf16[512,8192]{1,0:T(8,128)(2,1)S(1)}, bf16[512,8192]{1,0:T(8,128)(2,1)}, u32[]{:S(2)}) copy-start(bf16[512,8192]{1,0:T(8,128)(2,1)} %right.1) | copy-start | bytes 25165828
  12.4 0.9 copy-start.3
  19.0 2.0 copy-start.1
  20.9 10.1 %copy-start.13 = (s32[16]{0:T(128)S(1)}, s32[16]{0:T(128)}, u32[]{:S(2)}) copy-start(s32[16]{0:T(128)} %param.21) | copy-start | bytes 196
  20.9 71.3 %all-to-all-start = ((bf16[16,256,512]{2,1,0:T(8,128)(2,1)}), bf16[16,256,512]{2,1,0:T(8,128)(2,1)}, u32[]{:S(2)}, u32[]{:S(2)}) async-start(bf16[16,256,512]{2,1,0:T(8,128)(2,1)} %copy-done.1), calls=%async_computation | async-start | bytes 8388608 | tf_op jit(solution)/shard_map/all_to_all | solution.py:15
  29.3 65.9 %copy-start.9 = (bf16[256,512]{1,0:T(8,128)(2,1)S(1)}, bf16[256,512]{1,0:T(8,128)(2,1)}, u32[]{:S(2)}) copy-start(bf16[256,512]{1,0:T(8,128)(2,1)} %param.17) | copy-start | bytes 786436
  29.3 65.9 %copy-start.12 = (f32[512]{0:T(512)S(1)}, f32[512]{0:T(512)}, u32[]{:S(2)}) copy-start(f32[512]{0:T(512)} %param.18) | copy-start | bytes 6148
  29.3 34.7 %all-gather.7.cloned.1.call-start = ((), (), s32[]{:S(2)}) async-start(), calls=%async_computation.7 | async-start | bytes 1769472 | tf_op jit(solution)/shard_map/all_gather | solution.py:96
  92.2 3.2 %copy-start.19 = (bf16[512,3072]{1,0:T(8,128)(2,1)S(1)}, bf16[512,3072]{1,0:T(8,128)(2,1)}, u32[]{:S(2)}) copy-start(bf16[512,3072]{1,0:T(8,128)(2,1)} %param.19) | copy-start | bytes 9437188
  95.2 1.2 copy-start.4
  95.4 1.1 copy-start.10
  96.5 12.4 %copy-start.15 = (s32[256]{0:T(256)S(1)}, s32[256]{0:T(256)}, u32[]{:S(2)}) copy-start(s32[256]{0:T(256)} %param.20) | copy-start | bytes 3076
  97.9 34.6 %all-to-all-start.1 = ((bf16[16,144,384]{2,1,0:T(8,128)(2,1)}), bf16[16,144,384]{2,1,0:T(8,128)(2,1)}, u32[]{:S(2)}, u32[]{:S(2)}) async-start(bf16[16,144,384]{2,1,0:T(8,128)(2,1)} %bitcast.131), calls=%async_computation.1 | async-start | bytes 3538944 | tf_op jit(solution)/shard_map/all_to_all | solution.py:15
  108.1 60.2 %all-gather.9.cloned.1.call-start = ((), (), s32[]{:S(2)}) async-start(), calls=%async_computation.8 | async-start | bytes 1671168 | tf_op jit(solution)/shard_map/all_gather | solution.py:103
  109.0 29.1 %copy-start.17 = (f32[2,128]{1,0:T(2,128)}, f32[2,128]{1,0:T(2,128)S(1)}, u32[]{:S(2)}) copy-start(f32[2,128]{1,0:T(2,128)S(1)} %broadcast_maximum_fusion) | copy-start | bytes 3076
  138.1 33.4 %all-to-all-start.2 = ((bf16[16,128,384]{2,1,0:T(8,128)(2,1)}), bf16[16,128,384]{2,1,0:T(8,128)(2,1)}, u32[]{:S(2)}, u32[]{:S(2)}) async-start(bf16[16,128,384]{2,1,0:T(8,128)(2,1)} %broadcast_in_dim.24), calls=%async_computation.2 | async-start | bytes 3145728 | tf_op jit(solution)/shard_map/all_to_all | solution.py:15
  174.4 3.6 %copy-start.11 = (f32[3072]{0:T(1024)S(1)}, f32[3072]{0:T(1024)}, u32[]{:S(2)}) copy-start(f32[3072]{0:T(1024)} %param.24) | copy-start | bytes 36868
  178.0 3.6 %copy-start.5 = (bf16[3072,512]{1,0:T(8,128)(2,1)S(1)}, bf16[3072,512]{1,0:T(8,128)(2,1)}, u32[]{:S(2)}) copy-start(bf16[3072,512]{1,0:T(8,128)(2,1)} %param.26) | copy-start | bytes 9437188
  178.0 3.8 %copy-start.8 = (bf16[32,8,8,384]{3,1,2,0:T(8,128)(2,1)S(1)}, bf16[32,8,8,384]{3,1,2,0:T(8,128)(2,1)}, u32[]{:S(2)}) copy-start(bf16[32,8,8,384]{3,1,2,0:T(8,128)(2,1)} %copy.63) | copy-start | bytes 4718596
  182.8 1.9 copy-start.6
  182.8 2.0 copy-start.7
  188.9 6.6 %copy-start.14 = (f32[256]{0:T(256)S(1)}, f32[256]{0:T(256)}, u32[]{:S(2)}) copy-start(f32[256]{0:T(256)} %get-tuple-element.43) | copy-start | bytes 3076
  188.9 7.7 %copy-start.16 = (s32[256]{0:T(256)S(1)}, s32[256]{0:T(256)}, u32[]{:S(2)}) copy-start(s32[256]{0:T(256)} %param.20) | copy-start | bytes 3076
  189.0 7.7 %copy-start.18 = (f32[2,128]{1,0:T(2,128)S(1)}, f32[2,128]{1,0:T(2,128)}, u32[]{:S(2)}) copy-start(f32[2,128]{1,0:T(2,128)} %copy-done.17) | copy-start | bytes 3076
  189.0 49.0 %all-to-all-start.3 = ((bf16[16,2,16,3072]{3,2,1,0:T(8,128)(2,1)}), bf16[16,2,16,3072]{3,2,1,0:T(8,128)(2,1)}, u32[]{:S(2)}, u32[]{:S(2)}) async-start(bf16[16,2,16,3072]{3,2,1,0:T(8,128)(2,1)} %pad_maximum_fusion), calls=%async_computation.3 | async-start | bytes 6291456 | tf_op jit(solution)/shard_map/all_to_all | solution.py:15
  195.4 86.7 %all-gather.11.cloned.1.call-start = ((), (), s32[]{:S(2)}) async-start(), calls=%async_computation.9 | async-start | bytes 2359296 | tf_op jit(solution)/shard_map/all_gather | solution.py:152
  253.8 28.4 %all-to-all-start.5 = ((bf16[16,8,16,384]{3,2,1,0:T(8,128)(2,1)}), bf16[16,8,16,384]{3,2,1,0:T(8,128)(2,1)}, u32[]{:S(2)}, u32[]{:S(2)}) async-start(bf16[16,8,16,384]{3,2,1,0:T(8,128)(2,1)} %broadcast_in_dim.27), calls=%async_computation.5 | async-start | bytes 3145728 | tf_op jit(solution)/shard_map/all_to_all | solution.py:15
Sparse Core Ops, SparseCore 0:
  10.3 26.9 all-gather.4
  39.5 24.3 all-gather.6
  111.7 56.5 all-gather.8
  198.2 26.6 all-gather.10

commit v2 on v1

--- a/solution.py
+++ b/solution.py
@@ -31,29 +31,152 @@
     return lax.dot_general(left, right, (((1,), (1,)), ((), ())), preferred_element_type=full)
 
 
-def piece_kernel(left, right, out):
+SIDE = 4
+
+
+def step(value, along_y, along_z):
+    pairs = []
+    for y in range(SIDE):
+        for z in range(SIDE):
+            to = ((y + along_y) % SIDE) * SIDE + (z + along_z) % SIDE
+            pairs.append((y * SIDE + z, to))
+    return lax.ppermute(value, "mp", pairs)
+
+
+def piece_kernel(ids, left, right, out):
     out[0] = jnp.dot(left[...], right[...], preferred_element_type=full).astype(out.dtype)
 
 
-def product_in_pieces(left, right, pieces):
-    rows, depth = left.shape
-    width = right.shape[1] // pieces
+def product_pieces(left, right, block, ids, width):
+    depth = left.shape[1]
+    count = ids.shape[0]
     return pl.pallas_call(
         piece_kernel,
-        grid=(pieces,),
-        in_specs=[
-            pl.BlockSpec((rows, depth), lambda i: (0, 0)),
-            pl.BlockSpec((depth, width), lambda i: (0, i)),
-        ],
-        out_specs=pl.BlockSpec((1, rows, width), lambda i: (i, 0, 0)),
-        out_shape=jax.ShapeDtypeStruct((pieces, rows, width), half),
+        grid_spec=pltpu.PrefetchScalarGridSpec(
+            num_scalar_prefetch=1,
+            grid=(count,),
+            in_specs=[
+                pl.BlockSpec((BLK, depth), lambda i, ids: (block, 0)),
+                pl.BlockSpec((depth, width), lambda i, ids: (0, ids[i])),
+            ],
+            out_specs=pl.BlockSpec((1, BLK, width), lambda i, ids: (i, 0, 0)),
+        ),
+        out_shape=jax.ShapeDtypeStruct((count, BLK, width), half),
+        compiler_params=pltpu.CompilerParams(vmem_limit_bytes=48 * 1024 * 1024),
+        cost_estimate=pl.CostEstimate(
+            flops=2 * BLK * depth * width * count,
+            bytes_accessed=2 * (depth + BLK) * width * count,
+            transcendentals=0,
+        ),
+    )(ids, left, right)
+
+
+def total(values):
+    result = values[0].astype(full)
+    for value in values[1:]:
+        result = result + value.astype(full)
+    return result
+
+
+def teacher_terms(attention, out_proj, mp):
+    y, z = mp // SIDE, mp % SIDE
+    width = attention.shape[1]
+    along = jnp.arange(SIDE, dtype=jnp.int32)
+    kept, moved = {}, {}
+    for distance in (2, 1, 3, 0):
+        for block in (0, 1):
+            if block == 0:
+                ids = ((y + distance) % SIDE) * SIDE + along
+            else:
+                ids = along * SIDE + (z + distance) % SIDE
+            terms = product_pieces(attention, out_proj, block, ids.astype(jnp.int32), width)
+            if distance == 0:
+                kept[block] = terms
+            else:
+                moved[block, distance] = (
+                    step(terms, distance, 0) if block == 0 else step(terms, 0, distance)
+                )
+    results = []
+    for block in (0, 1):
+        here = z if block == 0 else y
+        arrays = [kept[block]] + [moved[block, distance] for distance in (2, 1, 3)]
+
+        def piece(distance):
+            at = (here + distance) % SIDE
+            return total([lax.dynamic_index_in_dim(a, at, 0, False) for a in arrays])
+
+        arrived = []
+        for distance in (2, 1, 3):
+            sent = piece(distance).astype(half)
+            arrived.append(step(sent, 0, distance) if block == 0 else step(sent, distance, 0))
+        results.append(piece(0) + total(arrived))
+    return results
+
+
+def normalise_kernel(pieces, gain, state, normed):
+    groups = state.shape[1] // pieces.shape[2]
+    cols = pieces.shape[2]
+    for block in range(state.shape[0] // BLK):
+        rows = pl.ds(block * BLK, BLK)
+        squares = jnp.zeros((BLK, 128), full)
+        for group in range(groups):
+            value = pieces[block * groups + group]
+            state[rows, pl.ds(group * cols, cols)] = value
+            wide = value.astype(full)
+            wide = wide * wide
+            for lane in range(0, cols, 128):
+                squares = squares + wide[:, lane : lane + 128]
+        mean = jnp.sum(squares, axis=1, keepdims=True) / state.shape[1]
+        inverse = lax.rsqrt(mean + epsilon)
+        for group in range(groups):
+            at = pl.ds(group * cols, cols)
+            wide = pieces[block * groups + group].astype(full)
+            normed[rows, at] = (wide * inverse * gain[:, at]).astype(normed.dtype)
+
+
+def normalise(pieces, gain, rows, width):
+    whole = pl.BlockSpec(memory_space=pltpu.VMEM)
+    shape = jax.ShapeDtypeStruct((rows, width), half)
+    return pl.pallas_call(
+        normalise_kernel,
+        in_specs=[whole, whole],
+        out_specs=[whole, whole],
+        out_shape=[shape, shape],
         compiler_params=pltpu.CompilerParams(vmem_limit_bytes=16 * 1024 * 1024),
         cost_estimate=pl.CostEstimate(
-            flops=2 * rows * depth * width * pieces,
-            bytes_accessed=2 * (depth + rows) * width * pieces,
-            transcendentals=0,
-        ),
-    )(left, right)
+            flops=6 * rows * width, bytes_accessed=6 * rows * width, transcendentals=rows
+        ),
+    )(pieces, gain[None])
+
+
+def slope_kernel(terms, dy, state, gain, out):
+    rows, width = dy.shape
+    cols = out.shape[2]
+    wide = state[...].astype(full)
+    inverse = lax.rsqrt(jnp.mean(wide * wide, axis=1, keepdims=True) + epsilon)
+    dn = terms[0].astype(full)
+    for source in range(1, terms.shape[0]):
+        dn = dn + terms[source].astype(full)
+    gained = gain[...] * dn
+    mean = jnp.mean(gained * wide, axis=1, keepdims=True)
+    dx = dy[...].astype(full) + inverse * gained - wide * (inverse * inverse * inverse) * mean
+    for group in range(out.shape[0]):
+        out[group] = dx[:, group * cols : (group + 1) * cols].astype(out.dtype)
+
+
+def slope(terms, dy, state, gain, groups):
+    rows, width = dy.shape
+    whole = pl.BlockSpec(memory_space=pltpu.VMEM)
+    return pl.pallas_call(
+        slope_kernel,
+        in_specs=[whole] * 4,
+        out_specs=whole,
+        out_shape=jax.ShapeDtypeStruct((groups, rows, width // groups), half),
+        compiler_params=pltpu.CompilerParams(vmem_limit_bytes=16 * 1024 * 1024),
+        cost_estimate=pl.CostEstimate(
+            flops=30 * rows * width, bytes_accessed=40 * rows * width, transcendentals=rows
+        ),
+    )(terms, dy, state, gain[None])
 
 
 def on_device(
@@ -91,19 +214,24 @@
     place = block_owner * slots + ranks
     my_place = lax.dynamic_slice_in_dim(place, dp * blocks, blocks)
 
-    def fetch(array):
-        by_slot = jnp.swapaxes(array[0], 0, 1)
-        everyone = lax.all_gather(by_slot, "dp", axis=0, tiled=True)
-        return jnp.stack(
-            [lax.dynamic_index_in_dim(everyone, my_place[k], 0, False) for k in range(blocks)]
-        )
-
-    sh_rows = fetch(student_hidden)
-    dy_rows = fetch(cotangent).reshape(mine_rows, student_width)
-    dy = lax.all_gather(dy_rows, "mp", axis=0, tiled=True)
-
-    terms = product_in_pieces(attention, out_proj, n_mp)
-    hidden = residual.astype(full) + jnp.sum(exchange(terms, "mp").astype(full), axis=0)
+    both = jnp.concatenate(
+        [jnp.swapaxes(student_hidden[0], 0, 1), jnp.swapaxes(cotangent[0], 0, 1)], axis=0
+    )
+    everyone = lax.all_gather(both, "dp", axis=0, tiled=False)
+
+    def fetch(offset):
+        picked = []
+        for k in range(blocks):
+            at = (my_place[k] // slots, my_place[k] % slots + offset, 0, 0)
+            piece = lax.dynamic_slice(everyone, at, (1, 1, rows, student_width))
+            picked.append(piece.reshape(rows, student_width))
+        return jnp.stack(picked)
+
+    sh_rows = fetch(0)
+    dy = lax.all_gather(fetch(slots), "mp", axis=0, tiled=False)
+    dy = jnp.swapaxes(dy, 0, 1).reshape(tokens, student_width)
+
+    hidden = residual.astype(full) + jnp.concatenate(teacher_terms(attention, out_proj, mp), axis=0)
     squares = jnp.sum(hidden * hidden, axis=1)
     gained_hidden = hidden * final_gain
     parts = jnp.einsum(
@@ -141,20 +269,14 @@
     )
     placed = (placed / counts_block[:, None]).astype(half).astype(full)
     state_here = (sh_here.astype(full) + placed).astype(half)
-    state = share(state_here, "mp")
-    state = state.reshape(blocks, groups, n_mp, rows, cols)
-    state = jnp.transpose(state, (2, 0, 3, 1, 4)).reshape(tokens, student_width)
+    state, normed_student = normalise(share(state_here, "mp"), student_gain, tokens, student_width)
 
     normed = (gained_hidden * inverse_rms[:, None]).astype(half).reshape(blocks, BLK, width_here)
     pooled = jnp.einsum("krt,ktd->krd", onehot, normed, preferred_element_type=full)
     pooled = (pooled / counts[:, :, None]).astype(half)
-    pooled = jnp.swapaxes(pooled.reshape(blocks, n_mp, rows, width_here), 0, 1)
-    pooled_all = lax.all_gather(pooled.reshape(1, n_mp, mine_rows, width_here), "dp", axis=0, tiled=True)
+    pooled_all = lax.all_gather(pooled.reshape(n_mp, mine_rows, width_here), "dp", axis=0, tiled=False)
     pooled_all = jnp.swapaxes(pooled_all, 0, 1).reshape(n_dp * tokens, width_here)
 
-    wide = state.astype(full)
-    inverse = lax.rsqrt(jnp.mean(wide * wide, axis=-1, keepdims=True) + epsilon)
-    normed_student = (wide * inverse * student_gain).astype(half)
     dh = jnp.dot(dy, down_weight, preferred_element_type=full)
     gate = jnp.dot(normed_student, gate_weight, preferred_element_type=full)
     up = jnp.dot(normed_student, up_weight, preferred_element_type=full)
@@ -165,20 +287,17 @@
     grad_up = (dh * silu).astype(half)
     dn = (times_rows(grad_gate, gate_weight) + times_rows(grad_up, up_weight)).astype(half)
     output = times_rows(act, down_weight).astype(half)
-    both = jnp.stack(
-        [
-            dn.reshape(n_mp, mine_rows, student_width),
-            output.reshape(n_mp, mine_rows, student_width),
-        ],
-        axis=1,
-    )
-    both = jnp.sum(exchange(both, "mp").astype(full), axis=0)
-    state_rows = lax.dynamic_slice_in_dim(state, mp * mine_rows, mine_rows, 0).astype(full)
-    inv_rows = lax.dynamic_slice_in_dim(inverse, mp * mine_rows, mine_rows, 0)
-    gained = student_gain * both[0]
-    dx = dy_rows.astype(full) + inv_rows * gained
-    dx = dx - state_rows * inv_rows**3 * jnp.mean(gained * state_rows, axis=-1, keepdims=True)
-    dproj = jnp.swapaxes(dx.astype(half).reshape(mine_rows, n_dp, out_cols), 0, 1)
+    dn = exchange(dn.reshape(n_mp, mine_rows, student_width), "mp")
+    output = jnp.swapaxes(output.reshape(blocks, n_mp, rows, student_width), 0, 1)
+    output = jnp.sum(exchange(output, "mp").astype(full), axis=0)
+    here = mp * mine_rows
+    dproj = slope(
+        dn,
+        lax.dynamic_slice_in_dim(dy, here, mine_rows, 0),
+        lax.dynamic_slice_in_dim(state, here, mine_rows, 0),
+        student_gain,
+        n_dp,
+    )
     dproj = share(exchange(dproj, "dp"), "mp")
     adapter_grad = lax.dot_general(
         pooled_all,
@@ -187,10 +306,13 @@
         preferred_element_type=full,
     )
 
-    out_rows = (state_rows + both[1]).astype(half)
-    back = lax.all_gather(
-        out_rows.reshape(blocks, rows, student_width), "dp", axis=0, tiled=True
-    )
+    state_rows = lax.dynamic_slice_in_dim(
+        state.reshape(blocks, BLK, student_width), mp * rows, rows, 1
+    )
+    out_rows = (state_rows.astype(full) + output).astype(half)
+    out_rows = jnp.concatenate([out_rows, state_rows[:1]], axis=0)
+    back = lax.all_gather(out_rows, "dp", axis=0, tiled=False)[:, :blocks]
+    back = back.reshape(n_dp * blocks, rows, student_width)
     mine = block_owner == dp
     picks = []
     for slot in range(slots):

time: 295 us -> 283 us (0.959)
  waiting for transfers between devices: 142 us -> 107 us
  Pallas kernels: 5.55 us -> 38.1 us
  blocking collectives: 23.2 us -> 0 us
  starting transfers between devices: 34.4 us -> 47.9 us
    pallas_call x1 -> x10, Pallas kernels: 5.55 us -> 38.1 us  [the longest x8 33.5 us: product_pieces(): pl.pallas_call(piece_kernel, grid_spec=pltpu.PrefetchScalarGridSpec(num_s...]
    all_gather x4, waiting for transfers between devices: 51.9 us -> 27 us  [the longest x1 27 us: on_device(): dy = lax.all_gather(fetch(slots), 'mp', axis=0, tiled=False)]
    ppermute x0 -> x12, starting transfers between devices: none -> 20.2 us  [step(): return lax.ppermute(value, 'mp', pairs)]
    all_to_all x5 -> x6, waiting for transfers between devices: 89.8 us -> 74.9 us  [exchange(): return lax.all_to_all(pieces, axis, split_axis=0, concat_axis=0, tiled=True)]
    all_gather x1 -> x0, blocking collectives: 13.4 us -> none  [on_device(): lax.all_gather(out_rows.reshape(blocks, rows, student_width), 'dp', axis=...]
    all_to_all x1 -> x0, blocking collectives: 9.85 us -> none  [exchange(): return lax.all_to_all(pieces, axis, split_axis=0, concat_axis=0, tiled=True)]
    reduce_sum x4 -> x1, other arithmetic: 8.32 us -> 1.64 us  [on_device(): output = jnp.sum(exchange(output, 'mp').astype(full), axis=0)]
    all_to_all x5 -> x6, starting transfers between devices: 34.3 us -> 27.6 us  [exchange(): return lax.all_to_all(pieces, axis, split_axis=0, concat_axis=0, tiled=True)]
  transfers between devices with their start and end apart: 9 -> 22, of which waited for: 6 -> 8; matrix products, arithmetic and copies ran while one was open for 9% -> 13% of each run, Pallas kernels for 2% -> 13%
where the time goes in v2:
time: 283 us; the launch traced here: 281 us
  waiting for transfers between devices  107 us (38%)
  starting transfers between devices  47.9 us (17%)
  Pallas kernels  38.1 us (13%)
  between operations  26.7 us (9%)
  other arithmetic  22.1 us (8%)
  local copies, waits for them, and re-layouts  20 us (7%)
  matrix products  18.8 us (7%)
    all_to_all x6, waiting for transfers between devices, exchange(): return lax.all_to_all(pieces, axis, split_axis=0, concat_axis=0, tiled=True)  74.9 us
    pallas_call x8, Pallas kernels, product_pieces(): pl.pallas_call(piece_kernel, grid_spec=pltpu.PrefetchScalarGridSpec(num_s...  33.5 us
    all_to_all x6, starting transfers between devices, exchange(): return lax.all_to_all(pieces, axis, split_axis=0, concat_axis=0, tiled=True)  27.6 us
    all_gather x1, waiting for transfers between devices, on_device(): dy = lax.all_gather(fetch(slots), 'mp', axis=0, tiled=False)  27 us
    ppermute x12, starting transfers between devices, step(): return lax.ppermute(value, 'mp', pairs)  20.2 us
    unnamed x41, local copies, waits for them, and re-layouts  6.8 us
    dot_general x3, matrix products, times_rows(): lax.dot_general(left, right, (((1,), (1,)), ((), ())), preferred_element_...  6.57 us
  transfers between devices with their start and end apart: 22, of which 8 were waited for; matrix products, arithmetic and copies ran while one was open for 13% of the time, Pallas kernels for 13%

profile of v2, /device:TPU:0, one launch (start us, length us, event | category | flops | bytes accessed | tf_op | source)
XLA Modules:
  0.0 280.9 jit_solution(11412906254855069013)
XLA Ops:
  10.4 4.4 %shard_map.141 = bf16[4,128,512]{2,1,0:T(8,128)(2,1)} custom-call(s32[4]{0:T(128)S(1)} %iota_add_fusion.2.ids, bf16[256,512]{1,0:T(8,128)(2,1)S(1)} %copy-done.1, bf16[512,8192]{1,0:T(8,128)(2,1)} %right.15), custom_call_target="tpu_custom_call" | custom-call | flops 268435456 | bytes 2621440 | tf_op jit(solution)/shard_map/pallas_call | solution.py:53
  14.8 3.3 %collective-permute-start = (bf16[4,128,512]{2,1,0:T(8,128)(2,1)}, bf16[4,128,512]{2,1,0:T(8,128)(2,1)}, u32[]{:S(2)}, u32[]{:S(2)}) collective-permute-start(bf16[4,128,512]{2,1,0:T(8,128)(2,1)} %shard_map.141), channel_id=1, source_target_pairs={{0,8},{1,9},{2,10},{3,11},{4,12},{5,13},{6,14},{7,15},{8,0},{9,1},... | collective-permute-start | bytes 1572872 | tf_op jit(solution)/shard_map/ppermute | solution.py:43
  18.1 4.5 %shard_map.142 = bf16[4,128,512]{2,1,0:T(8,128)(2,1)} custom-call(s32[4]{0:T(128)S(1)} %iota_add_fusion.1.ids, bf16[256,512]{1,0:T(8,128)(2,1)S(1)} %copy-done.2, bf16[512,8192]{1,0:T(8,128)(2,1)} %right.15), custom_call_target="tpu_custom_call" | custom-call | flops 268435456 | bytes 2621440 | tf_op jit(solution)/shard_map/pallas_call | solution.py:53
  23.2 4.5 %shard_map.143 = bf16[4,128,512]{2,1,0:T(8,128)(2,1)} custom-call(s32[4]{0:T(128)S(1)} %iota_add_fusion.ids, bf16[256,512]{1,0:T(8,128)(2,1)S(1)} %copy-done.2, bf16[512,8192]{1,0:T(8,128)(2,1)} %right.15), custom_call_target="tpu_custom_call" | custom-call | flops 268435456 | bytes 2621440 | tf_op jit(solution)/shard_map/pallas_call | solution.py:53
  27.7 2.6 collective-permute-start.2
  30.3 4.5 %shard_map.145 = bf16[4,128,512]{2,1,0:T(8,128)(2,1)} custom-call(s32[4]{0:T(128)S(1)} %fusion.46.ids, bf16[256,512]{1,0:T(8,128)(2,1)S(1)} %copy-done.2, bf16[512,8192]{1,0:T(8,128)(2,1)} %right.15), custom_call_target="tpu_custom_call" | custom-call | flops 268435456 | bytes 2621440 | tf_op jit(solution)/shard_map/pallas_call | solution.py:53
  34.8 3.9 %collective-permute-start.6 = (bf16[4,128,512]{2,1,0:T(8,128)(2,1)}, bf16[4,128,512]{2,1,0:T(8,128)(2,1)}, u32[]{:S(2)}, u32[]{:S(2)}) collective-permute-start(bf16[4,128,512]{2,1,0:T(8,128)(2,1)} %shard_map.145), channel_id=1, source_target_pairs={{0,2},{1,3},{2,0},{3,1},{4,6},{5,7},{6,4},{7,5},{8,10},{9,11},{10,... | collective-permute-start | bytes 1572872 | tf_op jit(solution)/shard_map/ppermute | solution.py:43
  38.6 4.4 %shard_map.146 = bf16[4,128,512]{2,1,0:T(8,128)(2,1)} custom-call(s32[4]{0:T(128)S(1)} %fusion.45.ids, bf16[256,512]{1,0:T(8,128)(2,1)S(1)} %copy-done.2, bf16[512,8192]{1,0:T(8,128)(2,1)} %right.15), custom_call_target="tpu_custom_call" | custom-call | flops 268435456 | bytes 2621440 | tf_op jit(solution)/shard_map/pallas_call | solution.py:53
  44.3 4.5 %shard_map.147 = bf16[4,128,512]{2,1,0:T(8,128)(2,1)} custom-call(s32[4]{0:T(128)S(1)} %fusion.44.ids, bf16[256,512]{1,0:T(8,128)(2,1)S(1)} %copy-done.2, bf16[512,8192]{1,0:T(8,128)(2,1)} %right.15), custom_call_target="tpu_custom_call" | custom-call | flops 268435456 | bytes 2621440 | tf_op jit(solution)/shard_map/pallas_call | solution.py:53
  52.5 3.4 %shard_map.140 = bf16[4,128,512]{2,1,0:T(8,128)(2,1)S(1)} custom-call(s32[4]{0:T(128)S(1)} %iota_add_fusion.3.ids, bf16[256,512]{1,0:T(8,128)(2,1)S(1)} %copy-done.2, bf16[512,8192]{1,0:T(8,128)(2,1)} %right.15), custom_call_target="tpu_custom_call" | custom-call | flops 268435456 | bytes 2621440 | tf_op jit(solution)/shard_map/pallas_call | solution.py:53
  59.8 2.4 collective-permute-start.5
  62.2 3.4 %shard_map.144 = bf16[4,128,512]{2,1,0:T(8,128)(2,1)S(1)} custom-call(s32[4]{0:T(128)S(1)} %fusion.47.ids, bf16[256,512]{1,0:T(8,128)(2,1)S(1)} %copy-done.2, bf16[512,8192]{1,0:T(8,128)(2,1)} %right.15), custom_call_target="tpu_custom_call" | custom-call | flops 268435456 | bytes 2621440 | tf_op jit(solution)/shard_map/pallas_call | solution.py:53
  73.5 3.2 %collective-permute-start.11 = (bf16[128,512]{1,0:T(8,128)(2,1)S(1)}, bf16[128,512]{1,0:T(8,128)(2,1)S(1)}, u32[]{:S(2)}, u32[]{:S(2)}) collective-permute-start(bf16[128,512]{1,0:T(8,128)(2,1)S(1)} %get-tuple-element.39), channel_id=1, source_target_pairs={{0,12},{1,13},{2,14},{3,15},{4,0},{5,1},{6,2},{7,3},{8,4},{9,5},{1... | collective-permute-start | bytes 393224 | tf_op jit(solution)/shard_map/ppermute | solution.py:43
  78.1 2.6 collective-permute-done.10
  80.7 2.5 collective-permute-done.9
  87.6 3.7 %copy.28 = bf16[64,8,3072]{2,1,0:T(8,128)(2,1)S(1)} copy(bf16[64,8,3072]{2,0,1:T(8,128)(2,1)} %all-gather.10.cloned.1.call-done) | data formatting | bytes 6291456 | tf_op jit(solution)/shard_map/all_gather | solution.py:220
  92.8 4.5 %all-to-all-start = ((bf16[16,144,384]{2,1,0:T(8,128)(2,1)}), bf16[16,144,384]{2,1,0:T(8,128)(2,1)}, u32[]{:S(2)}, u32[]{:S(2)}) async-start(bf16[16,144,384]{2,1,0:T(8,128)(2,1)} %bitcast.124), calls=%async_computation | async-start | bytes 3538944 | tf_op jit(solution)/shard_map/all_to_all | solution.py:15
  98.3 21.7 %all-to-all-done = bf16[16,144,384]{2,1,0:T(8,128)(2,1)} async-done(((bf16[16,144,384]{2,1,0:T(8,128)(2,1)}), bf16[16,144,384]{2,1,0:T(8,128)(2,1)}, u32[]{:S(2)}, u32[]{:S(2)}) %all-to-all-start) | async-done | bytes 1769504 | tf_op jit(solution)/shard_map/all_to_all | solution.py:15
  125.1 4.6 %all-to-all-start.1 = ((bf16[16,128,384]{2,1,0:T(8,128)(2,1)}), bf16[16,128,384]{2,1,0:T(8,128)(2,1)}, u32[]{:S(2)}, u32[]{:S(2)}) async-start(bf16[16,128,384]{2,1,0:T(8,128)(2,1)} %broadcast_in_dim.27), calls=%async_computation.1 | async-start | bytes 3145728 | tf_op jit(solution)/shard_map/all_to_all | solution.py:15
  129.7 27.0 %all-gather.14.cloned.1.call-done = bf16[32,8,3072]{2,1,0:T(8,128)(2,1)} async-done(((bf16[2,8,3072]{2,1,0:T(8,128)(2,1)}), bf16[32,8,3072]{2,1,0:T(8,128)(2,1)}) %all-gather.14.cloned.1.call-update) | async-done | bytes 1572880 | tf_op jit(solution)/shard_map/all_gather | solution.py:231
  171.1 5.4 %all-to-all-start.3 = ((bf16[16,16,3072]{2,1,0:T(8,128)(2,1)}), bf16[16,16,3072]{2,1,0:T(8,128)(2,1)}, u32[]{:S(2)}, u32[]{:S(2)}) async-start(bf16[16,16,3072]{2,1,0:T(8,128)(2,1)} %bitcast.126), calls=%async_computation.3 | async-start | bytes 3145728 | tf_op jit(solution)/shard_map/all_to_all | solution.py:15
  178.7 3.2 %convolution_convert_fusion = bf16[256,3072]{1,0:T(8,128)(2,1)S(1)} fusion(bf16[3072,512]{1,0:T(8,128)(2,1)} %param.27, f32[256,512]{1,0:T(8,128)} %copy-done.14, f32[256,512]{1,0:T(8,128)} %copy-done.9), kind=kOutput, calls=%fused_computation.2 | convolution fusion | flops 806879232 | bytes 5767168 | tf_op jit(solution)/shard_map/dot_general | solution.py:31
  183.3 17.1 %all-to-all-done.3.terms = bf16[16,16,3072]{2,1,0:T(8,128)(2,1)} async-done(((bf16[16,16,3072]{2,1,0:T(8,128)(2,1)}), bf16[16,16,3072]{2,1,0:T(8,128)(2,1)}, u32[]{:S(2)}, u32[]{:S(2)}) %all-to-all-start.3) | async-done | bytes 1572896 | tf_op jit(solution)/shard_map/all_to_all | solution.py:15
  200.4 4.4 %all-to-all-start.2 = ((bf16[16,2,8,3072]{3,2,1,0:T(8,128)(2,1)}), bf16[16,2,8,3072]{3,2,1,0:T(8,128)(2,1)}, u32[]{:S(2)}, u32[]{:S(2)}) async-start(bf16[16,2,8,3072]{3,2,1,0:T(8,128)(2,1)} %bitcast.125), calls=%async_computation.2 | async-start | bytes 3145728 | tf_op jit(solution)/shard_map/all_to_all | solution.py:15
  206.5 2.4 shard_map.149
  208.9 16.8 %all-to-all-done.2 = bf16[16,2,8,3072]{3,2,1,0:T(8,128)(2,1)} async-done(((bf16[16,2,8,3072]{3,2,1,0:T(8,128)(2,1)}), bf16[16,2,8,3072]{3,2,1,0:T(8,128)(2,1)}, u32[]{:S(2)}, u32[]{:S(2)}) %all-to-all-start.2) | async-done | bytes 1572896 | tf_op jit(solution)/shard_map/all_to_all | solution.py:15
  225.7 4.2 %all-to-all-start.4 = ((bf16[8,16,384]{2,1,0:T(8,128)(2,1)}), bf16[8,16,384]{2,1,0:T(8,128)(2,1)S(1)}, u32[]{:S(2)}, u32[]{:S(2)}) async-start(bf16[8,16,384]{2,1,0:T(8,128)(2,1)} %shard_map.149), calls=%async_computation.4 | async-start | bytes 196608 | tf_op jit(solution)/shard_map/all_to_all | solution.py:15
  231.6 4.2 %all-to-all-done.4 = bf16[8,16,384]{2,1,0:T(8,128)(2,1)S(1)} async-done(((bf16[8,16,384]{2,1,0:T(8,128)(2,1)}), bf16[8,16,384]{2,1,0:T(8,128)(2,1)S(1)}, u32[]{:S(2)}, u32[]{:S(2)}) %all-to-all-start.4) | async-done | bytes 98336 | tf_op jit(solution)/shard_map/all_to_all | solution.py:15
  237.1 4.4 %all-to-all-start.5 = ((bf16[16,8,16,384]{3,2,1,0:T(8,128)(2,1)}), bf16[16,8,16,384]{3,2,1,0:T(8,128)(2,1)}, u32[]{:S(2)}, u32[]{:S(2)}) async-start(bf16[16,8,16,384]{3,2,1,0:T(8,128)(2,1)} %broadcast_in_dim.56), calls=%async_computation.5 | async-start | bytes 3145728 | tf_op jit(solution)/shard_map/all_to_all | solution.py:15
  250.3 15.2 %all-to-all-done.5 = bf16[16,8,16,384]{3,2,1,0:T(8,128)(2,1)} async-done(((bf16[16,8,16,384]{3,2,1,0:T(8,128)(2,1)}), bf16[16,8,16,384]{3,2,1,0:T(8,128)(2,1)}, u32[]{:S(2)}, u32[]{:S(2)}) %all-to-all-start.5) | async-done | bytes 1572896 | tf_op jit(solution)/shard_map/all_to_all | solution.py:15
  265.5 4.2 %fusion.7 = f32[512,384]{1,0:T(8,128)} fusion(bf16[16,8,16,384]{3,2,1,0:T(8,128)(2,1)} %all-to-all-done.5, bf16[8,16,16,512]{3,2,0,1:T(8,128)(2,1)} %all-gather.8.cloned.1.call-done), kind=kOutput, calls=%fused_computation.14 | convolution fusion | flops 805306368 | bytes 4456448 | tf_op jit(solution)/shard_map/dot_general | solution.py:302
  271.0 2.5 select_bitcast_fusion.3
  (127 shorter events, 54.5 us)
Async XLA Ops:
  7.2 156.3 %copy-start = (bf16[3072,512]{1,0:T(8,128)(2,1)S(1)}, bf16[3072,512]{1,0:T(8,128)(2,1)}, u32[]{:S(2)}) copy-start(bf16[3072,512]{1,0:T(8,128)(2,1)} %param.25) | copy-start | bytes 9437188
  7.2 80.4 %all-gather.10.cloned.1.call-start = ((), (), s32[]{:S(2)}) async-start(), calls=%async_computation.7 | async-start | bytes 3538944 | tf_op jit(solution)/shard_map/all_gather | solution.py:220
  10.4 7.7 %copy-start.2 = (bf16[256,512]{1,0:T(8,128)(2,1)S(1)}, bf16[256,512]{1,0:T(8,128)(2,1)}, u32[]{:S(2)}) copy-start(bf16[256,512]{1,0:T(8,128)(2,1)} %left.15) | copy-start | bytes 786436
  14.8 34.6 %collective-permute-start = (bf16[4,128,512]{2,1,0:T(8,128)(2,1)}, bf16[4,128,512]{2,1,0:T(8,128)(2,1)}, u32[]{:S(2)}, u32[]{:S(2)}) collective-permute-start(bf16[4,128,512]{2,1,0:T(8,128)(2,1)} %shard_map.141), channel_id=1, source_target_pairs={{0,8},{1,9},{2,10},{3,11},{4,12},{5,13},{6,14},{7,15},{8,0},{9,1},... | collective-permute-start | bytes 1572872 | tf_op jit(solution)/shard_map/ppermute | solution.py:43
  22.6 34.1 %collective-permute-start.1 = (bf16[4,128,512]{2,1,0:T(8,128)(2,1)}, bf16[4,128,512]{2,1,0:T(8,128)(2,1)}, u32[]{:S(2)}, u32[]{:S(2)}) collective-permute-start(bf16[4,128,512]{2,1,0:T(8,128)(2,1)} %shard_map.142), channel_id=1, source_target_pairs={{0,4},{1,5},{2,6},{3,7},{4,8},{5,9},{6,10},{7,11},{8,12},{9,13},{1... | collective-permute-start | bytes 1572872 | tf_op jit(solution)/shard_map/ppermute | solution.py:43
  27.7 28.9 %collective-permute-start.2 = (bf16[4,128,512]{2,1,0:T(8,128)(2,1)}, bf16[4,128,512]{2,1,0:T(8,128)(2,1)}, u32[]{:S(2)}, u32[]{:S(2)}) collective-permute-start(bf16[4,128,512]{2,1,0:T(8,128)(2,1)} %shard_map.143), channel_id=1, source_target_pairs={{0,12},{1,13},{2,14},{3,15},{4,0},{5,1},{6,2},{7,3},{8,4},{9,5},{1... | collective-permute-start | bytes 1572872 | tf_op jit(solution)/shard_map/ppermute | solution.py:43
  34.8 25.0 %collective-permute-start.6 = (bf16[4,128,512]{2,1,0:T(8,128)(2,1)}, bf16[4,128,512]{2,1,0:T(8,128)(2,1)}, u32[]{:S(2)}, u32[]{:S(2)}) collective-permute-start(bf16[4,128,512]{2,1,0:T(8,128)(2,1)} %shard_map.145), channel_id=1, source_target_pairs={{0,2},{1,3},{2,0},{3,1},{4,6},{5,7},{6,4},{7,5},{8,10},{9,11},{10,... | collective-permute-start | bytes 1572872 | tf_op jit(solution)/shard_map/ppermute | solution.py:43
  38.6 5.4 %copy-start.16 = (s32[16]{0:T(128)S(1)}, s32[16]{0:T(128)}, u32[]{:S(2)}) copy-start(s32[16]{0:T(128)} %param.21) | copy-start | bytes 196
  43.1 28.7 %collective-permute-start.7 = (bf16[4,128,512]{2,1,0:T(8,128)(2,1)}, bf16[4,128,512]{2,1,0:T(8,128)(2,1)}, u32[]{:S(2)}, u32[]{:S(2)}) collective-permute-start(bf16[4,128,512]{2,1,0:T(8,128)(2,1)} %shard_map.146), channel_id=1, source_target_pairs={{0,1},{1,2},{2,3},{3,0},{4,5},{5,6},{6,7},{7,4},{8,9},{9,10},{10,1... | collective-permute-start | bytes 1572872 | tf_op jit(solution)/shard_map/ppermute | solution.py:43
  49.5 22.3 %collective-permute-start.8 = (bf16[4,128,512]{2,1,0:T(8,128)(2,1)}, bf16[4,128,512]{2,1,0:T(8,128)(2,1)}, u32[]{:S(2)}, u32[]{:S(2)}) collective-permute-start(bf16[4,128,512]{2,1,0:T(8,128)(2,1)} %shard_map.147), channel_id=1, source_target_pairs={{0,3},{1,0},{2,1},{3,2},{4,7},{5,4},{6,5},{7,6},{8,11},{9,8},{10,9... | collective-permute-start | bytes 1572872 | tf_op jit(solution)/shard_map/ppermute | solution.py:43
  58.9 17.8 %collective-permute-start.3 = (bf16[128,512]{1,0:T(8,128)(2,1)}, bf16[128,512]{1,0:T(8,128)(2,1)S(1)}, u32[]{:S(2)}, u32[]{:S(2)}) collective-permute-start(bf16[128,512]{1,0:T(8,128)(2,1)} %get-tuple-element.35), channel_id=1, source_target_pairs={{0,2},{1,3},{2,0},{3,1},{4,6},{5,7},{6,4},{7,5},{8,10},{9,11},{10,... | collective-permute-start | bytes 393224 | tf_op jit(solution)/shard_map/ppermute | solution.py:43
  58.9 17.8 %collective-permute-start.4 = (bf16[128,512]{1,0:T(8,128)(2,1)}, bf16[128,512]{1,0:T(8,128)(2,1)}, u32[]{:S(2)}, u32[]{:S(2)}) collective-permute-start(bf16[128,512]{1,0:T(8,128)(2,1)} %get-tuple-element.37), channel_id=1, source_target_pairs={{0,1},{1,2},{2,3},{3,0},{4,5},{5,6},{6,7},{7,4},{8,9},{9,10},{10,1... | collective-permute-start | bytes 393224 | tf_op jit(solution)/shard_map/ppermute | solution.py:43
  59.8 17.0 %collective-permute-start.5 = (bf16[128,512]{1,0:T(8,128)(2,1)}, bf16[128,512]{1,0:T(8,128)(2,1)}, u32[]{:S(2)}, u32[]{:S(2)}) collective-permute-start(bf16[128,512]{1,0:T(8,128)(2,1)} %get-tuple-element.36), channel_id=1, source_target_pairs={{0,3},{1,0},{2,1},{3,2},{4,7},{5,4},{6,5},{7,6},{8,11},{9,8},{10,9... | collective-permute-start | bytes 393224 | tf_op jit(solution)/shard_map/ppermute | solution.py:43
  71.7 13.5 %copy-start.13 = (bf16[256,512]{1,0:T(8,128)(2,1)S(1)}, bf16[256,512]{1,0:T(8,128)(2,1)}, u32[]{:S(2)}) copy-start(bf16[256,512]{1,0:T(8,128)(2,1)} %param.17) | copy-start | bytes 786436
  71.7 13.5 %copy-start.15 = (f32[512]{0:T(512)S(1)}, f32[512]{0:T(512)}, u32[]{:S(2)}) copy-start(f32[512]{0:T(512)} %param.18) | copy-start | bytes 6148
  73.4 11.9 %copy-start.18 = (bf16[512,3072]{1,0:T(8,128)(2,1)S(1)}, bf16[512,3072]{1,0:T(8,128)(2,1)}, u32[]{:S(2)}) copy-start(bf16[512,3072]{1,0:T(8,128)(2,1)} %param.19) | copy-start | bytes 9437188
  73.5 7.3 %collective-permute-start.10 = (bf16[128,512]{1,0:T(8,128)(2,1)S(1)}, bf16[128,512]{1,0:T(8,128)(2,1)S(1)}, u32[]{:S(2)}, u32[]{:S(2)}) collective-permute-start(bf16[128,512]{1,0:T(8,128)(2,1)S(1)} %get-tuple-element.40), channel_id=1, source_target_pairs={{0,4},{1,5},{2,6},{3,7},{4,8},{5,9},{6,10},{7,11},{8,12},{9,13},{1... | collective-permute-start | bytes 393224 | tf_op jit(solution)/shard_map/ppermute | solution.py:43
  73.5 7.2 %collective-permute-start.11 = (bf16[128,512]{1,0:T(8,128)(2,1)S(1)}, bf16[128,512]{1,0:T(8,128)(2,1)S(1)}, u32[]{:S(2)}, u32[]{:S(2)}) collective-permute-start(bf16[128,512]{1,0:T(8,128)(2,1)S(1)} %get-tuple-element.39), channel_id=1, source_target_pairs={{0,12},{1,13},{2,14},{3,15},{4,0},{5,1},{6,2},{7,3},{8,4},{9,5},{1... | collective-permute-start | bytes 393224 | tf_op jit(solution)/shard_map/ppermute | solution.py:43
  76.8 6.5 %collective-permute-start.9 = (bf16[128,512]{1,0:T(8,128)(2,1)S(1)}, bf16[128,512]{1,0:T(8,128)(2,1)S(1)}, u32[]{:S(2)}, u32[]{:S(2)}) collective-permute-start(bf16[128,512]{1,0:T(8,128)(2,1)S(1)} %get-tuple-element.38), channel_id=1, source_target_pairs={{0,8},{1,9},{2,10},{3,11},{4,12},{5,13},{6,14},{7,15},{8,0},{9,1},... | collective-permute-start | bytes 393224 | tf_op jit(solution)/shard_map/ppermute | solution.py:43
  87.6 3.8 %copy-start.12 = (bf16[2,8,128,384]{3,2,1,0:T(8,128)(2,1)S(1)}, bf16[2,8,128,384]{3,2,1,0:T(8,128)(2,1)}, u32[]{:S(2)}) copy-start(bf16[2,8,128,384]{3,2,1,0:T(8,128)(2,1)} %fusion.6) | copy-start | bytes 4718596
  92.8 5.3 %copy-start.17 = (s32[256]{0:T(256)S(1)}, s32[256]{0:T(256)}, u32[]{:S(2)}) copy-start(s32[256]{0:T(256)} %param.20) | copy-start | bytes 3076
  92.8 27.2 %all-to-all-start = ((bf16[16,144,384]{2,1,0:T(8,128)(2,1)}), bf16[16,144,384]{2,1,0:T(8,128)(2,1)}, u32[]{:S(2)}, u32[]{:S(2)}) async-start(bf16[16,144,384]{2,1,0:T(8,128)(2,1)} %bitcast.124), calls=%async_computation | async-start | bytes 3538944 | tf_op jit(solution)/shard_map/all_to_all | solution.py:15
  97.4 59.3 %all-gather.14.cloned.1.call-start = ((), (), s32[]{:S(2)}) async-start(), calls=%async_computation.9 | async-start | bytes 1671168 | tf_op jit(solution)/shard_map/all_gather | solution.py:231
  125.1 36.2 %all-to-all-start.1 = ((bf16[16,128,384]{2,1,0:T(8,128)(2,1)}), bf16[16,128,384]{2,1,0:T(8,128)(2,1)}, u32[]{:S(2)}, u32[]{:S(2)}) async-start(bf16[16,128,384]{2,1,0:T(8,128)(2,1)} %broadcast_in_dim.27), calls=%async_computation.1 | async-start | bytes 3145728 | tf_op jit(solution)/shard_map/all_to_all | solution.py:15
  156.7 2.8 %copy-start.19 = (bf16[3072,512]{1,0:T(8,128)(2,1)S(1)}, bf16[3072,512]{1,0:T(8,128)(2,1)}, u32[]{:S(2)}) copy-start(bf16[3072,512]{1,0:T(8,128)(2,1)} %param.27) | copy-start | bytes 9437188
  165.9 2.9 %copy-start.9 = (f32[256,512]{1,0:T(8,128)}, f32[256,512]{1,0:T(8,128)S(1)}, u32[]{:S(2)}) copy-start(f32[256,512]{1,0:T(8,128)S(1)} %fusion.57) | copy-start | bytes 1572868
  171.1 29.2 %all-to-all-start.3 = ((bf16[16,16,3072]{2,1,0:T(8,128)(2,1)}), bf16[16,16,3072]{2,1,0:T(8,128)(2,1)}, u32[]{:S(2)}, u32[]{:S(2)}) async-start(bf16[16,16,3072]{2,1,0:T(8,128)(2,1)} %bitcast.126), calls=%async_computation.3 | async-start | bytes 3145728 | tf_op jit(solution)/shard_map/all_to_all | solution.py:15
  176.6 73.8 %all-gather.8.cloned.1.call-start = ((), (), s32[]{:S(2)}) async-start(), calls=%async_computation.6 | async-start | bytes 2359296 | tf_op jit(solution)/shard_map/all_gather | solution.py:277
  200.4 25.4 %all-to-all-start.2 = ((bf16[16,2,8,3072]{3,2,1,0:T(8,128)(2,1)}), bf16[16,2,8,3072]{3,2,1,0:T(8,128)(2,1)}, u32[]{:S(2)}, u32[]{:S(2)}) async-start(bf16[16,2,8,3072]{3,2,1,0:T(8,128)(2,1)} %bitcast.125), calls=%async_computation.2 | async-start | bytes 3145728 | tf_op jit(solution)/shard_map/all_to_all | solution.py:15
  225.7 10.0 %all-to-all-start.4 = ((bf16[8,16,384]{2,1,0:T(8,128)(2,1)}), bf16[8,16,384]{2,1,0:T(8,128)(2,1)S(1)}, u32[]{:S(2)}, u32[]{:S(2)}) async-start(bf16[8,16,384]{2,1,0:T(8,128)(2,1)} %shard_map.149), calls=%async_computation.4 | async-start | bytes 196608 | tf_op jit(solution)/shard_map/all_to_all | solution.py:15
  237.1 28.4 %all-to-all-start.5 = ((bf16[16,8,16,384]{3,2,1,0:T(8,128)(2,1)}), bf16[16,8,16,384]{3,2,1,0:T(8,128)(2,1)}, u32[]{:S(2)}, u32[]{:S(2)}) async-start(bf16[16,8,16,384]{3,2,1,0:T(8,128)(2,1)} %broadcast_in_dim.56), calls=%async_computation.5 | async-start | bytes 3145728 | tf_op jit(solution)/shard_map/all_to_all | solution.py:15
  241.5 28.2 %all-gather.12.cloned.1.call-start = ((), (), s32[]{:S(2)}) async-start(), calls=%async_computation.8 | async-start | bytes 1327104 | tf_op jit(solution)/shard_map/all_gather | solution.py:314
  (10 other events, 12.5 us)
Sparse Core Ops, SparseCore 0:
  9.7 30.1 all-gather.9
  101.0 55.6 all-gather.13
  179.1 26.6 all-gather.7
  244.3 23.1 all-gather.11

commit v3 on v2

--- a/solution.py
+++ b/solution.py
@@ -43,32 +43,56 @@
     return lax.ppermute(value, "mp", pairs)
 
 
-def piece_kernel(ids, left, right, out):
-    out[0] = jnp.dot(left[...], right[...], preferred_element_type=full).astype(out.dtype)
-
-
-def product_pieces(left, right, block, ids, width):
-    depth = left.shape[1]
-    count = ids.shape[0]
+def terms_kernel(place, left, right, *refs):
+    outs, held, sems = refs[: 2 * SIDE], refs[2 * SIDE], refs[2 * SIDE + 1]
+    width = held.shape[2]
+    y, z = place[0], place[1]
+
+    def load(index):
+        piece = lax.rem(y + index // SIDE, SIDE) * SIDE + lax.rem(index, SIDE)
+        columns = pl.ds(pl.multiple_of(piece * width, width), width)
+        return pltpu.make_async_copy(right.at[:, columns], held.at[index], sems.at[index])
+
+    for index in range(SIDE * SIDE):
+        load(index).start()
+
+    @pl.loop(0, SIDE * SIDE)
+    def _(index):
+        load(index).wait()
+        value = jnp.dot(left[...], held[index], preferred_element_type=full).astype(half)
+        along_y, at_z = index // SIDE, lax.rem(index, SIDE)
+        at_y, along_z = lax.rem(y + along_y, SIDE), lax.rem(at_z - z + SIDE, SIDE)
+        for distance in range(SIDE):
+
+            @pl.when(along_y == distance)
+            def _():
+                outs[distance][at_z] = value[:BLK]
+
+            @pl.when(along_z == distance)
+            def _():
+                outs[SIDE + distance][at_y] = value[BLK:]
+
+
+def product_pieces(left, right, y, z):
+    rows, depth = left.shape
+    width = right.shape[1] // (SIDE * SIDE)
+    whole = pl.BlockSpec(memory_space=pltpu.VMEM)
     return pl.pallas_call(
-        piece_kernel,
-        grid_spec=pltpu.PrefetchScalarGridSpec(
-            num_scalar_prefetch=1,
-            grid=(count,),
-            in_specs=[
-                pl.BlockSpec((BLK, depth), lambda i, ids: (block, 0)),
-                pl.BlockSpec((depth, width), lambda i, ids: (0, ids[i])),
-            ],
-            out_specs=pl.BlockSpec((1, BLK, width), lambda i, ids: (i, 0, 0)),
-        ),
-        out_shape=jax.ShapeDtypeStruct((count, BLK, width), half),
-        compiler_params=pltpu.CompilerParams(vmem_limit_bytes=48 * 1024 * 1024),
+        terms_kernel,
+        in_specs=[pl.BlockSpec(memory_space=pltpu.SMEM), whole, pl.BlockSpec(memory_space=pl.ANY)],
+        out_specs=[whole] * (2 * SIDE),
+        out_shape=[jax.ShapeDtypeStruct((SIDE, BLK, width), half)] * (2 * SIDE),
+        scratch_shapes=[
+            pltpu.VMEM((SIDE * SIDE, depth, width), half),
+            pltpu.SemaphoreType.DMA((SIDE * SIDE,)),
+        ],
+        compiler_params=pltpu.CompilerParams(vmem_limit_bytes=56 * 1024 * 1024),
         cost_estimate=pl.CostEstimate(
-            flops=2 * BLK * depth * width * count,
-            bytes_accessed=2 * (depth + BLK) * width * count,
+            flops=2 * rows * right.size,
+            bytes_accessed=2 * right.size,
             transcendentals=0,
         ),
-    )(ids, left, right)
+    )(jnp.stack([y, z]).astype(jnp.int32), left, right)
 
 
 def total(values):
@@ -80,22 +104,12 @@
 
 def teacher_terms(attention, out_proj, mp):
     y, z = mp // SIDE, mp % SIDE
-    width = attention.shape[1]
-    along = jnp.arange(SIDE, dtype=jnp.int32)
-    kept, moved = {}, {}
-    for distance in (2, 1, 3, 0):
-        for block in (0, 1):
-            if block == 0:
-                ids = ((y + distance) % SIDE) * SIDE + along
-            else:
-                ids = along * SIDE + (z + distance) % SIDE
-            terms = product_pieces(attention, out_proj, block, ids.astype(jnp.int32), width)
-            if distance == 0:
-                kept[block] = terms
-            else:
-                moved[block, distance] = (
-                    step(terms, distance, 0) if block == 0 else step(terms, 0, distance)
-                )
+    pieces = product_pieces(attention, out_proj, y, z)
+    kept = {0: pieces[0], 1: pieces[SIDE]}
+    moved = {}
+    for distance in (2, 1, 3):
+        moved[0, distance] = step(pieces[distance], distance, 0)
+        moved[1, distance] = step(pieces[SIDE + distance], 0, distance)
     results = []
     for block in (0, 1):
         here = z if block == 0 else y
@@ -214,22 +228,19 @@
     place = block_owner * slots + ranks
     my_place = lax.dynamic_slice_in_dim(place, dp * blocks, blocks)
 
-    both = jnp.concatenate(
-        [jnp.swapaxes(student_hidden[0], 0, 1), jnp.swapaxes(cotangent[0], 0, 1)], axis=0
-    )
+    both = jnp.concatenate([student_hidden[0], cotangent[0]], axis=1)
     everyone = lax.all_gather(both, "dp", axis=0, tiled=False)
 
     def fetch(offset):
         picked = []
         for k in range(blocks):
-            at = (my_place[k] // slots, my_place[k] % slots + offset, 0, 0)
-            piece = lax.dynamic_slice(everyone, at, (1, 1, rows, student_width))
+            at = (my_place[k] // slots, 0, my_place[k] % slots + offset, 0)
+            piece = lax.dynamic_slice(everyone, at, (1, rows, 1, student_width))
             picked.append(piece.reshape(rows, student_width))
         return jnp.stack(picked)
 
     sh_rows = fetch(0)
     dy = lax.all_gather(fetch(slots), "mp", axis=0, tiled=False)
-    dy = jnp.swapaxes(dy, 0, 1).reshape(tokens, student_width)
 
     hidden = residual.astype(full) + jnp.concatenate(teacher_terms(attention, out_proj, mp), axis=0)
     squares = jnp.sum(hidden * hidden, axis=1)
@@ -277,19 +288,23 @@
     pooled_all = lax.all_gather(pooled.reshape(n_mp, mine_rows, width_here), "dp", axis=0, tiled=False)
     pooled_all = jnp.swapaxes(pooled_all, 0, 1).reshape(n_dp * tokens, width_here)
 
-    dh = jnp.dot(dy, down_weight, preferred_element_type=full)
     gate = jnp.dot(normed_student, gate_weight, preferred_element_type=full)
     up = jnp.dot(normed_student, up_weight, preferred_element_type=full)
     sigma = jax.nn.sigmoid(gate)
     silu = gate * sigma
     act = (silu * up).astype(half)
+    output = times_rows(act, down_weight).astype(half)
+    dy, _ = lax.optimization_barrier((dy, output[:8, :128]))
+    dy = jnp.swapaxes(dy, 0, 1).reshape(tokens, student_width)
+    dh = jnp.dot(dy, down_weight, preferred_element_type=full)
     grad_gate = (dh * up * sigma * (1.0 + gate * (1.0 - sigma))).astype(half)
     grad_up = (dh * silu).astype(half)
     dn = (times_rows(grad_gate, gate_weight) + times_rows(grad_up, up_weight)).astype(half)
-    output = times_rows(act, down_weight).astype(half)
+    output = jnp.swapaxes(output.reshape(blocks, n_mp, rows, student_width), 0, 1)
+    output = exchange(output, "mp")
+    dn, output = lax.optimization_barrier((dn, output))
     dn = exchange(dn.reshape(n_mp, mine_rows, student_width), "mp")
-    output = jnp.swapaxes(output.reshape(blocks, n_mp, rows, student_width), 0, 1)
-    output = jnp.sum(exchange(output, "mp").astype(full), axis=0)
+    output = jnp.sum(output.astype(full), axis=0)
     here = mp * mine_rows
     dproj = slope(
         dn,

time: 283 us -> 277 us (0.979)
  Pallas kernels: 38.1 us -> 13.9 us
  blocking collectives: 0 us -> 11.1 us
  waiting for transfers between devices: 107 us -> 117 us
    pallas_call x8 -> x1, Pallas kernels: 33.5 us -> 9.93 us  [product_pieces(): pl.pallas_call(terms_kernel, in_specs=[pl.BlockSpec(memory_space=pltpu.SM...]
    ppermute x12, waiting for transfers between devices: 5.15 us -> 22.2 us  [step(): return lax.ppermute(value, 'mp', pairs)]
    all_to_all x0 -> x1, blocking collectives: none -> 11.1 us  [exchange(): return lax.all_to_all(pieces, axis, split_axis=0, concat_axis=0, tiled=True)]
    all_to_all x6 -> x5, waiting for transfers between devices: 74.9 us -> 66.9 us  [exchange(): return lax.all_to_all(pieces, axis, split_axis=0, concat_axis=0, tiled=True)]
    all_gather x1 -> x0, local copies, waits for them, and re-layouts: 3.74 us -> none  [on_device(): everyone = lax.all_gather(both, 'dp', axis=0, tiled=False)]
    dynamic_slice x0 -> x2, local copies, waits for them, and re-layouts: none -> 3.36 us  [the longest x1 2.45 us: fetch(): piece = lax.dynamic_slice(everyone, at, (1, rows, 1, student_width))]
    unnamed x41 -> x36, local copies, waits for them, and re-layouts: 6.8 us -> 3.95 us
    all_to_all x6 -> x5, starting transfers between devices: 27.6 us -> 24.8 us  [exchange(): return lax.all_to_all(pieces, axis, split_axis=0, concat_axis=0, tiled=True)]
  transfers between devices with their start and end apart: 22 -> 21, of which waited for: 8 -> 8; matrix products, arithmetic and copies ran while one was open for 13% -> 14% of each run, Pallas kernels for 13% -> 4%
where the time goes in v3:
time: 277 us; the launch traced here: 276 us
  waiting for transfers between devices  117 us (42%)
  starting transfers between devices  46.4 us (17%)
  between operations  26.1 us (9%)
  other arithmetic  24.2 us (9%)
  matrix products  19.8 us (7%)
  local copies, waits for them, and re-layouts  17.6 us (6%)
  Pallas kernels  13.9 us (5%)
  blocking collectives  11.1 us (4%)
    all_to_all x5, waiting for transfers between devices, exchange(): return lax.all_to_all(pieces, axis, split_axis=0, concat_axis=0, tiled=True)  66.9 us
    all_gather x1, waiting for transfers between devices, on_device(): dy = lax.all_gather(fetch(slots), 'mp', axis=0, tiled=False)  27.4 us
    all_to_all x5, starting transfers between devices, exchange(): return lax.all_to_all(pieces, axis, split_axis=0, concat_axis=0, tiled=True)  24.8 us
    ppermute x12, waiting for transfers between devices, step(): return lax.ppermute(value, 'mp', pairs)  22.2 us
    ppermute x12, starting transfers between devices, step(): return lax.ppermute(value, 'mp', pairs)  21.5 us
    all_to_all x1, blocking collectives, exchange(): return lax.all_to_all(pieces, axis, split_axis=0, concat_axis=0, tiled=True)  11.1 us
    pallas_call x1, Pallas kernels, product_pieces(): pl.pallas_call(terms_kernel, in_specs=[pl.BlockSpec(memory_space=pltpu.SM...  9.93 us
  transfers between devices with their start and end apart: 21, of which 8 were waited for; matrix products, arithmetic and copies ran while one was open for 14% of the time, Pallas kernels for 4%

profile of v3, /device:TPU:0, one launch (start us, length us, event | category | flops | bytes accessed | tf_op | source)
XLA Modules:
  0.0 275.7 jit_solution(12516104104126215965)
XLA Ops:
  7.2 2.1 pad_maximum_fusion.1
  10.0 9.9 %shard_map.140 = (bf16[4,128,512]{2,1,0:T(8,128)(2,1)}, bf16[4,128,512]{2,1,0:T(8,128)(2,1)}, bf16[4,128,512]{2,1,0:T(8,128)(2,1)}, bf16[4,128,512]{2,1,0:T(8,12...) custom-call(s32[2]{0:T(128)} %pad_add_fusion.place, ...), custom_call_target="tpu_custom_call" | custom-call | flops 2147483648 | bytes 8388608 | tf_op jit(solution)/shard_map/pallas_call | solution.py:80
  19.9 4.2 %collective-permute-start.8 = (bf16[4,128,512]{2,1,0:T(8,128)(2,1)}, bf16[4,128,512]{2,1,0:T(8,128)(2,1)}, u32[]{:S(2)}, u32[]{:S(2)}) collective-permute-start(bf16[4,128,512]{2,1,0:T(8,128)(2,1)} %get-tuple-element.33), channel_id=1, source_target_pairs={{0,3},{1,0},{2,1},{3,2},{4,7},{5,4},{6,5},{7,6},{8,11},{9,8},{10,9... | collective-permute-start | bytes 1572872 | tf_op jit(solution)/shard_map/ppermute | solution.py:43
  24.1 1.9 collective-permute-start.6
  26.0 3.0 %collective-permute-start.2 = (bf16[4,128,512]{2,1,0:T(8,128)(2,1)}, bf16[4,128,512]{2,1,0:T(8,128)(2,1)}, u32[]{:S(2)}, u32[]{:S(2)}) collective-permute-start(bf16[4,128,512]{2,1,0:T(8,128)(2,1)} %get-tuple-element.29), channel_id=1, source_target_pairs={{0,12},{1,13},{2,14},{3,15},{4,0},{5,1},{6,2},{7,3},{8,4},{9,5},{1... | collective-permute-start | bytes 1572872 | tf_op jit(solution)/shard_map/ppermute | solution.py:43
  29.2 17.7 %collective-permute-done.8 = bf16[4,128,512]{2,1,0:T(8,128)(2,1)} collective-permute-done((bf16[4,128,512]{2,1,0:T(8,128)(2,1)}, bf16[4,128,512]{2,1,0:T(8,128)(2,1)}, u32[]{:S(2)}, u32[]{:S(2)}) %collective-permute-start.8) | collective-permute-done | bytes 524320 | tf_op jit(solution)/shard_map/ppermute | solution.py:43
  46.8 3.2 %collective-permute-start = (bf16[4,128,512]{2,1,0:T(8,128)(2,1)}, bf16[4,128,512]{2,1,0:T(8,128)(2,1)}, u32[]{:S(2)}, u32[]{:S(2)}) collective-permute-start(bf16[4,128,512]{2,1,0:T(8,128)(2,1)} %get-tuple-element.27), channel_id=1, source_target_pairs={{0,8},{1,9},{2,10},{3,11},{4,12},{5,13},{6,14},{7,15},{8,0},{9,1},... | collective-permute-start | bytes 1572872 | tf_op jit(solution)/shard_map/ppermute | solution.py:43
  51.5 2.3 fusion.21
  55.9 1.9 collective-permute-start.9
  65.3 3.8 %collective-permute-start.5 = (bf16[128,512]{1,0:T(8,128)(2,1)S(1)}, bf16[128,512]{1,0:T(8,128)(2,1)S(1)}, u32[]{:S(2)}, u32[]{:S(2)}) collective-permute-start(bf16[128,512]{1,0:T(8,128)(2,1)S(1)} %get-tuple-element.60), channel_id=1, source_target_pairs={{0,3},{1,0},{2,1},{3,2},{4,7},{5,4},{6,5},{7,6},{8,11},{9,8},{10,9... | collective-permute-start | bytes 393224 | tf_op jit(solution)/shard_map/ppermute | solution.py:43
  72.6 4.0 %collective-permute-done.4 = bf16[128,512]{1,0:T(8,128)(2,1)S(1)} collective-permute-done((bf16[128,512]{1,0:T(8,128)(2,1)S(1)}, bf16[128,512]{1,0:T(8,128)(2,1)S(1)}, u32[]{:S(2)}, u32[]{:S(2)}) %collective-permute-start.4) | collective-permute-done | bytes 131104 | tf_op jit(solution)/shard_map/ppermute | solution.py:43
  78.8 2.1 fusion.6
  80.9 2.4 constant_dynamic-slice_fusion.6
  83.4 2.8 %pad_maximum_fusion = bf16[2,8,144,384]{3,2,1,0:T(8,128)(2,1)} fusion(bf16[2,8,8,384]{3,2,1,0:T(8,128)(2,1)S(1)} %broadcast_in_dim.25, bf16[2,8,8,384]{3,2,1,0:T(8,128)(2,1)S(1)} %maximum_bitcast_fusion.1, bf16[2,8,128,384]{3,2,1,0:T(8,128)(2,1)} %fusion.6), kind=kLoop, calls=%fused_computation.10 | loop fusion | flops 5308416 | bytes 3538944 | tf_op jit(solution)/shard_map/concatenate | solution.py:256
  86.3 6.3 %all-to-all-start = ((bf16[16,144,384]{2,1,0:T(8,128)(2,1)}), bf16[16,144,384]{2,1,0:T(8,128)(2,1)}, u32[]{:S(2)}, u32[]{:S(2)}) async-start(bf16[16,144,384]{2,1,0:T(8,128)(2,1)} %bitcast.121), calls=%async_computation | async-start | bytes 3538944 | tf_op jit(solution)/shard_map/all_to_all | solution.py:15
  94.4 19.5 %all-to-all-done = bf16[16,144,384]{2,1,0:T(8,128)(2,1)} async-done(((bf16[16,144,384]{2,1,0:T(8,128)(2,1)}), bf16[16,144,384]{2,1,0:T(8,128)(2,1)}, u32[]{:S(2)}, u32[]{:S(2)}) %all-to-all-start) | async-done | bytes 1769504 | tf_op jit(solution)/shard_map/all_to_all | solution.py:15
  119.1 5.0 %all-to-all-start.1 = ((bf16[16,128,384]{2,1,0:T(8,128)(2,1)}), bf16[16,128,384]{2,1,0:T(8,128)(2,1)}, u32[]{:S(2)}, u32[]{:S(2)}) async-start(bf16[16,128,384]{2,1,0:T(8,128)(2,1)} %broadcast_in_dim.27), calls=%async_computation.1 | async-start | bytes 3145728 | tf_op jit(solution)/shard_map/all_to_all | solution.py:15
  124.1 27.4 %all-gather.12.cloned.1.call-done = bf16[32,8,3072]{2,1,0:T(8,128)(2,1)} async-done(((bf16[2,8,3072]{2,1,0:T(8,128)(2,1)}), bf16[32,8,3072]{2,1,0:T(8,128)(2,1)}) %all-gather.12.cloned.1.call-update) | async-done | bytes 1572880 | tf_op jit(solution)/shard_map/all_gather | solution.py:243
  151.5 2.7 copy.35
  154.2 2.2 shard_map.141
  156.4 3.5 %fusion.55 = f32[256,512]{1,0:T(8,128)S(1)} fusion(bf16[256,3072]{1,0:T(8,128)(2,1)S(1)} %get-tuple-element.35, bf16[3072,512]{1,0:T(8,128)(2,1)} %param.25), kind=kOutput, calls=%fused_computation.123 | convolution fusion | flops 805306368 | bytes 5242880 | tf_op jit(solution)/shard_map/dot_general | solution.py:291
  163.4 4.7 %all-to-all-start.2 = ((bf16[16,2,8,3072]{3,2,1,0:T(8,128)(2,1)}), bf16[16,2,8,3072]{3,2,1,0:T(8,128)(2,1)}, u32[]{:S(2)}, u32[]{:S(2)}) async-start(bf16[16,2,8,3072]{3,2,1,0:T(8,128)(2,1)} %bitcast.122), calls=%async_computation.2 | async-start | bytes 3145728 | tf_op jit(solution)/shard_map/all_to_all | solution.py:15
  168.1 2.5 fusion.53
  173.4 2.2 fusion
  175.6 16.2 %all-to-all-done.2 = bf16[16,2,8,3072]{3,2,1,0:T(8,128)(2,1)} async-done(((bf16[16,2,8,3072]{3,2,1,0:T(8,128)(2,1)}), bf16[16,2,8,3072]{3,2,1,0:T(8,128)(2,1)}, u32[]{:S(2)}, u32[]{:S(2)}) %all-to-all-start.2) | async-done | bytes 1572896 | tf_op jit(solution)/shard_map/all_to_all | solution.py:15
  197.2 4.4 %all-to-all-start.3 = ((bf16[16,16,3072]{2,1,0:T(8,128)(2,1)}), bf16[16,16,3072]{2,1,0:T(8,128)(2,1)}, u32[]{:S(2)}, u32[]{:S(2)}) async-start(bf16[16,16,3072]{2,1,0:T(8,128)(2,1)} %bitcast.123), calls=%async_computation.3 | async-start | bytes 3145728 | tf_op jit(solution)/shard_map/all_to_all | solution.py:15
  203.5 19.2 %all-to-all-done.3.terms = bf16[16,16,3072]{2,1,0:T(8,128)(2,1)} async-done(((bf16[16,16,3072]{2,1,0:T(8,128)(2,1)}), bf16[16,16,3072]{2,1,0:T(8,128)(2,1)}, u32[]{:S(2)}, u32[]{:S(2)}) %all-to-all-start.3) | async-done | bytes 1572896 | tf_op jit(solution)/shard_map/all_to_all | solution.py:15
  224.4 11.1 %all_to_all.30 = bf16[8,16,384]{2,1,0:T(8,128)(2,1)S(1)} all-to-all(bf16[8,16,384]{2,1,0:T(8,128)(2,1)S(1)} %shard_map.142), channel_id=1, replica_groups=mesh['dp'=8,'mp'=16] {'dp'}, dimensions={0} | all-to-all | bytes 196608 | tf_op jit(solution)/shard_map/all_to_all | solution.py:15
  236.9 4.4 %all-to-all-start.5 = ((bf16[16,8,16,384]{3,2,1,0:T(8,128)(2,1)}), bf16[16,8,16,384]{3,2,1,0:T(8,128)(2,1)}, u32[]{:S(2)}, u32[]{:S(2)}) async-start(bf16[16,8,16,384]{3,2,1,0:T(8,128)(2,1)} %broadcast_in_dim.56), calls=%async_computation.5 | async-start | bytes 3145728 | tf_op jit(solution)/shard_map/all_to_all | solution.py:15
  249.7 2.5 select_bitcast_fusion.3
  253.0 12.0 %all-to-all-done.5 = bf16[16,8,16,384]{3,2,1,0:T(8,128)(2,1)} async-done(((bf16[16,8,16,384]{3,2,1,0:T(8,128)(2,1)}), bf16[16,8,16,384]{3,2,1,0:T(8,128)(2,1)}, u32[]{:S(2)}, u32[]{:S(2)}) %all-to-all-start.5) | async-done | bytes 1572896 | tf_op jit(solution)/shard_map/all_to_all | solution.py:15
  265.0 4.2 %fusion.7 = f32[512,384]{1,0:T(8,128)} fusion(bf16[16,8,16,384]{3,2,1,0:T(8,128)(2,1)} %all-to-all-done.5, bf16[8,16,16,512]{3,2,0,1:T(8,128)(2,1)} %all-gather.8.cloned.1.call-done), kind=kOutput, calls=%fused_computation.14 | convolution fusion | flops 805306368 | bytes 4456448 | tf_op jit(solution)/shard_map/dot_general | solution.py:317
  (107 shorter events, 38.2 us)
Async XLA Ops:
  7.2 153.8 %copy-start = (bf16[3072,512]{1,0:T(8,128)(2,1)S(1)}, bf16[3072,512]{1,0:T(8,128)(2,1)}, u32[]{:S(2)}) copy-start(bf16[3072,512]{1,0:T(8,128)(2,1)} %param.27) | copy-start | bytes 9437188
  7.2 73.8 %all-gather.10.cloned.1.call-start = ((), (), s32[]{:S(2)}) async-start(), calls=%async_computation.7 | async-start | bytes 3538944 | tf_op jit(solution)/shard_map/all_gather | solution.py:232
  10.0 19.0 %copy-start.14 = (s32[16]{0:T(128)S(1)}, s32[16]{0:T(128)}, u32[]{:S(2)}) copy-start(s32[16]{0:T(128)} %param.21) | copy-start | bytes 196
  19.9 26.9 %collective-permute-start.8 = (bf16[4,128,512]{2,1,0:T(8,128)(2,1)}, bf16[4,128,512]{2,1,0:T(8,128)(2,1)}, u32[]{:S(2)}, u32[]{:S(2)}) collective-permute-start(bf16[4,128,512]{2,1,0:T(8,128)(2,1)} %get-tuple-element.33), channel_id=1, source_target_pairs={{0,3},{1,0},{2,1},{3,2},{4,7},{5,4},{6,5},{7,6},{8,11},{9,8},{10,9... | collective-permute-start | bytes 1572872 | tf_op jit(solution)/shard_map/ppermute | solution.py:43
  24.1 27.4 %collective-permute-start.7 = (bf16[4,128,512]{2,1,0:T(8,128)(2,1)}, bf16[4,128,512]{2,1,0:T(8,128)(2,1)}, u32[]{:S(2)}, u32[]{:S(2)}) collective-permute-start(bf16[4,128,512]{2,1,0:T(8,128)(2,1)} %get-tuple-element.32), channel_id=1, source_target_pairs={{0,1},{1,2},{2,3},{3,0},{4,5},{5,6},{6,7},{7,4},{8,9},{9,10},{10,1... | collective-permute-start | bytes 1572872 | tf_op jit(solution)/shard_map/ppermute | solution.py:43
  24.1 27.4 %collective-permute-start.6 = (bf16[4,128,512]{2,1,0:T(8,128)(2,1)}, bf16[4,128,512]{2,1,0:T(8,128)(2,1)}, u32[]{:S(2)}, u32[]{:S(2)}) collective-permute-start(bf16[4,128,512]{2,1,0:T(8,128)(2,1)} %get-tuple-element.31), channel_id=1, source_target_pairs={{0,2},{1,3},{2,0},{3,1},{4,6},{5,7},{6,4},{7,5},{8,10},{9,11},{10,... | collective-permute-start | bytes 1572872 | tf_op jit(solution)/shard_map/ppermute | solution.py:43
  26.0 30.0 %collective-permute-start.2 = (bf16[4,128,512]{2,1,0:T(8,128)(2,1)}, bf16[4,128,512]{2,1,0:T(8,128)(2,1)}, u32[]{:S(2)}, u32[]{:S(2)}) collective-permute-start(bf16[4,128,512]{2,1,0:T(8,128)(2,1)} %get-tuple-element.29), channel_id=1, source_target_pairs={{0,12},{1,13},{2,14},{3,15},{4,0},{5,1},{6,2},{7,3},{8,4},{9,5},{1... | collective-permute-start | bytes 1572872 | tf_op jit(solution)/shard_map/ppermute | solution.py:43
  29.0 34.1 %collective-permute-start.1 = (bf16[4,128,512]{2,1,0:T(8,128)(2,1)}, bf16[4,128,512]{2,1,0:T(8,128)(2,1)}, u32[]{:S(2)}, u32[]{:S(2)}) collective-permute-start(bf16[4,128,512]{2,1,0:T(8,128)(2,1)} %get-tuple-element.28), channel_id=1, source_target_pairs={{0,4},{1,5},{2,6},{3,7},{4,8},{5,9},{6,10},{7,11},{8,12},{9,13},{1... | collective-permute-start | bytes 1572872 | tf_op jit(solution)/shard_map/ppermute | solution.py:43
  46.8 16.8 %collective-permute-start = (bf16[4,128,512]{2,1,0:T(8,128)(2,1)}, bf16[4,128,512]{2,1,0:T(8,128)(2,1)}, u32[]{:S(2)}, u32[]{:S(2)}) collective-permute-start(bf16[4,128,512]{2,1,0:T(8,128)(2,1)} %get-tuple-element.27), channel_id=1, source_target_pairs={{0,8},{1,9},{2,10},{3,11},{4,12},{5,13},{6,14},{7,15},{8,0},{9,1},... | collective-permute-start | bytes 1572872 | tf_op jit(solution)/shard_map/ppermute | solution.py:43
  53.9 15.2 %collective-permute-start.11 = (bf16[128,512]{1,0:T(8,128)(2,1)}, bf16[128,512]{1,0:T(8,128)(2,1)S(1)}, u32[]{:S(2)}, u32[]{:S(2)}) collective-permute-start(bf16[128,512]{1,0:T(8,128)(2,1)} %get-tuple-element.63), channel_id=1, source_target_pairs={{0,12},{1,13},{2,14},{3,15},{4,0},{5,1},{6,2},{7,3},{8,4},{9,5},{1... | collective-permute-start | bytes 393224 | tf_op jit(solution)/shard_map/ppermute | solution.py:43
  55.6 15.0 %collective-permute-start.10 = (bf16[128,512]{1,0:T(8,128)(2,1)}, bf16[128,512]{1,0:T(8,128)(2,1)S(1)}, u32[]{:S(2)}, u32[]{:S(2)}) collective-permute-start(bf16[128,512]{1,0:T(8,128)(2,1)} %get-tuple-element.64), channel_id=1, source_target_pairs={{0,4},{1,5},{2,6},{3,7},{4,8},{5,9},{6,10},{7,11},{8,12},{9,13},{1... | collective-permute-start | bytes 393224 | tf_op jit(solution)/shard_map/ppermute | solution.py:43
  55.9 15.4 %collective-permute-start.9 = (bf16[128,512]{1,0:T(8,128)(2,1)S(1)}, bf16[128,512]{1,0:T(8,128)(2,1)}, u32[]{:S(2)}, u32[]{:S(2)}) collective-permute-start(bf16[128,512]{1,0:T(8,128)(2,1)S(1)} %get-tuple-element.62), channel_id=1, source_target_pairs={{0,8},{1,9},{2,10},{3,11},{4,12},{5,13},{6,14},{7,15},{8,0},{9,1},... | collective-permute-start | bytes 393224 | tf_op jit(solution)/shard_map/ppermute | solution.py:43
  63.6 15.0 %copy-start.9 = (bf16[256,512]{1,0:T(8,128)(2,1)S(1)}, bf16[256,512]{1,0:T(8,128)(2,1)}, u32[]{:S(2)}) copy-start(bf16[256,512]{1,0:T(8,128)(2,1)} %param.17) | copy-start | bytes 786436
  63.6 15.0 %copy-start.13 = (f32[512]{0:T(512)S(1)}, f32[512]{0:T(512)}, u32[]{:S(2)}) copy-start(f32[512]{0:T(512)} %param.18) | copy-start | bytes 6148
  65.3 13.5 %copy-start.16 = (bf16[512,3072]{1,0:T(8,128)(2,1)S(1)}, bf16[512,3072]{1,0:T(8,128)(2,1)}, u32[]{:S(2)}) copy-start(bf16[512,3072]{1,0:T(8,128)(2,1)} %param.19) | copy-start | bytes 9437188
  65.3 7.3 %collective-permute-start.5 = (bf16[128,512]{1,0:T(8,128)(2,1)S(1)}, bf16[128,512]{1,0:T(8,128)(2,1)S(1)}, u32[]{:S(2)}, u32[]{:S(2)}) collective-permute-start(bf16[128,512]{1,0:T(8,128)(2,1)S(1)} %get-tuple-element.60), channel_id=1, source_target_pairs={{0,3},{1,0},{2,1},{3,2},{4,7},{5,4},{6,5},{7,6},{8,11},{9,8},{10,9... | collective-permute-start | bytes 393224 | tf_op jit(solution)/shard_map/ppermute | solution.py:43
  69.1 7.6 %collective-permute-start.4 = (bf16[128,512]{1,0:T(8,128)(2,1)S(1)}, bf16[128,512]{1,0:T(8,128)(2,1)S(1)}, u32[]{:S(2)}, u32[]{:S(2)}) collective-permute-start(bf16[128,512]{1,0:T(8,128)(2,1)S(1)} %get-tuple-element.61), channel_id=1, source_target_pairs={{0,1},{1,2},{2,3},{3,0},{4,5},{5,6},{6,7},{7,4},{8,9},{9,10},{10,1... | collective-permute-start | bytes 393224 | tf_op jit(solution)/shard_map/ppermute | solution.py:43
  69.1 7.6 %collective-permute-start.3 = (bf16[128,512]{1,0:T(8,128)(2,1)S(1)}, bf16[128,512]{1,0:T(8,128)(2,1)S(1)}, u32[]{:S(2)}, u32[]{:S(2)}) collective-permute-start(bf16[128,512]{1,0:T(8,128)(2,1)S(1)} %get-tuple-element.59), channel_id=1, source_target_pairs={{0,2},{1,3},{2,0},{3,1},{4,6},{5,7},{6,4},{7,5},{8,10},{9,11},{10,... | collective-permute-start | bytes 393224 | tf_op jit(solution)/shard_map/ppermute | solution.py:43
  86.3 8.0 %copy-start.15 = (s32[256]{0:T(256)S(1)}, s32[256]{0:T(256)}, u32[]{:S(2)}) copy-start(s32[256]{0:T(256)} %param.20) | copy-start | bytes 3076
  86.3 27.7 %all-to-all-start = ((bf16[16,144,384]{2,1,0:T(8,128)(2,1)}), bf16[16,144,384]{2,1,0:T(8,128)(2,1)}, u32[]{:S(2)}, u32[]{:S(2)}) async-start(bf16[16,144,384]{2,1,0:T(8,128)(2,1)} %bitcast.121), calls=%async_computation | async-start | bytes 3538944 | tf_op jit(solution)/shard_map/all_to_all | solution.py:15
  92.6 59.0 %all-gather.12.cloned.1.call-start = ((), (), s32[]{:S(2)}) async-start(), calls=%async_computation.8 | async-start | bytes 1671168 | tf_op jit(solution)/shard_map/all_gather | solution.py:243
  119.1 35.1 %all-to-all-start.1 = ((bf16[16,128,384]{2,1,0:T(8,128)(2,1)}), bf16[16,128,384]{2,1,0:T(8,128)(2,1)}, u32[]{:S(2)}, u32[]{:S(2)}) async-start(bf16[16,128,384]{2,1,0:T(8,128)(2,1)} %broadcast_in_dim.27), calls=%async_computation.1 | async-start | bytes 3145728 | tf_op jit(solution)/shard_map/all_to_all | solution.py:15
  124.1 30.1 %copy-start.1 = (f32[3072]{0:T(1024)S(1)}, f32[3072]{0:T(1024)}, u32[]{:S(2)}) copy-start(f32[3072]{0:T(1024)} %param.24) | copy-start | bytes 36868
  156.4 3.5 %copy-start.2 = (bf16[256,3072]{1,0:T(8,128)(2,1)}, bf16[256,3072]{1,0:T(8,128)(2,1)S(1)}, u32[]{:S(2)}) copy-start(bf16[256,3072]{1,0:T(8,128)(2,1)S(1)} %get-tuple-element.34) | copy-start | bytes 4718596
  156.4 3.5 %copy-start.3 = (bf16[3072,512]{1,0:T(8,128)(2,1)S(1)}, bf16[3072,512]{1,0:T(8,128)(2,1)}, u32[]{:S(2)}) copy-start(bf16[3072,512]{1,0:T(8,128)(2,1)} %param.26) | copy-start | bytes 9437188
  163.4 28.5 %all-to-all-start.2 = ((bf16[16,2,8,3072]{3,2,1,0:T(8,128)(2,1)}), bf16[16,2,8,3072]{3,2,1,0:T(8,128)(2,1)}, u32[]{:S(2)}, u32[]{:S(2)}) async-start(bf16[16,2,8,3072]{3,2,1,0:T(8,128)(2,1)} %bitcast.122), calls=%async_computation.2 | async-start | bytes 3145728 | tf_op jit(solution)/shard_map/all_to_all | solution.py:15
  168.0 80.4 %all-gather.14.cloned.1.call-start = ((), (), s32[]{:S(2)}) async-start(), calls=%async_computation.9 | async-start | bytes 1327104 | tf_op jit(solution)/shard_map/all_gather | solution.py:329
  168.1 3.4 %copy-start.5 = (bf16[3072,512]{1,0:T(8,128)(2,1)S(1)}, bf16[3072,512]{1,0:T(8,128)(2,1)}, u32[]{:S(2)}) copy-start(bf16[3072,512]{1,0:T(8,128)(2,1)} %param.25) | copy-start | bytes 9437188
  168.1 3.4 %copy-start.8 = (f32[256,512]{1,0:T(8,128)S(1)}, f32[256,512]{1,0:T(8,128)}, u32[]{:S(2)}) copy-start(f32[256,512]{1,0:T(8,128)} %copy-done.7) | copy-start | bytes 1572868
  195.1 57.9 %all-gather.8.cloned.1.call-start = ((), (), s32[]{:S(2)}) async-start(), calls=%async_computation.6 | async-start | bytes 2359296 | tf_op jit(solution)/shard_map/all_gather | solution.py:288
  197.2 25.4 %all-to-all-start.3 = ((bf16[16,16,3072]{2,1,0:T(8,128)(2,1)}), bf16[16,16,3072]{2,1,0:T(8,128)(2,1)}, u32[]{:S(2)}, u32[]{:S(2)}) async-start(bf16[16,16,3072]{2,1,0:T(8,128)(2,1)} %bitcast.123), calls=%async_computation.3 | async-start | bytes 3145728 | tf_op jit(solution)/shard_map/all_to_all | solution.py:15
  236.9 28.1 %all-to-all-start.5 = ((bf16[16,8,16,384]{3,2,1,0:T(8,128)(2,1)}), bf16[16,8,16,384]{3,2,1,0:T(8,128)(2,1)}, u32[]{:S(2)}, u32[]{:S(2)}) async-start(bf16[16,8,16,384]{3,2,1,0:T(8,128)(2,1)} %broadcast_in_dim.56), calls=%async_computation.5 | async-start | bytes 3145728 | tf_op jit(solution)/shard_map/all_to_all | solution.py:15
  (6 other events, 8.7 us)
Sparse Core Ops, SparseCore 0:
  9.7 30.1 all-gather.9
  96.2 55.3 all-gather.11
  195.2 21.9 all-gather.13
  219.4 26.0 all-gather.7

commit v4 on v3

--- a/solution.py
+++ b/solution.py
@@ -44,7 +44,7 @@
 
 
 def terms_kernel(place, left, right, *refs):
-    outs, held, sems = refs[: 2 * SIDE], refs[2 * SIDE], refs[2 * SIDE + 1]
+    outs, held, sems = refs[:10], refs[10], refs[11]
     width = held.shape[2]
     y, z = place[0], place[1]
 
@@ -63,36 +63,110 @@
         along_y, at_z = index // SIDE, lax.rem(index, SIDE)
         at_y, along_z = lax.rem(y + along_y, SIDE), lax.rem(at_z - z + SIDE, SIDE)
         for distance in range(SIDE):
-
-            @pl.when(along_y == distance)
-            def _():
-                outs[distance][at_z] = value[:BLK]
-
-            @pl.when(along_z == distance)
-            def _():
-                outs[SIDE + distance][at_y] = value[BLK:]
-
-
-def product_pieces(left, right, y, z):
-    rows, depth = left.shape
-    width = right.shape[1] // (SIDE * SIDE)
-    whole = pl.BlockSpec(memory_space=pltpu.VMEM)
-    return pl.pallas_call(
+            for block, away, at in ((0, along_y, at_z), (1, along_z, at_y)):
+
+                @pl.when(away == distance)
+                def _():
+                    base, first = 5 * block, BLK * block
+                    if distance == 2:
+                        outs[base + 3][at] = value[first : first + BLK // 2]
+                        outs[base + 4][at] = value[first + BLK // 2 : first + BLK]
+                    else:
+                        outs[base + min(distance, 2)][at] = value[first : first + BLK]
+
+
+def merge_kernel(*refs):
+    ins, outs = refs[:8], refs[8:]
+    middle = BLK // 2
+    for block in (0, 1):
+        up, down, lower, upper = ins[4 * block : 4 * block + 4]
+        to_up, to_down = outs[2 * block], outs[2 * block + 1]
+        for piece in range(SIDE):
+            to_up[piece, :middle] = (
+                up[piece, :middle].astype(full) + lower[piece].astype(full)
+            ).astype(half)
+            to_up[piece, middle:] = up[piece, middle:]
+            to_down[piece, :middle] = down[piece, :middle]
+            to_down[piece, middle:] = (
+                down[piece, middle:].astype(full) + upper[piece].astype(full)
+            ).astype(half)
+
+
+def gather_kernel(place, *refs):
+    ins, outs = refs[:6], refs[8:]
+    for block in (0, 1):
+        kept, from_down, from_up = ins[3 * block : 3 * block + 3]
+        here = place[1 - block]
+        for distance in range(SIDE):
+            at = lax.rem(here + distance, SIDE)
+            value = kept[at].astype(full) + from_down[at].astype(full) + from_up[at].astype(full)
+            out = outs[SIDE * block + distance]
+            out[...] = value.astype(out.dtype)
+
+
+def teacher_terms(attention, out_proj, mp, order):
+    width = attention.shape[1]
+    whole = pl.BlockSpec(memory_space=pltpu.VMEM)
+    scalars = pl.BlockSpec(memory_space=pltpu.SMEM)
+    anywhere = pl.BlockSpec(memory_space=pl.ANY)
+    limit = pltpu.CompilerParams(vmem_limit_bytes=24 * 1024 * 1024)
+    place = jnp.stack([mp // SIDE, mp % SIDE]).astype(jnp.int32)
+    full_piece = jax.ShapeDtypeStruct((SIDE, BLK, width), half)
+    half_piece = jax.ShapeDtypeStruct((SIDE, BLK // 2, width), half)
+    moves = full_piece.size
+
+    kept0, up0, down0, lower0, upper0, kept1, up1, down1, lower1, upper1 = pl.pallas_call(
         terms_kernel,
-        in_specs=[pl.BlockSpec(memory_space=pltpu.SMEM), whole, pl.BlockSpec(memory_space=pl.ANY)],
-        out_specs=[whole] * (2 * SIDE),
-        out_shape=[jax.ShapeDtypeStruct((SIDE, BLK, width), half)] * (2 * SIDE),
+        in_specs=[scalars, whole, anywhere],
+        out_specs=[whole] * 10,
+        out_shape=[full_piece, full_piece, full_piece, half_piece, half_piece] * 2,
         scratch_shapes=[
-            pltpu.VMEM((SIDE * SIDE, depth, width), half),
+            pltpu.VMEM((SIDE * SIDE, width, width), half),
             pltpu.SemaphoreType.DMA((SIDE * SIDE,)),
         ],
-        compiler_params=pltpu.CompilerParams(vmem_limit_bytes=56 * 1024 * 1024),
-        cost_estimate=pl.CostEstimate(
-            flops=2 * rows * right.size,
-            bytes_accessed=2 * right.size,
+        compiler_params=limit,
+        cost_estimate=pl.CostEstimate(
+            flops=2 * attention.shape[0] * out_proj.size,
+            bytes_accessed=2 * out_proj.size,
             transcendentals=0,
         ),
-    )(jnp.stack([y, z]).astype(jnp.int32), left, right)
+    )(place, attention, out_proj)
+    lower0, upper0 = step(lower0, 1, 0), step(upper0, -1, 0)
+    lower1, upper1 = step(lower1, 0, 1), step(upper1, 0, -1)
+    up0, down0, up1, down1 = pl.pallas_call(
+        merge_kernel,
+        in_specs=[whole] * 8,
+        out_specs=[whole] * 4,
+        out_shape=[full_piece] * 4,
+        compiler_params=limit,
+        cost_estimate=pl.CostEstimate(
+            flops=4 * moves, bytes_accessed=20 * moves, transcendentals=0
+        ),
+    )(up0, down0, lower0, upper0, up1, down1, lower1, upper1)
+    from_down0, from_up0 = step(up0, 1, 0), step(down0, -1, 0)
+    from_down1, from_up1 = step(up1, 0, 1), step(down1, 0, -1)
+    sums = pl.pallas_call(
+        gather_kernel,
+        in_specs=[scalars] + [whole] * 6 + [anywhere] * 2,
+        out_specs=[whole] * (2 * SIDE),
+        out_shape=[
+            jax.ShapeDtypeStruct((BLK, width), half if distance else full)
+            for block in (0, 1)
+            for distance in range(SIDE)
+        ],
+        compiler_params=limit,
+        cost_estimate=pl.CostEstimate(
+            flops=4 * moves, bytes_accessed=16 * moves, transcendentals=0
+        ),
+    )(place, kept0, from_down0, from_up0, kept1, from_down1, from_up1, *order)
+    results = []
+    for block in (0, 1):
+        mine = sums[SIDE * block : SIDE * block + SIDE]
+        arrived = [
+            step(mine[d], 0, d) if block == 0 else step(mine[d], d, 0) for d in range(1, SIDE)
+        ]
+        results.append([mine[0]] + arrived)
+    return results
 
 
 def total(values):
@@ -102,32 +176,86 @@
     return result
 
 
-def teacher_terms(attention, out_proj, mp):
-    y, z = mp // SIDE, mp % SIDE
-    pieces = product_pieces(attention, out_proj, y, z)
-    kept = {0: pieces[0], 1: pieces[SIDE]}
-    moved = {}
-    for distance in (2, 1, 3):
-        moved[0, distance] = step(pieces[distance], distance, 0)
-        moved[1, distance] = step(pieces[SIDE + distance], 0, distance)
-    results = []
-    for block in (0, 1):
-        here = z if block == 0 else y
-        arrays = [kept[block]] + [moved[block, distance] for distance in (2, 1, 3)]
-
-        def piece(distance):
-            at = (here + distance) % SIDE
-            return total([lax.dynamic_index_in_dim(a, at, 0, False) for a in arrays])
-
-        arrived = []
-        for distance in (2, 1, 3):
-            sent = piece(distance).astype(half)
-            arrived.append(step(sent, 0, distance) if block == 0 else step(sent, distance, 0))
-        results.append(piece(0) + total(arrived))
-    return results
-
-
-def normalise_kernel(pieces, gain, state, normed):
+def backward_kernel(dy, down, gate, up, order, grad_gate, grad_up, dh):
+    del order
+    rows = 8
+    for chunk in range(2):
+        columns = pl.ds(chunk * (down.shape[1] // 2), down.shape[1] // 2)
+        value = jnp.dot(dy[...], down[:, columns], preferred_element_type=full)
+        for index in range(value.shape[0] // rows):
+            to = (index % 2) * BLK + (index // 2) * rows
+            dh[pl.ds(to, rows), columns] = value[index * rows : index * rows + rows]
+    gate_val = gate[...]
+    sigma = jax.nn.sigmoid(gate_val)
+    grad_gate[...] = (dh[...] * up[...] * sigma * (1.0 + gate_val * (1.0 - sigma))).astype(half)
+    grad_up[...] = (dh[...] * (gate_val * sigma)).astype(half)
+
+
+def backward(dy, down, gate, up, order):
+    whole = pl.BlockSpec(memory_space=pltpu.VMEM)
+    shape = jax.ShapeDtypeStruct(gate.shape, half)
+    return pl.pallas_call(
+        backward_kernel,
+        in_specs=[whole] * 4 + [pl.BlockSpec(memory_space=pl.ANY)],
+        out_specs=[whole, whole],
+        out_shape=[shape, shape],
+        scratch_shapes=[pltpu.VMEM(gate.shape, full)],
+        compiler_params=pltpu.CompilerParams(vmem_limit_bytes=24 * 1024 * 1024),
+        cost_estimate=pl.CostEstimate(
+            flops=2 * dy.shape[0] * down.size,
+            bytes_accessed=2 * (down.size + dy.size) + 16 * gate.size,
+            transcendentals=gate.size,
+        ),
+    )(dy, down, gate, up, order)
+
+
+def spread_kernel(piece, order, out):
+    del order
+    for index in range(out.shape[0]):
+        out[index] = piece[...]
+
+
+def spread(piece, count, order):
+    whole = pl.BlockSpec(memory_space=pltpu.VMEM)
+    return pl.pallas_call(
+        spread_kernel,
+        in_specs=[whole, pl.BlockSpec(memory_space=pl.ANY)],
+        out_specs=whole,
+        out_shape=jax.ShapeDtypeStruct((count,) + piece.shape, piece.dtype),
+        compiler_params=pltpu.CompilerParams(vmem_limit_bytes=16 * 1024 * 1024),
+        cost_estimate=pl.CostEstimate(
+            flops=0, bytes_accessed=4 * count * piece.size, transcendentals=0
+        ),
+    )(piece, order)
+
+
+def home_kernel(terms, state, order, out):
+    del order
+    value = state[...].astype(full)
+    for source in range(terms.shape[0]):
+        value = value + terms[source].astype(full)
+    rows = state.shape[0]
+    out[pl.ds(0, rows), :] = value.astype(half)
+    out[pl.ds(rows, rows), :] = jnp.zeros(state.shape, half)
+
+
+def home(terms, state, order):
+    rows, width = state.shape
+    whole = pl.BlockSpec(memory_space=pltpu.VMEM)
+    return pl.pallas_call(
+        home_kernel,
+        in_specs=[whole, whole, pl.BlockSpec(memory_space=pl.ANY)],
+        out_specs=whole,
+        out_shape=jax.ShapeDtypeStruct((2 * rows, width), half),
+        compiler_params=pltpu.CompilerParams(vmem_limit_bytes=16 * 1024 * 1024),
+        cost_estimate=pl.CostEstimate(
+            flops=17 * rows * width, bytes_accessed=40 * rows * width, transcendentals=0
+        ),
+    )(terms, state, order)
+
+
+def normalise_kernel(pieces, gain, order, state, normed):
+    del order
     groups = state.shape[1] // pieces.shape[2]
     cols = pieces.shape[2]
     for block in range(state.shape[0] // BLK):
@@ -148,19 +276,19 @@
             normed[rows, at] = (wide * inverse * gain[:, at]).astype(normed.dtype)
 
 
-def normalise(pieces, gain, rows, width):
+def normalise(pieces, gain, rows, width, order):
     whole = pl.BlockSpec(memory_space=pltpu.VMEM)
     shape = jax.ShapeDtypeStruct((rows, width), half)
     return pl.pallas_call(
         normalise_kernel,
-        in_specs=[whole, whole],
+        in_specs=[whole, whole, pl.BlockSpec(memory_space=pl.ANY)],
         out_specs=[whole, whole],
         out_shape=[shape, shape],
         compiler_params=pltpu.CompilerParams(vmem_limit_bytes=16 * 1024 * 1024),
         cost_estimate=pl.CostEstimate(
             flops=6 * rows * width, bytes_accessed=6 * rows * width, transcendentals=rows
         ),
-    )(pieces, gain[None])
+    )(pieces, gain[None], order)
 
 
 def slope_kernel(terms, dy, state, gain, out):
@@ -240,9 +368,12 @@
         return jnp.stack(picked)
 
     sh_rows = fetch(0)
-    dy = lax.all_gather(fetch(slots), "mp", axis=0, tiled=False)
-
-    hidden = residual.astype(full) + jnp.concatenate(teacher_terms(attention, out_proj, mp), axis=0)
+    dy_rows = fetch(slots)
+    dy = lax.all_gather(dy_rows, "mp", axis=0, tiled=False)
+
+    hidden = residual.astype(full) + jnp.concatenate(
+        [total(v) for v in teacher_terms(attention, out_proj, mp, (sh_rows, dy_rows))], axis=0
+    )
     squares = jnp.sum(hidden * hidden, axis=1)
     gained_hidden = hidden * final_gain
     parts = jnp.einsum(
@@ -280,13 +411,15 @@
     )
     placed = (placed / counts_block[:, None]).astype(half).astype(full)
     state_here = (sh_here.astype(full) + placed).astype(half)
-    state, normed_student = normalise(share(state_here, "mp"), student_gain, tokens, student_width)
-
     normed = (gained_hidden * inverse_rms[:, None]).astype(half).reshape(blocks, BLK, width_here)
     pooled = jnp.einsum("krt,ktd->krd", onehot, normed, preferred_element_type=full)
     pooled = (pooled / counts[:, :, None]).astype(half)
     pooled_all = lax.all_gather(pooled.reshape(n_mp, mine_rows, width_here), "dp", axis=0, tiled=False)
     pooled_all = jnp.swapaxes(pooled_all, 0, 1).reshape(n_dp * tokens, width_here)
+
+    state, normed_student = normalise(
+        share(state_here, "mp"), student_gain, tokens, student_width, pooled
+    )
 
     gate = jnp.dot(normed_student, gate_weight, preferred_element_type=full)
     up = jnp.dot(normed_student, up_weight, preferred_element_type=full)
@@ -294,26 +427,31 @@
     silu = gate * sigma
     act = (silu * up).astype(half)
     output = times_rows(act, down_weight).astype(half)
-    dy, _ = lax.optimization_barrier((dy, output[:8, :128]))
-    dy = jnp.swapaxes(dy, 0, 1).reshape(tokens, student_width)
-    dh = jnp.dot(dy, down_weight, preferred_element_type=full)
-    grad_gate = (dh * up * sigma * (1.0 + gate * (1.0 - sigma))).astype(half)
-    grad_up = (dh * silu).astype(half)
+    grad_gate, grad_up = backward(dy.reshape(tokens, student_width), down_weight, gate, up, output)
     dn = (times_rows(grad_gate, gate_weight) + times_rows(grad_up, up_weight)).astype(half)
     output = jnp.swapaxes(output.reshape(blocks, n_mp, rows, student_width), 0, 1)
     output = exchange(output, "mp")
     dn, output = lax.optimization_barrier((dn, output))
     dn = exchange(dn.reshape(n_mp, mine_rows, student_width), "mp")
-    output = jnp.sum(output.astype(full), axis=0)
     here = mp * mine_rows
     dproj = slope(
         dn,
-        lax.dynamic_slice_in_dim(dy, here, mine_rows, 0),
+        lax.dynamic_slice(
+            dy, ((mp % groups) * blocks, mp // groups, 0, 0), (blocks, 1, rows, student_width)
+        ).reshape(mine_rows, student_width),
         lax.dynamic_slice_in_dim(state, here, mine_rows, 0),
         student_gain,
         n_dp,
     )
-    dproj = share(exchange(dproj, "dp"), "mp")
+    state_rows = lax.dynamic_slice_in_dim(
+        state.reshape(blocks, BLK, student_width), mp * rows, rows, 1
+    )
+    out_rows = home(
+        output.reshape(n_mp, mine_rows, student_width),
+        state_rows.reshape(mine_rows, student_width),
+        dproj,
+    )
+    dproj = exchange(spread(exchange(dproj, "dp"), n_mp, out_rows), "mp")
     adapter_grad = lax.dot_general(
         pooled_all,
         dproj.reshape(n_dp * tokens, out_cols),
@@ -321,19 +459,14 @@
         preferred_element_type=full,
     )
 
-    state_rows = lax.dynamic_slice_in_dim(
-        state.reshape(blocks, BLK, student_width), mp * rows, rows, 1
-    )
-    out_rows = (state_rows.astype(full) + output).astype(half)
-    out_rows = jnp.concatenate([out_rows, state_rows[:1]], axis=0)
-    back = lax.all_gather(out_rows, "dp", axis=0, tiled=False)[:, :blocks]
-    back = back.reshape(n_dp * blocks, rows, student_width)
+    back = lax.all_gather(out_rows, "dp", axis=0, tiled=False)
     mine = block_owner == dp
     picks = []
     for slot in range(slots):
         chosen = mine & (ranks == slot)
         index = jnp.sum(jnp.where(chosen, jnp.arange(chosen.shape[0], dtype=jnp.int32), 0))
-        piece = lax.dynamic_index_in_dim(back, index, 0, False)
+        at = (index // blocks, (index % blocks) * rows, 0)
+        piece = lax.dynamic_slice(back, at, (1, rows, student_width))[0]
         picks.append(jnp.where(jnp.any(chosen), piece, jnp.zeros((), half)))
     student_out = jnp.stack(picks, axis=1)
     return (student_out[None], adapter_grad)

time: 277 us -> 256 us (0.924)
  waiting for transfers between devices: 117 us -> 85.2 us
  local copies, waits for them, and re-layouts: 17.6 us -> 37 us
  other arithmetic: 24.2 us -> 12.8 us
  blocking collectives: 11.1 us -> 0 us
  Pallas kernels: 13.9 us -> 21.3 us
  starting transfers between devices: 46.4 us -> 52.3 us
  matrix products: 19.8 us -> 16 us
  between operations: 26.1 us -> 29 us
    all_gather x2, waiting for transfers between devices: 27.4 us -> 0.02 us  [the longest x1 0.02 us: on_device(): dy = lax.all_gather(dy_rows, 'mp', axis=0, tiled=False)]
    unnamed x36 -> x77, local copies, waits for them, and re-layouts: 3.95 us -> 29.1 us
    all_to_all x1 -> x0, blocking collectives: 11.1 us -> none  [exchange(): return lax.all_to_all(pieces, axis, split_axis=0, concat_axis=0, tiled=True)]
    ppermute x12 -> x14, waiting for transfers between devices: 22.2 us -> 13.7 us  [step(): return lax.ppermute(value, 'mp', pairs)]
    pallas_call x2 -> x7, Pallas kernels: 12.1 us -> 18.9 us  [the longest x1 8.74 us: teacher_terms(): pl.pallas_call(terms_kernel, in_specs=[scalars, whole, anywhere], out_spe...]
    all_to_all x5 -> x6, starting transfers between devices: 24.8 us -> 30.1 us  [exchange(): return lax.all_to_all(pieces, axis, split_axis=0, concat_axis=0, tiled=True)]
    add x2, other arithmetic: 4.03 us -> 0.13 us  [total(): result = result + value.astype(full)]
    all_to_all x5 -> x6, waiting for transfers between devices: 66.9 us -> 70.2 us  [exchange(): return lax.all_to_all(pieces, axis, split_axis=0, concat_axis=0, tiled=True)]
  transfers between devices with their start and end apart: 21 -> 24, of which waited for: 8 -> 12; matrix products, arithmetic and copies ran while one was open for 14% -> 11% of each run, Pallas kernels for 4% -> 8%
where the time goes in v4:
time: 256 us; the launch traced here: 254 us
  waiting for transfers between devices  85.2 us (33%)
  starting transfers between devices  52.3 us (20%)
  local copies, waits for them, and re-layouts  37 us (14%)
  between operations  29 us (11%)
  Pallas kernels  21.3 us (8%)
  matrix products  16 us (6%)
  other arithmetic  12.8 us (5%)
    all_to_all x6, waiting for transfers between devices, exchange(): return lax.all_to_all(pieces, axis, split_axis=0, concat_axis=0, tiled=True)  70.2 us
    all_to_all x6, starting transfers between devices, exchange(): return lax.all_to_all(pieces, axis, split_axis=0, concat_axis=0, tiled=True)  30.1 us
    unnamed x77, local copies, waits for them, and re-layouts  29.1 us
    ppermute x14, starting transfers between devices, step(): return lax.ppermute(value, 'mp', pairs)  21.8 us
    ppermute x14, waiting for transfers between devices, step(): return lax.ppermute(value, 'mp', pairs)  13.7 us
    pallas_call x1, Pallas kernels, teacher_terms(): pl.pallas_call(terms_kernel, in_specs=[scalars, whole, anywhere], out_spe...  8.74 us
  transfers between devices with their start and end apart: 24, of which 12 were waited for; matrix products, arithmetic and copies ran while one was open for 11% of the time, Pallas kernels for 8%

profile of v4, /device:TPU:0, one launch (start us, length us, event | category | flops | bytes accessed | tf_op | source)
XLA Modules:
  0.0 253.6 jit_solution(1350346379362127746)
XLA Ops:
  7.2 2.1 pad_maximum_fusion.1
  9.5 3.4 %copy-done.1 = bf16[512,8192]{1,0:T(8,128)(2,1)S(1)} copy-done((bf16[512,8192]{1,0:T(8,128)(2,1)S(1)}, bf16[512,8192]{1,0:T(8,128)(2,1)}, u32[]{:S(2)}) %copy-start.1) | copy-done | bytes 8388632
  13.8 8.7 %shard_map.140 = (bf16[4,128,512]{2,1,0:T(8,128)(2,1)S(1)}, bf16[4,128,512]{2,1,0:T(8,128)(2,1)S(1)}, bf16[4,128,512]{2,1,0:T(8,128)(2,1)S(1)}, bf16[4,64,512]{2...) custom-call(s32[2]{0:T(128)S(1)} %pad_add_fusion.place, ...), custom_call_target="tpu_custom_call" | custom-call | flops 2147483648 | bytes 8388608 | tf_op jit(solution)/shard_map/pallas_call | solution.py:118
  30.7 2.0 collective-permute-start.2
  32.7 2.1 collective-permute-start.3
  46.1 2.6 %shard_map.141 = (bf16[4,128,512]{2,1,0:T(8,128)(2,1)}, bf16[4,128,512]{2,1,0:T(8,128)(2,1)}, bf16[4,128,512]{2,1,0:T(8,128)(2,1)}, bf16[4,128,512]{2,1,0:T(8,128)(2,1)}) custom-call(bf16[4,128,512]{2,1,0:T(8,128)(2,1)S(1)} %copy-done.19, bf16[4,128,512]{2,1,0:T(8,128)(2,1)S(1)} %copy-done.21, bf16[4,64,512]{2,1,0:T(8,128)(2,1)S(1)} %collective-permute-done.refs_2_, ...), custom_call_target="tpu_custom_call" | custom-call | flops 1048576 | bytes 5242880 | tf_op jit(solution)/shard_map/pallas_call | solution.py:136
  49.0 2.9 %collective-permute-start.5 = (bf16[4,128,512]{2,1,0:T(8,128)(2,1)}, bf16[4,128,512]{2,1,0:T(8,128)(2,1)}, u32[]{:S(2)}, u32[]{:S(2)}) collective-permute-start(bf16[4,128,512]{2,1,0:T(8,128)(2,1)} %get-tuple-element.52), channel_id=1, source_target_pairs={{0,12},{1,13},{2,14},{3,15},{4,0},{5,1},{6,2},{7,3},{8,4},{9,5},{1... | collective-permute-start | bytes 1572872 | tf_op jit(solution)/shard_map/ppermute | solution.py:43
  52.1 3.0 %collective-permute-start.7 = (bf16[4,128,512]{2,1,0:T(8,128)(2,1)}, bf16[4,128,512]{2,1,0:T(8,128)(2,1)}, u32[]{:S(2)}, u32[]{:S(2)}) collective-permute-start(bf16[4,128,512]{2,1,0:T(8,128)(2,1)} %get-tuple-element.55), channel_id=1, source_target_pairs={{0,3},{1,0},{2,1},{3,2},{4,7},{5,4},{6,5},{7,6},{8,11},{9,8},{10,9... | collective-permute-start | bytes 1572872 | tf_op jit(solution)/shard_map/ppermute | solution.py:43
  57.0 6.0 %collective-permute-done.4.refs_1_ = bf16[4,128,512]{2,1,0:T(8,128)(2,1)} collective-permute-done((bf16[4,128,512]{2,1,0:T(8,128)(2,1)}, bf16[4,128,512]{2,1,0:T(8,128)(2,1)}, u32[]{:S(2)}, u32[]{:S(2)}) %collective-permute-start.4) | collective-permute-done | bytes 524320 | tf_op jit(solution)/shard_map/ppermute | solution.py:43
  63.1 2.7 %collective-permute-done.6.refs_4_ = bf16[4,128,512]{2,1,0:T(8,128)(2,1)} collective-permute-done((bf16[4,128,512]{2,1,0:T(8,128)(2,1)}, bf16[4,128,512]{2,1,0:T(8,128)(2,1)}, u32[]{:S(2)}, u32[]{:S(2)}) %collective-permute-start.6) | collective-permute-done | bytes 524320 | tf_op jit(solution)/shard_map/ppermute | solution.py:43
  69.9 4.4 %collective-permute-start.9 = (bf16[128,512]{1,0:T(8,128)(2,1)S(1)}, bf16[128,512]{1,0:T(8,128)(2,1)S(1)}, u32[]{:S(2)}, u32[]{:S(2)}) collective-permute-start(bf16[128,512]{1,0:T(8,128)(2,1)S(1)} %get-tuple-element.58), channel_id=1, source_target_pairs={{0,2},{1,3},{2,0},{3,1},{4,6},{5,7},{6,4},{7,5},{8,10},{9,11},{10,... | collective-permute-start | bytes 393224 | tf_op jit(solution)/shard_map/ppermute | solution.py:43
  74.4 2.0 collective-permute-start.12
  79.3 2.7 %collective-permute-done.11 = bf16[128,512]{1,0:T(8,128)(2,1)S(1)} collective-permute-done((bf16[128,512]{1,0:T(8,128)(2,1)S(1)}, bf16[128,512]{1,0:T(8,128)(2,1)S(1)}, u32[]{:S(2)}, u32[]{:S(2)}) %collective-permute-start.11) | collective-permute-done | bytes 131104 | tf_op jit(solution)/shard_map/ppermute | solution.py:43
  86.4 5.6 %all-to-all-start = ((bf16[16,144,384]{2,1,0:T(8,128)(2,1)}), bf16[16,144,384]{2,1,0:T(8,128)(2,1)}, u32[]{:S(2)}, u32[]{:S(2)}) async-start(bf16[16,144,384]{2,1,0:T(8,128)(2,1)} %bitcast.119), calls=%async_computation | async-start | bytes 3538944 | tf_op jit(solution)/shard_map/all_to_all | solution.py:15
  92.9 19.1 %all-to-all-done = bf16[16,144,384]{2,1,0:T(8,128)(2,1)} async-done(((bf16[16,144,384]{2,1,0:T(8,128)(2,1)}), bf16[16,144,384]{2,1,0:T(8,128)(2,1)}, u32[]{:S(2)}, u32[]{:S(2)}) %all-to-all-start) | async-done | bytes 1769504 | tf_op jit(solution)/shard_map/all_to_all | solution.py:15
  117.1 5.3 %all-to-all-start.1 = ((bf16[16,128,384]{2,1,0:T(8,128)(2,1)}), bf16[16,128,384]{2,1,0:T(8,128)(2,1)}, u32[]{:S(2)}, u32[]{:S(2)}) async-start(bf16[16,128,384]{2,1,0:T(8,128)(2,1)} %broadcast_in_dim.46), calls=%async_computation.1 | async-start | bytes 3145728 | tf_op jit(solution)/shard_map/all_to_all | solution.py:15
  124.7 16.3 %all-to-all-done.1.pieces = bf16[16,128,384]{2,1,0:T(8,128)(2,1)} async-done(((bf16[16,128,384]{2,1,0:T(8,128)(2,1)}), bf16[16,128,384]{2,1,0:T(8,128)(2,1)}, u32[]{:S(2)}, u32[]{:S(2)}) %all-to-all-start.1) | async-done | bytes 1572896 | tf_op jit(solution)/shard_map/all_to_all | solution.py:15
  141.9 2.2 shard_map.143
  144.2 3.5 %fusion.42.up = f32[256,512]{1,0:T(8,128)S(1)} fusion(bf16[256,3072]{1,0:T(8,128)(2,1)S(1)} %get-tuple-element.64, bf16[3072,512]{1,0:T(8,128)(2,1)} %param.26), kind=kOutput, calls=%fused_computation.101 | convolution fusion | flops 805306368 | bytes 5242880 | tf_op jit(solution)/shard_map/dot_general | solution.py:425
  153.3 5.2 %all-to-all-start.2 = ((bf16[16,2,8,3072]{3,2,1,0:T(8,128)(2,1)}), bf16[16,2,8,3072]{3,2,1,0:T(8,128)(2,1)}, u32[]{:S(2)}, u32[]{:S(2)}) async-start(bf16[16,2,8,3072]{3,2,1,0:T(8,128)(2,1)} %bitcast.120), calls=%async_computation.2 | async-start | bytes 3145728 | tf_op jit(solution)/shard_map/all_to_all | solution.py:15
  168.3 2.2 fusion
  170.5 4.3 %all-to-all-done.2 = bf16[16,2,8,3072]{3,2,1,0:T(8,128)(2,1)} async-done(((bf16[16,2,8,3072]{3,2,1,0:T(8,128)(2,1)}), bf16[16,2,8,3072]{3,2,1,0:T(8,128)(2,1)}, u32[]{:S(2)}, u32[]{:S(2)}) %all-to-all-start.2) | async-done | bytes 1572896 | tf_op jit(solution)/shard_map/all_to_all | solution.py:15
  174.9 5.0 %all-to-all-start.3 = ((bf16[16,16,3072]{2,1,0:T(8,128)(2,1)}), bf16[16,16,3072]{2,1,0:T(8,128)(2,1)}, u32[]{:S(2)}, u32[]{:S(2)}) async-start(bf16[16,16,3072]{2,1,0:T(8,128)(2,1)} %bitcast.121), calls=%async_computation.3 | async-start | bytes 3145728 | tf_op jit(solution)/shard_map/all_to_all | solution.py:15
  181.7 14.4 %all-to-all-done.3.terms = bf16[16,16,3072]{2,1,0:T(8,128)(2,1)} async-done(((bf16[16,16,3072]{2,1,0:T(8,128)(2,1)}), bf16[16,16,3072]{2,1,0:T(8,128)(2,1)}, u32[]{:S(2)}, u32[]{:S(2)}) %all-to-all-start.3) | async-done | bytes 1572896 | tf_op jit(solution)/shard_map/all_to_all | solution.py:15
  196.1 2.4 shard_map.145.order
  198.5 4.7 %all-to-all-start.4 = ((bf16[8,16,384]{2,1,0:T(8,128)(2,1)}), bf16[8,16,384]{2,1,0:T(8,128)(2,1)S(1)}, u32[]{:S(2)}, u32[]{:S(2)}) async-start(bf16[8,16,384]{2,1,0:T(8,128)(2,1)} %shard_map.145.order), calls=%async_computation.4 | async-start | bytes 196608 | tf_op jit(solution)/shard_map/all_to_all | solution.py:15
  204.1 2.3 shard_map.146.order
  206.4 2.6 %all-to-all-done.4.piece = bf16[8,16,384]{2,1,0:T(8,128)(2,1)S(1)} async-done(((bf16[8,16,384]{2,1,0:T(8,128)(2,1)}), bf16[8,16,384]{2,1,0:T(8,128)(2,1)S(1)}, u32[]{:S(2)}, u32[]{:S(2)}) %all-to-all-start.4) | async-done | bytes 98336 | tf_op jit(solution)/shard_map/all_to_all | solution.py:15
  210.3 4.4 %all-to-all-start.5 = ((bf16[16,8,16,384]{3,2,1,0:T(8,128)(2,1)}), bf16[16,8,16,384]{3,2,1,0:T(8,128)(2,1)}, u32[]{:S(2)}, u32[]{:S(2)}) async-start(bf16[16,8,16,384]{3,2,1,0:T(8,128)(2,1)} %copy-done.2), calls=%async_computation.5 | async-start | bytes 3145728 | tf_op jit(solution)/shard_map/all_to_all | solution.py:15
  225.2 13.5 %all-to-all-done.5 = bf16[16,8,16,384]{3,2,1,0:T(8,128)(2,1)} async-done(((bf16[16,8,16,384]{3,2,1,0:T(8,128)(2,1)}), bf16[16,8,16,384]{3,2,1,0:T(8,128)(2,1)}, u32[]{:S(2)}, u32[]{:S(2)}) %all-to-all-start.5) | async-done | bytes 1572896 | tf_op jit(solution)/shard_map/all_to_all | solution.py:15
  238.7 4.2 %fusion.7 = f32[512,384]{1,0:T(8,128)} fusion(bf16[16,8,16,384]{3,2,1,0:T(8,128)(2,1)} %all-to-all-done.5, bf16[8,16,16,512]{3,2,0,1:T(8,128)(2,1)} %all-gather.8.cloned.1.call-done), kind=kOutput, calls=%fused_computation.13 | convolution fusion | flops 805306368 | bytes 4456448 | tf_op jit(solution)/shard_map/dot_general | solution.py:455
  242.9 3.3 %select_bitcast_fusion.3 = (bf16[8,1,3072]{2,0,1:T(8,128)(2,1)S(1)}, bf16[8,1,3072]{2,0,1:T(8,128)(2,1)S(1)}, bf16[8,1,3072]{2,0,1:T(8,128)(2,1)S(1)}, bf16[8,1,3072]{2,0,1:T(8,128)(2,1)S(1)}) fusion(bf16[8,32,3072]{2,1,0:T(8,128)(2,1)} %bitcast.131, s32[]{:T(128)S(6)} %select_n.237, s32[]{:T(128)S(6)} %select_n.239, pred[]{:T(512)} %get-tuple-element.74, ...), kind=kLoop, calls=%fused_computation.50 | loop fusion | flops 98304 | bytes 393252 | tf_op jit(solution)/shard_map/jit(_where)/select_n | solution.py:470
  (151 shorter events, 59.7 us)
Async XLA Ops:
  7.2 140.5 %copy-start = (bf16[3072,512]{1,0:T(8,128)(2,1)S(1)}, bf16[3072,512]{1,0:T(8,128)(2,1)}, u32[]{:S(2)}) copy-start(bf16[3072,512]{1,0:T(8,128)(2,1)} %param.25) | copy-start | bytes 9437188
  7.2 48.0 %all-gather.10.cloned.1.call-start = ((), (), s32[]{:S(2)}) async-start(), calls=%async_computation.7 | async-start | bytes 3538944 | tf_op jit(solution)/shard_map/all_gather | solution.py:360
  13.8 21.0 %copy-start.33 = (s32[16]{0:T(128)S(1)}, s32[16]{0:T(128)}, u32[]{:S(2)}) copy-start(s32[16]{0:T(128)} %param.21) | copy-start | bytes 196
  27.4 14.5 %collective-permute-start = (bf16[4,64,512]{2,1,0:T(8,128)(2,1)}, bf16[4,64,512]{2,1,0:T(8,128)(2,1)S(1)}, u32[]{:S(2)}, u32[]{:S(2)}) collective-permute-start(bf16[4,64,512]{2,1,0:T(8,128)(2,1)} %get-tuple-element.45), channel_id=1, source_target_pairs={{0,4},{1,5},{2,6},{3,7},{4,8},{5,9},{6,10},{7,11},{8,12},{9,13},{1... | collective-permute-start | bytes 786440 | tf_op jit(solution)/shard_map/ppermute | solution.py:43
  29.1 12.8 %collective-permute-start.1 = (bf16[4,64,512]{2,1,0:T(8,128)(2,1)}, bf16[4,64,512]{2,1,0:T(8,128)(2,1)}, u32[]{:S(2)}, u32[]{:S(2)}) collective-permute-start(bf16[4,64,512]{2,1,0:T(8,128)(2,1)} %get-tuple-element.46), channel_id=1, source_target_pairs={{0,12},{1,13},{2,14},{3,15},{4,0},{5,1},{6,2},{7,3},{8,4},{9,5},{1... | collective-permute-start | bytes 786440 | tf_op jit(solution)/shard_map/ppermute | solution.py:43
  30.7 11.2 %collective-permute-start.2 = (bf16[4,64,512]{2,1,0:T(8,128)(2,1)}, bf16[4,64,512]{2,1,0:T(8,128)(2,1)}, u32[]{:S(2)}, u32[]{:S(2)}) collective-permute-start(bf16[4,64,512]{2,1,0:T(8,128)(2,1)} %get-tuple-element.49), channel_id=1, source_target_pairs={{0,1},{1,2},{2,3},{3,0},{4,5},{5,6},{6,7},{7,4},{8,9},{9,10},{10,1... | collective-permute-start | bytes 786440 | tf_op jit(solution)/shard_map/ppermute | solution.py:43
  32.7 9.3 %collective-permute-start.3 = (bf16[4,64,512]{2,1,0:T(8,128)(2,1)}, bf16[4,64,512]{2,1,0:T(8,128)(2,1)}, u32[]{:S(2)}, u32[]{:S(2)}) collective-permute-start(bf16[4,64,512]{2,1,0:T(8,128)(2,1)} %get-tuple-element.50), channel_id=1, source_target_pairs={{0,3},{1,0},{2,1},{3,2},{4,7},{5,4},{6,5},{7,6},{8,11},{9,8},{10,9... | collective-permute-start | bytes 786440 | tf_op jit(solution)/shard_map/ppermute | solution.py:43
  48.7 14.4 %collective-permute-start.4 = (bf16[4,128,512]{2,1,0:T(8,128)(2,1)}, bf16[4,128,512]{2,1,0:T(8,128)(2,1)}, u32[]{:S(2)}, u32[]{:S(2)}) collective-permute-start(bf16[4,128,512]{2,1,0:T(8,128)(2,1)} %get-tuple-element.51), channel_id=1, source_target_pairs={{0,4},{1,5},{2,6},{3,7},{4,8},{5,9},{6,10},{7,11},{8,12},{9,13},{1... | collective-permute-start | bytes 1572872 | tf_op jit(solution)/shard_map/ppermute | solution.py:43
  49.0 14.0 %collective-permute-start.5 = (bf16[4,128,512]{2,1,0:T(8,128)(2,1)}, bf16[4,128,512]{2,1,0:T(8,128)(2,1)}, u32[]{:S(2)}, u32[]{:S(2)}) collective-permute-start(bf16[4,128,512]{2,1,0:T(8,128)(2,1)} %get-tuple-element.52), channel_id=1, source_target_pairs={{0,12},{1,13},{2,14},{3,15},{4,0},{5,1},{6,2},{7,3},{8,4},{9,5},{1... | collective-permute-start | bytes 1572872 | tf_op jit(solution)/shard_map/ppermute | solution.py:43
  51.9 13.8 %collective-permute-start.6 = (bf16[4,128,512]{2,1,0:T(8,128)(2,1)}, bf16[4,128,512]{2,1,0:T(8,128)(2,1)}, u32[]{:S(2)}, u32[]{:S(2)}) collective-permute-start(bf16[4,128,512]{2,1,0:T(8,128)(2,1)} %get-tuple-element.54), channel_id=1, source_target_pairs={{0,1},{1,2},{2,3},{3,0},{4,5},{5,6},{6,7},{7,4},{8,9},{9,10},{10,1... | collective-permute-start | bytes 1572872 | tf_op jit(solution)/shard_map/ppermute | solution.py:43
  52.1 13.6 %collective-permute-start.7 = (bf16[4,128,512]{2,1,0:T(8,128)(2,1)}, bf16[4,128,512]{2,1,0:T(8,128)(2,1)}, u32[]{:S(2)}, u32[]{:S(2)}) collective-permute-start(bf16[4,128,512]{2,1,0:T(8,128)(2,1)} %get-tuple-element.55), channel_id=1, source_target_pairs={{0,3},{1,0},{2,1},{3,2},{4,7},{5,4},{6,5},{7,6},{8,11},{9,8},{10,9... | collective-permute-start | bytes 1572872 | tf_op jit(solution)/shard_map/ppermute | solution.py:43
  57.0 22.3 %copy-start.9 = (bf16[2,8,3072]{2,1,0:T(8,128)(2,1)}, bf16[2,8,3072]{2,1,0:T(8,128)(2,1)S(1)}, u32[]{:S(2)}) copy-start(bf16[2,8,3072]{2,1,0:T(8,128)(2,1)S(1)} %pad_maximum_fusion.2.refs_7_) | copy-start | bytes 294916
  67.8 15.8 %copy-start.31 = (bf16[256,512]{1,0:T(8,128)(2,1)S(1)}, bf16[256,512]{1,0:T(8,128)(2,1)}, u32[]{:S(2)}) copy-start(bf16[256,512]{1,0:T(8,128)(2,1)} %param.17) | copy-start | bytes 786436
  67.8 15.8 %copy-start.32 = (f32[512]{0:T(512)S(1)}, f32[512]{0:T(512)}, u32[]{:S(2)}) copy-start(f32[512]{0:T(512)} %param.18) | copy-start | bytes 6148
  69.8 14.1 %copy-start.35 = (bf16[512,3072]{1,0:T(8,128)(2,1)S(1)}, bf16[512,3072]{1,0:T(8,128)(2,1)}, u32[]{:S(2)}) copy-start(bf16[512,3072]{1,0:T(8,128)(2,1)} %param.19) | copy-start | bytes 9437188
  69.8 6.6 %collective-permute-start.8 = (bf16[128,512]{1,0:T(8,128)(2,1)S(1)}, bf16[128,512]{1,0:T(8,128)(2,1)S(1)}, u32[]{:S(2)}, u32[]{:S(2)}) collective-permute-start(bf16[128,512]{1,0:T(8,128)(2,1)S(1)} %get-tuple-element.57), channel_id=1, source_target_pairs={{0,1},{1,2},{2,3},{3,0},{4,5},{5,6},{6,7},{7,4},{8,9},{9,10},{10,1... | collective-permute-start | bytes 393224 | tf_op jit(solution)/shard_map/ppermute | solution.py:43
  69.9 8.7 %collective-permute-start.9 = (bf16[128,512]{1,0:T(8,128)(2,1)S(1)}, bf16[128,512]{1,0:T(8,128)(2,1)S(1)}, u32[]{:S(2)}, u32[]{:S(2)}) collective-permute-start(bf16[128,512]{1,0:T(8,128)(2,1)S(1)} %get-tuple-element.58), channel_id=1, source_target_pairs={{0,2},{1,3},{2,0},{3,1},{4,6},{5,7},{6,4},{7,5},{8,10},{9,11},{10,... | collective-permute-start | bytes 393224 | tf_op jit(solution)/shard_map/ppermute | solution.py:43
  74.3 5.0 %collective-permute-start.10 = (bf16[128,512]{1,0:T(8,128)(2,1)S(1)}, bf16[128,512]{1,0:T(8,128)(2,1)S(1)}, u32[]{:S(2)}, u32[]{:S(2)}) collective-permute-start(bf16[128,512]{1,0:T(8,128)(2,1)S(1)} %get-tuple-element.59), channel_id=1, source_target_pairs={{0,3},{1,0},{2,1},{3,2},{4,7},{5,4},{6,5},{7,6},{8,11},{9,8},{10,9... | collective-permute-start | bytes 393224 | tf_op jit(solution)/shard_map/ppermute | solution.py:43
  74.3 7.7 %collective-permute-start.11 = (bf16[128,512]{1,0:T(8,128)(2,1)S(1)}, bf16[128,512]{1,0:T(8,128)(2,1)S(1)}, u32[]{:S(2)}, u32[]{:S(2)}) collective-permute-start(bf16[128,512]{1,0:T(8,128)(2,1)S(1)} %get-tuple-element.61), channel_id=1, source_target_pairs={{0,4},{1,5},{2,6},{3,7},{4,8},{5,9},{6,10},{7,11},{8,12},{9,13},{1... | collective-permute-start | bytes 393224 | tf_op jit(solution)/shard_map/ppermute | solution.py:43
  74.4 7.6 %collective-permute-start.12 = (bf16[128,512]{1,0:T(8,128)(2,1)S(1)}, bf16[128,512]{1,0:T(8,128)(2,1)S(1)}, u32[]{:S(2)}, u32[]{:S(2)}) collective-permute-start(bf16[128,512]{1,0:T(8,128)(2,1)S(1)} %get-tuple-element.62), channel_id=1, source_target_pairs={{0,8},{1,9},{2,10},{3,11},{4,12},{5,13},{6,14},{7,15},{8,0},{9,1},... | collective-permute-start | bytes 393224 | tf_op jit(solution)/shard_map/ppermute | solution.py:43
  76.4 6.5 %collective-permute-start.13 = (bf16[128,512]{1,0:T(8,128)(2,1)S(1)}, bf16[128,512]{1,0:T(8,128)(2,1)S(1)}, u32[]{:S(2)}, u32[]{:S(2)}) collective-permute-start(bf16[128,512]{1,0:T(8,128)(2,1)S(1)} %get-tuple-element.63), channel_id=1, source_target_pairs={{0,12},{1,13},{2,14},{3,15},{4,0},{5,1},{6,2},{7,3},{8,4},{9,5},{1... | collective-permute-start | bytes 393224 | tf_op jit(solution)/shard_map/ppermute | solution.py:43
  86.4 6.3 %copy-start.34 = (s32[256]{0:T(256)S(1)}, s32[256]{0:T(256)}, u32[]{:S(2)}) copy-start(s32[256]{0:T(256)} %param.20) | copy-start | bytes 3076
  86.4 25.6 %all-to-all-start = ((bf16[16,144,384]{2,1,0:T(8,128)(2,1)}), bf16[16,144,384]{2,1,0:T(8,128)(2,1)}, u32[]{:S(2)}, u32[]{:S(2)}) async-start(bf16[16,144,384]{2,1,0:T(8,128)(2,1)} %bitcast.119), calls=%async_computation | async-start | bytes 3538944 | tf_op jit(solution)/shard_map/all_to_all | solution.py:15
  91.9 66.6 %all-gather.12.cloned.1.call-start = ((), (), s32[]{:S(2)}) async-start(), calls=%async_computation.8 | async-start | bytes 1671168 | tf_op jit(solution)/shard_map/all_gather | solution.py:372
  117.1 23.9 %all-to-all-start.1 = ((bf16[16,128,384]{2,1,0:T(8,128)(2,1)}), bf16[16,128,384]{2,1,0:T(8,128)(2,1)}, u32[]{:S(2)}, u32[]{:S(2)}) async-start(bf16[16,128,384]{2,1,0:T(8,128)(2,1)} %broadcast_in_dim.46), calls=%async_computation.1 | async-start | bytes 3145728 | tf_op jit(solution)/shard_map/all_to_all | solution.py:15
  122.3 18.7 %copy-start.27 = (f32[3072]{0:T(1024)S(1)}, f32[3072]{0:T(1024)}, u32[]{:S(2)}) copy-start(f32[3072]{0:T(1024)} %param.24) | copy-start | bytes 36868
  122.3 102.8 %all-gather.8.cloned.1.call-start = ((), (), s32[]{:S(2)}) async-start(), calls=%async_computation.6 | async-start | bytes 2359296 | tf_op jit(solution)/shard_map/all_gather | solution.py:417
  153.3 21.6 %all-to-all-start.2 = ((bf16[16,2,8,3072]{3,2,1,0:T(8,128)(2,1)}), bf16[16,2,8,3072]{3,2,1,0:T(8,128)(2,1)}, u32[]{:S(2)}, u32[]{:S(2)}) async-start(bf16[16,2,8,3072]{3,2,1,0:T(8,128)(2,1)} %bitcast.120), calls=%async_computation.2 | async-start | bytes 3145728 | tf_op jit(solution)/shard_map/all_to_all | solution.py:15
  174.9 21.2 %all-to-all-start.3 = ((bf16[16,16,3072]{2,1,0:T(8,128)(2,1)}), bf16[16,16,3072]{2,1,0:T(8,128)(2,1)}, u32[]{:S(2)}, u32[]{:S(2)}) async-start(bf16[16,16,3072]{2,1,0:T(8,128)(2,1)} %bitcast.121), calls=%async_computation.3 | async-start | bytes 3145728 | tf_op jit(solution)/shard_map/all_to_all | solution.py:15
  198.5 10.5 %all-to-all-start.4 = ((bf16[8,16,384]{2,1,0:T(8,128)(2,1)}), bf16[8,16,384]{2,1,0:T(8,128)(2,1)S(1)}, u32[]{:S(2)}, u32[]{:S(2)}) async-start(bf16[8,16,384]{2,1,0:T(8,128)(2,1)} %shard_map.145.order), calls=%async_computation.4 | async-start | bytes 196608 | tf_op jit(solution)/shard_map/all_to_all | solution.py:15
  210.3 28.4 %all-to-all-start.5 = ((bf16[16,8,16,384]{3,2,1,0:T(8,128)(2,1)}), bf16[16,8,16,384]{3,2,1,0:T(8,128)(2,1)}, u32[]{:S(2)}, u32[]{:S(2)}) async-start(bf16[16,8,16,384]{3,2,1,0:T(8,128)(2,1)} %copy-done.2), calls=%async_computation.5 | async-start | bytes 3145728 | tf_op jit(solution)/shard_map/all_to_all | solution.py:15
  214.7 28.2 %all-gather.14.cloned.1.call-start = ((), (), s32[]{:S(2)}) async-start(), calls=%async_computation.9 | async-start | bytes 1769472 | tf_op jit(solution)/shard_map/all_gather | solution.py:462
  (28 other events, 35.8 us)
Sparse Core Ops, SparseCore 0:
  9.7 30.2 all-gather.9
  95.5 50.4 all-gather.11
  147.7 25.7 all-gather.7
  217.5 23.7 all-gather.13

commit v5 on v4

--- a/solution.py
+++ b/solution.py
@@ -13,11 +13,6 @@
 
 def exchange(pieces, axis):
     return lax.all_to_all(pieces, axis, split_axis=0, concat_axis=0, tiled=True)
-
-
-def share(piece, axis):
-    size = lax.axis_size(axis)
-    return exchange(jnp.broadcast_to(piece[None], (size,) + piece.shape), axis)
 
 
 def three_parts(value):
@@ -81,15 +76,10 @@
     for block in (0, 1):
         up, down, lower, upper = ins[4 * block : 4 * block + 4]
         to_up, to_down = outs[2 * block], outs[2 * block + 1]
-        for piece in range(SIDE):
-            to_up[piece, :middle] = (
-                up[piece, :middle].astype(full) + lower[piece].astype(full)
-            ).astype(half)
-            to_up[piece, middle:] = up[piece, middle:]
-            to_down[piece, :middle] = down[piece, :middle]
-            to_down[piece, middle:] = (
-                down[piece, middle:].astype(full) + upper[piece].astype(full)
-            ).astype(half)
+        to_up[0, :middle] = (up[0, :middle].astype(full) + lower[0].astype(full)).astype(half)
+        to_up[0, middle:] = up[0, middle:]
+        to_down[0, :middle] = down[0, :middle]
+        to_down[0, middle:] = (down[0, middle:].astype(full) + upper[0].astype(full)).astype(half)
 
 
 def gather_kernel(place, *refs):
@@ -109,22 +99,24 @@
     whole = pl.BlockSpec(memory_space=pltpu.VMEM)
     scalars = pl.BlockSpec(memory_space=pltpu.SMEM)
     anywhere = pl.BlockSpec(memory_space=pl.ANY)
-    limit = pltpu.CompilerParams(vmem_limit_bytes=24 * 1024 * 1024)
+    limit = pltpu.CompilerParams(vmem_limit_bytes=40 * 1024 * 1024)
     place = jnp.stack([mp // SIDE, mp % SIDE]).astype(jnp.int32)
     full_piece = jax.ShapeDtypeStruct((SIDE, BLK, width), half)
     half_piece = jax.ShapeDtypeStruct((SIDE, BLK // 2, width), half)
     moves = full_piece.size
+    one_piece = pl.BlockSpec((1, BLK, width), lambda i: (i, 0, 0))
+    one_half = pl.BlockSpec((1, BLK // 2, width), lambda i: (i, 0, 0))
 
     kept0, up0, down0, lower0, upper0, kept1, up1, down1, lower1, upper1 = pl.pallas_call(
         terms_kernel,
-        in_specs=[scalars, whole, anywhere],
+        in_specs=[scalars, whole, pl.BlockSpec(memory_space=pltpu.HBM)],
         out_specs=[whole] * 10,
         out_shape=[full_piece, full_piece, full_piece, half_piece, half_piece] * 2,
         scratch_shapes=[
             pltpu.VMEM((SIDE * SIDE, width, width), half),
             pltpu.SemaphoreType.DMA((SIDE * SIDE,)),
         ],
-        compiler_params=limit,
+        compiler_params=pltpu.CompilerParams(vmem_limit_bytes=48 * 1024 * 1024),
         cost_estimate=pl.CostEstimate(
             flops=2 * attention.shape[0] * out_proj.size,
             bytes_accessed=2 * out_proj.size,
@@ -135,8 +127,9 @@
     lower1, upper1 = step(lower1, 0, 1), step(upper1, 0, -1)
     up0, down0, up1, down1 = pl.pallas_call(
         merge_kernel,
-        in_specs=[whole] * 8,
-        out_specs=[whole] * 4,
+        grid=(SIDE,),
+        in_specs=[one_piece, one_piece, one_half, one_half] * 2,
+        out_specs=[one_piece] * 4,
         out_shape=[full_piece] * 4,
         compiler_params=limit,
         cost_estimate=pl.CostEstimate(
@@ -200,7 +193,7 @@
         out_specs=[whole, whole],
         out_shape=[shape, shape],
         scratch_shapes=[pltpu.VMEM(gate.shape, full)],
-        compiler_params=pltpu.CompilerParams(vmem_limit_bytes=24 * 1024 * 1024),
+        compiler_params=pltpu.CompilerParams(vmem_limit_bytes=56 * 1024 * 1024),
         cost_estimate=pl.CostEstimate(
             flops=2 * dy.shape[0] * down.size,
             bytes_accessed=2 * (down.size + dy.size) + 16 * gate.size,
@@ -209,28 +202,32 @@
     )(dy, down, gate, up, order)
 
 
-def spread_kernel(piece, order, out):
-    del order
-    for index in range(out.shape[0]):
-        out[index] = piece[...]
-
-
-def spread(piece, count, order):
+def spread_kernel(piece, out, sems):
+    copies = [
+        pltpu.make_async_copy(piece, out.at[to], sems.at[to]) for to in range(out.shape[0])
+    ]
+    for copy in copies:
+        copy.start()
+    for copy in copies:
+        copy.wait()
+
+
+def spread(piece, count):
     whole = pl.BlockSpec(memory_space=pltpu.VMEM)
     return pl.pallas_call(
         spread_kernel,
-        in_specs=[whole, pl.BlockSpec(memory_space=pl.ANY)],
-        out_specs=whole,
+        in_specs=[whole],
+        out_specs=pl.BlockSpec(memory_space=pltpu.HBM),
+        scratch_shapes=[pltpu.SemaphoreType.DMA((count,))],
         out_shape=jax.ShapeDtypeStruct((count,) + piece.shape, piece.dtype),
         compiler_params=pltpu.CompilerParams(vmem_limit_bytes=16 * 1024 * 1024),
         cost_estimate=pl.CostEstimate(
             flops=0, bytes_accessed=4 * count * piece.size, transcendentals=0
         ),
-    )(piece, order)
-
-
-def home_kernel(terms, state, order, out):
-    del order
+    )(piece)
+
+
+def home_kernel(terms, state, out):
     value = state[...].astype(full)
     for source in range(terms.shape[0]):
         value = value + terms[source].astype(full)
@@ -239,25 +236,99 @@
     out[pl.ds(rows, rows), :] = jnp.zeros(state.shape, half)
 
 
-def home(terms, state, order):
+def home(terms, state):
     rows, width = state.shape
     whole = pl.BlockSpec(memory_space=pltpu.VMEM)
     return pl.pallas_call(
         home_kernel,
-        in_specs=[whole, whole, pl.BlockSpec(memory_space=pl.ANY)],
+        in_specs=[whole, whole],
         out_specs=whole,
         out_shape=jax.ShapeDtypeStruct((2 * rows, width), half),
         compiler_params=pltpu.CompilerParams(vmem_limit_bytes=16 * 1024 * 1024),
         cost_estimate=pl.CostEstimate(
             flops=17 * rows * width, bytes_accessed=40 * rows * width, transcendentals=0
         ),
-    )(terms, state, order)
-
-
-def normalise_kernel(pieces, gain, order, state, normed):
+    )(terms, state)
+
+
+def pool_kernel(place, message, token_slot, out, inverse, sh, weights, state, sems):
+    sources, _, cols = message.shape
+    rows = BLK // sources
+    token_proj = message[0, :BLK].astype(full)
+    for source in range(1, sources):
+        token_proj = token_proj + message[source, :BLK].astype(full)
+    squares = jnp.zeros((rows, cols), full)
+    for source in range(sources):
+        tail = message[source, BLK:].astype(full)
+        sh[pl.ds(source * rows, rows), :] = tail[:rows]
+        squares = squares + tail[rows:]
+    tokens = token_slot.shape[1]
+    squares = jnp.sum(squares, axis=0, keepdims=True)[:, :tokens]
+    inverse[...] = lax.rsqrt(squares / place[1].astype(full) + epsilon)
+    slots = jnp.where(place[0] == 0, token_slot[:, :BLK], token_slot[:, BLK:])
+    scale = jnp.where(place[0] == 0, inverse[:, :BLK], inverse[:, BLK:])
+    hits = slots == lax.broadcasted_iota(jnp.int32, (BLK, BLK), 0)
+    counts = jnp.maximum(jnp.sum(hits.astype(full), axis=1, keepdims=True), 1.0)
+    weights[...] = jnp.where(hits, scale, 0.0)
+    first = weights[...].astype(half)
+    second = (weights[...] - lax.reduce_precision(weights[...], 8, 7)).astype(half)
+    token_proj = token_proj.astype(half)
+    placed = jnp.dot(first, token_proj, preferred_element_type=full)
+    placed = placed + jnp.dot(second, token_proj, preferred_element_type=full)
+    placed = (placed / counts).astype(half).astype(full)
+    state[...] = (sh[...] + placed).astype(half)
+    copies = [
+        pltpu.make_async_copy(state, out.at[to], sems.at[to]) for to in range(sources)
+    ]
+    for copy in copies:
+        copy.start()
+    for copy in copies:
+        copy.wait()
+
+
+def pool(message, token_slot, block, width_full):
+    sources, _, cols = message.shape
+    whole = pl.BlockSpec(memory_space=pltpu.VMEM)
+    tokens = token_slot.shape[0]
+    place = jnp.stack([block, jnp.full_like(block, width_full)]).astype(jnp.int32)
+    return pl.pallas_call(
+        pool_kernel,
+        in_specs=[pl.BlockSpec(memory_space=pltpu.SMEM), whole, whole],
+        out_specs=[pl.BlockSpec(memory_space=pltpu.HBM), whole],
+        out_shape=[
+            jax.ShapeDtypeStruct((sources, BLK, cols), half),
+            jax.ShapeDtypeStruct((1, tokens), full),
+        ],
+        scratch_shapes=[
+            pltpu.VMEM((BLK, cols), full),
+            pltpu.VMEM((BLK, BLK), full),
+            pltpu.VMEM((BLK, cols), half),
+            pltpu.SemaphoreType.DMA((sources,)),
+        ],
+        compiler_params=pltpu.CompilerParams(vmem_limit_bytes=40 * 1024 * 1024),
+        cost_estimate=pl.CostEstimate(
+            flops=6 * message.size, bytes_accessed=4 * message.size, transcendentals=tokens
+        ),
+    )(place, message, token_slot[None])
+
+
+def forward_kernel(
+    pieces, gain, order, gate_hbm, up_hbm, down_hbm, state, gate, up, out, normed, act, held, sems
+):
     del order
-    groups = state.shape[1] // pieces.shape[2]
+    loads = []
+    for index, source in enumerate((gate_hbm, up_hbm, down_hbm)):
+        part = source.shape[0] // 3
+        for third in range(3):
+            at = pl.ds(third * part, part)
+            load = pltpu.make_async_copy(
+                source.at[at], held.at[index, at], sems.at[3 * index + third]
+            )
+            load.start()
+            loads.append(load)
+    gate_w, up_w, down_w = held.at[0], held.at[1], held.at[2]
     cols = pieces.shape[2]
+    groups = state.shape[1] // cols
     for block in range(state.shape[0] // BLK):
         rows = pl.ds(block * BLK, BLK)
         squares = jnp.zeros((BLK, 128), full)
@@ -274,24 +345,64 @@
             at = pl.ds(group * cols, cols)
             wide = pieces[block * groups + group].astype(full)
             normed[rows, at] = (wide * inverse * gain[:, at]).astype(normed.dtype)
-
-
-def normalise(pieces, gain, rows, width, order):
-    whole = pl.BlockSpec(memory_space=pltpu.VMEM)
-    shape = jax.ShapeDtypeStruct((rows, width), half)
+    for load in loads[:6]:
+        load.wait()
+    chunk = gate.shape[1] // 2
+    for index in range(2):
+        at = pl.ds(index * chunk, chunk)
+        gate_val = jnp.dot(normed[...], gate_w[:, at], preferred_element_type=full)
+        up_val = jnp.dot(normed[...], up_w[:, at], preferred_element_type=full)
+        gate[:, at] = gate_val
+        up[:, at] = up_val
+        act[:, at] = (gate_val * jax.nn.sigmoid(gate_val) * up_val).astype(half)
+    for load in loads[6:]:
+        load.wait()
+    rows = out.shape[1] // 2
+    wide_chunk = 512
+
+    @pl.loop(0, state.shape[1] // wide_chunk)
+    def _(index):
+        at = pl.ds(pl.multiple_of(index * wide_chunk, wide_chunk), wide_chunk)
+        value = times_rows(act[...], down_w[at, :])
+        for to in range(out.shape[0]):
+            first = value[to * rows : to * rows + rows]
+            second = value[BLK + to * rows : BLK + to * rows + rows]
+            out[to, :, at] = jnp.concatenate([first, second], axis=0).astype(half)
+
+
+def forward(pieces, gain, gate_w, up_w, down_w, order):
+    width, hidden = gate_w.shape
+    n_mp = pieces.shape[0]
+    rows = 2 * BLK
+    whole = pl.BlockSpec(memory_space=pltpu.VMEM)
     return pl.pallas_call(
-        normalise_kernel,
-        in_specs=[whole, whole, pl.BlockSpec(memory_space=pl.ANY)],
-        out_specs=[whole, whole],
-        out_shape=[shape, shape],
-        compiler_params=pltpu.CompilerParams(vmem_limit_bytes=16 * 1024 * 1024),
-        cost_estimate=pl.CostEstimate(
-            flops=6 * rows * width, bytes_accessed=6 * rows * width, transcendentals=rows
-        ),
-    )(pieces, gain[None], order)
-
-
-def slope_kernel(terms, dy, state, gain, out):
+        forward_kernel,
+        in_specs=[whole, whole, pl.BlockSpec(memory_space=pl.ANY)]
+        + [pl.BlockSpec(memory_space=pltpu.HBM)] * 3,
+        out_specs=[whole] * 4,
+        out_shape=[
+            jax.ShapeDtypeStruct((rows, width), half),
+            jax.ShapeDtypeStruct((rows, hidden), full),
+            jax.ShapeDtypeStruct((rows, hidden), full),
+            jax.ShapeDtypeStruct((n_mp, rows // n_mp, width), half),
+        ],
+        scratch_shapes=[
+            pltpu.VMEM((rows, width), half),
+            pltpu.VMEM((rows, hidden), half),
+            pltpu.VMEM((3, width, hidden), half),
+            pltpu.SemaphoreType.DMA((9,)),
+        ],
+        compiler_params=pltpu.CompilerParams(vmem_limit_bytes=56 * 1024 * 1024),
+        cost_estimate=pl.CostEstimate(
+            flops=6 * rows * width * hidden,
+            bytes_accessed=6 * width * hidden + 10 * rows * width,
+            transcendentals=rows * hidden,
+        ),
+    )(pieces, gain[None], order, gate_w, up_w, down_w)
+
+
+def slope_kernel(terms, dy, state, gain, order, out):
+    del order
     rows, width = dy.shape
     cols = out.shape[2]
     wide = state[...].astype(full)
@@ -306,19 +417,19 @@
         out[group] = dx[:, group * cols : (group + 1) * cols].astype(out.dtype)
 
 
-def slope(terms, dy, state, gain, groups):
+def slope(terms, dy, state, gain, groups, order):
     rows, width = dy.shape
     whole = pl.BlockSpec(memory_space=pltpu.VMEM)
     return pl.pallas_call(
         slope_kernel,
-        in_specs=[whole] * 4,
+        in_specs=[whole] * 4 + [pl.BlockSpec(memory_space=pl.ANY)],
         out_specs=whole,
         out_shape=jax.ShapeDtypeStruct((groups, rows, width // groups), half),
         compiler_params=pltpu.CompilerParams(vmem_limit_bytes=16 * 1024 * 1024),
         cost_estimate=pl.CostEstimate(
             flops=30 * rows * width, bytes_accessed=40 * rows * width, transcendentals=rows
         ),
-    )(terms, dy, state, gain[None])
+    )(terms, dy, state, gain[None], order)
 
 
 def on_device(
@@ -393,47 +504,32 @@
         axis=2,
     )
     message = exchange(message.reshape(n_mp, BLK + rows + 8, cols), "mp")
-    token_proj = jnp.sum(message[:, :BLK].astype(full), axis=0)
-    sh_here = message[:, BLK : BLK + rows].reshape(BLK, cols)
-    squares_all = jnp.sum(message[:, BLK + rows : BLK + rows + 3].astype(full), axis=(0, 1))[:tokens]
-    inverse_rms = lax.rsqrt(squares_all / width_full + epsilon)
+    states, inverse_rms = pool(message, token_slot, mp // groups, width_full)
+    states = exchange(states, "mp")
 
     slots_block = token_slot.reshape(blocks, BLK)
     onehot = slots_block[:, None, :] == jnp.arange(BLK, dtype=jnp.int32)[None, :, None]
     counts = jnp.maximum(jnp.sum(onehot.astype(full), axis=2), 1.0)
     onehot = onehot.astype(half)
-    my_block = mp // groups
-    inv_block = lax.dynamic_index_in_dim(inverse_rms.reshape(blocks, BLK), my_block, 0, False)
-    onehot_block = lax.dynamic_index_in_dim(onehot, my_block, 0, False)
-    counts_block = lax.dynamic_index_in_dim(counts, my_block, 0, False)
-    placed = jnp.dot(
-        onehot_block, (token_proj * inv_block[:, None]).astype(half), preferred_element_type=full
-    )
-    placed = (placed / counts_block[:, None]).astype(half).astype(full)
-    state_here = (sh_here.astype(full) + placed).astype(half)
-    normed = (gained_hidden * inverse_rms[:, None]).astype(half).reshape(blocks, BLK, width_here)
+    normed = (gained_hidden * inverse_rms.reshape(tokens, 1)).astype(half).reshape(blocks, BLK, width_here)
     pooled = jnp.einsum("krt,ktd->krd", onehot, normed, preferred_element_type=full)
     pooled = (pooled / counts[:, :, None]).astype(half)
     pooled_all = lax.all_gather(pooled.reshape(n_mp, mine_rows, width_here), "dp", axis=0, tiled=False)
     pooled_all = jnp.swapaxes(pooled_all, 0, 1).reshape(n_dp * tokens, width_here)
 
-    state, normed_student = normalise(
-        share(state_here, "mp"), student_gain, tokens, student_width, pooled
-    )
-
-    gate = jnp.dot(normed_student, gate_weight, preferred_element_type=full)
-    up = jnp.dot(normed_student, up_weight, preferred_element_type=full)
-    sigma = jax.nn.sigmoid(gate)
-    silu = gate * sigma
-    act = (silu * up).astype(half)
-    output = times_rows(act, down_weight).astype(half)
+    state, gate, up, output = forward(
+        states, student_gain, gate_weight, up_weight, down_weight, pooled
+    )
     grad_gate, grad_up = backward(dy.reshape(tokens, student_width), down_weight, gate, up, output)
     dn = (times_rows(grad_gate, gate_weight) + times_rows(grad_up, up_weight)).astype(half)
-    output = jnp.swapaxes(output.reshape(blocks, n_mp, rows, student_width), 0, 1)
     output = exchange(output, "mp")
     dn, output = lax.optimization_barrier((dn, output))
     dn = exchange(dn.reshape(n_mp, mine_rows, student_width), "mp")
     here = mp * mine_rows
+    state_rows = lax.dynamic_slice_in_dim(
+        state.reshape(blocks, BLK, student_width), mp * rows, rows, 1
+    )
+    out_rows = home(output, state_rows.reshape(mine_rows, student_width))
     dproj = slope(
         dn,
         lax.dynamic_slice(
@@ -442,16 +538,9 @@
         lax.dynamic_slice_in_dim(state, here, mine_rows, 0),
         student_gain,
         n_dp,
-    )
-    state_rows = lax.dynamic_slice_in_dim(
-        state.reshape(blocks, BLK, student_width), mp * rows, rows, 1
-    )
-    out_rows = home(
-        output.reshape(n_mp, mine_rows, student_width),
-        state_rows.reshape(mine_rows, student_width),
-        dproj,
-    )
-    dproj = exchange(spread(exchange(dproj, "dp"), n_mp, out_rows), "mp")
+        out_rows,
+    )
+    dproj = exchange(spread(exchange(dproj, "dp"), n_mp), "mp")
     adapter_grad = lax.dot_general(
         pooled_all,
         dproj.reshape(n_dp * tokens, out_cols),

time: 256 us -> 227 us (0.89)
  local copies, waits for them, and re-layouts: 37 us -> 9.52 us
  Pallas kernels: 21.3 us -> 32.2 us
  blocking collectives: 0 us -> 9.72 us
  starting transfers between devices: 52.3 us -> 45.9 us
  matrix products: 16 us -> 10 us
  waiting for transfers between devices: 85.2 us -> 79.2 us
  other arithmetic: 12.8 us -> 10.1 us
    unnamed x77 -> x31, local copies, waits for them, and re-layouts: 29.1 us -> 4.31 us
    all_to_all x0 -> x1, blocking collectives: none -> 9.72 us  [exchange(): return lax.all_to_all(pieces, axis, split_axis=0, concat_axis=0, tiled=True)]
    pallas_call x6 -> x7, Pallas kernels: 18.3 us -> 26.6 us  [the longest x1 9.9 us: forward(): pl.pallas_call(forward_kernel, in_specs=[whole, whole, pl.BlockSpec(memor...]
    all_to_all x6 -> x5, starting transfers between devices: 30.1 us -> 24.1 us  [exchange(): return lax.all_to_all(pieces, axis, split_axis=0, concat_axis=0, tiled=True)]
    dot_general x3 -> x0, matrix products: 5.62 us -> none  [the longest x1 3.47 us: on_device(): up = jnp.dot(normed_student, up_weight, preferred_element_type=full)]
    all_to_all x6 -> x5, waiting for transfers between devices: 70.2 us -> 66.1 us  [exchange(): return lax.all_to_all(pieces, axis, split_axis=0, concat_axis=0, tiled=True)]
    pallas_call x1, Pallas kernels: 1.06 us -> 4.64 us  [backward(): pl.pallas_call(backward_kernel, in_specs=[whole] * 4 + [pl.BlockSpec(memo...]
    reduce_sum x2 -> x0, other arithmetic: 2.58 us -> none  [the longest x1 1.64 us: on_device(): token_proj = jnp.sum(message[:, :BLK].astype(full), axis=0)]
  transfers between devices with their start and end apart: 24 -> 23, of which waited for: 12 -> 12; matrix products, arithmetic and copies ran while one was open for 11% -> 8% of each run, Pallas kernels for 8% -> 13%
where the time goes in v5:
time: 227 us; the launch traced here: 226 us
  waiting for transfers between devices  79.2 us (35%)
  starting transfers between devices  45.9 us (20%)
  Pallas kernels  32.2 us (14%)
  between operations  29 us (13%)
  other arithmetic  10.1 us (4%)
  matrix products  10 us (4%)
  blocking collectives  9.72 us (4%)
  local copies, waits for them, and re-layouts  9.52 us (4%)
    all_to_all x5, waiting for transfers between devices, exchange(): return lax.all_to_all(pieces, axis, split_axis=0, concat_axis=0, tiled=True)  66.1 us
    all_to_all x5, starting transfers between devices, exchange(): return lax.all_to_all(pieces, axis, split_axis=0, concat_axis=0, tiled=True)  24.1 us
    ppermute x14, starting transfers between devices, step(): return lax.ppermute(value, 'mp', pairs)  21.6 us
    ppermute x14, waiting for transfers between devices, step(): return lax.ppermute(value, 'mp', pairs)  11.8 us
    pallas_call x1, Pallas kernels, forward(): pl.pallas_call(forward_kernel, in_specs=[whole, whole, pl.BlockSpec(memor...  9.9 us
    all_to_all x1, blocking collectives, exchange(): return lax.all_to_all(pieces, axis, split_axis=0, concat_axis=0, tiled=True)  9.72 us
    pallas_call x1, Pallas kernels, teacher_terms(): pl.pallas_call(terms_kernel, in_specs=[scalars, whole, pl.BlockSpec(memor...  8.47 us
    pallas_call x1, Pallas kernels, backward(): pl.pallas_call(backward_kernel, in_specs=[whole] * 4 + [pl.BlockSpec(memo...  4.64 us
  transfers between devices with their start and end apart: 23, of which 12 were waited for; matrix products, arithmetic and copies ran while one was open for 8% of the time, Pallas kernels for 13%

profile of v5, /device:TPU:0, one launch (start us, length us, event | category | flops | bytes accessed | tf_op | source)
XLA Modules:
  0.0 225.6 jit_solution(4047110048300057290)
XLA Ops:
  7.2 2.0 pad_maximum_fusion.1
  10.3 8.5 %shard_map.140 = (bf16[4,128,512]{2,1,0:T(8,128)(2,1)S(1)}, bf16[4,128,512]{2,1,0:T(8,128)(2,1)S(1)}, bf16[4,128,512]{2,1,0:T(8,128)(2,1)S(1)}, bf16[4,64,512]{2...) custom-call(s32[2]{0:T(128)S(1)} %pad_add_fusion.1.place, ...), custom_call_target="tpu_custom_call" | custom-call | flops 2147483648 | bytes 8388608 | tf_op jit(solution)/shard_map/pallas_call | solution.py:110
  18.7 1.7 collective-permute-start
  22.0 2.0 collective-permute-start.2
  24.0 2.1 collective-permute-start.3
  33.5 3.5 %shard_map.141 = (bf16[4,128,512]{2,1,0:T(8,128)(2,1)}, bf16[4,128,512]{2,1,0:T(8,128)(2,1)}, bf16[4,128,512]{2,1,0:T(8,128)(2,1)}, bf16[4,128,512]{2,1,0:T(8,128)(2,1)}) custom-call(bf16[4,128,512]{2,1,0:T(8,128)(2,1)S(1)} %get-tuple-element.47.refs_0_, bf16[4,128,512]{2,1,0:T(8,128)(2,1)S(1)} %get-tuple-element.48.refs_1_, ...), custom_call_target="tpu_custom_call" | custom-call | flops 1048576 | bytes 5242880 | tf_op jit(solution)/shard_map/pallas_call | solution.py:128
  37.3 2.9 %collective-permute-start.5 = (bf16[4,128,512]{2,1,0:T(8,128)(2,1)}, bf16[4,128,512]{2,1,0:T(8,128)(2,1)S(1)}, u32[]{:S(2)}, u32[]{:S(2)}) collective-permute-start(bf16[4,128,512]{2,1,0:T(8,128)(2,1)} %get-tuple-element.56), channel_id=1, source_target_pairs={{0,12},{1,13},{2,14},{3,15},{4,0},{5,1},{6,2},{7,3},{8,4},{9,5},{1... | collective-permute-start | bytes 1572872 | tf_op jit(solution)/shard_map/ppermute | solution.py:38
  40.3 3.1 %collective-permute-start.7 = (bf16[4,128,512]{2,1,0:T(8,128)(2,1)}, bf16[4,128,512]{2,1,0:T(8,128)(2,1)S(1)}, u32[]{:S(2)}, u32[]{:S(2)}) collective-permute-start(bf16[4,128,512]{2,1,0:T(8,128)(2,1)} %get-tuple-element.59), channel_id=1, source_target_pairs={{0,3},{1,0},{2,1},{3,2},{4,7},{5,4},{6,5},{7,6},{8,11},{9,8},{10,9... | collective-permute-start | bytes 1572872 | tf_op jit(solution)/shard_map/ppermute | solution.py:38
  43.4 1.8 constant_dynamic-slice_fusion.2
  47.4 3.9 %collective-permute-done.4.refs_1_ = bf16[4,128,512]{2,1,0:T(8,128)(2,1)S(1)} collective-permute-done((bf16[4,128,512]{2,1,0:T(8,128)(2,1)}, bf16[4,128,512]{2,1,0:T(8,128)(2,1)S(1)}, u32[]{:S(2)}, u32[]{:S(2)}) %collective-permute-start.4) | collective-permute-done | bytes 524320 | tf_op jit(solution)/shard_map/ppermute | solution.py:38
  51.4 2.7 %collective-permute-done.6.refs_4_ = bf16[4,128,512]{2,1,0:T(8,128)(2,1)S(1)} collective-permute-done((bf16[4,128,512]{2,1,0:T(8,128)(2,1)}, bf16[4,128,512]{2,1,0:T(8,128)(2,1)S(1)}, u32[]{:S(2)}, u32[]{:S(2)}) %collective-permute-start.6) | collective-permute-done | bytes 524320 | tf_op jit(solution)/shard_map/ppermute | solution.py:38
  55.1 4.4 %collective-permute-start.9 = (bf16[128,512]{1,0:T(8,128)(2,1)S(1)}, bf16[128,512]{1,0:T(8,128)(2,1)S(1)}, u32[]{:S(2)}, u32[]{:S(2)}) collective-permute-start(bf16[128,512]{1,0:T(8,128)(2,1)S(1)} %get-tuple-element.62), channel_id=1, source_target_pairs={{0,2},{1,3},{2,0},{3,1},{4,6},{5,7},{6,4},{7,5},{8,10},{9,11},{10,... | collective-permute-start | bytes 393224 | tf_op jit(solution)/shard_map/ppermute | solution.py:38
  59.6 1.9 collective-permute-start.12
  64.5 2.7 %collective-permute-done.11 = bf16[128,512]{1,0:T(8,128)(2,1)S(1)} collective-permute-done((bf16[128,512]{1,0:T(8,128)(2,1)S(1)}, bf16[128,512]{1,0:T(8,128)(2,1)S(1)}, u32[]{:S(2)}, u32[]{:S(2)}) %collective-permute-start.11) | collective-permute-done | bytes 131104 | tf_op jit(solution)/shard_map/ppermute | solution.py:38
  70.9 5.4 %all-to-all-start = ((bf16[16,144,384]{2,1,0:T(8,128)(2,1)}), bf16[16,144,384]{2,1,0:T(8,128)(2,1)S(1)}, u32[]{:S(2)}, u32[]{:S(2)}) async-start(bf16[16,144,384]{2,1,0:T(8,128)(2,1)} %bitcast.22), calls=%async_computation | async-start | bytes 3538944 | tf_op jit(solution)/shard_map/all_to_all | solution.py:15
  77.1 19.4 %all-to-all-done.message = bf16[16,144,384]{2,1,0:T(8,128)(2,1)S(1)} async-done(((bf16[16,144,384]{2,1,0:T(8,128)(2,1)}), bf16[16,144,384]{2,1,0:T(8,128)(2,1)S(1)}, u32[]{:S(2)}, u32[]{:S(2)}) %all-to-all-start) | async-done | bytes 1769504 | tf_op jit(solution)/shard_map/all_to_all | solution.py:15
  96.5 2.3 %shard_map.143 = (bf16[16,128,384]{2,1,0:T(8,128)(2,1)}, f32[1,256]{1,0:T(1,128)S(1)}) custom-call(s32[2]{0:T(128)S(1)} %pad_add_fusion.place, bf16[16,144,384]{2,1,0:T(8,128)(2,1)S(1)} %all-to-all-done.message, s32[1,256]{1,0:T(1,128)S(1)} %bitcast.93), custom_call_target="tpu_custom_call" | custom-call | flops 5308416 | bytes 3538944 | tf_op jit(solution)/shard_map/pallas_call | solution.py:294
  98.8 5.1 %all-to-all-start.1 = ((bf16[16,128,384]{2,1,0:T(8,128)(2,1)}), bf16[16,128,384]{2,1,0:T(8,128)(2,1)S(1)}, u32[]{:S(2)}, u32[]{:S(2)}) async-start(bf16[16,128,384]{2,1,0:T(8,128)(2,1)} %get-tuple-element.68), calls=%async_computation.1 | async-start | bytes 3145728 | tf_op jit(solution)/shard_map/all_to_all | solution.py:15
  105.0 16.3 %all-to-all-done.1.pieces = bf16[16,128,384]{2,1,0:T(8,128)(2,1)S(1)} async-done(((bf16[16,128,384]{2,1,0:T(8,128)(2,1)}), bf16[16,128,384]{2,1,0:T(8,128)(2,1)S(1)}, u32[]{:S(2)}, u32[]{:S(2)}) %all-to-all-start.1) | async-done | bytes 1572896 | tf_op jit(solution)/shard_map/all_to_all | solution.py:15
  122.5 9.9 %shard_map.144 = (bf16[256,3072]{1,0:T(8,128)(2,1)}, f32[256,512]{1,0:T(8,128)}, f32[256,512]{1,0:T(8,128)}, bf16[16,16,3072]{2,1,0:T(8,128)(2,1)}) custom-call(bf16[16,128,384]{2,1,0:T(8,128)(2,1)} %copy-done.6, f32[1,3072]{1,0:T(1,128)} %bitcast.91, bf16[2,128,512]{2,1,0:T(8,128)(2,1)} %fusion.10.order, bf16[3072,512]{1,0:T(8,128)(2,1)} %gate_hbm.1, ...), custom_call_target="tpu_custom_call" | custom-call | flops 2415919104 | bytes 17301504 | tf_op jit(solution)/shard_map/pallas_call | solution.py:378
  132.4 6.2 %all-to-all-start.2 = ((bf16[16,16,3072]{2,1,0:T(8,128)(2,1)}), bf16[16,16,3072]{2,1,0:T(8,128)(2,1)S(1)}, u32[]{:S(2)}, u32[]{:S(2)}) async-start(bf16[16,16,3072]{2,1,0:T(8,128)(2,1)} %get-tuple-element.72.order), calls=%async_computation.2 | async-start | bytes 3145728 | tf_op jit(solution)/shard_map/all_to_all | solution.py:15
  138.7 4.6 %shard_map.145 = (bf16[256,512]{1,0:T(8,128)(2,1)}, bf16[256,512]{1,0:T(8,128)(2,1)}) custom-call(bf16[256,3072]{1,0:T(8,128)(2,1)} %bitcast.97, bf16[3072,512]{1,0:T(8,128)(2,1)} %down.1, f32[256,512]{1,0:T(8,128)} %get-tuple-element.70.gate, f32[256,512]{1,0:T(8,128)} %get-tuple-element.71.up, bf16[16,16,3072]{2,1,0:T(8,128)(2,1)} %get-tuple-element.72.order), custom_call_target="tpu_custom_call" | custom-call | flops 805306368 | bytes 6815744 | tf_op jit(solution)/shard_map/pallas_call | solution.py:190
  144.2 2.1 fusion.28
  146.4 2.3 fusion
  148.6 6.3 %all-to-all-done.2.terms = bf16[16,16,3072]{2,1,0:T(8,128)(2,1)S(1)} async-done(((bf16[16,16,3072]{2,1,0:T(8,128)(2,1)}), bf16[16,16,3072]{2,1,0:T(8,128)(2,1)S(1)}, u32[]{:S(2)}, u32[]{:S(2)}) %all-to-all-start.2) | async-done | bytes 1572896 | tf_op jit(solution)/shard_map/all_to_all | solution.py:15
  156.4 3.7 %all-to-all-start.3 = ((bf16[16,16,3072]{2,1,0:T(8,128)(2,1)}), bf16[16,16,3072]{2,1,0:T(8,128)(2,1)S(1)}, u32[]{:S(2)}, u32[]{:S(2)}) async-start(bf16[16,16,3072]{2,1,0:T(8,128)(2,1)} %bitcast.39), calls=%async_computation.3 | async-start | bytes 3145728 | tf_op jit(solution)/shard_map/all_to_all | solution.py:15
  162.0 14.3 %all-to-all-done.3.terms = bf16[16,16,3072]{2,1,0:T(8,128)(2,1)S(1)} async-done(((bf16[16,16,3072]{2,1,0:T(8,128)(2,1)}), bf16[16,16,3072]{2,1,0:T(8,128)(2,1)S(1)}, u32[]{:S(2)}, u32[]{:S(2)}) %all-to-all-start.3) | async-done | bytes 1572896 | tf_op jit(solution)/shard_map/all_to_all | solution.py:15
  176.6 9.7 %all_to_all.30.piece = bf16[8,16,384]{2,1,0:T(8,128)(2,1)S(1)} all-to-all(bf16[8,16,384]{2,1,0:T(8,128)(2,1)S(1)} %shard_map.147), channel_id=1, replica_groups=mesh['dp'=8,'mp'=16] {'dp'}, dimensions={0} | all-to-all | bytes 196608 | tf_op jit(solution)/shard_map/all_to_all | solution.py:15
  187.6 3.7 %all-to-all-start.5 = ((bf16[16,8,16,384]{3,2,1,0:T(8,128)(2,1)}), bf16[16,8,16,384]{3,2,1,0:T(8,128)(2,1)S(1)}, u32[]{:S(2)}, u32[]{:S(2)}) async-start(bf16[16,8,16,384]{3,2,1,0:T(8,128)(2,1)} %shard_map.148), calls=%async_computation.5 | async-start | bytes 3145728 | tf_op jit(solution)/shard_map/all_to_all | solution.py:15
  201.2 3.4 %select_bitcast_fusion.3 = (bf16[8,1,3072]{2,0,1:T(8,128)(2,1)S(1)}, bf16[8,1,3072]{2,0,1:T(8,128)(2,1)S(1)}, bf16[8,1,3072]{2,0,1:T(8,128)(2,1)S(1)}, bf16[8,1,3072]{2,0,1:T(8,128)(2,1)S(1)}) fusion(bf16[8,32,3072]{2,1,0:T(8,128)(2,1)} %bitcast.109, s32[]{:T(128)S(6)} %select_n.228, s32[]{:T(128)S(6)} %select_n.230, pred[]{:T(512)} %get-tuple-element.82, ...), kind=kLoop, calls=%fused_computation.34 | loop fusion | flops 98304 | bytes 393252 | tf_op jit(solution)/shard_map/jit(_where)/select_n | solution.py:559
  205.4 9.9 %all-to-all-done.5 = bf16[16,8,16,384]{3,2,1,0:T(8,128)(2,1)S(1)} async-done(((bf16[16,8,16,384]{3,2,1,0:T(8,128)(2,1)}), bf16[16,8,16,384]{3,2,1,0:T(8,128)(2,1)S(1)}, u32[]{:S(2)}, u32[]{:S(2)}) %all-to-all-start.5) | async-done | bytes 1572896 | tf_op jit(solution)/shard_map/all_to_all | solution.py:15
  215.3 3.7 %fusion.7 = f32[512,384]{1,0:T(8,128)} fusion(bf16[16,8,16,384]{3,2,1,0:T(8,128)(2,1)S(1)} %all-to-all-done.5, bf16[8,16,16,512]{3,2,0,1:T(8,128)(2,1)} %all-gather.8.cloned.1.call-done), kind=kOutput, calls=%fused_computation.10 | convolution fusion | flops 805306368 | bytes 4456448 | tf_op jit(solution)/shard_map/dot_general | solution.py:544
  (94 shorter events, 25.3 us)
Async XLA Ops:
  7.2 36.3 %all-gather.10.cloned.1.call-start = ((), (), s32[]{:S(2)}) async-start(), calls=%async_computation.7 | async-start | bytes 3538944 | tf_op jit(solution)/shard_map/all_gather | solution.py:471
  10.3 15.9 %copy-start.11 = (s32[16]{0:T(128)S(1)}, s32[16]{0:T(128)}, u32[]{:S(2)}) copy-start(s32[16]{0:T(128)} %param.21) | copy-start | bytes 196
  18.7 14.7 %collective-permute-start = (bf16[4,64,512]{2,1,0:T(8,128)(2,1)}, bf16[4,64,512]{2,1,0:T(8,128)(2,1)S(1)}, u32[]{:S(2)}, u32[]{:S(2)}) collective-permute-start(bf16[4,64,512]{2,1,0:T(8,128)(2,1)} %get-tuple-element.49), channel_id=1, source_target_pairs={{0,4},{1,5},{2,6},{3,7},{4,8},{5,9},{6,10},{7,11},{8,12},{9,13},{1... | collective-permute-start | bytes 786440 | tf_op jit(solution)/shard_map/ppermute | solution.py:38
  20.5 13.0 %collective-permute-start.1 = (bf16[4,64,512]{2,1,0:T(8,128)(2,1)}, bf16[4,64,512]{2,1,0:T(8,128)(2,1)}, u32[]{:S(2)}, u32[]{:S(2)}) collective-permute-start(bf16[4,64,512]{2,1,0:T(8,128)(2,1)} %get-tuple-element.50), channel_id=1, source_target_pairs={{0,12},{1,13},{2,14},{3,15},{4,0},{5,1},{6,2},{7,3},{8,4},{9,5},{1... | collective-permute-start | bytes 786440 | tf_op jit(solution)/shard_map/ppermute | solution.py:38
  22.0 11.4 %collective-permute-start.2 = (bf16[4,64,512]{2,1,0:T(8,128)(2,1)}, bf16[4,64,512]{2,1,0:T(8,128)(2,1)}, u32[]{:S(2)}, u32[]{:S(2)}) collective-permute-start(bf16[4,64,512]{2,1,0:T(8,128)(2,1)} %get-tuple-element.53), channel_id=1, source_target_pairs={{0,1},{1,2},{2,3},{3,0},{4,5},{5,6},{6,7},{7,4},{8,9},{9,10},{10,1... | collective-permute-start | bytes 786440 | tf_op jit(solution)/shard_map/ppermute | solution.py:38
  24.0 9.4 %collective-permute-start.3 = (bf16[4,64,512]{2,1,0:T(8,128)(2,1)}, bf16[4,64,512]{2,1,0:T(8,128)(2,1)}, u32[]{:S(2)}, u32[]{:S(2)}) collective-permute-start(bf16[4,64,512]{2,1,0:T(8,128)(2,1)} %get-tuple-element.54), channel_id=1, source_target_pairs={{0,3},{1,0},{2,1},{3,2},{4,7},{5,4},{6,5},{7,6},{8,11},{9,8},{10,9... | collective-permute-start | bytes 786440 | tf_op jit(solution)/shard_map/ppermute | solution.py:38
  37.0 14.4 %collective-permute-start.4 = (bf16[4,128,512]{2,1,0:T(8,128)(2,1)}, bf16[4,128,512]{2,1,0:T(8,128)(2,1)S(1)}, u32[]{:S(2)}, u32[]{:S(2)}) collective-permute-start(bf16[4,128,512]{2,1,0:T(8,128)(2,1)} %get-tuple-element.55), channel_id=1, source_target_pairs={{0,4},{1,5},{2,6},{3,7},{4,8},{5,9},{6,10},{7,11},{8,12},{9,13},{1... | collective-permute-start | bytes 1572872 | tf_op jit(solution)/shard_map/ppermute | solution.py:38
  37.3 14.1 %collective-permute-start.5 = (bf16[4,128,512]{2,1,0:T(8,128)(2,1)}, bf16[4,128,512]{2,1,0:T(8,128)(2,1)S(1)}, u32[]{:S(2)}, u32[]{:S(2)}) collective-permute-start(bf16[4,128,512]{2,1,0:T(8,128)(2,1)} %get-tuple-element.56), channel_id=1, source_target_pairs={{0,12},{1,13},{2,14},{3,15},{4,0},{5,1},{6,2},{7,3},{8,4},{9,5},{1... | collective-permute-start | bytes 1572872 | tf_op jit(solution)/shard_map/ppermute | solution.py:38
  40.2 13.9 %collective-permute-start.6 = (bf16[4,128,512]{2,1,0:T(8,128)(2,1)}, bf16[4,128,512]{2,1,0:T(8,128)(2,1)S(1)}, u32[]{:S(2)}, u32[]{:S(2)}) collective-permute-start(bf16[4,128,512]{2,1,0:T(8,128)(2,1)} %get-tuple-element.58), channel_id=1, source_target_pairs={{0,1},{1,2},{2,3},{3,0},{4,5},{5,6},{6,7},{7,4},{8,9},{9,10},{10,1... | collective-permute-start | bytes 1572872 | tf_op jit(solution)/shard_map/ppermute | solution.py:38
  40.3 13.7 %collective-permute-start.7 = (bf16[4,128,512]{2,1,0:T(8,128)(2,1)}, bf16[4,128,512]{2,1,0:T(8,128)(2,1)S(1)}, u32[]{:S(2)}, u32[]{:S(2)}) collective-permute-start(bf16[4,128,512]{2,1,0:T(8,128)(2,1)} %get-tuple-element.59), channel_id=1, source_target_pairs={{0,3},{1,0},{2,1},{3,2},{4,7},{5,4},{6,5},{7,6},{8,11},{9,8},{10,9... | collective-permute-start | bytes 1572872 | tf_op jit(solution)/shard_map/ppermute | solution.py:38
  46.6 18.0 %copy-start = (bf16[2,8,3072]{2,1,0:T(8,128)(2,1)}, bf16[2,8,3072]{2,1,0:T(8,128)(2,1)S(1)}, u32[]{:S(2)}) copy-start(bf16[2,8,3072]{2,1,0:T(8,128)(2,1)S(1)} %pad_maximum_fusion.2.refs_7_) | copy-start | bytes 294916
  54.1 14.1 %copy-start.7 = (bf16[256,512]{1,0:T(8,128)(2,1)S(1)}, bf16[256,512]{1,0:T(8,128)(2,1)}, u32[]{:S(2)}) copy-start(bf16[256,512]{1,0:T(8,128)(2,1)} %param.17) | copy-start | bytes 786436
  54.1 14.1 %copy-start.10 = (f32[512]{0:T(512)S(1)}, f32[512]{0:T(512)}, u32[]{:S(2)}) copy-start(f32[512]{0:T(512)} %param.18) | copy-start | bytes 6148
  55.0 13.4 %copy-start.12 = (bf16[512,3072]{1,0:T(8,128)(2,1)S(1)}, bf16[512,3072]{1,0:T(8,128)(2,1)}, u32[]{:S(2)}) copy-start(bf16[512,3072]{1,0:T(8,128)(2,1)} %param.19) | copy-start | bytes 9437188
  55.0 6.7 %collective-permute-start.8 = (bf16[128,512]{1,0:T(8,128)(2,1)S(1)}, bf16[128,512]{1,0:T(8,128)(2,1)S(1)}, u32[]{:S(2)}, u32[]{:S(2)}) collective-permute-start(bf16[128,512]{1,0:T(8,128)(2,1)S(1)} %get-tuple-element.61), channel_id=1, source_target_pairs={{0,1},{1,2},{2,3},{3,0},{4,5},{5,6},{6,7},{7,4},{8,9},{9,10},{10,1... | collective-permute-start | bytes 393224 | tf_op jit(solution)/shard_map/ppermute | solution.py:38
  55.1 8.7 %collective-permute-start.9 = (bf16[128,512]{1,0:T(8,128)(2,1)S(1)}, bf16[128,512]{1,0:T(8,128)(2,1)S(1)}, u32[]{:S(2)}, u32[]{:S(2)}) collective-permute-start(bf16[128,512]{1,0:T(8,128)(2,1)S(1)} %get-tuple-element.62), channel_id=1, source_target_pairs={{0,2},{1,3},{2,0},{3,1},{4,6},{5,7},{6,4},{7,5},{8,10},{9,11},{10,... | collective-permute-start | bytes 393224 | tf_op jit(solution)/shard_map/ppermute | solution.py:38
  59.5 5.0 %collective-permute-start.10 = (bf16[128,512]{1,0:T(8,128)(2,1)S(1)}, bf16[128,512]{1,0:T(8,128)(2,1)S(1)}, u32[]{:S(2)}, u32[]{:S(2)}) collective-permute-start(bf16[128,512]{1,0:T(8,128)(2,1)S(1)} %get-tuple-element.63), channel_id=1, source_target_pairs={{0,3},{1,0},{2,1},{3,2},{4,7},{5,4},{6,5},{7,6},{8,11},{9,8},{10,9... | collective-permute-start | bytes 393224 | tf_op jit(solution)/shard_map/ppermute | solution.py:38
  59.5 7.7 %collective-permute-start.11 = (bf16[128,512]{1,0:T(8,128)(2,1)S(1)}, bf16[128,512]{1,0:T(8,128)(2,1)S(1)}, u32[]{:S(2)}, u32[]{:S(2)}) collective-permute-start(bf16[128,512]{1,0:T(8,128)(2,1)S(1)} %get-tuple-element.65), channel_id=1, source_target_pairs={{0,4},{1,5},{2,6},{3,7},{4,8},{5,9},{6,10},{7,11},{8,12},{9,13},{1... | collective-permute-start | bytes 393224 | tf_op jit(solution)/shard_map/ppermute | solution.py:38
  59.6 7.6 %collective-permute-start.12 = (bf16[128,512]{1,0:T(8,128)(2,1)S(1)}, bf16[128,512]{1,0:T(8,128)(2,1)S(1)}, u32[]{:S(2)}, u32[]{:S(2)}) collective-permute-start(bf16[128,512]{1,0:T(8,128)(2,1)S(1)} %get-tuple-element.66), channel_id=1, source_target_pairs={{0,8},{1,9},{2,10},{3,11},{4,12},{5,13},{6,14},{7,15},{8,0},{9,1},... | collective-permute-start | bytes 393224 | tf_op jit(solution)/shard_map/ppermute | solution.py:38
  61.7 6.4 %collective-permute-start.13 = (bf16[128,512]{1,0:T(8,128)(2,1)S(1)}, bf16[128,512]{1,0:T(8,128)(2,1)S(1)}, u32[]{:S(2)}, u32[]{:S(2)}) collective-permute-start(bf16[128,512]{1,0:T(8,128)(2,1)S(1)} %get-tuple-element.67), channel_id=1, source_target_pairs={{0,12},{1,13},{2,14},{3,15},{4,0},{5,1},{6,2},{7,3},{8,4},{9,5},{1... | collective-permute-start | bytes 393224 | tf_op jit(solution)/shard_map/ppermute | solution.py:38
  70.9 25.6 %copy-start.3 = (s32[256]{0:T(256)S(1)}, s32[256]{0:T(256)}, u32[]{:S(2)}) copy-start(s32[256]{0:T(256)} %param.20) | copy-start | bytes 3076
  70.9 25.6 %all-to-all-start = ((bf16[16,144,384]{2,1,0:T(8,128)(2,1)}), bf16[16,144,384]{2,1,0:T(8,128)(2,1)S(1)}, u32[]{:S(2)}, u32[]{:S(2)}) async-start(bf16[16,144,384]{2,1,0:T(8,128)(2,1)} %bitcast.22), calls=%async_computation | async-start | bytes 3538944 | tf_op jit(solution)/shard_map/all_to_all | solution.py:15
  76.3 62.4 %all-gather.12.cloned.1.call-start = ((), (), s32[]{:S(2)}) async-start(), calls=%async_computation.8 | async-start | bytes 1671168 | tf_op jit(solution)/shard_map/all_gather | solution.py:483
  96.5 7.5 %copy-start.8 = (bf16[256,512]{1,0:T(8,128)(2,1)S(1)}, bf16[256,512]{1,0:T(8,128)(2,1)}, u32[]{:S(2)}) copy-start(bf16[256,512]{1,0:T(8,128)(2,1)} %param.17) | copy-start | bytes 786436
  98.8 22.5 %all-to-all-start.1 = ((bf16[16,128,384]{2,1,0:T(8,128)(2,1)}), bf16[16,128,384]{2,1,0:T(8,128)(2,1)S(1)}, u32[]{:S(2)}, u32[]{:S(2)}) async-start(bf16[16,128,384]{2,1,0:T(8,128)(2,1)} %get-tuple-element.68), calls=%async_computation.1 | async-start | bytes 3145728 | tf_op jit(solution)/shard_map/all_to_all | solution.py:15
  132.4 22.5 %all-to-all-start.2 = ((bf16[16,16,3072]{2,1,0:T(8,128)(2,1)}), bf16[16,16,3072]{2,1,0:T(8,128)(2,1)S(1)}, u32[]{:S(2)}, u32[]{:S(2)}) async-start(bf16[16,16,3072]{2,1,0:T(8,128)(2,1)} %get-tuple-element.72.order), calls=%async_computation.2 | async-start | bytes 3145728 | tf_op jit(solution)/shard_map/all_to_all | solution.py:15
  138.6 62.6 %all-gather.14.cloned.1.call-start = ((), (), s32[]{:S(2)}) async-start(), calls=%async_computation.9 | async-start | bytes 1769472 | tf_op jit(solution)/shard_map/all_gather | solution.py:551
  138.6 5.6 %copy-start.4 = (bf16[3072,512]{1,0:T(8,128)(2,1)S(1)}, bf16[3072,512]{1,0:T(8,128)(2,1)}, u32[]{:S(2)}) copy-start(bf16[3072,512]{1,0:T(8,128)(2,1)} %gate_hbm.1) | copy-start | bytes 9437188
  155.8 20.4 %copy-start.2 = (f32[3072]{0:T(1024)S(1)}, f32[3072]{0:T(1024)}, u32[]{:S(2)}) copy-start(f32[3072]{0:T(1024)} %param.24) | copy-start | bytes 36868
  155.8 49.6 %all-gather.8.cloned.1.call-start = ((), (), s32[]{:S(2)}) async-start(), calls=%async_computation.6 | async-start | bytes 2359296 | tf_op jit(solution)/shard_map/all_gather | solution.py:517
  156.4 19.8 %all-to-all-start.3 = ((bf16[16,16,3072]{2,1,0:T(8,128)(2,1)}), bf16[16,16,3072]{2,1,0:T(8,128)(2,1)S(1)}, u32[]{:S(2)}, u32[]{:S(2)}) async-start(bf16[16,16,3072]{2,1,0:T(8,128)(2,1)} %bitcast.39), calls=%async_computation.3 | async-start | bytes 3145728 | tf_op jit(solution)/shard_map/all_to_all | solution.py:15
  187.6 27.8 %all-to-all-start.5 = ((bf16[16,8,16,384]{3,2,1,0:T(8,128)(2,1)}), bf16[16,8,16,384]{3,2,1,0:T(8,128)(2,1)S(1)}, u32[]{:S(2)}, u32[]{:S(2)}) async-start(bf16[16,8,16,384]{3,2,1,0:T(8,128)(2,1)} %shard_map.148), calls=%async_computation.5 | async-start | bytes 3145728 | tf_op jit(solution)/shard_map/all_to_all | solution.py:15
  (4 other events, 6.4 us)
Sparse Core Ops, SparseCore 0:
  9.7 30.1 all-gather.9
  79.9 50.7 all-gather.11
  155.9 21.8 all-gather.13
  179.4 25.0 all-gather.7

commit v6 on v5

--- a/solution.py
+++ b/solution.py
@@ -38,8 +38,30 @@
     return lax.ppermute(value, "mp", pairs)
 
 
-def terms_kernel(place, left, right, *refs):
-    outs, held, sems = refs[:10], refs[10], refs[11]
+def far_kernel(place, left, right, lower0, upper0, lower1, upper1, held, sems):
+    width = held.shape[2]
+    y, z = lax.rem(place[0] + 2, SIDE), lax.rem(place[1] + 2, SIDE)
+    middle = BLK // 2
+    loads = []
+    for index in range(2 * SIDE):
+        piece = y * SIDE + index if index < SIDE else (index - SIDE) * SIDE + z
+        columns = pl.ds(pl.multiple_of(piece * width, width), width)
+        load = pltpu.make_async_copy(right.at[:, columns], held.at[index], sems.at[index])
+        load.start()
+        loads.append(load)
+    for index in range(2 * SIDE):
+        loads[index].wait()
+        block, at = index // SIDE, index % SIDE
+        value = jnp.dot(
+            left[pl.ds(block * BLK, BLK), :], held[index], preferred_element_type=full
+        ).astype(half)
+        lower, upper = (lower0, upper0) if block == 0 else (lower1, upper1)
+        lower[at] = value[:middle]
+        upper[at] = value[middle:]
+
+
+def near_kernel(place, left, right, kept0, up0, down0, kept1, up1, down1, held, sems):
+    outs = {0: (kept0, kept1), 1: (up0, up1), 3: (down0, down1)}
     width = held.shape[2]
     y, z = place[0], place[1]
 
@@ -57,17 +79,15 @@
         value = jnp.dot(left[...], held[index], preferred_element_type=full).astype(half)
         along_y, at_z = index // SIDE, lax.rem(index, SIDE)
         at_y, along_z = lax.rem(y + along_y, SIDE), lax.rem(at_z - z + SIDE, SIDE)
-        for distance in range(SIDE):
-            for block, away, at in ((0, along_y, at_z), (1, along_z, at_y)):
-
-                @pl.when(away == distance)
-                def _():
-                    base, first = 5 * block, BLK * block
-                    if distance == 2:
-                        outs[base + 3][at] = value[first : first + BLK // 2]
-                        outs[base + 4][at] = value[first + BLK // 2 : first + BLK]
-                    else:
-                        outs[base + min(distance, 2)][at] = value[first : first + BLK]
+        for distance, (first, second) in outs.items():
+
+            @pl.when(along_y == distance)
+            def _():
+                first[at_z] = value[:BLK]
+
+            @pl.when(along_z == distance)
+            def _():
+                second[at_y] = value[BLK:]
 
 
 def merge_kernel(*refs):
@@ -107,22 +127,26 @@
     one_piece = pl.BlockSpec((1, BLK, width), lambda i: (i, 0, 0))
     one_half = pl.BlockSpec((1, BLK // 2, width), lambda i: (i, 0, 0))
 
-    kept0, up0, down0, lower0, upper0, kept1, up1, down1, lower1, upper1 = pl.pallas_call(
-        terms_kernel,
-        in_specs=[scalars, whole, pl.BlockSpec(memory_space=pltpu.HBM)],
-        out_specs=[whole] * 10,
-        out_shape=[full_piece, full_piece, full_piece, half_piece, half_piece] * 2,
-        scratch_shapes=[
-            pltpu.VMEM((SIDE * SIDE, width, width), half),
-            pltpu.SemaphoreType.DMA((SIDE * SIDE,)),
-        ],
-        compiler_params=pltpu.CompilerParams(vmem_limit_bytes=48 * 1024 * 1024),
-        cost_estimate=pl.CostEstimate(
-            flops=2 * attention.shape[0] * out_proj.size,
-            bytes_accessed=2 * out_proj.size,
-            transcendentals=0,
-        ),
-    )(place, attention, out_proj)
+    def terms(kernel, pieces, count, blocks):
+        return pl.pallas_call(
+            kernel,
+            in_specs=[scalars, whole, pl.BlockSpec(memory_space=pltpu.HBM)],
+            out_specs=[whole] * len(pieces),
+            out_shape=pieces,
+            scratch_shapes=[
+                pltpu.VMEM((count, width, width), half),
+                pltpu.SemaphoreType.DMA((count,)),
+            ],
+            compiler_params=pltpu.CompilerParams(vmem_limit_bytes=48 * 1024 * 1024),
+            cost_estimate=pl.CostEstimate(
+                flops=2 * blocks * BLK * count * width * width,
+                bytes_accessed=2 * count * width * width,
+                transcendentals=0,
+            ),
+        )(place, attention, out_proj)
+
+    lower0, upper0, lower1, upper1 = terms(far_kernel, [half_piece] * 4, 2 * SIDE, 1)
+    kept0, up0, down0, kept1, up1, down1 = terms(near_kernel, [full_piece] * 6, SIDE * SIDE, 2)
     lower0, upper0 = step(lower0, 1, 0), step(upper0, -1, 0)
     lower1, upper1 = step(lower1, 0, 1), step(upper1, 0, -1)
     up0, down0, up1, down1 = pl.pallas_call(
@@ -202,7 +226,8 @@
     )(dy, down, gate, up, order)
 
 
-def spread_kernel(piece, out, sems):
+def spread_kernel(piece, order, out, sems):
+    del order
     copies = [
         pltpu.make_async_copy(piece, out.at[to], sems.at[to]) for to in range(out.shape[0])
     ]
@@ -212,11 +237,11 @@
         copy.wait()
 
 
-def spread(piece, count):
+def spread(piece, count, order):
     whole = pl.BlockSpec(memory_space=pltpu.VMEM)
     return pl.pallas_call(
         spread_kernel,
-        in_specs=[whole],
+        in_specs=[whole, pl.BlockSpec(memory_space=pl.ANY)],
         out_specs=pl.BlockSpec(memory_space=pltpu.HBM),
         scratch_shapes=[pltpu.SemaphoreType.DMA((count,))],
         out_shape=jax.ShapeDtypeStruct((count,) + piece.shape, piece.dtype),
@@ -224,7 +249,7 @@
         cost_estimate=pl.CostEstimate(
             flops=0, bytes_accessed=4 * count * piece.size, transcendentals=0
         ),
-    )(piece)
+    )(piece, order)
 
 
 def home_kernel(terms, state, out):
@@ -251,7 +276,8 @@
     )(terms, state)
 
 
-def pool_kernel(place, message, token_slot, out, inverse, sh, weights, state, sems):
+def pool_kernel(place, message, token_slot, order, out, inverse, sh, weights, state, sems):
+    del order
     sources, _, cols = message.shape
     rows = BLK // sources
     token_proj = message[0, :BLK].astype(full)
@@ -286,14 +312,15 @@
         copy.wait()
 
 
-def pool(message, token_slot, block, width_full):
+def pool(message, token_slot, block, width_full, order):
     sources, _, cols = message.shape
     whole = pl.BlockSpec(memory_space=pltpu.VMEM)
     tokens = token_slot.shape[0]
     place = jnp.stack([block, jnp.full_like(block, width_full)]).astype(jnp.int32)
     return pl.pallas_call(
         pool_kernel,
-        in_specs=[pl.BlockSpec(memory_space=pltpu.SMEM), whole, whole],
+        in_specs=[pl.BlockSpec(memory_space=pltpu.SMEM), whole, whole]
+        + [pl.BlockSpec(memory_space=pl.ANY)],
         out_specs=[pl.BlockSpec(memory_space=pltpu.HBM), whole],
         out_shape=[
             jax.ShapeDtypeStruct((sources, BLK, cols), half),
@@ -309,7 +336,7 @@
         cost_estimate=pl.CostEstimate(
             flops=6 * message.size, bytes_accessed=4 * message.size, transcendentals=tokens
         ),
-    )(place, message, token_slot[None])
+    )(place, message, token_slot[None], order)
 
 
 def forward_kernel(
@@ -504,7 +531,7 @@
         axis=2,
     )
     message = exchange(message.reshape(n_mp, BLK + rows + 8, cols), "mp")
-    states, inverse_rms = pool(message, token_slot, mp // groups, width_full)
+    states, inverse_rms = pool(message, token_slot, mp // groups, width_full, dy[0, 0, :, :128])
     states = exchange(states, "mp")
 
     slots_block = token_slot.reshape(blocks, BLK)
@@ -540,7 +567,7 @@
         n_dp,
         out_rows,
     )
-    dproj = exchange(spread(exchange(dproj, "dp"), n_mp), "mp")
+    dproj = exchange(spread(exchange(dproj, "dp"), n_mp, pooled_all[:16, :128]), "mp")
     adapter_grad = lax.dot_general(
         pooled_all,
         dproj.reshape(n_dp * tokens, out_cols),

time: 227 us -> 257 us (1.13)
  blocking collectives: 9.72 us -> 26.7 us
  waiting for transfers between devices: 79.2 us -> 88.3 us
  Pallas kernels: 32.2 us -> 35.6 us
    all_gather x1, waiting for transfers between devices: 0.02 us -> 29.7 us  [on_device(): dy = lax.all_gather(dy_rows, 'mp', axis=0, tiled=False)]
    all_to_all x5, waiting for transfers between devices: 66.1 us -> 45.2 us  [exchange(): return lax.all_to_all(pieces, axis, split_axis=0, concat_axis=0, tiled=True)]
    all_to_all x1, blocking collectives: 9.72 us -> 26.7 us  [exchange(): return lax.all_to_all(pieces, axis, split_axis=0, concat_axis=0, tiled=True)]
    pallas_call x2 -> x3, Pallas kernels: 9.75 us -> 12.2 us  [the longest x2 10.9 us: terms(): pl.pallas_call(kernel, in_specs=[scalars, whole, pl.BlockSpec(memory_spac...]
    unnamed x31 -> x39, local copies, waits for them, and re-layouts: 4.31 us -> 5.51 us
  transfers between devices with their start and end apart: 23 -> 23, of which waited for: 12 -> 10; matrix products, arithmetic and copies ran while one was open for 8% -> 8% of each run, Pallas kernels for 13% -> 12%
where the time goes in v6:
time: 257 us; the launch traced here: 256 us
  waiting for transfers between devices  88.3 us (34%)
  starting transfers between devices  43.5 us (17%)
  Pallas kernels  35.6 us (14%)
  between operations  29.1 us (11%)
  blocking collectives  26.7 us (10%)
  local copies, waits for them, and re-layouts  12 us (5%)
  other arithmetic  10.3 us (4%)
  matrix products  10.1 us (4%)
    all_to_all x5, waiting for transfers between devices, exchange(): return lax.all_to_all(pieces, axis, split_axis=0, concat_axis=0, tiled=True)  45.2 us
    all_gather x1, waiting for transfers between devices, on_device(): dy = lax.all_gather(dy_rows, 'mp', axis=0, tiled=False)  29.7 us
    all_to_all x1, blocking collectives, exchange(): return lax.all_to_all(pieces, axis, split_axis=0, concat_axis=0, tiled=True)  26.7 us
    ppermute x14, starting transfers between devices, step(): return lax.ppermute(value, 'mp', pairs)  21.8 us
    all_to_all x5, starting transfers between devices, exchange(): return lax.all_to_all(pieces, axis, split_axis=0, concat_axis=0, tiled=True)  21.5 us
    ppermute x14, waiting for transfers between devices, step(): return lax.ppermute(value, 'mp', pairs)  13.4 us
    pallas_call x2, Pallas kernels, terms(): pl.pallas_call(kernel, in_specs=[scalars, whole, pl.BlockSpec(memory_spac...  10.9 us
    pallas_call x1, Pallas kernels, forward(): pl.pallas_call(forward_kernel, in_specs=[whole, whole, pl.BlockSpec(memor...  9.84 us
  transfers between devices with their start and end apart: 23, of which 10 were waited for; matrix products, arithmetic and copies ran while one was open for 8% of the time, Pallas kernels for 12%

profile of v6, /device:TPU:0, one launch (start us, length us, event | category | flops | bytes accessed | tf_op | source)
XLA Modules:
  0.0 255.5 jit_solution(16464420246239285522)
XLA Ops:
  7.2 2.0 pad_maximum_fusion.1
  10.3 3.6 %shard_map.141 = (bf16[4,64,512]{2,1,0:T(8,128)(2,1)S(1)}, bf16[4,64,512]{2,1,0:T(8,128)(2,1)S(1)}, bf16[4,64,512]{2,1,0:T(8,128)(2,1)S(1)}, bf16[4,64,512]{2,1,0:T(8,128)(2,1)S(1)}) custom-call(s32[2]{0:T(128)S(1)} %pad_add_fusion.1.place, bf16[256,512]{1,0:T(8,128)(2,1)S(1)} %copy-done, bf16[512,8192]{1,0:T(8,128)(2,1)} %right.3), custom_call_target="tpu_custom_call" | custom-call | flops 536870912 | bytes 4194304 | tf_op jit(solution)/shard_map/pallas_call | solution.py:131
  17.2 2.0 collective-permute-start.2
  19.2 2.1 collective-permute-start.3
  28.9 7.3 %shard_map.140 = (bf16[4,128,512]{2,1,0:T(8,128)(2,1)S(1)}, bf16[4,128,512]{2,1,0:T(8,128)(2,1)S(1)}, bf16[4,128,512]{2,1,0:T(8,128)(2,1)S(1)}, bf16[4,128,512]{...) custom-call(s32[2]{0:T(128)S(1)} %pad_add_fusion.1.place, ...), custom_call_target="tpu_custom_call" | custom-call | flops 2147483648 | bytes 8388608 | tf_op jit(solution)/shard_map/pallas_call | solution.py:131
  36.2 1.9 shard_map.142
  38.4 2.9 %collective-permute-start.5 = (bf16[4,128,512]{2,1,0:T(8,128)(2,1)}, bf16[4,128,512]{2,1,0:T(8,128)(2,1)S(1)}, u32[]{:S(2)}, u32[]{:S(2)}) collective-permute-start(bf16[4,128,512]{2,1,0:T(8,128)(2,1)} %get-tuple-element.56), channel_id=1, source_target_pairs={{0,12},{1,13},{2,14},{3,15},{4,0},{5,1},{6,2},{7,3},{8,4},{9,5},{1... | collective-permute-start | bytes 1572872 | tf_op jit(solution)/shard_map/ppermute | solution.py:38
  41.4 3.2 %collective-permute-start.7 = (bf16[4,128,512]{2,1,0:T(8,128)(2,1)}, bf16[4,128,512]{2,1,0:T(8,128)(2,1)}, u32[]{:S(2)}, u32[]{:S(2)}) collective-permute-start(bf16[4,128,512]{2,1,0:T(8,128)(2,1)} %get-tuple-element.59), channel_id=1, source_target_pairs={{0,3},{1,0},{2,1},{3,2},{4,7},{5,4},{6,5},{7,6},{8,11},{9,8},{10,9... | collective-permute-start | bytes 1572872 | tf_op jit(solution)/shard_map/ppermute | solution.py:38
  47.0 5.4 %collective-permute-done.4.refs_1_ = bf16[4,128,512]{2,1,0:T(8,128)(2,1)S(1)} collective-permute-done((bf16[4,128,512]{2,1,0:T(8,128)(2,1)}, bf16[4,128,512]{2,1,0:T(8,128)(2,1)S(1)}, u32[]{:S(2)}, u32[]{:S(2)}) %collective-permute-start.4) | collective-permute-done | bytes 524320 | tf_op jit(solution)/shard_map/ppermute | solution.py:38
  52.5 2.7 %collective-permute-done.6.refs_4_ = bf16[4,128,512]{2,1,0:T(8,128)(2,1)S(1)} collective-permute-done((bf16[4,128,512]{2,1,0:T(8,128)(2,1)}, bf16[4,128,512]{2,1,0:T(8,128)(2,1)S(1)}, u32[]{:S(2)}, u32[]{:S(2)}) %collective-permute-start.6) | collective-permute-done | bytes 524320 | tf_op jit(solution)/shard_map/ppermute | solution.py:38
  55.1 2.1 shard_map.143
  58.7 4.3 %collective-permute-start.9 = (bf16[128,512]{1,0:T(8,128)(2,1)}, bf16[128,512]{1,0:T(8,128)(2,1)S(1)}, u32[]{:S(2)}, u32[]{:S(2)}) collective-permute-start(bf16[128,512]{1,0:T(8,128)(2,1)} %get-tuple-element.62), channel_id=1, source_target_pairs={{0,2},{1,3},{2,0},{3,1},{4,6},{5,7},{6,4},{7,5},{8,10},{9,11},{10,... | collective-permute-start | bytes 393224 | tf_op jit(solution)/shard_map/ppermute | solution.py:38
  64.3 1.9 collective-permute-start.12
  68.3 3.7 %collective-permute-done.11 = bf16[128,512]{1,0:T(8,128)(2,1)S(1)} collective-permute-done((bf16[128,512]{1,0:T(8,128)(2,1)}, bf16[128,512]{1,0:T(8,128)(2,1)S(1)}, u32[]{:S(2)}, u32[]{:S(2)}) %collective-permute-start.11) | collective-permute-done | bytes 131104 | tf_op jit(solution)/shard_map/ppermute | solution.py:38
  76.4 5.8 %all-to-all-start = ((bf16[16,144,384]{2,1,0:T(8,128)(2,1)}), bf16[16,144,384]{2,1,0:T(8,128)(2,1)S(1)}, u32[]{:S(2)}, u32[]{:S(2)}) async-start(bf16[16,144,384]{2,1,0:T(8,128)(2,1)} %bitcast.22), calls=%async_computation | async-start | bytes 3538944 | tf_op jit(solution)/shard_map/all_to_all | solution.py:15
  82.4 29.7 %all-gather.12.cloned.1.call-done = bf16[32,8,3072]{2,1,0:T(8,128)(2,1)} async-done(((bf16[2,8,3072]{2,1,0:T(8,128)(2,1)}), bf16[32,8,3072]{2,1,0:T(8,128)(2,1)}) %all-gather.12.cloned.1.call-update) | async-done | bytes 1572880 | tf_op jit(solution)/shard_map/all_gather | solution.py:510
  112.8 3.1 %shard_map.144 = (bf16[16,128,384]{2,1,0:T(8,128)(2,1)S(1)}, f32[1,256]{1,0:T(1,128)S(1)}) custom-call(s32[2]{0:T(128)S(1)} %pad_add_fusion.place, bf16[16,144,384]{2,1,0:T(8,128)(2,1)S(1)} %all-to-all-done.message, s32[1,256]{1,0:T(1,128)S(1)} %bitcast.96, bf16[8,128]{1,0:T(8,128)(2,1)S(1)} %slice_bitcast_fusion.order), custom_call_target="tpu_custom_call" | custom-call | flops 5308416 | bytes 3538944 | tf_op jit(solution)/shard_map/pallas_call | solution.py:320
  118.1 26.7 %all_to_all.30.pieces = bf16[16,128,384]{2,1,0:T(8,128)(2,1)} all-to-all(bf16[16,128,384]{2,1,0:T(8,128)(2,1)S(1)} %get-tuple-element.68), channel_id=1, replica_groups=mesh['dp'=8,'mp'=16] {'mp'}, dimensions={0} | all-to-all | bytes 3145728 | tf_op jit(solution)/shard_map/all_to_all | solution.py:15
  144.8 9.8 %shard_map.145 = (bf16[256,3072]{1,0:T(8,128)(2,1)}, f32[256,512]{1,0:T(8,128)}, f32[256,512]{1,0:T(8,128)}, bf16[16,16,3072]{2,1,0:T(8,128)(2,1)}) custom-call(bf16[16,128,384]{2,1,0:T(8,128)(2,1)} %all_to_all.30.pieces, f32[1,3072]{1,0:T(1,128)} %bitcast.93, bf16[2,128,512]{2,1,0:T(8,128)(2,1)} %fusion.10.order, bf16[3072,512]{1,0:T(8,128)(2,1)} %gate_hbm.1, ...), custom_call_target="tpu_custom_call" | custom-call | flops 2415919104 | bytes 17301504 | tf_op jit(solution)/shard_map/pallas_call | solution.py:405
  154.7 3.7 %all-to-all-start.2 = ((bf16[16,16,3072]{2,1,0:T(8,128)(2,1)}), bf16[16,16,3072]{2,1,0:T(8,128)(2,1)S(1)}, u32[]{:S(2)}, u32[]{:S(2)}) async-start(bf16[16,16,3072]{2,1,0:T(8,128)(2,1)} %get-tuple-element.72.order), calls=%async_computation.2 | async-start | bytes 3145728 | tf_op jit(solution)/shard_map/all_to_all | solution.py:15
  158.5 4.6 %shard_map.146 = (bf16[256,512]{1,0:T(8,128)(2,1)}, bf16[256,512]{1,0:T(8,128)(2,1)}) custom-call(bf16[256,3072]{1,0:T(8,128)(2,1)} %bitcast.101, bf16[3072,512]{1,0:T(8,128)(2,1)} %down.1, f32[256,512]{1,0:T(8,128)} %get-tuple-element.70.gate, f32[256,512]{1,0:T(8,128)} %get-tuple-element.71.up, bf16[16,16,3072]{2,1,0:T(8,128)(2,1)} %get-tuple-element.72.order), custom_call_target="tpu_custom_call" | custom-call | flops 805306368 | bytes 6815744 | tf_op jit(solution)/shard_map/pallas_call | solution.py:214
  164.0 2.1 fusion.28
  166.1 2.2 fusion
  168.4 10.9 %all-to-all-done.2.terms = bf16[16,16,3072]{2,1,0:T(8,128)(2,1)S(1)} async-done(((bf16[16,16,3072]{2,1,0:T(8,128)(2,1)}), bf16[16,16,3072]{2,1,0:T(8,128)(2,1)S(1)}, u32[]{:S(2)}, u32[]{:S(2)}) %all-to-all-start.2) | async-done | bytes 1572896 | tf_op jit(solution)/shard_map/all_to_all | solution.py:15
  180.2 3.7 %all-to-all-start.3 = ((bf16[16,16,3072]{2,1,0:T(8,128)(2,1)}), bf16[16,16,3072]{2,1,0:T(8,128)(2,1)S(1)}, u32[]{:S(2)}, u32[]{:S(2)}) async-start(bf16[16,16,3072]{2,1,0:T(8,128)(2,1)} %bitcast.41), calls=%async_computation.3 | async-start | bytes 3145728 | tf_op jit(solution)/shard_map/all_to_all | solution.py:15
  185.8 19.2 %all-to-all-done.3.terms = bf16[16,16,3072]{2,1,0:T(8,128)(2,1)S(1)} async-done(((bf16[16,16,3072]{2,1,0:T(8,128)(2,1)}), bf16[16,16,3072]{2,1,0:T(8,128)(2,1)S(1)}, u32[]{:S(2)}, u32[]{:S(2)}) %all-to-all-start.3) | async-done | bytes 1572896 | tf_op jit(solution)/shard_map/all_to_all | solution.py:15
  206.0 4.5 %all-to-all-start.4 = ((bf16[8,16,384]{2,1,0:T(8,128)(2,1)}), bf16[8,16,384]{2,1,0:T(8,128)(2,1)S(1)}, u32[]{:S(2)}, u32[]{:S(2)}) async-start(bf16[8,16,384]{2,1,0:T(8,128)(2,1)} %shard_map.148), calls=%async_computation.4 | async-start | bytes 196608 | tf_op jit(solution)/shard_map/all_to_all | solution.py:15
  211.2 5.1 %all-to-all-done.4.piece = bf16[8,16,384]{2,1,0:T(8,128)(2,1)S(1)} async-done(((bf16[8,16,384]{2,1,0:T(8,128)(2,1)}), bf16[8,16,384]{2,1,0:T(8,128)(2,1)S(1)}, u32[]{:S(2)}, u32[]{:S(2)}) %all-to-all-start.4) | async-done | bytes 98336 | tf_op jit(solution)/shard_map/all_to_all | solution.py:15
  217.6 3.8 %all-to-all-start.5 = ((bf16[16,8,16,384]{3,2,1,0:T(8,128)(2,1)}), bf16[16,8,16,384]{3,2,1,0:T(8,128)(2,1)S(1)}, u32[]{:S(2)}, u32[]{:S(2)}) async-start(bf16[16,8,16,384]{3,2,1,0:T(8,128)(2,1)} %shard_map.149), calls=%async_computation.5 | async-start | bytes 3145728 | tf_op jit(solution)/shard_map/all_to_all | solution.py:15
  231.1 3.4 %select_bitcast_fusion.3 = (bf16[8,1,3072]{2,0,1:T(8,128)(2,1)S(1)}, bf16[8,1,3072]{2,0,1:T(8,128)(2,1)S(1)}, bf16[8,1,3072]{2,0,1:T(8,128)(2,1)S(1)}, bf16[8,1,3072]{2,0,1:T(8,128)(2,1)S(1)}) fusion(bf16[8,32,3072]{2,1,0:T(8,128)(2,1)} %bitcast.113, s32[]{:T(128)S(6)} %select_n.228, s32[]{:T(128)S(6)} %select_n.230, pred[]{:T(512)} %get-tuple-element.82, ...), kind=kLoop, calls=%fused_computation.34 | loop fusion | flops 98304 | bytes 393252 | tf_op jit(solution)/shard_map/jit(_where)/select_n | solution.py:586
  235.3 9.9 %all-to-all-done.5 = bf16[16,8,16,384]{3,2,1,0:T(8,128)(2,1)S(1)} async-done(((bf16[16,8,16,384]{3,2,1,0:T(8,128)(2,1)}), bf16[16,8,16,384]{3,2,1,0:T(8,128)(2,1)S(1)}, u32[]{:S(2)}, u32[]{:S(2)}) %all-to-all-start.5) | async-done | bytes 1572896 | tf_op jit(solution)/shard_map/all_to_all | solution.py:15
  245.2 3.8 %fusion.7 = f32[512,384]{1,0:T(8,128)} fusion(bf16[16,8,16,384]{3,2,1,0:T(8,128)(2,1)S(1)} %all-to-all-done.5, bf16[8,16,16,512]{3,2,0,1:T(8,128)(2,1)} %all-gather.8.cloned.1.call-done), kind=kOutput, calls=%fused_computation.10 | convolution fusion | flops 805306368 | bytes 4456448 | tf_op jit(solution)/shard_map/dot_general | solution.py:571
  (105 shorter events, 29.2 us)
Async XLA Ops:
  7.2 37.4 %all-gather.10.cloned.1.call-start = ((), (), s32[]{:S(2)}) async-start(), calls=%async_computation.7 | async-start | bytes 3538944 | tf_op jit(solution)/shard_map/all_gather | solution.py:498
  9.2 102.9 %all-gather.12.cloned.1.call-start = ((), (), s32[]{:S(2)}) async-start(), calls=%async_computation.8 | async-start | bytes 1671168 | tf_op jit(solution)/shard_map/all_gather | solution.py:510
  10.3 11.0 %copy-start.15 = (s32[16]{0:T(128)S(1)}, s32[16]{0:T(128)}, u32[]{:S(2)}) copy-start(s32[16]{0:T(128)} %param.21) | copy-start | bytes 196
  10.3 18.5 %copy-start.1 = (bf16[256,512]{1,0:T(8,128)(2,1)S(1)}, bf16[256,512]{1,0:T(8,128)(2,1)}, u32[]{:S(2)}) copy-start(bf16[256,512]{1,0:T(8,128)(2,1)} %left.3) | copy-start | bytes 786436
  13.9 22.3 %collective-permute-start = (bf16[4,64,512]{2,1,0:T(8,128)(2,1)S(1)}, bf16[4,64,512]{2,1,0:T(8,128)(2,1)S(1)}, u32[]{:S(2)}, u32[]{:S(2)}) collective-permute-start(bf16[4,64,512]{2,1,0:T(8,128)(2,1)S(1)} %get-tuple-element.49), channel_id=1, source_target_pairs={{0,4},{1,5},{2,6},{3,7},{4,8},{5,9},{6,10},{7,11},{8,12},{9,13},{1... | collective-permute-start | bytes 786440 | tf_op jit(solution)/shard_map/ppermute | solution.py:38
  15.6 20.6 %collective-permute-start.1 = (bf16[4,64,512]{2,1,0:T(8,128)(2,1)S(1)}, bf16[4,64,512]{2,1,0:T(8,128)(2,1)S(1)}, u32[]{:S(2)}, u32[]{:S(2)}) collective-permute-start(bf16[4,64,512]{2,1,0:T(8,128)(2,1)S(1)} %get-tuple-element.50), channel_id=1, source_target_pairs={{0,12},{1,13},{2,14},{3,15},{4,0},{5,1},{6,2},{7,3},{8,4},{9,5},{1... | collective-permute-start | bytes 786440 | tf_op jit(solution)/shard_map/ppermute | solution.py:38
  17.2 19.0 %collective-permute-start.2 = (bf16[4,64,512]{2,1,0:T(8,128)(2,1)S(1)}, bf16[4,64,512]{2,1,0:T(8,128)(2,1)S(1)}, u32[]{:S(2)}, u32[]{:S(2)}) collective-permute-start(bf16[4,64,512]{2,1,0:T(8,128)(2,1)S(1)} %get-tuple-element.53), channel_id=1, source_target_pairs={{0,1},{1,2},{2,3},{3,0},{4,5},{5,6},{6,7},{7,4},{8,9},{9,10},{10,1... | collective-permute-start | bytes 786440 | tf_op jit(solution)/shard_map/ppermute | solution.py:38
  19.2 17.0 %collective-permute-start.3 = (bf16[4,64,512]{2,1,0:T(8,128)(2,1)S(1)}, bf16[4,64,512]{2,1,0:T(8,128)(2,1)S(1)}, u32[]{:S(2)}, u32[]{:S(2)}) collective-permute-start(bf16[4,64,512]{2,1,0:T(8,128)(2,1)S(1)} %get-tuple-element.54), channel_id=1, source_target_pairs={{0,3},{1,0},{2,1},{3,2},{4,7},{5,4},{6,5},{7,6},{8,11},{9,8},{10,9... | collective-permute-start | bytes 786440 | tf_op jit(solution)/shard_map/ppermute | solution.py:38
  38.1 14.3 %collective-permute-start.4 = (bf16[4,128,512]{2,1,0:T(8,128)(2,1)}, bf16[4,128,512]{2,1,0:T(8,128)(2,1)S(1)}, u32[]{:S(2)}, u32[]{:S(2)}) collective-permute-start(bf16[4,128,512]{2,1,0:T(8,128)(2,1)} %get-tuple-element.55), channel_id=1, source_target_pairs={{0,4},{1,5},{2,6},{3,7},{4,8},{5,9},{6,10},{7,11},{8,12},{9,13},{1... | collective-permute-start | bytes 1572872 | tf_op jit(solution)/shard_map/ppermute | solution.py:38
  38.4 14.0 %collective-permute-start.5 = (bf16[4,128,512]{2,1,0:T(8,128)(2,1)}, bf16[4,128,512]{2,1,0:T(8,128)(2,1)S(1)}, u32[]{:S(2)}, u32[]{:S(2)}) collective-permute-start(bf16[4,128,512]{2,1,0:T(8,128)(2,1)} %get-tuple-element.56), channel_id=1, source_target_pairs={{0,12},{1,13},{2,14},{3,15},{4,0},{5,1},{6,2},{7,3},{8,4},{9,5},{1... | collective-permute-start | bytes 1572872 | tf_op jit(solution)/shard_map/ppermute | solution.py:38
  41.4 13.8 %collective-permute-start.6 = (bf16[4,128,512]{2,1,0:T(8,128)(2,1)}, bf16[4,128,512]{2,1,0:T(8,128)(2,1)S(1)}, u32[]{:S(2)}, u32[]{:S(2)}) collective-permute-start(bf16[4,128,512]{2,1,0:T(8,128)(2,1)} %get-tuple-element.58), channel_id=1, source_target_pairs={{0,1},{1,2},{2,3},{3,0},{4,5},{5,6},{6,7},{7,4},{8,9},{9,10},{10,1... | collective-permute-start | bytes 1572872 | tf_op jit(solution)/shard_map/ppermute | solution.py:38
  41.4 13.8 %collective-permute-start.7 = (bf16[4,128,512]{2,1,0:T(8,128)(2,1)}, bf16[4,128,512]{2,1,0:T(8,128)(2,1)}, u32[]{:S(2)}, u32[]{:S(2)}) collective-permute-start(bf16[4,128,512]{2,1,0:T(8,128)(2,1)} %get-tuple-element.59), channel_id=1, source_target_pairs={{0,3},{1,0},{2,1},{3,2},{4,7},{5,4},{6,5},{7,6},{8,11},{9,8},{10,9... | collective-permute-start | bytes 1572872 | tf_op jit(solution)/shard_map/ppermute | solution.py:38
  47.0 16.0 %copy-start.2 = (bf16[2,8,3072]{2,1,0:T(8,128)(2,1)}, bf16[2,8,3072]{2,1,0:T(8,128)(2,1)S(1)}, u32[]{:S(2)}) copy-start(bf16[2,8,3072]{2,1,0:T(8,128)(2,1)S(1)} %pad_maximum_fusion.2.refs_7_) | copy-start | bytes 294916
  55.1 18.6 %copy-start.14 = (f32[512]{0:T(512)S(1)}, f32[512]{0:T(512)}, u32[]{:S(2)}) copy-start(f32[512]{0:T(512)} %param.18) | copy-start | bytes 6148
  58.5 15.2 %copy-start.11 = (bf16[256,512]{1,0:T(8,128)(2,1)S(1)}, bf16[256,512]{1,0:T(8,128)(2,1)}, u32[]{:S(2)}) copy-start(bf16[256,512]{1,0:T(8,128)(2,1)} %param.17) | copy-start | bytes 786436
  58.5 7.7 %collective-permute-start.8 = (bf16[128,512]{1,0:T(8,128)(2,1)}, bf16[128,512]{1,0:T(8,128)(2,1)S(1)}, u32[]{:S(2)}, u32[]{:S(2)}) collective-permute-start(bf16[128,512]{1,0:T(8,128)(2,1)} %get-tuple-element.61), channel_id=1, source_target_pairs={{0,1},{1,2},{2,3},{3,0},{4,5},{5,6},{6,7},{7,4},{8,9},{9,10},{10,1... | collective-permute-start | bytes 393224 | tf_op jit(solution)/shard_map/ppermute | solution.py:38
  58.7 8.9 %collective-permute-start.9 = (bf16[128,512]{1,0:T(8,128)(2,1)}, bf16[128,512]{1,0:T(8,128)(2,1)S(1)}, u32[]{:S(2)}, u32[]{:S(2)}) collective-permute-start(bf16[128,512]{1,0:T(8,128)(2,1)} %get-tuple-element.62), channel_id=1, source_target_pairs={{0,2},{1,3},{2,0},{3,1},{4,6},{5,7},{6,4},{7,5},{8,10},{9,11},{10,... | collective-permute-start | bytes 393224 | tf_op jit(solution)/shard_map/ppermute | solution.py:38
  63.0 5.2 %collective-permute-start.10 = (bf16[128,512]{1,0:T(8,128)(2,1)}, bf16[128,512]{1,0:T(8,128)(2,1)S(1)}, u32[]{:S(2)}, u32[]{:S(2)}) collective-permute-start(bf16[128,512]{1,0:T(8,128)(2,1)} %get-tuple-element.63), channel_id=1, source_target_pairs={{0,3},{1,0},{2,1},{3,2},{4,7},{5,4},{6,5},{7,6},{8,11},{9,8},{10,9... | collective-permute-start | bytes 393224 | tf_op jit(solution)/shard_map/ppermute | solution.py:38
  63.1 10.9 %copy-start.16 = (bf16[512,3072]{1,0:T(8,128)(2,1)S(1)}, bf16[512,3072]{1,0:T(8,128)(2,1)}, u32[]{:S(2)}) copy-start(bf16[512,3072]{1,0:T(8,128)(2,1)} %param.19) | copy-start | bytes 9437188
  64.2 7.9 %collective-permute-start.11 = (bf16[128,512]{1,0:T(8,128)(2,1)}, bf16[128,512]{1,0:T(8,128)(2,1)S(1)}, u32[]{:S(2)}, u32[]{:S(2)}) collective-permute-start(bf16[128,512]{1,0:T(8,128)(2,1)} %copy-done.6), channel_id=1, source_target_pairs={{0,4},{1,5},{2,6},{3,7},{4,8},{5,9},{6,10},{7,11},{8,12},{9,13},{1... | collective-permute-start | bytes 393224 | tf_op jit(solution)/shard_map/ppermute | solution.py:38
  64.3 7.8 %collective-permute-start.12 = (bf16[128,512]{1,0:T(8,128)(2,1)}, bf16[128,512]{1,0:T(8,128)(2,1)S(1)}, u32[]{:S(2)}, u32[]{:S(2)}) collective-permute-start(bf16[128,512]{1,0:T(8,128)(2,1)} %copy-done.5), channel_id=1, source_target_pairs={{0,8},{1,9},{2,10},{3,11},{4,12},{5,13},{6,14},{7,15},{8,0},{9,1},... | collective-permute-start | bytes 393224 | tf_op jit(solution)/shard_map/ppermute | solution.py:38
  66.2 6.7 %collective-permute-start.13 = (bf16[128,512]{1,0:T(8,128)(2,1)S(1)}, bf16[128,512]{1,0:T(8,128)(2,1)S(1)}, u32[]{:S(2)}, u32[]{:S(2)}) collective-permute-start(bf16[128,512]{1,0:T(8,128)(2,1)S(1)} %get-tuple-element.67), channel_id=1, source_target_pairs={{0,12},{1,13},{2,14},{3,15},{4,0},{5,1},{6,2},{7,3},{8,4},{9,5},{1... | collective-permute-start | bytes 393224 | tf_op jit(solution)/shard_map/ppermute | solution.py:38
  68.3 6.7 %copy-start.9 = (f32[128,512]{1,0:T(8,128)}, f32[128,512]{1,0:T(8,128)S(1)}, u32[]{:S(2)}) copy-start(f32[128,512]{1,0:T(8,128)S(1)} %convert_add_fusion.1) | copy-start | bytes 786436
  76.4 5.9 %copy-start.4 = (s32[256]{0:T(256)S(1)}, s32[256]{0:T(256)}, u32[]{:S(2)}) copy-start(s32[256]{0:T(256)} %param.20) | copy-start | bytes 3076
  76.4 36.4 %all-to-all-start = ((bf16[16,144,384]{2,1,0:T(8,128)(2,1)}), bf16[16,144,384]{2,1,0:T(8,128)(2,1)S(1)}, u32[]{:S(2)}, u32[]{:S(2)}) async-start(bf16[16,144,384]{2,1,0:T(8,128)(2,1)} %bitcast.22), calls=%async_computation | async-start | bytes 3538944 | tf_op jit(solution)/shard_map/all_to_all | solution.py:15
  82.2 128.4 %all-gather.8.cloned.1.call-start = ((), (), s32[]{:S(2)}) async-start(), calls=%async_computation.6 | async-start | bytes 2359296 | tf_op jit(solution)/shard_map/all_gather | solution.py:544
  154.7 24.6 %all-to-all-start.2 = ((bf16[16,16,3072]{2,1,0:T(8,128)(2,1)}), bf16[16,16,3072]{2,1,0:T(8,128)(2,1)S(1)}, u32[]{:S(2)}, u32[]{:S(2)}) async-start(bf16[16,16,3072]{2,1,0:T(8,128)(2,1)} %get-tuple-element.72.order), calls=%async_computation.2 | async-start | bytes 3145728 | tf_op jit(solution)/shard_map/all_to_all | solution.py:15
  158.4 72.7 %all-gather.14.cloned.1.call-start = ((), (), s32[]{:S(2)}) async-start(), calls=%async_computation.9 | async-start | bytes 1769472 | tf_op jit(solution)/shard_map/all_gather | solution.py:578
  180.2 24.8 %copy-start.3 = (f32[3072]{0:T(1024)S(1)}, f32[3072]{0:T(1024)}, u32[]{:S(2)}) copy-start(f32[3072]{0:T(1024)} %param.24) | copy-start | bytes 36868
  180.2 24.8 %all-to-all-start.3 = ((bf16[16,16,3072]{2,1,0:T(8,128)(2,1)}), bf16[16,16,3072]{2,1,0:T(8,128)(2,1)S(1)}, u32[]{:S(2)}, u32[]{:S(2)}) async-start(bf16[16,16,3072]{2,1,0:T(8,128)(2,1)} %bitcast.41), calls=%async_computation.3 | async-start | bytes 3145728 | tf_op jit(solution)/shard_map/all_to_all | solution.py:15
  206.0 10.3 %all-to-all-start.4 = ((bf16[8,16,384]{2,1,0:T(8,128)(2,1)}), bf16[8,16,384]{2,1,0:T(8,128)(2,1)S(1)}, u32[]{:S(2)}, u32[]{:S(2)}) async-start(bf16[8,16,384]{2,1,0:T(8,128)(2,1)} %shard_map.148), calls=%async_computation.4 | async-start | bytes 196608 | tf_op jit(solution)/shard_map/all_to_all | solution.py:15
  217.6 27.6 %all-to-all-start.5 = ((bf16[16,8,16,384]{3,2,1,0:T(8,128)(2,1)}), bf16[16,8,16,384]{3,2,1,0:T(8,128)(2,1)S(1)}, u32[]{:S(2)}, u32[]{:S(2)}) async-start(bf16[16,8,16,384]{3,2,1,0:T(8,128)(2,1)} %shard_map.149), calls=%async_computation.5 | async-start | bytes 3145728 | tf_op jit(solution)/shard_map/all_to_all | solution.py:15
  (8 other events, 13.4 us)
Sparse Core Ops, SparseCore 0:
  9.7 30.1 all-gather.9
  63.2 48.8 all-gather.11
  118.2 24.3 all-gather.7
  180.4 23.2 all-gather.13

commit v7 on v6

--- a/solution.py
+++ b/solution.py
@@ -103,7 +103,7 @@
 
 
 def gather_kernel(place, *refs):
-    ins, outs = refs[:6], refs[8:]
+    ins, outs = refs[:6], refs[7:]
     for block in (0, 1):
         kept, from_down, from_up = ins[3 * block : 3 * block + 3]
         here = place[1 - block]
@@ -164,7 +164,7 @@
     from_down1, from_up1 = step(up1, 0, 1), step(down1, 0, -1)
     sums = pl.pallas_call(
         gather_kernel,
-        in_specs=[scalars] + [whole] * 6 + [anywhere] * 2,
+        in_specs=[scalars] + [whole] * 6 + [anywhere],
         out_specs=[whole] * (2 * SIDE),
         out_shape=[
             jax.ShapeDtypeStruct((BLK, width), half if distance else full)
@@ -226,8 +226,7 @@
     )(dy, down, gate, up, order)
 
 
-def spread_kernel(piece, order, out, sems):
-    del order
+def spread_kernel(piece, out, sems):
     copies = [
         pltpu.make_async_copy(piece, out.at[to], sems.at[to]) for to in range(out.shape[0])
     ]
@@ -237,11 +236,11 @@
         copy.wait()
 
 
-def spread(piece, count, order):
+def spread(piece, count):
     whole = pl.BlockSpec(memory_space=pltpu.VMEM)
     return pl.pallas_call(
         spread_kernel,
-        in_specs=[whole, pl.BlockSpec(memory_space=pl.ANY)],
+        in_specs=[whole],
         out_specs=pl.BlockSpec(memory_space=pltpu.HBM),
         scratch_shapes=[pltpu.SemaphoreType.DMA((count,))],
         out_shape=jax.ShapeDtypeStruct((count,) + piece.shape, piece.dtype),
@@ -249,7 +248,7 @@
         cost_estimate=pl.CostEstimate(
             flops=0, bytes_accessed=4 * count * piece.size, transcendentals=0
         ),
-    )(piece, order)
+    )(piece)
 
 
 def home_kernel(terms, state, out):
@@ -276,8 +275,7 @@
     )(terms, state)
 
 
-def pool_kernel(place, message, token_slot, order, out, inverse, sh, weights, state, sems):
-    del order
+def pool_kernel(place, message, token_slot, out, inverse, sh, weights, state, sems):
     sources, _, cols = message.shape
     rows = BLK // sources
     token_proj = message[0, :BLK].astype(full)
@@ -312,15 +310,14 @@
         copy.wait()
 
 
-def pool(message, token_slot, block, width_full, order):
+def pool(message, token_slot, block, width_full):
     sources, _, cols = message.shape
     whole = pl.BlockSpec(memory_space=pltpu.VMEM)
     tokens = token_slot.shape[0]
     place = jnp.stack([block, jnp.full_like(block, width_full)]).astype(jnp.int32)
     return pl.pallas_call(
         pool_kernel,
-        in_specs=[pl.BlockSpec(memory_space=pltpu.SMEM), whole, whole]
-        + [pl.BlockSpec(memory_space=pl.ANY)],
+        in_specs=[pl.BlockSpec(memory_space=pltpu.SMEM), whole, whole],
         out_specs=[pl.BlockSpec(memory_space=pltpu.HBM), whole],
         out_shape=[
             jax.ShapeDtypeStruct((sources, BLK, cols), half),
@@ -336,24 +333,25 @@
         cost_estimate=pl.CostEstimate(
             flops=6 * message.size, bytes_accessed=4 * message.size, transcendentals=tokens
         ),
-    )(place, message, token_slot[None], order)
+    )(place, message, token_slot[None])
 
 
 def forward_kernel(
     pieces, gain, order, gate_hbm, up_hbm, down_hbm, state, gate, up, out, normed, act, held, sems
 ):
     del order
-    loads = []
-    for index, source in enumerate((gate_hbm, up_hbm, down_hbm)):
-        part = source.shape[0] // 3
-        for third in range(3):
-            at = pl.ds(third * part, part)
-            load = pltpu.make_async_copy(
-                source.at[at], held.at[index, at], sems.at[3 * index + third]
-            )
-            load.start()
-            loads.append(load)
-    gate_w, up_w, down_w = held.at[0], held.at[1], held.at[2]
+    parts = 3
+    part = gate_hbm.shape[0] // parts
+
+    def load(which, source, third):
+        at = pl.ds(third * part, part)
+        return pltpu.make_async_copy(
+            source.at[at], held.at[which, at], sems.at[parts * which + third]
+        )
+
+    for third in range(parts):
+        load(0, gate_hbm, third).start()
+        load(1, up_hbm, third).start()
     cols = pieces.shape[2]
     groups = state.shape[1] // cols
     for block in range(state.shape[0] // BLK):
@@ -372,18 +370,24 @@
             at = pl.ds(group * cols, cols)
             wide = pieces[block * groups + group].astype(full)
             normed[rows, at] = (wide * inverse * gain[:, at]).astype(normed.dtype)
-    for load in loads[:6]:
-        load.wait()
-    chunk = gate.shape[1] // 2
-    for index in range(2):
-        at = pl.ds(index * chunk, chunk)
-        gate_val = jnp.dot(normed[...], gate_w[:, at], preferred_element_type=full)
-        up_val = jnp.dot(normed[...], up_w[:, at], preferred_element_type=full)
-        gate[:, at] = gate_val
-        up[:, at] = up_val
-        act[:, at] = (gate_val * jax.nn.sigmoid(gate_val) * up_val).astype(half)
-    for load in loads[6:]:
-        load.wait()
+    half_hidden = gate.shape[1] // 2
+    for third in range(parts):
+        load(0, gate_hbm, third).wait()
+        load(1, up_hbm, third).wait()
+        load(2, down_hbm, third).start()
+        depth = pl.ds(third * part, part)
+        for index in range(2):
+            at = pl.ds(index * half_hidden, half_hidden)
+            for which, total_ref in ((0, gate), (1, up)):
+                value = jnp.dot(
+                    normed[:, depth], held[which, depth, at], preferred_element_type=full
+                )
+                total_ref[:, at] = value if third == 0 else total_ref[:, at] + value
+    gate_val = gate[...]
+    act[...] = (gate_val * jax.nn.sigmoid(gate_val) * up[...]).astype(half)
+    for third in range(parts):
+        load(2, down_hbm, third).wait()
+    down_w = held.at[2]
     rows = out.shape[1] // 2
     wide_chunk = 512
 
@@ -489,28 +493,30 @@
     out_cols = student_width // n_dp
     mine_rows = blocks * rows
 
-    owned = block_owner[None, :] == jnp.arange(n_dp, dtype=jnp.int32)[:, None]
-    ranks = jnp.sum(jnp.where(owned, jnp.cumsum(owned.astype(jnp.int32), axis=1) - 1, 0), axis=0)
-    place = block_owner * slots + ranks
-    my_place = lax.dynamic_slice_in_dim(place, dp * blocks, blocks)
-
-    both = jnp.concatenate([student_hidden[0], cotangent[0]], axis=1)
-    everyone = lax.all_gather(both, "dp", axis=0, tiled=False)
-
-    def fetch(offset):
+    ids = jnp.arange(block_owner.shape[0], dtype=jnp.int32)
+    my_ids = dp * blocks + jnp.arange(blocks, dtype=jnp.int32)
+    my_owner = lax.dynamic_slice_in_dim(block_owner, dp * blocks, blocks)
+    my_slot = jnp.sum(
+        (block_owner[None, :] == my_owner[:, None]) & (ids[None, :] < my_ids[:, None]),
+        axis=1,
+        dtype=jnp.int32,
+    )
+
+    def fetch(array):
+        everyone = lax.all_gather(array[0], "dp", axis=0, tiled=False)
         picked = []
         for k in range(blocks):
-            at = (my_place[k] // slots, 0, my_place[k] % slots + offset, 0)
+            at = (my_owner[k], 0, my_slot[k], 0)
             piece = lax.dynamic_slice(everyone, at, (1, rows, 1, student_width))
             picked.append(piece.reshape(rows, student_width))
         return jnp.stack(picked)
 
-    sh_rows = fetch(0)
-    dy_rows = fetch(slots)
+    sh_rows = fetch(student_hidden)
+    dy_rows = fetch(cotangent)
     dy = lax.all_gather(dy_rows, "mp", axis=0, tiled=False)
 
     hidden = residual.astype(full) + jnp.concatenate(
-        [total(v) for v in teacher_terms(attention, out_proj, mp, (sh_rows, dy_rows))], axis=0
+        [total(v) for v in teacher_terms(attention, out_proj, mp, (sh_rows,))], axis=0
     )
     squares = jnp.sum(hidden * hidden, axis=1)
     gained_hidden = hidden * final_gain
@@ -531,7 +537,7 @@
         axis=2,
     )
     message = exchange(message.reshape(n_mp, BLK + rows + 8, cols), "mp")
-    states, inverse_rms = pool(message, token_slot, mp // groups, width_full, dy[0, 0, :, :128])
+    states, inverse_rms = pool(message, token_slot, mp // groups, width_full)
     states = exchange(states, "mp")
 
     slots_block = token_slot.reshape(blocks, BLK)
@@ -567,7 +573,7 @@
         n_dp,
         out_rows,
     )
-    dproj = exchange(spread(exchange(dproj, "dp"), n_mp, pooled_all[:16, :128]), "mp")
+    dproj = exchange(spread(exchange(dproj, "dp"), n_mp), "mp")
     adapter_grad = lax.dot_general(
         pooled_all,
         dproj.reshape(n_dp * tokens, out_cols),
@@ -576,11 +582,13 @@
     )
 
     back = lax.all_gather(out_rows, "dp", axis=0, tiled=False)
+    before = (block_owner[None, :] == block_owner[:, None]) & (ids[None, :] < ids[:, None])
+    ranks = jnp.sum(before, axis=1, dtype=jnp.int32)
     mine = block_owner == dp
     picks = []
     for slot in range(slots):
         chosen = mine & (ranks == slot)
-        index = jnp.sum(jnp.where(chosen, jnp.arange(chosen.shape[0], dtype=jnp.int32), 0))
+        index = jnp.sum(jnp.where(chosen, ids, 0))
         at = (index // blocks, (index % blocks) * rows, 0)
         piece = lax.dynamic_slice(back, at, (1, rows, student_width))[0]
         picks.append(jnp.where(jnp.any(chosen), piece, jnp.zeros((), half)))

time: 257 us -> 229 us (0.89)
  blocking collectives: 26.7 us -> 9.64 us
  waiting for transfers between devices: 88.3 us -> 79.1 us
  Pallas kernels: 35.6 us -> 32.6 us
  between operations: 29.1 us -> 31.7 us
    all_gather x1, waiting for transfers between devices: 29.7 us -> 0.02 us  [on_device(): dy = lax.all_gather(dy_rows, 'mp', axis=0, tiled=False)]
    all_to_all x5, waiting for transfers between devices: 45.2 us -> 63.3 us  [exchange(): return lax.all_to_all(pieces, axis, split_axis=0, concat_axis=0, tiled=True)]
    all_to_all x1, blocking collectives: 26.7 us -> 9.64 us  [exchange(): return lax.all_to_all(pieces, axis, split_axis=0, concat_axis=0, tiled=True)]
    all_to_all x5, starting transfers between devices: 21.5 us -> 24.1 us  [exchange(): return lax.all_to_all(pieces, axis, split_axis=0, concat_axis=0, tiled=True)]
    unnamed x39 -> x29, local copies, waits for them, and re-layouts: 5.51 us -> 5.45 us
  transfers between devices with their start and end apart: 23 -> 24, of which waited for: 10 -> 12; matrix products, arithmetic and copies ran while one was open for 8% -> 9% of each run, Pallas kernels for 12% -> 14%
where the time goes in v7:
time: 229 us; the launch traced here: 228 us
  waiting for transfers between devices  79.1 us (35%)
  starting transfers between devices  45.7 us (20%)
  Pallas kernels  32.6 us (14%)
  between operations  31.7 us (14%)
  local copies, waits for them, and re-layouts  11.1 us (5%)
  matrix products  10.1 us (4%)
  blocking collectives  9.64 us (4%)
  other arithmetic  7.99 us (3%)
    all_to_all x5, waiting for transfers between devices, exchange(): return lax.all_to_all(pieces, axis, split_axis=0, concat_axis=0, tiled=True)  63.3 us
    all_to_all x5, starting transfers between devices, exchange(): return lax.all_to_all(pieces, axis, split_axis=0, concat_axis=0, tiled=True)  24.1 us
    ppermute x14, starting transfers between devices, step(): return lax.ppermute(value, 'mp', pairs)  21.4 us
    ppermute x14, waiting for transfers between devices, step(): return lax.ppermute(value, 'mp', pairs)  15.1 us
    pallas_call x2, Pallas kernels, terms(): pl.pallas_call(kernel, in_specs=[scalars, whole, pl.BlockSpec(memory_spac...  10.8 us
    all_to_all x1, blocking collectives, exchange(): return lax.all_to_all(pieces, axis, split_axis=0, concat_axis=0, tiled=True)  9.64 us
    pallas_call x1, Pallas kernels, forward(): pl.pallas_call(forward_kernel, in_specs=[whole, whole, pl.BlockSpec(memor...  9.51 us
    unnamed x29, local copies, waits for them, and re-layouts  5.45 us
  transfers between devices with their start and end apart: 24, of which 12 were waited for; matrix products, arithmetic and copies ran while one was open for 9% of the time, Pallas kernels for 14%

profile of v7, /device:TPU:0, one launch (start us, length us, event | category | flops | bytes accessed | tf_op | source)
XLA Modules:
  0.0 227.9 jit_solution(12744880031614914039)
XLA Ops:
  7.2 1.7 copy.35
  10.0 3.6 %shard_map.141 = (bf16[4,64,512]{2,1,0:T(8,128)(2,1)S(1)}, bf16[4,64,512]{2,1,0:T(8,128)(2,1)S(1)}, bf16[4,64,512]{2,1,0:T(8,128)(2,1)S(1)}, bf16[4,64,512]{2,1,0:T(8,128)(2,1)S(1)}) custom-call(s32[2]{0:T(128)S(1)} %pad_add_fusion.1.place, bf16[256,512]{1,0:T(8,128)(2,1)S(1)} %copy-done, bf16[512,8192]{1,0:T(8,128)(2,1)} %right.3), custom_call_target="tpu_custom_call" | custom-call | flops 536870912 | bytes 4194304 | tf_op jit(solution)/shard_map/pallas_call | solution.py:131
  13.6 1.7 collective-permute-start
  16.9 2.0 collective-permute-start.2
  18.9 2.1 collective-permute-start.3
  30.5 7.3 %shard_map.140 = (bf16[4,128,512]{2,1,0:T(8,128)(2,1)S(1)}, bf16[4,128,512]{2,1,0:T(8,128)(2,1)S(1)}, bf16[4,128,512]{2,1,0:T(8,128)(2,1)S(1)}, bf16[4,128,512]{...) custom-call(s32[2]{0:T(128)S(1)} %pad_add_fusion.1.place, ...), custom_call_target="tpu_custom_call" | custom-call | flops 2147483648 | bytes 8388608 | tf_op jit(solution)/shard_map/pallas_call | solution.py:131
  37.9 1.9 shard_map.142
  40.1 2.9 %collective-permute-start.5 = (bf16[4,128,512]{2,1,0:T(8,128)(2,1)}, bf16[4,128,512]{2,1,0:T(8,128)(2,1)S(1)}, u32[]{:S(2)}, u32[]{:S(2)}) collective-permute-start(bf16[4,128,512]{2,1,0:T(8,128)(2,1)} %get-tuple-element.56), channel_id=1, source_target_pairs={{0,12},{1,13},{2,14},{3,15},{4,0},{5,1},{6,2},{7,3},{8,4},{9,5},{1... | collective-permute-start | bytes 1572872 | tf_op jit(solution)/shard_map/ppermute | solution.py:38
  43.0 3.2 %collective-permute-start.7 = (bf16[4,128,512]{2,1,0:T(8,128)(2,1)}, bf16[4,128,512]{2,1,0:T(8,128)(2,1)S(1)}, u32[]{:S(2)}, u32[]{:S(2)}) collective-permute-start(bf16[4,128,512]{2,1,0:T(8,128)(2,1)} %get-tuple-element.59), channel_id=1, source_target_pairs={{0,3},{1,0},{2,1},{3,2},{4,7},{5,4},{6,5},{7,6},{8,11},{9,8},{10,9... | collective-permute-start | bytes 1572872 | tf_op jit(solution)/shard_map/ppermute | solution.py:38
  47.0 7.1 %collective-permute-done.4.refs_1_ = bf16[4,128,512]{2,1,0:T(8,128)(2,1)S(1)} collective-permute-done((bf16[4,128,512]{2,1,0:T(8,128)(2,1)}, bf16[4,128,512]{2,1,0:T(8,128)(2,1)S(1)}, u32[]{:S(2)}, u32[]{:S(2)}) %collective-permute-start.4) | collective-permute-done | bytes 524320 | tf_op jit(solution)/shard_map/ppermute | solution.py:38
  54.1 2.7 %collective-permute-done.6.refs_4_ = bf16[4,128,512]{2,1,0:T(8,128)(2,1)S(1)} collective-permute-done((bf16[4,128,512]{2,1,0:T(8,128)(2,1)}, bf16[4,128,512]{2,1,0:T(8,128)(2,1)S(1)}, u32[]{:S(2)}, u32[]{:S(2)}) %collective-permute-start.6) | collective-permute-done | bytes 524320 | tf_op jit(solution)/shard_map/ppermute | solution.py:38
  57.8 4.4 %collective-permute-start.9 = (bf16[128,512]{1,0:T(8,128)(2,1)S(1)}, bf16[128,512]{1,0:T(8,128)(2,1)S(1)}, u32[]{:S(2)}, u32[]{:S(2)}) collective-permute-start(bf16[128,512]{1,0:T(8,128)(2,1)S(1)} %get-tuple-element.62), channel_id=1, source_target_pairs={{0,2},{1,3},{2,0},{3,1},{4,6},{5,7},{6,4},{7,5},{8,10},{9,11},{10,... | collective-permute-start | bytes 393224 | tf_op jit(solution)/shard_map/ppermute | solution.py:38
  62.2 1.9 collective-permute-start.12
  67.3 2.5 %collective-permute-done.11 = bf16[128,512]{1,0:T(8,128)(2,1)S(1)} collective-permute-done((bf16[128,512]{1,0:T(8,128)(2,1)S(1)}, bf16[128,512]{1,0:T(8,128)(2,1)S(1)}, u32[]{:S(2)}, u32[]{:S(2)}) %collective-permute-start.11) | collective-permute-done | bytes 131104 | tf_op jit(solution)/shard_map/ppermute | solution.py:38
  73.5 5.4 %all-to-all-start = ((bf16[16,144,384]{2,1,0:T(8,128)(2,1)}), bf16[16,144,384]{2,1,0:T(8,128)(2,1)S(1)}, u32[]{:S(2)}, u32[]{:S(2)}) async-start(bf16[16,144,384]{2,1,0:T(8,128)(2,1)} %bitcast.21), calls=%async_computation | async-start | bytes 3538944 | tf_op jit(solution)/shard_map/all_to_all | solution.py:15
  80.6 18.6 %all-to-all-done.message = bf16[16,144,384]{2,1,0:T(8,128)(2,1)S(1)} async-done(((bf16[16,144,384]{2,1,0:T(8,128)(2,1)}), bf16[16,144,384]{2,1,0:T(8,128)(2,1)S(1)}, u32[]{:S(2)}, u32[]{:S(2)}) %all-to-all-start) | async-done | bytes 1769504 | tf_op jit(solution)/shard_map/all_to_all | solution.py:15
  99.2 2.3 %shard_map.144 = (bf16[16,128,384]{2,1,0:T(8,128)(2,1)}, f32[1,256]{1,0:T(1,128)S(1)}) custom-call(s32[2]{0:T(128)S(1)} %pad_add_fusion.place, bf16[16,144,384]{2,1,0:T(8,128)(2,1)S(1)} %all-to-all-done.message, s32[1,256]{1,0:T(1,128)S(1)} %bitcast.86), custom_call_target="tpu_custom_call" | custom-call | flops 5308416 | bytes 3538944 | tf_op jit(solution)/shard_map/pallas_call | solution.py:318
  101.5 5.1 %all-to-all-start.1 = ((bf16[16,128,384]{2,1,0:T(8,128)(2,1)}), bf16[16,128,384]{2,1,0:T(8,128)(2,1)S(1)}, u32[]{:S(2)}, u32[]{:S(2)}) async-start(bf16[16,128,384]{2,1,0:T(8,128)(2,1)} %get-tuple-element.68), calls=%async_computation.1 | async-start | bytes 3145728 | tf_op jit(solution)/shard_map/all_to_all | solution.py:15
  107.7 16.3 %all-to-all-done.1.pieces = bf16[16,128,384]{2,1,0:T(8,128)(2,1)S(1)} async-done(((bf16[16,128,384]{2,1,0:T(8,128)(2,1)}), bf16[16,128,384]{2,1,0:T(8,128)(2,1)S(1)}, u32[]{:S(2)}, u32[]{:S(2)}) %all-to-all-start.1) | async-done | bytes 1572896 | tf_op jit(solution)/shard_map/all_to_all | solution.py:15
  125.2 9.5 %shard_map.145 = (bf16[256,3072]{1,0:T(8,128)(2,1)}, f32[256,512]{1,0:T(8,128)}, f32[256,512]{1,0:T(8,128)}, bf16[16,16,3072]{2,1,0:T(8,128)(2,1)}) custom-call(bf16[16,128,384]{2,1,0:T(8,128)(2,1)} %copy-done.6, f32[1,3072]{1,0:T(1,128)} %bitcast.84, bf16[2,128,512]{2,1,0:T(8,128)(2,1)} %fusion.10.order, bf16[3072,512]{1,0:T(8,128)(2,1)} %gate_hbm.1, ...), custom_call_target="tpu_custom_call" | custom-call | flops 2415919104 | bytes 17301504 | tf_op jit(solution)/shard_map/pallas_call | solution.py:409
  134.7 6.2 %all-to-all-start.2 = ((bf16[16,16,3072]{2,1,0:T(8,128)(2,1)}), bf16[16,16,3072]{2,1,0:T(8,128)(2,1)S(1)}, u32[]{:S(2)}, u32[]{:S(2)}) async-start(bf16[16,16,3072]{2,1,0:T(8,128)(2,1)} %get-tuple-element.72.order), calls=%async_computation.2 | async-start | bytes 3145728 | tf_op jit(solution)/shard_map/all_to_all | solution.py:15
  141.0 4.6 %shard_map.146 = (bf16[256,512]{1,0:T(8,128)(2,1)}, bf16[256,512]{1,0:T(8,128)(2,1)}) custom-call(bf16[256,3072]{1,0:T(8,128)(2,1)} %bitcast.90, bf16[3072,512]{1,0:T(8,128)(2,1)} %down.1, f32[256,512]{1,0:T(8,128)} %get-tuple-element.70.gate, f32[256,512]{1,0:T(8,128)} %get-tuple-element.71.up, bf16[16,16,3072]{2,1,0:T(8,128)(2,1)} %get-tuple-element.72.order), custom_call_target="tpu_custom_call" | custom-call | flops 805306368 | bytes 6815744 | tf_op jit(solution)/shard_map/pallas_call | solution.py:214
  146.5 2.1 fusion.30
  148.7 2.2 fusion
  150.9 6.3 %all-to-all-done.2.terms = bf16[16,16,3072]{2,1,0:T(8,128)(2,1)S(1)} async-done(((bf16[16,16,3072]{2,1,0:T(8,128)(2,1)}), bf16[16,16,3072]{2,1,0:T(8,128)(2,1)S(1)}, u32[]{:S(2)}, u32[]{:S(2)}) %all-to-all-start.2) | async-done | bytes 1572896 | tf_op jit(solution)/shard_map/all_to_all | solution.py:15
  158.7 3.7 %all-to-all-start.3 = ((bf16[16,16,3072]{2,1,0:T(8,128)(2,1)}), bf16[16,16,3072]{2,1,0:T(8,128)(2,1)S(1)}, u32[]{:S(2)}, u32[]{:S(2)}) async-start(bf16[16,16,3072]{2,1,0:T(8,128)(2,1)} %bitcast.38), calls=%async_computation.3 | async-start | bytes 3145728 | tf_op jit(solution)/shard_map/all_to_all | solution.py:15
  164.3 14.3 %all-to-all-done.3.terms = bf16[16,16,3072]{2,1,0:T(8,128)(2,1)S(1)} async-done(((bf16[16,16,3072]{2,1,0:T(8,128)(2,1)}), bf16[16,16,3072]{2,1,0:T(8,128)(2,1)S(1)}, u32[]{:S(2)}, u32[]{:S(2)}) %all-to-all-start.3) | async-done | bytes 1572896 | tf_op jit(solution)/shard_map/all_to_all | solution.py:15
  178.9 9.6 %all_to_all.30.piece = bf16[8,16,384]{2,1,0:T(8,128)(2,1)S(1)} all-to-all(bf16[8,16,384]{2,1,0:T(8,128)(2,1)S(1)} %shard_map.148), channel_id=1, replica_groups=mesh['dp'=8,'mp'=16] {'dp'}, dimensions={0} | all-to-all | bytes 196608 | tf_op jit(solution)/shard_map/all_to_all | solution.py:15
  189.8 3.7 %all-to-all-start.5 = ((bf16[16,8,16,384]{3,2,1,0:T(8,128)(2,1)}), bf16[16,8,16,384]{3,2,1,0:T(8,128)(2,1)S(1)}, u32[]{:S(2)}, u32[]{:S(2)}) async-start(bf16[16,8,16,384]{3,2,1,0:T(8,128)(2,1)} %shard_map.149), calls=%async_computation.5 | async-start | bytes 3145728 | tf_op jit(solution)/shard_map/all_to_all | solution.py:15
  205.5 3.3 %select_bitcast_fusion.3 = (bf16[8,1,3072]{2,0,1:T(8,128)(2,1)S(1)}, bf16[8,1,3072]{2,0,1:T(8,128)(2,1)S(1)}, bf16[8,1,3072]{2,0,1:T(8,128)(2,1)S(1)}, bf16[8,1,3072]{2,0,1:T(8,128)(2,1)S(1)}) fusion(bf16[8,32,3072]{2,1,0:T(8,128)(2,1)} %bitcast.99, s32[]{:T(128)S(6)} %select_n.193, s32[]{:T(128)S(6)} %select_n.195, pred[]{:T(512)} %get-tuple-element.84, ...), kind=kLoop, calls=%fused_computation.31 | loop fusion | flops 98304 | bytes 393252 | tf_op jit(solution)/shard_map/jit(_where)/select_n | solution.py:594
  209.6 7.9 %all-to-all-done.5 = bf16[16,8,16,384]{3,2,1,0:T(8,128)(2,1)S(1)} async-done(((bf16[16,8,16,384]{3,2,1,0:T(8,128)(2,1)}), bf16[16,8,16,384]{3,2,1,0:T(8,128)(2,1)S(1)}, u32[]{:S(2)}, u32[]{:S(2)}) %all-to-all-start.5) | async-done | bytes 1572896 | tf_op jit(solution)/shard_map/all_to_all | solution.py:15
  217.6 3.8 %fusion.7 = f32[512,384]{1,0:T(8,128)} fusion(bf16[16,8,16,384]{3,2,1,0:T(8,128)(2,1)S(1)} %all-to-all-done.5, bf16[8,16,16,512]{3,2,0,1:T(8,128)(2,1)} %all-gather.12.cloned.1.call-done), kind=kOutput, calls=%fused_computation.10 | convolution fusion | flops 805306368 | bytes 4456448 | tf_op jit(solution)/shard_map/dot_general | solution.py:577
  (96 shorter events, 26.4 us)
Async XLA Ops:
  7.2 39.0 %all-gather.10.cloned.1.call-start = ((), (), s32[]{:S(2)}) async-start(), calls=%async_computation.7 | async-start | bytes 1769472 | tf_op jit(solution)/shard_map/all_gather | solution.py:506
  8.9 70.1 %all-gather.8.cloned.1.call-start = ((), (), s32[]{:S(2)}) async-start(), calls=%async_computation.6 | async-start | bytes 1769472 | tf_op jit(solution)/shard_map/all_gather | solution.py:506
  10.0 11.0 %copy-start.9 = (bf16[1,8,4,3072]{3,2,1,0:T(4,128)(2,1)S(1)}, bf16[1,8,4,3072]{3,2,1,0:T(4,128)(2,1)}, u32[]{:S(2)}) copy-start(bf16[1,8,4,3072]{3,2,1,0:T(4,128)(2,1)} %param.23) | copy-start | bytes 589828
  10.0 11.8 %copy-start.11 = (s32[16]{0:T(128)S(1)}, s32[16]{0:T(128)}, u32[]{:S(2)}) copy-start(s32[16]{0:T(128)} %param.21) | copy-start | bytes 196
  10.0 20.5 %copy-start.1 = (bf16[256,512]{1,0:T(8,128)(2,1)S(1)}, bf16[256,512]{1,0:T(8,128)(2,1)}, u32[]{:S(2)}) copy-start(bf16[256,512]{1,0:T(8,128)(2,1)} %left.3) | copy-start | bytes 786436
  13.6 24.2 %collective-permute-start = (bf16[4,64,512]{2,1,0:T(8,128)(2,1)S(1)}, bf16[4,64,512]{2,1,0:T(8,128)(2,1)S(1)}, u32[]{:S(2)}, u32[]{:S(2)}) collective-permute-start(bf16[4,64,512]{2,1,0:T(8,128)(2,1)S(1)} %get-tuple-element.49), channel_id=1, source_target_pairs={{0,4},{1,5},{2,6},{3,7},{4,8},{5,9},{6,10},{7,11},{8,12},{9,13},{1... | collective-permute-start | bytes 786440 | tf_op jit(solution)/shard_map/ppermute | solution.py:38
  15.3 22.5 %collective-permute-start.1 = (bf16[4,64,512]{2,1,0:T(8,128)(2,1)S(1)}, bf16[4,64,512]{2,1,0:T(8,128)(2,1)S(1)}, u32[]{:S(2)}, u32[]{:S(2)}) collective-permute-start(bf16[4,64,512]{2,1,0:T(8,128)(2,1)S(1)} %get-tuple-element.50), channel_id=1, source_target_pairs={{0,12},{1,13},{2,14},{3,15},{4,0},{5,1},{6,2},{7,3},{8,4},{9,5},{1... | collective-permute-start | bytes 786440 | tf_op jit(solution)/shard_map/ppermute | solution.py:38
  16.9 21.0 %collective-permute-start.2 = (bf16[4,64,512]{2,1,0:T(8,128)(2,1)S(1)}, bf16[4,64,512]{2,1,0:T(8,128)(2,1)S(1)}, u32[]{:S(2)}, u32[]{:S(2)}) collective-permute-start(bf16[4,64,512]{2,1,0:T(8,128)(2,1)S(1)} %get-tuple-element.53), channel_id=1, source_target_pairs={{0,1},{1,2},{2,3},{3,0},{4,5},{5,6},{6,7},{7,4},{8,9},{9,10},{10,1... | collective-permute-start | bytes 786440 | tf_op jit(solution)/shard_map/ppermute | solution.py:38
  18.9 19.0 %collective-permute-start.3 = (bf16[4,64,512]{2,1,0:T(8,128)(2,1)S(1)}, bf16[4,64,512]{2,1,0:T(8,128)(2,1)S(1)}, u32[]{:S(2)}, u32[]{:S(2)}) collective-permute-start(bf16[4,64,512]{2,1,0:T(8,128)(2,1)S(1)} %get-tuple-element.54), channel_id=1, source_target_pairs={{0,3},{1,0},{2,1},{3,2},{4,7},{5,4},{6,5},{7,6},{8,11},{9,8},{10,9... | collective-permute-start | bytes 786440 | tf_op jit(solution)/shard_map/ppermute | solution.py:38
  39.7 14.4 %collective-permute-start.4 = (bf16[4,128,512]{2,1,0:T(8,128)(2,1)}, bf16[4,128,512]{2,1,0:T(8,128)(2,1)S(1)}, u32[]{:S(2)}, u32[]{:S(2)}) collective-permute-start(bf16[4,128,512]{2,1,0:T(8,128)(2,1)} %get-tuple-element.55), channel_id=1, source_target_pairs={{0,4},{1,5},{2,6},{3,7},{4,8},{5,9},{6,10},{7,11},{8,12},{9,13},{1... | collective-permute-start | bytes 1572872 | tf_op jit(solution)/shard_map/ppermute | solution.py:38
  40.1 14.0 %collective-permute-start.5 = (bf16[4,128,512]{2,1,0:T(8,128)(2,1)}, bf16[4,128,512]{2,1,0:T(8,128)(2,1)S(1)}, u32[]{:S(2)}, u32[]{:S(2)}) collective-permute-start(bf16[4,128,512]{2,1,0:T(8,128)(2,1)} %get-tuple-element.56), channel_id=1, source_target_pairs={{0,12},{1,13},{2,14},{3,15},{4,0},{5,1},{6,2},{7,3},{8,4},{9,5},{1... | collective-permute-start | bytes 1572872 | tf_op jit(solution)/shard_map/ppermute | solution.py:38
  43.0 13.8 %collective-permute-start.6 = (bf16[4,128,512]{2,1,0:T(8,128)(2,1)}, bf16[4,128,512]{2,1,0:T(8,128)(2,1)S(1)}, u32[]{:S(2)}, u32[]{:S(2)}) collective-permute-start(bf16[4,128,512]{2,1,0:T(8,128)(2,1)} %get-tuple-element.58), channel_id=1, source_target_pairs={{0,1},{1,2},{2,3},{3,0},{4,5},{5,6},{6,7},{7,4},{8,9},{9,10},{10,1... | collective-permute-start | bytes 1572872 | tf_op jit(solution)/shard_map/ppermute | solution.py:38
  43.0 13.8 %collective-permute-start.7 = (bf16[4,128,512]{2,1,0:T(8,128)(2,1)}, bf16[4,128,512]{2,1,0:T(8,128)(2,1)S(1)}, u32[]{:S(2)}, u32[]{:S(2)}) collective-permute-start(bf16[4,128,512]{2,1,0:T(8,128)(2,1)} %get-tuple-element.59), channel_id=1, source_target_pairs={{0,3},{1,0},{2,1},{3,2},{4,7},{5,4},{6,5},{7,6},{8,11},{9,8},{10,9... | collective-permute-start | bytes 1572872 | tf_op jit(solution)/shard_map/ppermute | solution.py:38
  56.8 14.2 %copy-start.12 = (bf16[512,3072]{1,0:T(8,128)(2,1)S(1)}, bf16[512,3072]{1,0:T(8,128)(2,1)}, u32[]{:S(2)}) copy-start(bf16[512,3072]{1,0:T(8,128)(2,1)} %param.19) | copy-start | bytes 9437188
  57.7 13.1 %copy-start.7 = (bf16[256,512]{1,0:T(8,128)(2,1)S(1)}, bf16[256,512]{1,0:T(8,128)(2,1)}, u32[]{:S(2)}) copy-start(bf16[256,512]{1,0:T(8,128)(2,1)} %param.17) | copy-start | bytes 786436
  57.7 13.1 %copy-start.10 = (f32[512]{0:T(512)S(1)}, f32[512]{0:T(512)}, u32[]{:S(2)}) copy-start(f32[512]{0:T(512)} %param.18) | copy-start | bytes 6148
  57.7 6.7 %collective-permute-start.8 = (bf16[128,512]{1,0:T(8,128)(2,1)S(1)}, bf16[128,512]{1,0:T(8,128)(2,1)S(1)}, u32[]{:S(2)}, u32[]{:S(2)}) collective-permute-start(bf16[128,512]{1,0:T(8,128)(2,1)S(1)} %get-tuple-element.61), channel_id=1, source_target_pairs={{0,1},{1,2},{2,3},{3,0},{4,5},{5,6},{6,7},{7,4},{8,9},{9,10},{10,1... | collective-permute-start | bytes 393224 | tf_op jit(solution)/shard_map/ppermute | solution.py:38
  57.8 8.7 %collective-permute-start.9 = (bf16[128,512]{1,0:T(8,128)(2,1)S(1)}, bf16[128,512]{1,0:T(8,128)(2,1)S(1)}, u32[]{:S(2)}, u32[]{:S(2)}) collective-permute-start(bf16[128,512]{1,0:T(8,128)(2,1)S(1)} %get-tuple-element.62), channel_id=1, source_target_pairs={{0,2},{1,3},{2,0},{3,1},{4,6},{5,7},{6,4},{7,5},{8,10},{9,11},{10,... | collective-permute-start | bytes 393224 | tf_op jit(solution)/shard_map/ppermute | solution.py:38
  62.2 5.0 %collective-permute-start.10 = (bf16[128,512]{1,0:T(8,128)(2,1)S(1)}, bf16[128,512]{1,0:T(8,128)(2,1)S(1)}, u32[]{:S(2)}, u32[]{:S(2)}) collective-permute-start(bf16[128,512]{1,0:T(8,128)(2,1)S(1)} %get-tuple-element.63), channel_id=1, source_target_pairs={{0,3},{1,0},{2,1},{3,2},{4,7},{5,4},{6,5},{7,6},{8,11},{9,8},{10,9... | collective-permute-start | bytes 393224 | tf_op jit(solution)/shard_map/ppermute | solution.py:38
  62.2 7.6 %collective-permute-start.11 = (bf16[128,512]{1,0:T(8,128)(2,1)S(1)}, bf16[128,512]{1,0:T(8,128)(2,1)S(1)}, u32[]{:S(2)}, u32[]{:S(2)}) collective-permute-start(bf16[128,512]{1,0:T(8,128)(2,1)S(1)} %get-tuple-element.65), channel_id=1, source_target_pairs={{0,4},{1,5},{2,6},{3,7},{4,8},{5,9},{6,10},{7,11},{8,12},{9,13},{1... | collective-permute-start | bytes 393224 | tf_op jit(solution)/shard_map/ppermute | solution.py:38
  62.2 7.6 %collective-permute-start.12 = (bf16[128,512]{1,0:T(8,128)(2,1)S(1)}, bf16[128,512]{1,0:T(8,128)(2,1)S(1)}, u32[]{:S(2)}, u32[]{:S(2)}) collective-permute-start(bf16[128,512]{1,0:T(8,128)(2,1)S(1)} %get-tuple-element.66), channel_id=1, source_target_pairs={{0,8},{1,9},{2,10},{3,11},{4,12},{5,13},{6,14},{7,15},{8,0},{9,1},... | collective-permute-start | bytes 393224 | tf_op jit(solution)/shard_map/ppermute | solution.py:38
  64.5 6.2 %collective-permute-start.13 = (bf16[128,512]{1,0:T(8,128)(2,1)S(1)}, bf16[128,512]{1,0:T(8,128)(2,1)S(1)}, u32[]{:S(2)}, u32[]{:S(2)}) collective-permute-start(bf16[128,512]{1,0:T(8,128)(2,1)S(1)} %get-tuple-element.67), channel_id=1, source_target_pairs={{0,12},{1,13},{2,14},{3,15},{4,0},{5,1},{6,2},{7,3},{8,4},{9,5},{1... | collective-permute-start | bytes 393224 | tf_op jit(solution)/shard_map/ppermute | solution.py:38
  73.5 25.7 %copy-start.3 = (s32[256]{0:T(256)S(1)}, s32[256]{0:T(256)}, u32[]{:S(2)}) copy-start(s32[256]{0:T(256)} %param.20) | copy-start | bytes 3076
  73.5 25.7 %all-to-all-start = ((bf16[16,144,384]{2,1,0:T(8,128)(2,1)}), bf16[16,144,384]{2,1,0:T(8,128)(2,1)S(1)}, u32[]{:S(2)}, u32[]{:S(2)}) async-start(bf16[16,144,384]{2,1,0:T(8,128)(2,1)} %bitcast.21), calls=%async_computation | async-start | bytes 3538944 | tf_op jit(solution)/shard_map/all_to_all | solution.py:15
  78.9 62.0 %all-gather.14.cloned.1.call-start = ((), (), s32[]{:S(2)}) async-start(), calls=%async_computation.9 | async-start | bytes 1671168 | tf_op jit(solution)/shard_map/all_gather | solution.py:516
  101.5 22.5 %all-to-all-start.1 = ((bf16[16,128,384]{2,1,0:T(8,128)(2,1)}), bf16[16,128,384]{2,1,0:T(8,128)(2,1)S(1)}, u32[]{:S(2)}, u32[]{:S(2)}) async-start(bf16[16,128,384]{2,1,0:T(8,128)(2,1)} %get-tuple-element.68), calls=%async_computation.1 | async-start | bytes 3145728 | tf_op jit(solution)/shard_map/all_to_all | solution.py:15
  134.7 22.5 %all-to-all-start.2 = ((bf16[16,16,3072]{2,1,0:T(8,128)(2,1)}), bf16[16,16,3072]{2,1,0:T(8,128)(2,1)S(1)}, u32[]{:S(2)}, u32[]{:S(2)}) async-start(bf16[16,16,3072]{2,1,0:T(8,128)(2,1)} %get-tuple-element.72.order), calls=%async_computation.2 | async-start | bytes 3145728 | tf_op jit(solution)/shard_map/all_to_all | solution.py:15
  140.9 64.6 %all-gather.16.cloned.1.call-start = ((), (), s32[]{:S(2)}) async-start(), calls=%async_computation.10 | async-start | bytes 1769472 | tf_op jit(solution)/shard_map/all_gather | solution.py:584
  158.1 51.5 %all-gather.12.cloned.1.call-start = ((), (), s32[]{:S(2)}) async-start(), calls=%async_computation.8 | async-start | bytes 2359296 | tf_op jit(solution)/shard_map/all_gather | solution.py:550
  158.7 19.8 %copy-start.2 = (f32[3072]{0:T(1024)S(1)}, f32[3072]{0:T(1024)}, u32[]{:S(2)}) copy-start(f32[3072]{0:T(1024)} %param.24) | copy-start | bytes 36868
  158.7 19.8 %all-to-all-start.3 = ((bf16[16,16,3072]{2,1,0:T(8,128)(2,1)}), bf16[16,16,3072]{2,1,0:T(8,128)(2,1)S(1)}, u32[]{:S(2)}, u32[]{:S(2)}) async-start(bf16[16,16,3072]{2,1,0:T(8,128)(2,1)} %bitcast.38), calls=%async_computation.3 | async-start | bytes 3145728 | tf_op jit(solution)/shard_map/all_to_all | solution.py:15
  189.8 27.8 %all-to-all-start.5 = ((bf16[16,8,16,384]{3,2,1,0:T(8,128)(2,1)}), bf16[16,8,16,384]{3,2,1,0:T(8,128)(2,1)S(1)}, u32[]{:S(2)}, u32[]{:S(2)}) async-start(bf16[16,8,16,384]{3,2,1,0:T(8,128)(2,1)} %shard_map.149), calls=%async_computation.5 | async-start | bytes 3145728 | tf_op jit(solution)/shard_map/all_to_all | solution.py:15
  (5 other events, 12.0 us)
Sparse Core Ops, SparseCore 0:
  10.3 26.9 all-gather.9
  38.9 24.6 all-gather.7
  82.5 50.8 all-gather.13
  158.2 21.8 all-gather.15
  181.6 25.1 all-gather.11

commit v8 on v7

--- a/solution.py
+++ b/solution.py
@@ -13,6 +13,10 @@
 
 def exchange(pieces, axis):
     return lax.all_to_all(pieces, axis, split_axis=0, concat_axis=0, tiled=True)
+
+
+def take(array, starts, sizes):
+    return lax.dynamic_slice(array, starts, sizes, allow_negative_indices=False)
 
 
 def three_parts(value):
@@ -337,7 +341,8 @@
 
 
 def forward_kernel(
-    pieces, gain, order, gate_hbm, up_hbm, down_hbm, state, gate, up, out, normed, act, held, sems
+    place, pieces, gain, order, gate_hbm, up_hbm, down_hbm,
+    home_state, here_state, gate, up, out_hbm, normed, act, held, out, sems, out_sems,
 ):
     del order
     parts = 3
@@ -353,18 +358,29 @@
         load(0, gate_hbm, third).start()
         load(1, up_hbm, third).start()
     cols = pieces.shape[2]
-    groups = state.shape[1] // cols
-    for block in range(state.shape[0] // BLK):
+    width = normed.shape[1]
+    groups = width // cols
+    mine = here_state.shape[0]
+    mp = place[0]
+    rows = pl.multiple_of(lax.rem(mp, groups) * mine, mine)
+    pair = pl.multiple_of((mp // 2) * mine, mine)
+    for group in range(groups):
+        at = pl.ds(group * cols, cols)
+        here_state[:, at] = pieces[(mp // groups) * groups + group, pl.ds(rows, mine), :]
+        halves = []
+        for block in range(2):
+            two = pieces[block * groups + group, pl.ds(pair, mine), :].astype(full)
+            halves.append(jnp.where(lax.rem(mp, 2) == 0, two[: mine // 2], two[mine // 2 :]))
+        home_state[:, at] = jnp.concatenate(halves, axis=0).astype(half)
+    for block in range(normed.shape[0] // BLK):
         rows = pl.ds(block * BLK, BLK)
         squares = jnp.zeros((BLK, 128), full)
         for group in range(groups):
-            value = pieces[block * groups + group]
-            state[rows, pl.ds(group * cols, cols)] = value
-            wide = value.astype(full)
+            wide = pieces[block * groups + group].astype(full)
             wide = wide * wide
             for lane in range(0, cols, 128):
                 squares = squares + wide[:, lane : lane + 128]
-        mean = jnp.sum(squares, axis=1, keepdims=True) / state.shape[1]
+        mean = jnp.sum(squares, axis=1, keepdims=True) / width
         inverse = lax.rsqrt(mean + epsilon)
         for group in range(groups):
             at = pl.ds(group * cols, cols)
@@ -391,7 +407,11 @@
     rows = out.shape[1] // 2
     wide_chunk = 512
 
-    @pl.loop(0, state.shape[1] // wide_chunk)
+    def leave(index):
+        at = pl.ds(pl.multiple_of(index * wide_chunk, wide_chunk), wide_chunk)
+        return pltpu.make_async_copy(out.at[:, :, at], out_hbm.at[:, :, at], out_sems.at[index])
+
+    @pl.loop(0, width // wide_chunk)
     def _(index):
         at = pl.ds(pl.multiple_of(index * wide_chunk, wide_chunk), wide_chunk)
         value = times_rows(act[...], down_w[at, :])
@@ -399,29 +419,38 @@
             first = value[to * rows : to * rows + rows]
             second = value[BLK + to * rows : BLK + to * rows + rows]
             out[to, :, at] = jnp.concatenate([first, second], axis=0).astype(half)
-
-
-def forward(pieces, gain, gate_w, up_w, down_w, order):
+        leave(index).start()
+
+    for index in range(width // wide_chunk):
+        leave(index).wait()
+
+
+def forward(pieces, gain, gate_w, up_w, down_w, mp, order):
     width, hidden = gate_w.shape
     n_mp = pieces.shape[0]
     rows = 2 * BLK
+    mine = rows // n_mp
     whole = pl.BlockSpec(memory_space=pltpu.VMEM)
+    far = pl.BlockSpec(memory_space=pltpu.HBM)
     return pl.pallas_call(
         forward_kernel,
-        in_specs=[whole, whole, pl.BlockSpec(memory_space=pl.ANY)]
-        + [pl.BlockSpec(memory_space=pltpu.HBM)] * 3,
-        out_specs=[whole] * 4,
+        in_specs=[pl.BlockSpec(memory_space=pltpu.SMEM), whole, whole]
+        + [pl.BlockSpec(memory_space=pl.ANY), far, far, far],
+        out_specs=[whole] * 4 + [far],
         out_shape=[
-            jax.ShapeDtypeStruct((rows, width), half),
+            jax.ShapeDtypeStruct((mine, width), half),
+            jax.ShapeDtypeStruct((mine, width), half),
             jax.ShapeDtypeStruct((rows, hidden), full),
             jax.ShapeDtypeStruct((rows, hidden), full),
-            jax.ShapeDtypeStruct((n_mp, rows // n_mp, width), half),
+            jax.ShapeDtypeStruct((n_mp, mine, width), half),
         ],
         scratch_shapes=[
             pltpu.VMEM((rows, width), half),
             pltpu.VMEM((rows, hidden), half),
             pltpu.VMEM((3, width, hidden), half),
+            pltpu.VMEM((n_mp, mine, width), half),
             pltpu.SemaphoreType.DMA((9,)),
+            pltpu.SemaphoreType.DMA((width // 512,)),
         ],
         compiler_params=pltpu.CompilerParams(vmem_limit_bytes=56 * 1024 * 1024),
         cost_estimate=pl.CostEstimate(
@@ -429,7 +458,7 @@
             bytes_accessed=6 * width * hidden + 10 * rows * width,
             transcendentals=rows * hidden,
         ),
-    )(pieces, gain[None], order, gate_w, up_w, down_w)
+    )(mp[None].astype(jnp.int32), pieces, gain[None], order, gate_w, up_w, down_w)
 
 
 def slope_kernel(terms, dy, state, gain, order, out):
@@ -495,7 +524,7 @@
 
     ids = jnp.arange(block_owner.shape[0], dtype=jnp.int32)
     my_ids = dp * blocks + jnp.arange(blocks, dtype=jnp.int32)
-    my_owner = lax.dynamic_slice_in_dim(block_owner, dp * blocks, blocks)
+    my_owner = take(block_owner, (dp * blocks,), (blocks,))
     my_slot = jnp.sum(
         (block_owner[None, :] == my_owner[:, None]) & (ids[None, :] < my_ids[:, None]),
         axis=1,
@@ -507,7 +536,7 @@
         picked = []
         for k in range(blocks):
             at = (my_owner[k], 0, my_slot[k], 0)
-            piece = lax.dynamic_slice(everyone, at, (1, rows, 1, student_width))
+            piece = take(everyone, at, (1, rows, 1, student_width))
             picked.append(piece.reshape(rows, student_width))
         return jnp.stack(picked)
 
@@ -550,25 +579,21 @@
     pooled_all = lax.all_gather(pooled.reshape(n_mp, mine_rows, width_here), "dp", axis=0, tiled=False)
     pooled_all = jnp.swapaxes(pooled_all, 0, 1).reshape(n_dp * tokens, width_here)
 
-    state, gate, up, output = forward(
-        states, student_gain, gate_weight, up_weight, down_weight, pooled
+    home_state, here_state, gate, up, output = forward(
+        states, student_gain, gate_weight, up_weight, down_weight, mp, pooled
     )
     grad_gate, grad_up = backward(dy.reshape(tokens, student_width), down_weight, gate, up, output)
     dn = (times_rows(grad_gate, gate_weight) + times_rows(grad_up, up_weight)).astype(half)
     output = exchange(output, "mp")
     dn, output = lax.optimization_barrier((dn, output))
     dn = exchange(dn.reshape(n_mp, mine_rows, student_width), "mp")
-    here = mp * mine_rows
-    state_rows = lax.dynamic_slice_in_dim(
-        state.reshape(blocks, BLK, student_width), mp * rows, rows, 1
-    )
-    out_rows = home(output, state_rows.reshape(mine_rows, student_width))
+    out_rows = home(output, home_state)
     dproj = slope(
         dn,
-        lax.dynamic_slice(
+        take(
             dy, ((mp % groups) * blocks, mp // groups, 0, 0), (blocks, 1, rows, student_width)
         ).reshape(mine_rows, student_width),
-        lax.dynamic_slice_in_dim(state, here, mine_rows, 0),
+        here_state,
         student_gain,
         n_dp,
         out_rows,
@@ -590,7 +615,7 @@
         chosen = mine & (ranks == slot)
         index = jnp.sum(jnp.where(chosen, ids, 0))
         at = (index // blocks, (index % blocks) * rows, 0)
-        piece = lax.dynamic_slice(back, at, (1, rows, student_width))[0]
+        piece = take(back, at, (1, rows, student_width))[0]
         picks.append(jnp.where(jnp.any(chosen), piece, jnp.zeros((), half)))
     student_out = jnp.stack(picks, axis=1)
     return (student_out[None], adapter_grad)

time: 229 us -> 236 us (1.031)
  waiting for transfers between devices: 79.1 us -> 88.7 us
  between operations: 31.7 us -> 24.3 us
  local copies, waits for them, and re-layouts: 11.1 us -> 14.3 us
  Pallas kernels: 32.6 us -> 35.1 us
    all_to_all x5, waiting for transfers between devices: 63.3 us -> 75.6 us  [exchange(): return lax.all_to_all(pieces, axis, split_axis=0, concat_axis=0, tiled=True)]
    ppermute x14, waiting for transfers between devices: 15.1 us -> 12.5 us  [step(): return lax.ppermute(value, 'mp', pairs)]
    another operation x1, local copies, waits for them, and re-layouts: 0.84 us -> 3.33 us  [fetch(): return jnp.stack(picked)]
    unnamed x29 -> x33, local copies, waits for them, and re-layouts: 5.45 us -> 5.43 us
  transfers between devices with their start and end apart: 24 -> 24, of which waited for: 12 -> 11; matrix products, arithmetic and copies ran while one was open for 9% -> 11% of each run, Pallas kernels for 14% -> 15%
where the time goes in v8:
time: 236 us; the launch traced here: 235 us
  waiting for transfers between devices  88.7 us (38%)
  starting transfers between devices  46 us (19%)
  Pallas kernels  35.1 us (15%)
  between operations  24.3 us (10%)
  local copies, waits for them, and re-layouts  14.3 us (6%)
  matrix products  9.98 us (4%)
  blocking collectives  8.18 us (3%)
  other arithmetic  8.12 us (3%)
    all_to_all x5, waiting for transfers between devices, exchange(): return lax.all_to_all(pieces, axis, split_axis=0, concat_axis=0, tiled=True)  75.6 us
    all_to_all x5, starting transfers between devices, exchange(): return lax.all_to_all(pieces, axis, split_axis=0, concat_axis=0, tiled=True)  24.2 us
    ppermute x14, starting transfers between devices, step(): return lax.ppermute(value, 'mp', pairs)  21.7 us
    ppermute x14, waiting for transfers between devices, step(): return lax.ppermute(value, 'mp', pairs)  12.5 us
    pallas_call x2, Pallas kernels, terms(): pl.pallas_call(kernel, in_specs=[scalars, whole, pl.BlockSpec(memory_spac...  11.6 us
    pallas_call x1, Pallas kernels, forward(): pl.pallas_call(forward_kernel, in_specs=[pl.BlockSpec(memory_space=pltpu....  9.61 us
    all_to_all x1, blocking collectives, exchange(): return lax.all_to_all(pieces, axis, split_axis=0, concat_axis=0, tiled=True)  8.18 us
    unnamed x33, local copies, waits for them, and re-layouts  5.43 us
  transfers between devices with their start and end apart: 24, of which 11 were waited for; matrix products, arithmetic and copies ran while one was open for 11% of the time, Pallas kernels for 15%

profile of v8, /device:TPU:0, one launch (start us, length us, event | category | flops | bytes accessed | tf_op | source)
XLA Modules:
  0.0 234.8 jit_solution(17935359180873882503)
XLA Ops:
  10.0 4.3 %shard_map.141 = (bf16[4,64,512]{2,1,0:T(8,128)(2,1)}, bf16[4,64,512]{2,1,0:T(8,128)(2,1)}, bf16[4,64,512]{2,1,0:T(8,128)(2,1)}, bf16[4,64,512]{2,1,0:T(8,128)(2,1)}) custom-call(s32[2]{0:T(128)S(1)} %pad_add_fusion.1.place, bf16[256,512]{1,0:T(8,128)(2,1)S(1)} %copy-done, bf16[512,8192]{1,0:T(8,128)(2,1)} %right.3), custom_call_target="tpu_custom_call" | custom-call | flops 536870912 | bytes 4194304 | tf_op jit(solution)/shard_map/pallas_call | solution.py:135
  17.6 2.0 collective-permute-start.2
  19.6 2.1 collective-permute-start.3
  22.5 7.3 %shard_map.140 = (bf16[4,128,512]{2,1,0:T(8,128)(2,1)S(1)}, bf16[4,128,512]{2,1,0:T(8,128)(2,1)S(1)}, bf16[4,128,512]{2,1,0:T(8,128)(2,1)S(1)}, bf16[4,128,512]{...) custom-call(s32[2]{0:T(128)S(1)} %pad_add_fusion.1.place, ...), custom_call_target="tpu_custom_call" | custom-call | flops 2147483648 | bytes 8388608 | tf_op jit(solution)/shard_map/pallas_call | solution.py:135
  31.4 3.6 %shard_map.142 = (bf16[4,128,512]{2,1,0:T(8,128)(2,1)}, bf16[4,128,512]{2,1,0:T(8,128)(2,1)}, bf16[4,128,512]{2,1,0:T(8,128)(2,1)}, bf16[4,128,512]{2,1,0:T(8,128)(2,1)}) custom-call(bf16[4,128,512]{2,1,0:T(8,128)(2,1)S(1)} %get-tuple-element.48.refs_0_, bf16[4,128,512]{2,1,0:T(8,128)(2,1)S(1)} %get-tuple-element.49.refs_1_, ...), custom_call_target="tpu_custom_call" | custom-call | flops 1048576 | bytes 5242880 | tf_op jit(solution)/shard_map/pallas_call | solution.py:156
  35.3 2.9 %collective-permute-start.5 = (bf16[4,128,512]{2,1,0:T(8,128)(2,1)}, bf16[4,128,512]{2,1,0:T(8,128)(2,1)S(1)}, u32[]{:S(2)}, u32[]{:S(2)}) collective-permute-start(bf16[4,128,512]{2,1,0:T(8,128)(2,1)} %get-tuple-element.57), channel_id=1, source_target_pairs={{0,12},{1,13},{2,14},{3,15},{4,0},{5,1},{6,2},{7,3},{8,4},{9,5},{1... | collective-permute-start | bytes 1572872 | tf_op jit(solution)/shard_map/ppermute | solution.py:42
  38.2 3.2 %collective-permute-start.7 = (bf16[4,128,512]{2,1,0:T(8,128)(2,1)}, bf16[4,128,512]{2,1,0:T(8,128)(2,1)S(1)}, u32[]{:S(2)}, u32[]{:S(2)}) collective-permute-start(bf16[4,128,512]{2,1,0:T(8,128)(2,1)} %get-tuple-element.60), channel_id=1, source_target_pairs={{0,3},{1,0},{2,1},{3,2},{4,7},{5,4},{6,5},{7,6},{8,11},{9,8},{10,9... | collective-permute-start | bytes 1572872 | tf_op jit(solution)/shard_map/ppermute | solution.py:42
  41.4 3.3 %constant_dynamic-slice_fusion.1 = (bf16[1,8,1,3072]{3,1,2,0:T(8,128)(2,1)S(1)}, bf16[1,8,1,3072]{3,1,2,0:T(8,128)(2,1)S(1)}) fusion(bf16[8,8,4,3072]{3,1,2,0:T(8,128)(2,1)} %all-gather.10.cloned.1.call-done, s32[]{:T(128)} %bitcast, s32[]{:T(128)} %bitcast.1, s32[]{:T(128)} %bitcast.3, s32[]{:T(128)} %bitcast.4), kind=kLoop, calls=%fused_computation.48 | loop fusion | bytes 196624 | tf_op jit(solution)/shard_map/dynamic_slice | solution.py:19
  44.8 4.6 %collective-permute-done.4.refs_1_ = bf16[4,128,512]{2,1,0:T(8,128)(2,1)S(1)} collective-permute-done((bf16[4,128,512]{2,1,0:T(8,128)(2,1)}, bf16[4,128,512]{2,1,0:T(8,128)(2,1)S(1)}, u32[]{:S(2)}, u32[]{:S(2)}) %collective-permute-start.4) | collective-permute-done | bytes 524320 | tf_op jit(solution)/shard_map/ppermute | solution.py:42
  49.4 2.7 %collective-permute-done.6.refs_4_ = bf16[4,128,512]{2,1,0:T(8,128)(2,1)S(1)} collective-permute-done((bf16[4,128,512]{2,1,0:T(8,128)(2,1)}, bf16[4,128,512]{2,1,0:T(8,128)(2,1)S(1)}, u32[]{:S(2)}, u32[]{:S(2)}) %collective-permute-start.6) | collective-permute-done | bytes 524320 | tf_op jit(solution)/shard_map/ppermute | solution.py:42
  53.0 3.0 %collective-permute-start.10 = (bf16[128,512]{1,0:T(8,128)(2,1)S(1)}, bf16[128,512]{1,0:T(8,128)(2,1)S(1)}, u32[]{:S(2)}, u32[]{:S(2)}) collective-permute-start(bf16[128,512]{1,0:T(8,128)(2,1)S(1)} %get-tuple-element.64), channel_id=1, source_target_pairs={{0,3},{1,0},{2,1},{3,2},{4,7},{5,4},{6,5},{7,6},{8,11},{9,8},{10,9... | collective-permute-start | bytes 393224 | tf_op jit(solution)/shard_map/ppermute | solution.py:42
  57.5 1.9 collective-permute-start.12
  60.9 2.7 %collective-permute-done.8 = bf16[128,512]{1,0:T(8,128)(2,1)S(1)} collective-permute-done((bf16[128,512]{1,0:T(8,128)(2,1)S(1)}, bf16[128,512]{1,0:T(8,128)(2,1)S(1)}, u32[]{:S(2)}, u32[]{:S(2)}) %collective-permute-start.8) | collective-permute-done | bytes 131104 | tf_op jit(solution)/shard_map/ppermute | solution.py:42
  68.8 6.0 %all-to-all-start = ((bf16[16,144,384]{2,1,0:T(8,128)(2,1)}), bf16[16,144,384]{2,1,0:T(8,128)(2,1)S(1)}, u32[]{:S(2)}, u32[]{:S(2)}) async-start(bf16[16,144,384]{2,1,0:T(8,128)(2,1)} %bitcast.22), calls=%async_computation | async-start | bytes 3538944 | tf_op jit(solution)/shard_map/all_to_all | solution.py:15
  74.8 3.3 %dynamic-slice_bitcast_fusion.2 = (bf16[1,8,3072]{2,1,0:T(8,128)(2,1)S(1)}, bf16[1,8,3072]{2,1,0:T(8,128)(2,1)S(1)}) fusion(bf16[8,8,4,3072]{3,1,2,0:T(8,128)(2,1)} %all-gather.8.cloned.1.call-done, s32[]{:T(128)} %bitcast, s32[]{:T(128)} %bitcast.1, s32[]{:T(128)} %bitcast.3, s32[]{:T(128)} %bitcast.4), kind=kLoop, calls=%fused_computation.32 | loop fusion | bytes 196624 | tf_op jit(solution)/shard_map/stack;reshape | solution.py:541
  78.9 16.4 %all-to-all-done.message = bf16[16,144,384]{2,1,0:T(8,128)(2,1)S(1)} async-done(((bf16[16,144,384]{2,1,0:T(8,128)(2,1)}), bf16[16,144,384]{2,1,0:T(8,128)(2,1)S(1)}, u32[]{:S(2)}, u32[]{:S(2)}) %all-to-all-start) | async-done | bytes 1769504 | tf_op jit(solution)/shard_map/all_to_all | solution.py:15
  95.3 2.3 shard_map.144
  97.6 5.0 %all-to-all-start.1 = ((bf16[16,128,384]{2,1,0:T(8,128)(2,1)}), bf16[16,128,384]{2,1,0:T(8,128)(2,1)S(1)}, u32[]{:S(2)}, u32[]{:S(2)}) async-start(bf16[16,128,384]{2,1,0:T(8,128)(2,1)} %get-tuple-element.69), calls=%async_computation.1 | async-start | bytes 3145728 | tf_op jit(solution)/shard_map/all_to_all | solution.py:15
  103.8 18.9 %all-to-all-done.1.pieces = bf16[16,128,384]{2,1,0:T(8,128)(2,1)S(1)} async-done(((bf16[16,128,384]{2,1,0:T(8,128)(2,1)}), bf16[16,128,384]{2,1,0:T(8,128)(2,1)S(1)}, u32[]{:S(2)}, u32[]{:S(2)}) %all-to-all-start.1) | async-done | bytes 1572896 | tf_op jit(solution)/shard_map/all_to_all | solution.py:15
  123.9 9.6 %shard_map.145 = (bf16[16,3072]{1,0:T(8,128)(2,1)}, bf16[16,3072]{1,0:T(8,128)(2,1)}, f32[256,512]{1,0:T(8,128)}, f32[256,512]{1,0:T(8,128)}, bf16[16,16,3072]{2,1,0:T(8,128)(2,1)}) custom-call(s32[1]{0:T(128)} %bitcast.7.place, bf16[16,128,384]{2,1,0:T(8,128)(2,1)} %copy-done.8, f32[1,3072]{1,0:T(1,128)} %bitcast.82, bf16[2,128,512]{2,1,0:T(8,128)(2,1)} %fusion.10.order, ...), custom_call_target="tpu_custom_call" | custom-call | flops 2415919104 | bytes 17301504 | tf_op jit(solution)/shard_map/pallas_call | solution.py:435
  133.5 5.7 %all-to-all-start.2 = ((bf16[16,16,3072]{2,1,0:T(8,128)(2,1)}), bf16[16,16,3072]{2,1,0:T(8,128)(2,1)S(1)}, u32[]{:S(2)}, u32[]{:S(2)}) async-start(bf16[16,16,3072]{2,1,0:T(8,128)(2,1)} %get-tuple-element.73.order), calls=%async_computation.2 | async-start | bytes 3145728 | tf_op jit(solution)/shard_map/all_to_all | solution.py:15
  139.3 4.6 %shard_map.146 = (bf16[256,512]{1,0:T(8,128)(2,1)}, bf16[256,512]{1,0:T(8,128)(2,1)}) custom-call(bf16[256,3072]{1,0:T(8,128)(2,1)} %bitcast.88, bf16[3072,512]{1,0:T(8,128)(2,1)} %down.1, f32[256,512]{1,0:T(8,128)} %get-tuple-element.71.gate, f32[256,512]{1,0:T(8,128)} %get-tuple-element.72.up, bf16[16,16,3072]{2,1,0:T(8,128)(2,1)} %get-tuple-element.73.order), custom_call_target="tpu_custom_call" | custom-call | flops 805306368 | bytes 6815744 | tf_op jit(solution)/shard_map/pallas_call | solution.py:218
  143.9 2.1 fusion.30
  146.1 2.2 fusion
  148.3 11.5 %all-to-all-done.2.terms = bf16[16,16,3072]{2,1,0:T(8,128)(2,1)S(1)} async-done(((bf16[16,16,3072]{2,1,0:T(8,128)(2,1)}), bf16[16,16,3072]{2,1,0:T(8,128)(2,1)S(1)}, u32[]{:S(2)}, u32[]{:S(2)}) %all-to-all-start.2) | async-done | bytes 1572896 | tf_op jit(solution)/shard_map/all_to_all | solution.py:15
  161.3 3.7 %all-to-all-start.3 = ((bf16[16,16,3072]{2,1,0:T(8,128)(2,1)}), bf16[16,16,3072]{2,1,0:T(8,128)(2,1)S(1)}, u32[]{:S(2)}, u32[]{:S(2)}) async-start(bf16[16,16,3072]{2,1,0:T(8,128)(2,1)} %bitcast.37), calls=%async_computation.3 | async-start | bytes 3145728 | tf_op jit(solution)/shard_map/all_to_all | solution.py:15
  165.9 21.1 %all-to-all-done.3.terms = bf16[16,16,3072]{2,1,0:T(8,128)(2,1)S(1)} async-done(((bf16[16,16,3072]{2,1,0:T(8,128)(2,1)}), bf16[16,16,3072]{2,1,0:T(8,128)(2,1)S(1)}, u32[]{:S(2)}, u32[]{:S(2)}) %all-to-all-start.3) | async-done | bytes 1572896 | tf_op jit(solution)/shard_map/all_to_all | solution.py:15
  187.4 8.2 %all_to_all.30.piece = bf16[8,16,384]{2,1,0:T(8,128)(2,1)S(1)} all-to-all(bf16[8,16,384]{2,1,0:T(8,128)(2,1)S(1)} %shard_map.148), channel_id=1, replica_groups=mesh['dp'=8,'mp'=16] {'dp'}, dimensions={0} | all-to-all | bytes 196608 | tf_op jit(solution)/shard_map/all_to_all | solution.py:15
  196.8 3.7 %all-to-all-start.5 = ((bf16[16,8,16,384]{3,2,1,0:T(8,128)(2,1)}), bf16[16,8,16,384]{3,2,1,0:T(8,128)(2,1)S(1)}, u32[]{:S(2)}, u32[]{:S(2)}) async-start(bf16[16,8,16,384]{3,2,1,0:T(8,128)(2,1)} %shard_map.149), calls=%async_computation.5 | async-start | bytes 3145728 | tf_op jit(solution)/shard_map/all_to_all | solution.py:15
  212.4 3.4 %select_bitcast_fusion.3 = (bf16[8,1,3072]{2,0,1:T(8,128)(2,1)S(1)}, bf16[8,1,3072]{2,0,1:T(8,128)(2,1)S(1)}, bf16[8,1,3072]{2,0,1:T(8,128)(2,1)S(1)}, bf16[8,1,3072]{2,0,1:T(8,128)(2,1)S(1)}) fusion(bf16[8,32,3072]{2,1,0:T(8,128)(2,1)} %bitcast.97, s32[]{:T(128)S(6)} %select_n.131, s32[]{:T(128)S(6)} %mul.47, pred[]{:T(512)} %get-tuple-element.86, ...), kind=kLoop, calls=%fused_computation.30 | loop fusion | flops 98304 | bytes 393252 | tf_op jit(solution)/shard_map/jit(_where)/select_n | solution.py:619
  216.7 7.8 %all-to-all-done.5 = bf16[16,8,16,384]{3,2,1,0:T(8,128)(2,1)S(1)} async-done(((bf16[16,8,16,384]{3,2,1,0:T(8,128)(2,1)}), bf16[16,8,16,384]{3,2,1,0:T(8,128)(2,1)S(1)}, u32[]{:S(2)}, u32[]{:S(2)}) %all-to-all-start.5) | async-done | bytes 1572896 | tf_op jit(solution)/shard_map/all_to_all | solution.py:15
  224.5 3.8 %fusion.7 = f32[512,384]{1,0:T(8,128)} fusion(bf16[16,8,16,384]{3,2,1,0:T(8,128)(2,1)S(1)} %all-to-all-done.5, bf16[8,16,16,512]{3,2,0,1:T(8,128)(2,1)} %all-gather.12.cloned.1.call-done), kind=kOutput, calls=%fused_computation.10 | convolution fusion | flops 805306368 | bytes 4456448 | tf_op jit(solution)/shard_map/dot_general | solution.py:602
  (98 shorter events, 27.7 us)
Async XLA Ops:
  7.2 34.3 %all-gather.10.cloned.1.call-start = ((), (), s32[]{:S(2)}) async-start(), calls=%async_computation.7 | async-start | bytes 1769472 | tf_op jit(solution)/shard_map/all_gather | solution.py:535
  8.9 65.9 %all-gather.8.cloned.1.call-start = ((), (), s32[]{:S(2)}) async-start(), calls=%async_computation.6 | async-start | bytes 1769472 | tf_op jit(solution)/shard_map/all_gather | solution.py:535
  10.0 12.5 %copy-start.1 = (bf16[256,512]{1,0:T(8,128)(2,1)S(1)}, bf16[256,512]{1,0:T(8,128)(2,1)}, u32[]{:S(2)}) copy-start(bf16[256,512]{1,0:T(8,128)(2,1)} %left.3) | copy-start | bytes 786436
  14.3 17.0 %collective-permute-start = (bf16[4,64,512]{2,1,0:T(8,128)(2,1)}, bf16[4,64,512]{2,1,0:T(8,128)(2,1)}, u32[]{:S(2)}, u32[]{:S(2)}) collective-permute-start(bf16[4,64,512]{2,1,0:T(8,128)(2,1)} %get-tuple-element.50), channel_id=1, source_target_pairs={{0,4},{1,5},{2,6},{3,7},{4,8},{5,9},{6,10},{7,11},{8,12},{9,13},{1... | collective-permute-start | bytes 786440 | tf_op jit(solution)/shard_map/ppermute | solution.py:42
  16.1 15.3 %collective-permute-start.1 = (bf16[4,64,512]{2,1,0:T(8,128)(2,1)}, bf16[4,64,512]{2,1,0:T(8,128)(2,1)}, u32[]{:S(2)}, u32[]{:S(2)}) collective-permute-start(bf16[4,64,512]{2,1,0:T(8,128)(2,1)} %get-tuple-element.51), channel_id=1, source_target_pairs={{0,12},{1,13},{2,14},{3,15},{4,0},{5,1},{6,2},{7,3},{8,4},{9,5},{1... | collective-permute-start | bytes 786440 | tf_op jit(solution)/shard_map/ppermute | solution.py:42
  17.6 13.7 %collective-permute-start.2 = (bf16[4,64,512]{2,1,0:T(8,128)(2,1)}, bf16[4,64,512]{2,1,0:T(8,128)(2,1)}, u32[]{:S(2)}, u32[]{:S(2)}) collective-permute-start(bf16[4,64,512]{2,1,0:T(8,128)(2,1)} %get-tuple-element.54), channel_id=1, source_target_pairs={{0,1},{1,2},{2,3},{3,0},{4,5},{5,6},{6,7},{7,4},{8,9},{9,10},{10,1... | collective-permute-start | bytes 786440 | tf_op jit(solution)/shard_map/ppermute | solution.py:42
  19.6 11.7 %collective-permute-start.3 = (bf16[4,64,512]{2,1,0:T(8,128)(2,1)}, bf16[4,64,512]{2,1,0:T(8,128)(2,1)}, u32[]{:S(2)}, u32[]{:S(2)}) collective-permute-start(bf16[4,64,512]{2,1,0:T(8,128)(2,1)} %get-tuple-element.55), channel_id=1, source_target_pairs={{0,3},{1,0},{2,1},{3,2},{4,7},{5,4},{6,5},{7,6},{8,11},{9,8},{10,9... | collective-permute-start | bytes 786440 | tf_op jit(solution)/shard_map/ppermute | solution.py:42
  35.0 14.4 %collective-permute-start.4 = (bf16[4,128,512]{2,1,0:T(8,128)(2,1)}, bf16[4,128,512]{2,1,0:T(8,128)(2,1)S(1)}, u32[]{:S(2)}, u32[]{:S(2)}) collective-permute-start(bf16[4,128,512]{2,1,0:T(8,128)(2,1)} %get-tuple-element.56), channel_id=1, source_target_pairs={{0,4},{1,5},{2,6},{3,7},{4,8},{5,9},{6,10},{7,11},{8,12},{9,13},{1... | collective-permute-start | bytes 1572872 | tf_op jit(solution)/shard_map/ppermute | solution.py:42
  35.3 14.0 %collective-permute-start.5 = (bf16[4,128,512]{2,1,0:T(8,128)(2,1)}, bf16[4,128,512]{2,1,0:T(8,128)(2,1)S(1)}, u32[]{:S(2)}, u32[]{:S(2)}) collective-permute-start(bf16[4,128,512]{2,1,0:T(8,128)(2,1)} %get-tuple-element.57), channel_id=1, source_target_pairs={{0,12},{1,13},{2,14},{3,15},{4,0},{5,1},{6,2},{7,3},{8,4},{9,5},{1... | collective-permute-start | bytes 1572872 | tf_op jit(solution)/shard_map/ppermute | solution.py:42
  38.2 13.9 %collective-permute-start.6 = (bf16[4,128,512]{2,1,0:T(8,128)(2,1)}, bf16[4,128,512]{2,1,0:T(8,128)(2,1)S(1)}, u32[]{:S(2)}, u32[]{:S(2)}) collective-permute-start(bf16[4,128,512]{2,1,0:T(8,128)(2,1)} %get-tuple-element.59), channel_id=1, source_target_pairs={{0,1},{1,2},{2,3},{3,0},{4,5},{5,6},{6,7},{7,4},{8,9},{9,10},{10,1... | collective-permute-start | bytes 1572872 | tf_op jit(solution)/shard_map/ppermute | solution.py:42
  38.2 13.9 %collective-permute-start.7 = (bf16[4,128,512]{2,1,0:T(8,128)(2,1)}, bf16[4,128,512]{2,1,0:T(8,128)(2,1)S(1)}, u32[]{:S(2)}, u32[]{:S(2)}) collective-permute-start(bf16[4,128,512]{2,1,0:T(8,128)(2,1)} %get-tuple-element.60), channel_id=1, source_target_pairs={{0,3},{1,0},{2,1},{3,2},{4,7},{5,4},{6,5},{7,6},{8,11},{9,8},{10,9... | collective-permute-start | bytes 1572872 | tf_op jit(solution)/shard_map/ppermute | solution.py:42
  52.0 14.1 %copy-start.9 = (bf16[256,512]{1,0:T(8,128)(2,1)S(1)}, bf16[256,512]{1,0:T(8,128)(2,1)}, u32[]{:S(2)}) copy-start(bf16[256,512]{1,0:T(8,128)(2,1)} %param.17) | copy-start | bytes 786436
  52.0 14.1 %copy-start.12 = (f32[512]{0:T(512)S(1)}, f32[512]{0:T(512)}, u32[]{:S(2)}) copy-start(f32[512]{0:T(512)} %param.18) | copy-start | bytes 6148
  52.0 14.3 %copy-start.14 = (bf16[512,3072]{1,0:T(8,128)(2,1)S(1)}, bf16[512,3072]{1,0:T(8,128)(2,1)}, u32[]{:S(2)}) copy-start(bf16[512,3072]{1,0:T(8,128)(2,1)} %param.19) | copy-start | bytes 9437188
  53.0 6.6 %collective-permute-start.10 = (bf16[128,512]{1,0:T(8,128)(2,1)S(1)}, bf16[128,512]{1,0:T(8,128)(2,1)S(1)}, u32[]{:S(2)}, u32[]{:S(2)}) collective-permute-start(bf16[128,512]{1,0:T(8,128)(2,1)S(1)} %get-tuple-element.64), channel_id=1, source_target_pairs={{0,3},{1,0},{2,1},{3,2},{4,7},{5,4},{6,5},{7,6},{8,11},{9,8},{10,9... | collective-permute-start | bytes 393224 | tf_op jit(solution)/shard_map/ppermute | solution.py:42
  56.0 7.6 %collective-permute-start.8 = (bf16[128,512]{1,0:T(8,128)(2,1)S(1)}, bf16[128,512]{1,0:T(8,128)(2,1)S(1)}, u32[]{:S(2)}, u32[]{:S(2)}) collective-permute-start(bf16[128,512]{1,0:T(8,128)(2,1)S(1)} %get-tuple-element.62), channel_id=1, source_target_pairs={{0,1},{1,2},{2,3},{3,0},{4,5},{5,6},{6,7},{7,4},{8,9},{9,10},{10,1... | collective-permute-start | bytes 393224 | tf_op jit(solution)/shard_map/ppermute | solution.py:42
  56.0 7.6 %collective-permute-start.9 = (bf16[128,512]{1,0:T(8,128)(2,1)S(1)}, bf16[128,512]{1,0:T(8,128)(2,1)S(1)}, u32[]{:S(2)}, u32[]{:S(2)}) collective-permute-start(bf16[128,512]{1,0:T(8,128)(2,1)S(1)} %get-tuple-element.63), channel_id=1, source_target_pairs={{0,2},{1,3},{2,0},{3,1},{4,6},{5,7},{6,4},{7,5},{8,10},{9,11},{10,... | collective-permute-start | bytes 393224 | tf_op jit(solution)/shard_map/ppermute | solution.py:42
  57.5 7.6 %collective-permute-start.11 = (bf16[128,512]{1,0:T(8,128)(2,1)S(1)}, bf16[128,512]{1,0:T(8,128)(2,1)S(1)}, u32[]{:S(2)}, u32[]{:S(2)}) collective-permute-start(bf16[128,512]{1,0:T(8,128)(2,1)S(1)} %get-tuple-element.66), channel_id=1, source_target_pairs={{0,4},{1,5},{2,6},{3,7},{4,8},{5,9},{6,10},{7,11},{8,12},{9,13},{1... | collective-permute-start | bytes 393224 | tf_op jit(solution)/shard_map/ppermute | solution.py:42
  57.5 7.6 %collective-permute-start.12 = (bf16[128,512]{1,0:T(8,128)(2,1)S(1)}, bf16[128,512]{1,0:T(8,128)(2,1)S(1)}, u32[]{:S(2)}, u32[]{:S(2)}) collective-permute-start(bf16[128,512]{1,0:T(8,128)(2,1)S(1)} %get-tuple-element.67), channel_id=1, source_target_pairs={{0,8},{1,9},{2,10},{3,11},{4,12},{5,13},{6,14},{7,15},{8,0},{9,1},... | collective-permute-start | bytes 393224 | tf_op jit(solution)/shard_map/ppermute | solution.py:42
  59.6 6.4 %collective-permute-start.13 = (bf16[128,512]{1,0:T(8,128)(2,1)S(1)}, bf16[128,512]{1,0:T(8,128)(2,1)S(1)}, u32[]{:S(2)}, u32[]{:S(2)}) collective-permute-start(bf16[128,512]{1,0:T(8,128)(2,1)S(1)} %get-tuple-element.68), channel_id=1, source_target_pairs={{0,12},{1,13},{2,14},{3,15},{4,0},{5,1},{6,2},{7,3},{8,4},{9,5},{1... | collective-permute-start | bytes 393224 | tf_op jit(solution)/shard_map/ppermute | solution.py:42
  68.8 26.5 %copy-start.5 = (s32[256]{0:T(256)S(1)}, s32[256]{0:T(256)}, u32[]{:S(2)}) copy-start(s32[256]{0:T(256)} %param.20) | copy-start | bytes 3076
  68.8 26.5 %all-to-all-start = ((bf16[16,144,384]{2,1,0:T(8,128)(2,1)}), bf16[16,144,384]{2,1,0:T(8,128)(2,1)S(1)}, u32[]{:S(2)}, u32[]{:S(2)}) async-start(bf16[16,144,384]{2,1,0:T(8,128)(2,1)} %bitcast.22), calls=%async_computation | async-start | bytes 3538944 | tf_op jit(solution)/shard_map/all_to_all | solution.py:15
  74.7 64.5 %all-gather.14.cloned.1.call-start = ((), (), s32[]{:S(2)}) async-start(), calls=%async_computation.9 | async-start | bytes 1671168 | tf_op jit(solution)/shard_map/all_gather | solution.py:545
  97.6 25.1 %all-to-all-start.1 = ((bf16[16,128,384]{2,1,0:T(8,128)(2,1)}), bf16[16,128,384]{2,1,0:T(8,128)(2,1)S(1)}, u32[]{:S(2)}, u32[]{:S(2)}) async-start(bf16[16,128,384]{2,1,0:T(8,128)(2,1)} %get-tuple-element.69), calls=%async_computation.1 | async-start | bytes 3145728 | tf_op jit(solution)/shard_map/all_to_all | solution.py:15
  133.5 26.3 %all-to-all-start.2 = ((bf16[16,16,3072]{2,1,0:T(8,128)(2,1)}), bf16[16,16,3072]{2,1,0:T(8,128)(2,1)S(1)}, u32[]{:S(2)}, u32[]{:S(2)}) async-start(bf16[16,16,3072]{2,1,0:T(8,128)(2,1)} %get-tuple-element.73.order), calls=%async_computation.2 | async-start | bytes 3145728 | tf_op jit(solution)/shard_map/all_to_all | solution.py:15
  139.2 73.2 %all-gather.16.cloned.1.call-start = ((), (), s32[]{:S(2)}) async-start(), calls=%async_computation.10 | async-start | bytes 1769472 | tf_op jit(solution)/shard_map/all_gather | solution.py:609
  146.1 13.7 %copy-start.3 = (bf16[16,3072]{1,0:T(8,128)(2,1)S(1)}, bf16[16,3072]{1,0:T(8,128)(2,1)}, u32[]{:S(2)}) copy-start(bf16[16,3072]{1,0:T(8,128)(2,1)} %get-tuple-element.77.state) | copy-start | bytes 294916
  160.7 26.3 %copy-start.2 = (bf16[16,3072]{1,0:T(8,128)(2,1)S(1)}, bf16[16,3072]{1,0:T(8,128)(2,1)}, u32[]{:S(2)}) copy-start(bf16[16,3072]{1,0:T(8,128)(2,1)} %get-tuple-element.79.state) | copy-start | bytes 294916
  160.7 26.3 %copy-start.4 = (f32[3072]{0:T(1024)S(1)}, f32[3072]{0:T(1024)}, u32[]{:S(2)}) copy-start(f32[3072]{0:T(1024)} %param.24) | copy-start | bytes 36868
  160.7 56.0 %all-gather.12.cloned.1.call-start = ((), (), s32[]{:S(2)}) async-start(), calls=%async_computation.8 | async-start | bytes 2359296 | tf_op jit(solution)/shard_map/all_gather | solution.py:579
  161.3 25.7 %all-to-all-start.3 = ((bf16[16,16,3072]{2,1,0:T(8,128)(2,1)}), bf16[16,16,3072]{2,1,0:T(8,128)(2,1)S(1)}, u32[]{:S(2)}, u32[]{:S(2)}) async-start(bf16[16,16,3072]{2,1,0:T(8,128)(2,1)} %bitcast.37), calls=%async_computation.3 | async-start | bytes 3145728 | tf_op jit(solution)/shard_map/all_to_all | solution.py:15
  196.8 27.7 %all-to-all-start.5 = ((bf16[16,8,16,384]{3,2,1,0:T(8,128)(2,1)}), bf16[16,8,16,384]{3,2,1,0:T(8,128)(2,1)S(1)}, u32[]{:S(2)}, u32[]{:S(2)}) async-start(bf16[16,8,16,384]{3,2,1,0:T(8,128)(2,1)} %shard_map.149), calls=%async_computation.5 | async-start | bytes 3145728 | tf_op jit(solution)/shard_map/all_to_all | solution.py:15
  (7 other events, 30.1 us)
Sparse Core Ops, SparseCore 0:
  10.3 26.9 all-gather.9
  38.9 24.7 all-gather.7
  79.0 52.5 all-gather.13
  160.8 20.8 all-gather.15
  183.3 25.0 all-gather.11

commit v9 on v8

--- a/solution.py
+++ b/solution.py
@@ -340,23 +340,42 @@
     )(place, message, token_slot[None])
 
 
+def bring_kernel(order, *refs):
+    del order
+    count = len(refs) // 2
+    sources, outs, sems = refs[:count], refs[count : 2 * count], refs[2 * count]
+    copies = [
+        pltpu.make_async_copy(source, out, sems.at[index])
+        for index, (source, out) in enumerate(zip(sources, outs))
+    ]
+    for copy in copies:
+        copy.start()
+    for copy in copies:
+        copy.wait()
+
+
+def bring(arrays, order):
+    return pl.pallas_call(
+        bring_kernel,
+        in_specs=[pl.BlockSpec(memory_space=pl.ANY)] + [pl.BlockSpec(memory_space=pltpu.HBM)] * len(arrays),
+        out_specs=[pl.BlockSpec(memory_space=pltpu.VMEM)] * len(arrays),
+        out_shape=[jax.ShapeDtypeStruct(a.shape, a.dtype) for a in arrays],
+        scratch_shapes=[pltpu.SemaphoreType.DMA((len(arrays),))],
+        compiler_params=pltpu.CompilerParams(vmem_limit_bytes=48 * 1024 * 1024),
+        cost_estimate=pl.CostEstimate(
+            flops=0, bytes_accessed=12 * arrays[0].size, transcendentals=0
+        ),
+    )(order, *arrays)
+
+
 def forward_kernel(
-    place, pieces, gain, order, gate_hbm, up_hbm, down_hbm,
-    home_state, here_state, gate, up, out_hbm, normed, act, held, out, sems, out_sems,
+    place, pieces, gain, order, gate_w, up_w, down_hbm,
+    home_state, here_state, gate_hbm, up_hbm, out_hbm,
+    normed, act, out, down_w, gate, up, out_sems, sems,
 ):
     del order
-    parts = 3
-    part = gate_hbm.shape[0] // parts
-
-    def load(which, source, third):
-        at = pl.ds(third * part, part)
-        return pltpu.make_async_copy(
-            source.at[at], held.at[which, at], sems.at[parts * which + third]
-        )
-
-    for third in range(parts):
-        load(0, gate_hbm, third).start()
-        load(1, up_hbm, third).start()
+    down_load = pltpu.make_async_copy(down_hbm, down_w, sems.at[0])
+    down_load.start()
     cols = pieces.shape[2]
     width = normed.shape[1]
     groups = width // cols
@@ -387,23 +406,17 @@
             wide = pieces[block * groups + group].astype(full)
             normed[rows, at] = (wide * inverse * gain[:, at]).astype(normed.dtype)
     half_hidden = gate.shape[1] // 2
-    for third in range(parts):
-        load(0, gate_hbm, third).wait()
-        load(1, up_hbm, third).wait()
-        load(2, down_hbm, third).start()
-        depth = pl.ds(third * part, part)
-        for index in range(2):
-            at = pl.ds(index * half_hidden, half_hidden)
-            for which, total_ref in ((0, gate), (1, up)):
-                value = jnp.dot(
-                    normed[:, depth], held[which, depth, at], preferred_element_type=full
-                )
-                total_ref[:, at] = value if third == 0 else total_ref[:, at] + value
+    for index in range(2):
+        at = pl.ds(index * half_hidden, half_hidden)
+        gate[:, at] = jnp.dot(normed[...], gate_w[:, at], preferred_element_type=full)
+        up[:, at] = jnp.dot(normed[...], up_w[:, at], preferred_element_type=full)
+    gate_leaves = pltpu.make_async_copy(gate, gate_hbm, sems.at[1])
+    up_leaves = pltpu.make_async_copy(up, up_hbm, sems.at[2])
+    gate_leaves.start()
+    up_leaves.start()
     gate_val = gate[...]
     act[...] = (gate_val * jax.nn.sigmoid(gate_val) * up[...]).astype(half)
-    for third in range(parts):
-        load(2, down_hbm, third).wait()
-    down_w = held.at[2]
+    down_load.wait()
     rows = out.shape[1] // 2
     wide_chunk = 512
 
@@ -423,6 +436,8 @@
 
     for index in range(width // wide_chunk):
         leave(index).wait()
+    gate_leaves.wait()
+    up_leaves.wait()
 
 
 def forward(pieces, gain, gate_w, up_w, down_w, mp, order):
@@ -435,8 +450,8 @@
     return pl.pallas_call(
         forward_kernel,
         in_specs=[pl.BlockSpec(memory_space=pltpu.SMEM), whole, whole]
-        + [pl.BlockSpec(memory_space=pl.ANY), far, far, far],
-        out_specs=[whole] * 4 + [far],
+        + [pl.BlockSpec(memory_space=pl.ANY), whole, whole, far],
+        out_specs=[whole, whole, far, far, far],
         out_shape=[
             jax.ShapeDtypeStruct((mine, width), half),
             jax.ShapeDtypeStruct((mine, width), half),
@@ -447,12 +462,14 @@
         scratch_shapes=[
             pltpu.VMEM((rows, width), half),
             pltpu.VMEM((rows, hidden), half),
-            pltpu.VMEM((3, width, hidden), half),
             pltpu.VMEM((n_mp, mine, width), half),
-            pltpu.SemaphoreType.DMA((9,)),
+            pltpu.VMEM((width, hidden), half),
+            pltpu.VMEM((rows, hidden), full),
+            pltpu.VMEM((rows, hidden), full),
             pltpu.SemaphoreType.DMA((width // 512,)),
+            pltpu.SemaphoreType.DMA((3,)),
         ],
-        compiler_params=pltpu.CompilerParams(vmem_limit_bytes=56 * 1024 * 1024),
+        compiler_params=pltpu.CompilerParams(vmem_limit_bytes=48 * 1024 * 1024),
         cost_estimate=pl.CostEstimate(
             flops=6 * rows * width * hidden,
             bytes_accessed=6 * width * hidden + 10 * rows * width,
@@ -579,8 +596,9 @@
     pooled_all = lax.all_gather(pooled.reshape(n_mp, mine_rows, width_here), "dp", axis=0, tiled=False)
     pooled_all = jnp.swapaxes(pooled_all, 0, 1).reshape(n_dp * tokens, width_here)
 
+    weights = bring((gate_weight, up_weight), inverse_rms)
     home_state, here_state, gate, up, output = forward(
-        states, student_gain, gate_weight, up_weight, down_weight, mp, pooled
+        states, student_gain, *weights, down_weight, mp, pooled
     )
     grad_gate, grad_up = backward(dy.reshape(tokens, student_width), down_weight, gate, up, output)
     dn = (times_rows(grad_gate, gate_weight) + times_rows(grad_up, up_weight)).astype(half)

time: 236 us -> 235 us (level)
  waiting for transfers between devices: 88.7 us -> 81.4 us
  Pallas kernels: 35.1 us -> 38.6 us
  local copies, waits for them, and re-layouts: 14.3 us -> 16.7 us
    all_to_all x5, waiting for transfers between devices: 75.6 us -> 68.5 us  [exchange(): return lax.all_to_all(pieces, axis, split_axis=0, concat_axis=0, tiled=True)]
    pallas_call x0 -> x1, Pallas kernels: none -> 4.5 us  [bring(): pl.pallas_call(bring_kernel, in_specs=[pl.BlockSpec(memory_space=pl.ANY)]...]
    unnamed x33 -> x35, local copies, waits for them, and re-layouts: 5.43 us -> 7.51 us
  transfers between devices with their start and end apart: 24 -> 24, of which waited for: 11 -> 11; matrix products, arithmetic and copies ran while one was open for 11% -> 10% of each run, Pallas kernels for 15% -> 16%
where the time goes in v9:
time: 235 us; the launch traced here: 233 us
  waiting for transfers between devices  81.4 us (35%)
  starting transfers between devices  46.3 us (20%)
  Pallas kernels  38.6 us (16%)
  between operations  24.1 us (10%)
  local copies, waits for them, and re-layouts  16.7 us (7%)
  matrix products  9.28 us (4%)
  blocking collectives  8.76 us (4%)
  other arithmetic  8.16 us (3%)
    all_to_all x5, waiting for transfers between devices, exchange(): return lax.all_to_all(pieces, axis, split_axis=0, concat_axis=0, tiled=True)  68.5 us
    all_to_all x5, starting transfers between devices, exchange(): return lax.all_to_all(pieces, axis, split_axis=0, concat_axis=0, tiled=True)  24.4 us
    ppermute x14, starting transfers between devices, step(): return lax.ppermute(value, 'mp', pairs)  21.7 us
    ppermute x14, waiting for transfers between devices, step(): return lax.ppermute(value, 'mp', pairs)  12.3 us
    pallas_call x2, Pallas kernels, terms(): pl.pallas_call(kernel, in_specs=[scalars, whole, pl.BlockSpec(memory_spac...  11.6 us
    all_to_all x1, blocking collectives, exchange(): return lax.all_to_all(pieces, axis, split_axis=0, concat_axis=0, tiled=True)  8.76 us
    pallas_call x1, Pallas kernels, forward(): pl.pallas_call(forward_kernel, in_specs=[pl.BlockSpec(memory_space=pltpu....  8.52 us
    unnamed x35, local copies, waits for them, and re-layouts  7.51 us
  transfers between devices with their start and end apart: 24, of which 11 were waited for; matrix products, arithmetic and copies ran while one was open for 10% of the time, Pallas kernels for 16%

profile of v9, /device:TPU:0, one launch (start us, length us, event | category | flops | bytes accessed | tf_op | source)
XLA Modules:
  0.0 233.3 jit_solution(5335157664079878946)
XLA Ops:
  10.0 4.3 %shard_map.141 = (bf16[4,64,512]{2,1,0:T(8,128)(2,1)}, bf16[4,64,512]{2,1,0:T(8,128)(2,1)}, bf16[4,64,512]{2,1,0:T(8,128)(2,1)}, bf16[4,64,512]{2,1,0:T(8,128)(2,1)}) custom-call(s32[2]{0:T(128)S(1)} %pad_add_fusion.1.place, bf16[256,512]{1,0:T(8,128)(2,1)S(1)} %copy-done.1, bf16[512,8192]{1,0:T(8,128)(2,1)} %right.3), custom_call_target="tpu_custom_call" | custom-call | flops 536870912 | bytes 4194304 | tf_op jit(solution)/shard_map/pallas_call | solution.py:135
  17.6 2.0 collective-permute-start.2
  19.6 2.1 collective-permute-start.3
  22.5 7.3 %shard_map.140 = (bf16[4,128,512]{2,1,0:T(8,128)(2,1)S(1)}, bf16[4,128,512]{2,1,0:T(8,128)(2,1)S(1)}, bf16[4,128,512]{2,1,0:T(8,128)(2,1)S(1)}, bf16[4,128,512]{...) custom-call(s32[2]{0:T(128)S(1)} %pad_add_fusion.1.place, ...), custom_call_target="tpu_custom_call" | custom-call | flops 2147483648 | bytes 8388608 | tf_op jit(solution)/shard_map/pallas_call | solution.py:135
  31.4 3.6 %shard_map.142 = (bf16[4,128,512]{2,1,0:T(8,128)(2,1)}, bf16[4,128,512]{2,1,0:T(8,128)(2,1)}, bf16[4,128,512]{2,1,0:T(8,128)(2,1)}, bf16[4,128,512]{2,1,0:T(8,128)(2,1)}) custom-call(bf16[4,128,512]{2,1,0:T(8,128)(2,1)S(1)} %get-tuple-element.50.refs_0_, bf16[4,128,512]{2,1,0:T(8,128)(2,1)S(1)} %get-tuple-element.51.refs_1_, ...), custom_call_target="tpu_custom_call" | custom-call | flops 1048576 | bytes 5242880 | tf_op jit(solution)/shard_map/pallas_call | solution.py:156
  35.4 2.9 %collective-permute-start.5 = (bf16[4,128,512]{2,1,0:T(8,128)(2,1)}, bf16[4,128,512]{2,1,0:T(8,128)(2,1)S(1)}, u32[]{:S(2)}, u32[]{:S(2)}) collective-permute-start(bf16[4,128,512]{2,1,0:T(8,128)(2,1)} %get-tuple-element.59), channel_id=1, source_target_pairs={{0,12},{1,13},{2,14},{3,15},{4,0},{5,1},{6,2},{7,3},{8,4},{9,5},{1... | collective-permute-start | bytes 1572872 | tf_op jit(solution)/shard_map/ppermute | solution.py:42
  38.2 3.2 %collective-permute-start.7 = (bf16[4,128,512]{2,1,0:T(8,128)(2,1)}, bf16[4,128,512]{2,1,0:T(8,128)(2,1)S(1)}, u32[]{:S(2)}, u32[]{:S(2)}) collective-permute-start(bf16[4,128,512]{2,1,0:T(8,128)(2,1)} %get-tuple-element.62), channel_id=1, source_target_pairs={{0,3},{1,0},{2,1},{3,2},{4,7},{5,4},{6,5},{7,6},{8,11},{9,8},{10,9... | collective-permute-start | bytes 1572872 | tf_op jit(solution)/shard_map/ppermute | solution.py:42
  41.5 3.4 %constant_dynamic-slice_fusion.1 = (bf16[1,8,1,3072]{3,1,2,0:T(8,128)(2,1)S(1)}, bf16[1,8,1,3072]{3,1,2,0:T(8,128)(2,1)S(1)}) fusion(bf16[8,8,4,3072]{3,1,2,0:T(8,128)(2,1)} %all-gather.10.cloned.1.call-done, s32[]{:T(128)} %bitcast, s32[]{:T(128)} %bitcast.1, s32[]{:T(128)} %bitcast.3, s32[]{:T(128)} %bitcast.4), kind=kLoop, calls=%fused_computation.48 | loop fusion | bytes 196624 | tf_op jit(solution)/shard_map/dynamic_slice | solution.py:19
  44.9 4.5 %collective-permute-done.4.refs_1_ = bf16[4,128,512]{2,1,0:T(8,128)(2,1)S(1)} collective-permute-done((bf16[4,128,512]{2,1,0:T(8,128)(2,1)}, bf16[4,128,512]{2,1,0:T(8,128)(2,1)S(1)}, u32[]{:S(2)}, u32[]{:S(2)}) %collective-permute-start.4) | collective-permute-done | bytes 524320 | tf_op jit(solution)/shard_map/ppermute | solution.py:42
  49.4 2.7 %collective-permute-done.6.refs_4_ = bf16[4,128,512]{2,1,0:T(8,128)(2,1)S(1)} collective-permute-done((bf16[4,128,512]{2,1,0:T(8,128)(2,1)}, bf16[4,128,512]{2,1,0:T(8,128)(2,1)S(1)}, u32[]{:S(2)}, u32[]{:S(2)}) %collective-permute-start.6) | collective-permute-done | bytes 524320 | tf_op jit(solution)/shard_map/ppermute | solution.py:42
  53.0 3.0 %collective-permute-start.10 = (bf16[128,512]{1,0:T(8,128)(2,1)S(1)}, bf16[128,512]{1,0:T(8,128)(2,1)S(1)}, u32[]{:S(2)}, u32[]{:S(2)}) collective-permute-start(bf16[128,512]{1,0:T(8,128)(2,1)S(1)} %get-tuple-element.66), channel_id=1, source_target_pairs={{0,3},{1,0},{2,1},{3,2},{4,7},{5,4},{6,5},{7,6},{8,11},{9,8},{10,9... | collective-permute-start | bytes 393224 | tf_op jit(solution)/shard_map/ppermute | solution.py:42
  60.9 2.7 %collective-permute-done.8 = bf16[128,512]{1,0:T(8,128)(2,1)S(1)} collective-permute-done((bf16[128,512]{1,0:T(8,128)(2,1)S(1)}, bf16[128,512]{1,0:T(8,128)(2,1)S(1)}, u32[]{:S(2)}, u32[]{:S(2)}) %collective-permute-start.8) | collective-permute-done | bytes 131104 | tf_op jit(solution)/shard_map/ppermute | solution.py:42
  68.8 6.0 %all-to-all-start = ((bf16[16,144,384]{2,1,0:T(8,128)(2,1)}), bf16[16,144,384]{2,1,0:T(8,128)(2,1)S(1)}, u32[]{:S(2)}, u32[]{:S(2)}) async-start(bf16[16,144,384]{2,1,0:T(8,128)(2,1)} %bitcast.22), calls=%async_computation | async-start | bytes 3538944 | tf_op jit(solution)/shard_map/all_to_all | solution.py:15
  74.8 3.4 %dynamic-slice_bitcast_fusion.2 = (bf16[1,8,3072]{2,1,0:T(8,128)(2,1)S(1)}, bf16[1,8,3072]{2,1,0:T(8,128)(2,1)S(1)}) fusion(bf16[8,8,4,3072]{3,1,2,0:T(8,128)(2,1)} %all-gather.8.cloned.1.call-done, s32[]{:T(128)} %bitcast, s32[]{:T(128)} %bitcast.1, s32[]{:T(128)} %bitcast.3, s32[]{:T(128)} %bitcast.4), kind=kLoop, calls=%fused_computation.32 | loop fusion | bytes 196624 | tf_op jit(solution)/shard_map/stack;reshape | solution.py:558
  79.0 16.3 %all-to-all-done.message = bf16[16,144,384]{2,1,0:T(8,128)(2,1)S(1)} async-done(((bf16[16,144,384]{2,1,0:T(8,128)(2,1)}), bf16[16,144,384]{2,1,0:T(8,128)(2,1)S(1)}, u32[]{:S(2)}, u32[]{:S(2)}) %all-to-all-start) | async-done | bytes 1769504 | tf_op jit(solution)/shard_map/all_to_all | solution.py:15
  95.3 2.3 shard_map.144
  97.6 5.0 %all-to-all-start.1 = ((bf16[16,128,384]{2,1,0:T(8,128)(2,1)}), bf16[16,128,384]{2,1,0:T(8,128)(2,1)S(1)}, u32[]{:S(2)}, u32[]{:S(2)}) async-start(bf16[16,128,384]{2,1,0:T(8,128)(2,1)} %get-tuple-element.71), calls=%async_computation.1 | async-start | bytes 3145728 | tf_op jit(solution)/shard_map/all_to_all | solution.py:15
  102.8 4.5 %shard_map.145 = (bf16[3072,512]{1,0:T(8,128)(2,1)S(1)}, bf16[3072,512]{1,0:T(8,128)(2,1)}) custom-call(f32[1,256]{1,0:T(1,128)S(1)} %get-tuple-element.72.order, bf16[3072,512]{1,0:T(8,128)(2,1)} %refs_0_.1, bf16[3072,512]{1,0:T(8,128)(2,1)} %refs_1_.1), custom_call_target="tpu_custom_call" | custom-call | bytes 18874368 | tf_op jit(solution)/shard_map/pallas_call | solution.py:358
  109.3 13.4 %all-to-all-done.1.pieces = bf16[16,128,384]{2,1,0:T(8,128)(2,1)S(1)} async-done(((bf16[16,128,384]{2,1,0:T(8,128)(2,1)}), bf16[16,128,384]{2,1,0:T(8,128)(2,1)S(1)}, u32[]{:S(2)}, u32[]{:S(2)}) %all-to-all-start.1) | async-done | bytes 1572896 | tf_op jit(solution)/shard_map/all_to_all | solution.py:15
  122.7 8.5 %shard_map.146 = (bf16[16,3072]{1,0:T(8,128)(2,1)S(1)}, bf16[16,3072]{1,0:T(8,128)(2,1)S(1)}, f32[256,512]{1,0:T(8,128)S(1)}, f32[256,512]{1,0:T(8,128)S(1)}, bf16[16,16,3072]{2,1,0:T(8,128)(2,1)}) custom-call(s32[1]{0:T(128)} %bitcast.7.place, bf16[16,128,384]{2,1,0:T(8,128)(2,1)S(1)} %all-to-all-done.1.pieces, f32[1,3072]{1,0:T(1,128)S(1)} %bitcast.83, ...), custom_call_target="tpu_custom_call" | custom-call | flops 2415919104 | bytes 17301504 | tf_op jit(solution)/shard_map/pallas_call | solution.py:450
  132.8 5.9 %all-to-all-start.2 = ((bf16[16,16,3072]{2,1,0:T(8,128)(2,1)}), bf16[16,16,3072]{2,1,0:T(8,128)(2,1)S(1)}, u32[]{:S(2)}, u32[]{:S(2)}) async-start(bf16[16,16,3072]{2,1,0:T(8,128)(2,1)} %get-tuple-element.77.order), calls=%async_computation.2 | async-start | bytes 3145728 | tf_op jit(solution)/shard_map/all_to_all | solution.py:15
  138.9 4.6 %shard_map.147 = (bf16[256,512]{1,0:T(8,128)(2,1)}, bf16[256,512]{1,0:T(8,128)(2,1)}) custom-call(bf16[256,3072]{1,0:T(8,128)(2,1)} %bitcast.89, bf16[3072,512]{1,0:T(8,128)(2,1)} %down.1, f32[256,512]{1,0:T(8,128)} %copy-done.4, f32[256,512]{1,0:T(8,128)} %copy-done.5, bf16[16,16,3072]{2,1,0:T(8,128)(2,1)} %get-tuple-element.77.order), custom_call_target="tpu_custom_call" | custom-call | flops 805306368 | bytes 6815744 | tf_op jit(solution)/shard_map/pallas_call | solution.py:218
  143.5 2.1 fusion.30
  145.6 2.2 fusion
  147.9 11.2 %all-to-all-done.2.terms = bf16[16,16,3072]{2,1,0:T(8,128)(2,1)S(1)} async-done(((bf16[16,16,3072]{2,1,0:T(8,128)(2,1)}), bf16[16,16,3072]{2,1,0:T(8,128)(2,1)S(1)}, u32[]{:S(2)}, u32[]{:S(2)}) %all-to-all-start.2) | async-done | bytes 1572896 | tf_op jit(solution)/shard_map/all_to_all | solution.py:15
  160.6 3.7 %all-to-all-start.3 = ((bf16[16,16,3072]{2,1,0:T(8,128)(2,1)}), bf16[16,16,3072]{2,1,0:T(8,128)(2,1)S(1)}, u32[]{:S(2)}, u32[]{:S(2)}) async-start(bf16[16,16,3072]{2,1,0:T(8,128)(2,1)} %bitcast.37), calls=%async_computation.3 | async-start | bytes 3145728 | tf_op jit(solution)/shard_map/all_to_all | solution.py:15
  165.2 19.8 %all-to-all-done.3.terms = bf16[16,16,3072]{2,1,0:T(8,128)(2,1)S(1)} async-done(((bf16[16,16,3072]{2,1,0:T(8,128)(2,1)}), bf16[16,16,3072]{2,1,0:T(8,128)(2,1)S(1)}, u32[]{:S(2)}, u32[]{:S(2)}) %all-to-all-start.3) | async-done | bytes 1572896 | tf_op jit(solution)/shard_map/all_to_all | solution.py:15
  185.4 8.8 %all_to_all.30.piece = bf16[8,16,384]{2,1,0:T(8,128)(2,1)S(1)} all-to-all(bf16[8,16,384]{2,1,0:T(8,128)(2,1)S(1)} %shard_map.149), channel_id=1, replica_groups=mesh['dp'=8,'mp'=16] {'dp'}, dimensions={0} | all-to-all | bytes 196608 | tf_op jit(solution)/shard_map/all_to_all | solution.py:15
  195.4 3.7 %all-to-all-start.5 = ((bf16[16,8,16,384]{3,2,1,0:T(8,128)(2,1)}), bf16[16,8,16,384]{3,2,1,0:T(8,128)(2,1)S(1)}, u32[]{:S(2)}, u32[]{:S(2)}) async-start(bf16[16,8,16,384]{3,2,1,0:T(8,128)(2,1)} %shard_map.150), calls=%async_computation.5 | async-start | bytes 3145728 | tf_op jit(solution)/shard_map/all_to_all | solution.py:15
  210.8 3.5 %select_bitcast_fusion.3 = (bf16[8,1,3072]{2,0,1:T(8,128)(2,1)S(1)}, bf16[8,1,3072]{2,0,1:T(8,128)(2,1)S(1)}, bf16[8,1,3072]{2,0,1:T(8,128)(2,1)S(1)}, bf16[8,1,3072]{2,0,1:T(8,128)(2,1)S(1)}) fusion(bf16[8,32,3072]{2,1,0:T(8,128)(2,1)} %bitcast.97, s32[]{:T(128)S(6)} %select_n.131, s32[]{:T(128)S(6)} %mul.47, pred[]{:T(512)} %get-tuple-element.90, ...), kind=kLoop, calls=%fused_computation.30 | loop fusion | flops 98304 | bytes 393252 | tf_op jit(solution)/shard_map/jit(_where)/select_n | solution.py:637
  215.2 7.8 %all-to-all-done.5 = bf16[16,8,16,384]{3,2,1,0:T(8,128)(2,1)S(1)} async-done(((bf16[16,8,16,384]{3,2,1,0:T(8,128)(2,1)}), bf16[16,8,16,384]{3,2,1,0:T(8,128)(2,1)S(1)}, u32[]{:S(2)}, u32[]{:S(2)}) %all-to-all-start.5) | async-done | bytes 1572896 | tf_op jit(solution)/shard_map/all_to_all | solution.py:15
  223.1 3.8 %fusion.7 = f32[512,384]{1,0:T(8,128)} fusion(bf16[16,8,16,384]{3,2,1,0:T(8,128)(2,1)S(1)} %all-to-all-done.5, bf16[8,16,16,512]{3,2,0,1:T(8,128)(2,1)} %all-gather.12.cloned.1.call-done), kind=kOutput, calls=%fused_computation.10 | convolution fusion | flops 805306368 | bytes 4456448 | tf_op jit(solution)/shard_map/dot_general | solution.py:620
  (101 shorter events, 31.0 us)
Async XLA Ops:
  7.2 34.3 %all-gather.10.cloned.1.call-start = ((), (), s32[]{:S(2)}) async-start(), calls=%async_computation.7 | async-start | bytes 1769472 | tf_op jit(solution)/shard_map/all_gather | solution.py:552
  8.9 65.9 %all-gather.8.cloned.1.call-start = ((), (), s32[]{:S(2)}) async-start(), calls=%async_computation.6 | async-start | bytes 1769472 | tf_op jit(solution)/shard_map/all_gather | solution.py:552
  10.0 11.8 %copy-start.12 = (bf16[1,8,4,3072]{3,2,1,0:T(4,128)(2,1)S(1)}, bf16[1,8,4,3072]{3,2,1,0:T(4,128)(2,1)}, u32[]{:S(2)}) copy-start(bf16[1,8,4,3072]{3,2,1,0:T(4,128)(2,1)} %param.23) | copy-start | bytes 589828
  10.0 12.5 %copy-start.2 = (bf16[256,512]{1,0:T(8,128)(2,1)S(1)}, bf16[256,512]{1,0:T(8,128)(2,1)}, u32[]{:S(2)}) copy-start(bf16[256,512]{1,0:T(8,128)(2,1)} %left.3) | copy-start | bytes 786436
  14.3 17.1 %collective-permute-start = (bf16[4,64,512]{2,1,0:T(8,128)(2,1)}, bf16[4,64,512]{2,1,0:T(8,128)(2,1)}, u32[]{:S(2)}, u32[]{:S(2)}) collective-permute-start(bf16[4,64,512]{2,1,0:T(8,128)(2,1)} %get-tuple-element.52), channel_id=1, source_target_pairs={{0,4},{1,5},{2,6},{3,7},{4,8},{5,9},{6,10},{7,11},{8,12},{9,13},{1... | collective-permute-start | bytes 786440 | tf_op jit(solution)/shard_map/ppermute | solution.py:42
  16.1 15.3 %collective-permute-start.1 = (bf16[4,64,512]{2,1,0:T(8,128)(2,1)}, bf16[4,64,512]{2,1,0:T(8,128)(2,1)}, u32[]{:S(2)}, u32[]{:S(2)}) collective-permute-start(bf16[4,64,512]{2,1,0:T(8,128)(2,1)} %get-tuple-element.53), channel_id=1, source_target_pairs={{0,12},{1,13},{2,14},{3,15},{4,0},{5,1},{6,2},{7,3},{8,4},{9,5},{1... | collective-permute-start | bytes 786440 | tf_op jit(solution)/shard_map/ppermute | solution.py:42
  17.6 13.8 %collective-permute-start.2 = (bf16[4,64,512]{2,1,0:T(8,128)(2,1)}, bf16[4,64,512]{2,1,0:T(8,128)(2,1)}, u32[]{:S(2)}, u32[]{:S(2)}) collective-permute-start(bf16[4,64,512]{2,1,0:T(8,128)(2,1)} %get-tuple-element.56), channel_id=1, source_target_pairs={{0,1},{1,2},{2,3},{3,0},{4,5},{5,6},{6,7},{7,4},{8,9},{9,10},{10,1... | collective-permute-start | bytes 786440 | tf_op jit(solution)/shard_map/ppermute | solution.py:42
  19.6 11.8 %collective-permute-start.3 = (bf16[4,64,512]{2,1,0:T(8,128)(2,1)}, bf16[4,64,512]{2,1,0:T(8,128)(2,1)}, u32[]{:S(2)}, u32[]{:S(2)}) collective-permute-start(bf16[4,64,512]{2,1,0:T(8,128)(2,1)} %get-tuple-element.57), channel_id=1, source_target_pairs={{0,3},{1,0},{2,1},{3,2},{4,7},{5,4},{6,5},{7,6},{8,11},{9,8},{10,9... | collective-permute-start | bytes 786440 | tf_op jit(solution)/shard_map/ppermute | solution.py:42
  35.0 14.4 %collective-permute-start.4 = (bf16[4,128,512]{2,1,0:T(8,128)(2,1)}, bf16[4,128,512]{2,1,0:T(8,128)(2,1)S(1)}, u32[]{:S(2)}, u32[]{:S(2)}) collective-permute-start(bf16[4,128,512]{2,1,0:T(8,128)(2,1)} %get-tuple-element.58), channel_id=1, source_target_pairs={{0,4},{1,5},{2,6},{3,7},{4,8},{5,9},{6,10},{7,11},{8,12},{9,13},{1... | collective-permute-start | bytes 1572872 | tf_op jit(solution)/shard_map/ppermute | solution.py:42
  35.4 14.0 %collective-permute-start.5 = (bf16[4,128,512]{2,1,0:T(8,128)(2,1)}, bf16[4,128,512]{2,1,0:T(8,128)(2,1)S(1)}, u32[]{:S(2)}, u32[]{:S(2)}) collective-permute-start(bf16[4,128,512]{2,1,0:T(8,128)(2,1)} %get-tuple-element.59), channel_id=1, source_target_pairs={{0,12},{1,13},{2,14},{3,15},{4,0},{5,1},{6,2},{7,3},{8,4},{9,5},{1... | collective-permute-start | bytes 1572872 | tf_op jit(solution)/shard_map/ppermute | solution.py:42
  38.2 13.8 %collective-permute-start.6 = (bf16[4,128,512]{2,1,0:T(8,128)(2,1)}, bf16[4,128,512]{2,1,0:T(8,128)(2,1)S(1)}, u32[]{:S(2)}, u32[]{:S(2)}) collective-permute-start(bf16[4,128,512]{2,1,0:T(8,128)(2,1)} %get-tuple-element.61), channel_id=1, source_target_pairs={{0,1},{1,2},{2,3},{3,0},{4,5},{5,6},{6,7},{7,4},{8,9},{9,10},{10,1... | collective-permute-start | bytes 1572872 | tf_op jit(solution)/shard_map/ppermute | solution.py:42
  38.2 13.8 %collective-permute-start.7 = (bf16[4,128,512]{2,1,0:T(8,128)(2,1)}, bf16[4,128,512]{2,1,0:T(8,128)(2,1)S(1)}, u32[]{:S(2)}, u32[]{:S(2)}) collective-permute-start(bf16[4,128,512]{2,1,0:T(8,128)(2,1)} %get-tuple-element.62), channel_id=1, source_target_pairs={{0,3},{1,0},{2,1},{3,2},{4,7},{5,4},{6,5},{7,6},{8,11},{9,8},{10,9... | collective-permute-start | bytes 1572872 | tf_op jit(solution)/shard_map/ppermute | solution.py:42
  52.1 14.1 %copy-start.10 = (bf16[256,512]{1,0:T(8,128)(2,1)S(1)}, bf16[256,512]{1,0:T(8,128)(2,1)}, u32[]{:S(2)}) copy-start(bf16[256,512]{1,0:T(8,128)(2,1)} %param.17) | copy-start | bytes 786436
  52.1 14.1 %copy-start.13 = (f32[512]{0:T(512)S(1)}, f32[512]{0:T(512)}, u32[]{:S(2)}) copy-start(f32[512]{0:T(512)} %param.18) | copy-start | bytes 6148
  52.1 14.3 %copy-start.15 = (bf16[512,3072]{1,0:T(8,128)(2,1)S(1)}, bf16[512,3072]{1,0:T(8,128)(2,1)}, u32[]{:S(2)}) copy-start(bf16[512,3072]{1,0:T(8,128)(2,1)} %param.19) | copy-start | bytes 9437188
  53.0 6.6 %collective-permute-start.10 = (bf16[128,512]{1,0:T(8,128)(2,1)S(1)}, bf16[128,512]{1,0:T(8,128)(2,1)S(1)}, u32[]{:S(2)}, u32[]{:S(2)}) collective-permute-start(bf16[128,512]{1,0:T(8,128)(2,1)S(1)} %get-tuple-element.66), channel_id=1, source_target_pairs={{0,3},{1,0},{2,1},{3,2},{4,7},{5,4},{6,5},{7,6},{8,11},{9,8},{10,9... | collective-permute-start | bytes 393224 | tf_op jit(solution)/shard_map/ppermute | solution.py:42
  56.0 7.6 %collective-permute-start.8 = (bf16[128,512]{1,0:T(8,128)(2,1)S(1)}, bf16[128,512]{1,0:T(8,128)(2,1)S(1)}, u32[]{:S(2)}, u32[]{:S(2)}) collective-permute-start(bf16[128,512]{1,0:T(8,128)(2,1)S(1)} %get-tuple-element.64), channel_id=1, source_target_pairs={{0,1},{1,2},{2,3},{3,0},{4,5},{5,6},{6,7},{7,4},{8,9},{9,10},{10,1... | collective-permute-start | bytes 393224 | tf_op jit(solution)/shard_map/ppermute | solution.py:42
  56.0 7.6 %collective-permute-start.9 = (bf16[128,512]{1,0:T(8,128)(2,1)S(1)}, bf16[128,512]{1,0:T(8,128)(2,1)S(1)}, u32[]{:S(2)}, u32[]{:S(2)}) collective-permute-start(bf16[128,512]{1,0:T(8,128)(2,1)S(1)} %get-tuple-element.65), channel_id=1, source_target_pairs={{0,2},{1,3},{2,0},{3,1},{4,6},{5,7},{6,4},{7,5},{8,10},{9,11},{10,... | collective-permute-start | bytes 393224 | tf_op jit(solution)/shard_map/ppermute | solution.py:42
  57.6 7.6 %collective-permute-start.11 = (bf16[128,512]{1,0:T(8,128)(2,1)S(1)}, bf16[128,512]{1,0:T(8,128)(2,1)S(1)}, u32[]{:S(2)}, u32[]{:S(2)}) collective-permute-start(bf16[128,512]{1,0:T(8,128)(2,1)S(1)} %get-tuple-element.68), channel_id=1, source_target_pairs={{0,4},{1,5},{2,6},{3,7},{4,8},{5,9},{6,10},{7,11},{8,12},{9,13},{1... | collective-permute-start | bytes 393224 | tf_op jit(solution)/shard_map/ppermute | solution.py:42
  57.6 7.6 %collective-permute-start.12 = (bf16[128,512]{1,0:T(8,128)(2,1)S(1)}, bf16[128,512]{1,0:T(8,128)(2,1)S(1)}, u32[]{:S(2)}, u32[]{:S(2)}) collective-permute-start(bf16[128,512]{1,0:T(8,128)(2,1)S(1)} %get-tuple-element.69), channel_id=1, source_target_pairs={{0,8},{1,9},{2,10},{3,11},{4,12},{5,13},{6,14},{7,15},{8,0},{9,1},... | collective-permute-start | bytes 393224 | tf_op jit(solution)/shard_map/ppermute | solution.py:42
  59.6 6.4 %collective-permute-start.13 = (bf16[128,512]{1,0:T(8,128)(2,1)S(1)}, bf16[128,512]{1,0:T(8,128)(2,1)S(1)}, u32[]{:S(2)}, u32[]{:S(2)}) collective-permute-start(bf16[128,512]{1,0:T(8,128)(2,1)S(1)} %get-tuple-element.70), channel_id=1, source_target_pairs={{0,12},{1,13},{2,14},{3,15},{4,0},{5,1},{6,2},{7,3},{8,4},{9,5},{1... | collective-permute-start | bytes 393224 | tf_op jit(solution)/shard_map/ppermute | solution.py:42
  68.8 26.5 %copy-start.7 = (s32[256]{0:T(256)S(1)}, s32[256]{0:T(256)}, u32[]{:S(2)}) copy-start(s32[256]{0:T(256)} %param.20) | copy-start | bytes 3076
  68.8 26.5 %all-to-all-start = ((bf16[16,144,384]{2,1,0:T(8,128)(2,1)}), bf16[16,144,384]{2,1,0:T(8,128)(2,1)S(1)}, u32[]{:S(2)}, u32[]{:S(2)}) async-start(bf16[16,144,384]{2,1,0:T(8,128)(2,1)} %bitcast.22), calls=%async_computation | async-start | bytes 3538944 | tf_op jit(solution)/shard_map/all_to_all | solution.py:15
  74.8 64.1 %all-gather.14.cloned.1.call-start = ((), (), s32[]{:S(2)}) async-start(), calls=%async_computation.9 | async-start | bytes 1671168 | tf_op jit(solution)/shard_map/all_gather | solution.py:562
  97.6 25.1 %all-to-all-start.1 = ((bf16[16,128,384]{2,1,0:T(8,128)(2,1)}), bf16[16,128,384]{2,1,0:T(8,128)(2,1)S(1)}, u32[]{:S(2)}, u32[]{:S(2)}) async-start(bf16[16,128,384]{2,1,0:T(8,128)(2,1)} %get-tuple-element.71), calls=%async_computation.1 | async-start | bytes 3145728 | tf_op jit(solution)/shard_map/all_to_all | solution.py:15
  109.0 13.7 %copy-start.6 = (f32[3072]{0:T(1024)S(1)}, f32[3072]{0:T(1024)}, u32[]{:S(2)}) copy-start(f32[3072]{0:T(1024)} %param.24) | copy-start | bytes 36868
  109.3 21.9 %copy-start.3 = (bf16[2,128,512]{2,1,0:T(8,128)(2,1)}, bf16[2,128,512]{2,1,0:T(8,128)(2,1)S(1)}, u32[]{:S(2)}) copy-start(bf16[2,128,512]{2,1,0:T(8,128)(2,1)S(1)} %fusion.10.order) | copy-start | bytes 786436
  132.8 26.3 %all-to-all-start.2 = ((bf16[16,16,3072]{2,1,0:T(8,128)(2,1)}), bf16[16,16,3072]{2,1,0:T(8,128)(2,1)S(1)}, u32[]{:S(2)}, u32[]{:S(2)}) async-start(bf16[16,16,3072]{2,1,0:T(8,128)(2,1)} %get-tuple-element.77.order), calls=%async_computation.2 | async-start | bytes 3145728 | tf_op jit(solution)/shard_map/all_to_all | solution.py:15
  138.8 72.1 %all-gather.16.cloned.1.call-start = ((), (), s32[]{:S(2)}) async-start(), calls=%async_computation.10 | async-start | bytes 1769472 | tf_op jit(solution)/shard_map/all_gather | solution.py:627
  160.0 55.2 %all-gather.12.cloned.1.call-start = ((), (), s32[]{:S(2)}) async-start(), calls=%async_computation.8 | async-start | bytes 2359296 | tf_op jit(solution)/shard_map/all_gather | solution.py:596
  160.6 24.4 %all-to-all-start.3 = ((bf16[16,16,3072]{2,1,0:T(8,128)(2,1)}), bf16[16,16,3072]{2,1,0:T(8,128)(2,1)S(1)}, u32[]{:S(2)}, u32[]{:S(2)}) async-start(bf16[16,16,3072]{2,1,0:T(8,128)(2,1)} %bitcast.37), calls=%async_computation.3 | async-start | bytes 3145728 | tf_op jit(solution)/shard_map/all_to_all | solution.py:15
  195.4 27.6 %all-to-all-start.5 = ((bf16[16,8,16,384]{3,2,1,0:T(8,128)(2,1)}), bf16[16,8,16,384]{3,2,1,0:T(8,128)(2,1)S(1)}, u32[]{:S(2)}, u32[]{:S(2)}) async-start(bf16[16,8,16,384]{3,2,1,0:T(8,128)(2,1)} %shard_map.150), calls=%async_computation.5 | async-start | bytes 3145728 | tf_op jit(solution)/shard_map/all_to_all | solution.py:15
  (8 other events, 20.4 us)
Sparse Core Ops, SparseCore 0:
  10.3 26.9 all-gather.9
  39.0 24.6 all-gather.7
  79.1 52.4 all-gather.13
  160.1 20.9 all-gather.15
  182.7 25.1 all-gather.11

commit v10 on v7

--- a/solution.py
+++ b/solution.py
@@ -13,6 +13,10 @@
 
 def exchange(pieces, axis):
     return lax.all_to_all(pieces, axis, split_axis=0, concat_axis=0, tiled=True)
+
+
+def take(array, starts, sizes):
+    return lax.dynamic_slice(array, starts, sizes, allow_negative_indices=False)
 
 
 def three_parts(value):
@@ -103,7 +107,7 @@
 
 
 def gather_kernel(place, *refs):
-    ins, outs = refs[:6], refs[7:]
+    ins, outs = refs[:6], refs[8:]
     for block in (0, 1):
         kept, from_down, from_up = ins[3 * block : 3 * block + 3]
         here = place[1 - block]
@@ -164,7 +168,7 @@
     from_down1, from_up1 = step(up1, 0, 1), step(down1, 0, -1)
     sums = pl.pallas_call(
         gather_kernel,
-        in_specs=[scalars] + [whole] * 6 + [anywhere],
+        in_specs=[scalars] + [whole] * 6 + [anywhere] * 2,
         out_specs=[whole] * (2 * SIDE),
         out_shape=[
             jax.ShapeDtypeStruct((BLK, width), half if distance else full)
@@ -337,9 +341,9 @@
 
 
 def forward_kernel(
-    pieces, gain, order, gate_hbm, up_hbm, down_hbm, state, gate, up, out, normed, act, held, sems
+    pieces, gain, order, other, gate_hbm, up_hbm, down_hbm, state, gate, up, out, normed, act, held, sems
 ):
-    del order
+    del order, other
     parts = 3
     part = gate_hbm.shape[0] // parts
 
@@ -401,14 +405,14 @@
             out[to, :, at] = jnp.concatenate([first, second], axis=0).astype(half)
 
 
-def forward(pieces, gain, gate_w, up_w, down_w, order):
+def forward(pieces, gain, gate_w, up_w, down_w, order, other):
     width, hidden = gate_w.shape
     n_mp = pieces.shape[0]
     rows = 2 * BLK
     whole = pl.BlockSpec(memory_space=pltpu.VMEM)
     return pl.pallas_call(
         forward_kernel,
-        in_specs=[whole, whole, pl.BlockSpec(memory_space=pl.ANY)]
+        in_specs=[whole, whole] + [pl.BlockSpec(memory_space=pl.ANY)] * 2
         + [pl.BlockSpec(memory_space=pltpu.HBM)] * 3,
         out_specs=[whole] * 4,
         out_shape=[
@@ -429,7 +433,7 @@
             bytes_accessed=6 * width * hidden + 10 * rows * width,
             transcendentals=rows * hidden,
         ),
-    )(pieces, gain[None], order, gate_w, up_w, down_w)
+    )(pieces, gain[None], order, other, gate_w, up_w, down_w)
 
 
 def slope_kernel(terms, dy, state, gain, order, out):
@@ -495,28 +499,31 @@
 
     ids = jnp.arange(block_owner.shape[0], dtype=jnp.int32)
     my_ids = dp * blocks + jnp.arange(blocks, dtype=jnp.int32)
-    my_owner = lax.dynamic_slice_in_dim(block_owner, dp * blocks, blocks)
+    my_owner = take(block_owner, (dp * blocks,), (blocks,))
     my_slot = jnp.sum(
         (block_owner[None, :] == my_owner[:, None]) & (ids[None, :] < my_ids[:, None]),
         axis=1,
         dtype=jnp.int32,
     )
 
-    def fetch(array):
-        everyone = lax.all_gather(array[0], "dp", axis=0, tiled=False)
+    both = jnp.concatenate([student_hidden[0], cotangent[0]], axis=1)
+    everyone = lax.all_gather(both, "dp", axis=0, tiled=False)
+
+    def fetch(offset):
         picked = []
         for k in range(blocks):
-            at = (my_owner[k], 0, my_slot[k], 0)
-            piece = lax.dynamic_slice(everyone, at, (1, rows, 1, student_width))
-            picked.append(piece.reshape(rows, student_width))
+            at = (my_owner[k], 0, my_slot[k] + offset, 0)
+            picked.append(
+                take(everyone, at, (1, rows, 1, student_width)).reshape(rows, student_width)
+            )
         return jnp.stack(picked)
 
-    sh_rows = fetch(student_hidden)
-    dy_rows = fetch(cotangent)
+    sh_rows = fetch(0)
+    dy_rows = fetch(student_hidden.shape[2])
     dy = lax.all_gather(dy_rows, "mp", axis=0, tiled=False)
 
     hidden = residual.astype(full) + jnp.concatenate(
-        [total(v) for v in teacher_terms(attention, out_proj, mp, (sh_rows,))], axis=0
+        [total(v) for v in teacher_terms(attention, out_proj, mp, (sh_rows, dy_rows))], axis=0
     )
     squares = jnp.sum(hidden * hidden, axis=1)
     gained_hidden = hidden * final_gain
@@ -551,7 +558,7 @@
     pooled_all = jnp.swapaxes(pooled_all, 0, 1).reshape(n_dp * tokens, width_here)
 
     state, gate, up, output = forward(
-        states, student_gain, gate_weight, up_weight, down_weight, pooled
+        states, student_gain, gate_weight, up_weight, down_weight, pooled, dy[0, 0, :, :128]
     )
     grad_gate, grad_up = backward(dy.reshape(tokens, student_width), down_weight, gate, up, output)
     dn = (times_rows(grad_gate, gate_weight) + times_rows(grad_up, up_weight)).astype(half)
@@ -559,16 +566,18 @@
     dn, output = lax.optimization_barrier((dn, output))
     dn = exchange(dn.reshape(n_mp, mine_rows, student_width), "mp")
     here = mp * mine_rows
-    state_rows = lax.dynamic_slice_in_dim(
-        state.reshape(blocks, BLK, student_width), mp * rows, rows, 1
+    state_rows = take(
+        state.reshape(blocks, BLK, student_width),
+        (0, mp * rows, 0),
+        (blocks, rows, student_width),
     )
     out_rows = home(output, state_rows.reshape(mine_rows, student_width))
     dproj = slope(
         dn,
-        lax.dynamic_slice(
+        take(
             dy, ((mp % groups) * blocks, mp // groups, 0, 0), (blocks, 1, rows, student_width)
         ).reshape(mine_rows, student_width),
-        lax.dynamic_slice_in_dim(state, here, mine_rows, 0),
+        take(state, (here, 0), (mine_rows, student_width)),
         student_gain,
         n_dp,
         out_rows,
@@ -590,7 +599,7 @@
         chosen = mine & (ranks == slot)
         index = jnp.sum(jnp.where(chosen, ids, 0))
         at = (index // blocks, (index % blocks) * rows, 0)
-        piece = lax.dynamic_slice(back, at, (1, rows, student_width))[0]
+        piece = take(back, at, (1, rows, student_width))[0]
         picks.append(jnp.where(jnp.any(chosen), piece, jnp.zeros((), half)))
     student_out = jnp.stack(picks, axis=1)
     return (student_out[None], adapter_grad)

time: 229 us -> 234 us (1.022)
  between operations: 31.7 us -> 25.6 us
  local copies, waits for them, and re-layouts: 11.1 us -> 15.1 us
  waiting for transfers between devices: 79.1 us -> 82.7 us
    ppermute x14, waiting for transfers between devices: 15.1 us -> 11.2 us  [step(): return lax.ppermute(value, 'mp', pairs)]
    all_gather x1, waiting for transfers between devices: 0.02 us -> 3.89 us  [on_device(): dy = lax.all_gather(dy_rows, 'mp', axis=0, tiled=False)]
    all_to_all x5, waiting for transfers between devices: 63.3 us -> 66.8 us  [exchange(): return lax.all_to_all(pieces, axis, split_axis=0, concat_axis=0, tiled=True)]
    dynamic_slice x3, local copies, waits for them, and re-layouts: 1.81 us -> 5.27 us  [take(): return lax.dynamic_slice(array, starts, sizes, allow_negative_indices=False)]
    unnamed x29 -> x37, local copies, waits for them, and re-layouts: 5.45 us -> 5.46 us
  transfers between devices with their start and end apart: 24 -> 23, of which waited for: 12 -> 12; matrix products, arithmetic and copies ran while one was open for 9% -> 11% of each run, Pallas kernels for 14% -> 9%
where the time goes in v10:
time: 234 us; the launch traced here: 232 us
  waiting for transfers between devices  82.7 us (35%)
  starting transfers between devices  46.2 us (20%)
  Pallas kernels  33.7 us (14%)
  between operations  25.6 us (11%)
  local copies, waits for them, and re-layouts  15.1 us (6%)
  matrix products  10 us (4%)
  blocking collectives  9.88 us (4%)
  other arithmetic  9.31 us (4%)
    all_to_all x5, waiting for transfers between devices, exchange(): return lax.all_to_all(pieces, axis, split_axis=0, concat_axis=0, tiled=True)  66.8 us
    all_to_all x5, starting transfers between devices, exchange(): return lax.all_to_all(pieces, axis, split_axis=0, concat_axis=0, tiled=True)  24.1 us
    ppermute x14, starting transfers between devices, step(): return lax.ppermute(value, 'mp', pairs)  21.9 us
    ppermute x14, waiting for transfers between devices, step(): return lax.ppermute(value, 'mp', pairs)  11.2 us
    pallas_call x2, Pallas kernels, terms(): pl.pallas_call(kernel, in_specs=[scalars, whole, pl.BlockSpec(memory_spac...  10.9 us
    all_to_all x1, blocking collectives, exchange(): return lax.all_to_all(pieces, axis, split_axis=0, concat_axis=0, tiled=True)  9.88 us
    pallas_call x1, Pallas kernels, forward(): pl.pallas_call(forward_kernel, in_specs=[whole, whole] + [pl.BlockSpec(me...  9.41 us
    unnamed x37, local copies, waits for them, and re-layouts  5.46 us
  transfers between devices with their start and end apart: 23, of which 12 were waited for; matrix products, arithmetic and copies ran while one was open for 11% of the time, Pallas kernels for 9%

profile of v10, /device:TPU:0, one launch (start us, length us, event | category | flops | bytes accessed | tf_op | source)
XLA Modules:
  0.0 232.4 jit_solution(14912528181993046023)
XLA Ops:
  7.2 2.0 pad_maximum_fusion.1
  10.3 3.6 %shard_map.141 = (bf16[4,64,512]{2,1,0:T(8,128)(2,1)S(1)}, bf16[4,64,512]{2,1,0:T(8,128)(2,1)S(1)}, bf16[4,64,512]{2,1,0:T(8,128)(2,1)S(1)}, bf16[4,64,512]{2,1,0:T(8,128)(2,1)S(1)}) custom-call(s32[2]{0:T(128)S(1)} %pad_add_fusion.1.place, bf16[256,512]{1,0:T(8,128)(2,1)S(1)} %copy-done, bf16[512,8192]{1,0:T(8,128)(2,1)} %right.3), custom_call_target="tpu_custom_call" | custom-call | flops 536870912 | bytes 4194304 | tf_op jit(solution)/shard_map/pallas_call | solution.py:135
  17.2 2.0 collective-permute-start.2
  19.2 2.1 collective-permute-start.3
  24.1 7.3 %shard_map.140 = (bf16[4,128,512]{2,1,0:T(8,128)(2,1)S(1)}, bf16[4,128,512]{2,1,0:T(8,128)(2,1)S(1)}, bf16[4,128,512]{2,1,0:T(8,128)(2,1)S(1)}, bf16[4,128,512]{...) custom-call(s32[2]{0:T(128)S(1)} %pad_add_fusion.1.place, ...), custom_call_target="tpu_custom_call" | custom-call | flops 2147483648 | bytes 8388608 | tf_op jit(solution)/shard_map/pallas_call | solution.py:135
  33.6 2.9 %collective-permute-start.5 = (bf16[4,128,512]{2,1,0:T(8,128)(2,1)}, bf16[4,128,512]{2,1,0:T(8,128)(2,1)S(1)}, u32[]{:S(2)}, u32[]{:S(2)}) collective-permute-start(bf16[4,128,512]{2,1,0:T(8,128)(2,1)} %get-tuple-element.56), channel_id=1, source_target_pairs={{0,12},{1,13},{2,14},{3,15},{4,0},{5,1},{6,2},{7,3},{8,4},{9,5},{1... | collective-permute-start | bytes 1572872 | tf_op jit(solution)/shard_map/ppermute | solution.py:42
  36.5 3.2 %collective-permute-start.7 = (bf16[4,128,512]{2,1,0:T(8,128)(2,1)}, bf16[4,128,512]{2,1,0:T(8,128)(2,1)}, u32[]{:S(2)}, u32[]{:S(2)}) collective-permute-start(bf16[4,128,512]{2,1,0:T(8,128)(2,1)} %get-tuple-element.59), channel_id=1, source_target_pairs={{0,3},{1,0},{2,1},{3,2},{4,7},{5,4},{6,5},{7,6},{8,11},{9,8},{10,9... | collective-permute-start | bytes 1572872 | tf_op jit(solution)/shard_map/ppermute | solution.py:42
  39.9 4.3 %constant_dynamic-slice_fusion.2 = (bf16[1,8,1,3072]{3,2,1,0:T(2,128)(2,1)S(1)}, bf16[1,8,1,3072]{3,2,1,0:T(2,128)(2,1)S(1)}, bf16[1,8,1,3072]{3,2,1,0:T(2,128)(2,1)S(1)}, bf16[1,8,1,3072]{3,2,1,0:T(2,128)(2,1)S(1)}) fusion(bf16[8,8,8,3072]{3,2,1,0:T(8,128)(2,1)} %bitcast.111, s32[]{:T(128)} %bitcast.3, s32[]{:T(128)} %bitcast.4, s32[]{:T(128)} %bitcast.6, ...), kind=kLoop, calls=%fused_computation.51 | loop fusion | bytes 393240 | tf_op jit(solution)/shard_map/dynamic_slice | solution.py:19
  44.4 3.3 %collective-permute-done.4.refs_1_ = bf16[4,128,512]{2,1,0:T(8,128)(2,1)S(1)} collective-permute-done((bf16[4,128,512]{2,1,0:T(8,128)(2,1)}, bf16[4,128,512]{2,1,0:T(8,128)(2,1)S(1)}, u32[]{:S(2)}, u32[]{:S(2)}) %collective-permute-start.4) | collective-permute-done | bytes 524320 | tf_op jit(solution)/shard_map/ppermute | solution.py:42
  47.7 2.7 %collective-permute-done.6.refs_4_ = bf16[4,128,512]{2,1,0:T(8,128)(2,1)S(1)} collective-permute-done((bf16[4,128,512]{2,1,0:T(8,128)(2,1)}, bf16[4,128,512]{2,1,0:T(8,128)(2,1)S(1)}, u32[]{:S(2)}, u32[]{:S(2)}) %collective-permute-start.6) | collective-permute-done | bytes 524320 | tf_op jit(solution)/shard_map/ppermute | solution.py:42
  50.3 2.1 shard_map.143
  53.9 4.3 %collective-permute-start.9 = (bf16[128,512]{1,0:T(8,128)(2,1)}, bf16[128,512]{1,0:T(8,128)(2,1)S(1)}, u32[]{:S(2)}, u32[]{:S(2)}) collective-permute-start(bf16[128,512]{1,0:T(8,128)(2,1)} %get-tuple-element.62), channel_id=1, source_target_pairs={{0,2},{1,3},{2,0},{3,1},{4,6},{5,7},{6,4},{7,5},{8,10},{9,11},{10,... | collective-permute-start | bytes 393224 | tf_op jit(solution)/shard_map/ppermute | solution.py:42
  63.5 3.8 %collective-permute-done.11 = bf16[128,512]{1,0:T(8,128)(2,1)S(1)} collective-permute-done((bf16[128,512]{1,0:T(8,128)(2,1)}, bf16[128,512]{1,0:T(8,128)(2,1)S(1)}, u32[]{:S(2)}, u32[]{:S(2)}) %collective-permute-start.11) | collective-permute-done | bytes 131104 | tf_op jit(solution)/shard_map/ppermute | solution.py:42
  70.9 5.8 %all-to-all-start = ((bf16[16,144,384]{2,1,0:T(8,128)(2,1)}), bf16[16,144,384]{2,1,0:T(8,128)(2,1)S(1)}, u32[]{:S(2)}, u32[]{:S(2)}) async-start(bf16[16,144,384]{2,1,0:T(8,128)(2,1)} %bitcast.24), calls=%async_computation | async-start | bytes 3538944 | tf_op jit(solution)/shard_map/all_to_all | solution.py:15
  76.8 20.1 %all-to-all-done.message = bf16[16,144,384]{2,1,0:T(8,128)(2,1)S(1)} async-done(((bf16[16,144,384]{2,1,0:T(8,128)(2,1)}), bf16[16,144,384]{2,1,0:T(8,128)(2,1)S(1)}, u32[]{:S(2)}, u32[]{:S(2)}) %all-to-all-start) | async-done | bytes 1769504 | tf_op jit(solution)/shard_map/all_to_all | solution.py:15
  96.9 2.3 shard_map.144
  99.2 7.2 %all-to-all-start.1 = ((bf16[16,128,384]{2,1,0:T(8,128)(2,1)}), bf16[16,128,384]{2,1,0:T(8,128)(2,1)S(1)}, u32[]{:S(2)}, u32[]{:S(2)}) async-start(bf16[16,128,384]{2,1,0:T(8,128)(2,1)} %get-tuple-element.68), calls=%async_computation.1 | async-start | bytes 3145728 | tf_op jit(solution)/shard_map/all_to_all | solution.py:15
  107.6 3.9 %all-gather.12.cloned.1.call-done = bf16[32,8,3072]{2,1,0:T(8,128)(2,1)} async-done(((bf16[2,8,3072]{2,1,0:T(8,128)(2,1)}), bf16[32,8,3072]{2,1,0:T(8,128)(2,1)}) %all-gather.12.cloned.1.call-update) | async-done | bytes 1572880 | tf_op jit(solution)/shard_map/all_gather | solution.py:523
  112.7 11.2 %all-to-all-done.1.pieces = bf16[16,128,384]{2,1,0:T(8,128)(2,1)S(1)} async-done(((bf16[16,128,384]{2,1,0:T(8,128)(2,1)}), bf16[16,128,384]{2,1,0:T(8,128)(2,1)S(1)}, u32[]{:S(2)}, u32[]{:S(2)}) %all-to-all-start.1) | async-done | bytes 1572896 | tf_op jit(solution)/shard_map/all_to_all | solution.py:15
  125.1 9.4 %shard_map.145 = (bf16[256,3072]{1,0:T(8,128)(2,1)}, f32[256,512]{1,0:T(8,128)}, f32[256,512]{1,0:T(8,128)}, bf16[16,16,3072]{2,1,0:T(8,128)(2,1)}) custom-call(bf16[16,128,384]{2,1,0:T(8,128)(2,1)} %copy-done.9, f32[1,3072]{1,0:T(1,128)} %bitcast.93, bf16[2,128,512]{2,1,0:T(8,128)(2,1)} %fusion.10.order, bf16[8,128]{1,0:T(8,128)(2,1)} %slice_bitcast_fusion.other, ...), custom_call_target="tpu_custom_call" | custom-call | flops 2415919104 | bytes 17301504 | tf_op jit(solution)/shard_map/pallas_call | solution.py:413
  134.5 3.7 %all-to-all-start.2 = ((bf16[16,16,3072]{2,1,0:T(8,128)(2,1)}), bf16[16,16,3072]{2,1,0:T(8,128)(2,1)S(1)}, u32[]{:S(2)}, u32[]{:S(2)}) async-start(bf16[16,16,3072]{2,1,0:T(8,128)(2,1)} %get-tuple-element.72.order), calls=%async_computation.2 | async-start | bytes 3145728 | tf_op jit(solution)/shard_map/all_to_all | solution.py:15
  138.3 4.6 %shard_map.146 = (bf16[256,512]{1,0:T(8,128)(2,1)}, bf16[256,512]{1,0:T(8,128)(2,1)}) custom-call(bf16[256,3072]{1,0:T(8,128)(2,1)} %bitcast.100, bf16[3072,512]{1,0:T(8,128)(2,1)} %down.1, f32[256,512]{1,0:T(8,128)} %get-tuple-element.70.gate, f32[256,512]{1,0:T(8,128)} %get-tuple-element.71.up, bf16[16,16,3072]{2,1,0:T(8,128)(2,1)} %get-tuple-element.72.order), custom_call_target="tpu_custom_call" | custom-call | flops 805306368 | bytes 6815744 | tf_op jit(solution)/shard_map/pallas_call | solution.py:218
  143.9 2.1 fusion.30
  146.0 2.2 fusion
  148.3 8.9 %all-to-all-done.2.terms = bf16[16,16,3072]{2,1,0:T(8,128)(2,1)S(1)} async-done(((bf16[16,16,3072]{2,1,0:T(8,128)(2,1)}), bf16[16,16,3072]{2,1,0:T(8,128)(2,1)S(1)}, u32[]{:S(2)}, u32[]{:S(2)}) %all-to-all-start.2) | async-done | bytes 1572896 | tf_op jit(solution)/shard_map/all_to_all | solution.py:15
  158.7 3.7 %all-to-all-start.3 = ((bf16[16,16,3072]{2,1,0:T(8,128)(2,1)}), bf16[16,16,3072]{2,1,0:T(8,128)(2,1)S(1)}, u32[]{:S(2)}, u32[]{:S(2)}) async-start(bf16[16,16,3072]{2,1,0:T(8,128)(2,1)} %bitcast.43), calls=%async_computation.3 | async-start | bytes 3145728 | tf_op jit(solution)/shard_map/all_to_all | solution.py:15
  164.3 18.7 %all-to-all-done.3.terms = bf16[16,16,3072]{2,1,0:T(8,128)(2,1)S(1)} async-done(((bf16[16,16,3072]{2,1,0:T(8,128)(2,1)}), bf16[16,16,3072]{2,1,0:T(8,128)(2,1)S(1)}, u32[]{:S(2)}, u32[]{:S(2)}) %all-to-all-start.3) | async-done | bytes 1572896 | tf_op jit(solution)/shard_map/all_to_all | solution.py:15
  183.3 9.9 %all_to_all.30.piece = bf16[8,16,384]{2,1,0:T(8,128)(2,1)S(1)} all-to-all(bf16[8,16,384]{2,1,0:T(8,128)(2,1)S(1)} %shard_map.148), channel_id=1, replica_groups=mesh['dp'=8,'mp'=16] {'dp'}, dimensions={0} | all-to-all | bytes 196608 | tf_op jit(solution)/shard_map/all_to_all | solution.py:15
  194.5 3.7 %all-to-all-start.5 = ((bf16[16,8,16,384]{3,2,1,0:T(8,128)(2,1)}), bf16[16,8,16,384]{3,2,1,0:T(8,128)(2,1)S(1)}, u32[]{:S(2)}, u32[]{:S(2)}) async-start(bf16[16,8,16,384]{3,2,1,0:T(8,128)(2,1)} %shard_map.149), calls=%async_computation.5 | async-start | bytes 3145728 | tf_op jit(solution)/shard_map/all_to_all | solution.py:15
  210.1 3.3 %select_bitcast_fusion.3 = (bf16[8,1,3072]{2,0,1:T(8,128)(2,1)S(1)}, bf16[8,1,3072]{2,0,1:T(8,128)(2,1)S(1)}, bf16[8,1,3072]{2,0,1:T(8,128)(2,1)S(1)}, bf16[8,1,3072]{2,0,1:T(8,128)(2,1)S(1)}) fusion(bf16[8,32,3072]{2,1,0:T(8,128)(2,1)} %bitcast.112, s32[]{:T(128)S(6)} %select_n.131, s32[]{:T(128)S(6)} %mul.54, pred[]{:T(512)} %get-tuple-element.84, ...), kind=kLoop, calls=%fused_computation.34 | loop fusion | flops 98304 | bytes 393252 | tf_op jit(solution)/shard_map/jit(_where)/select_n | solution.py:603
  214.3 7.9 %all-to-all-done.5 = bf16[16,8,16,384]{3,2,1,0:T(8,128)(2,1)S(1)} async-done(((bf16[16,8,16,384]{3,2,1,0:T(8,128)(2,1)}), bf16[16,8,16,384]{3,2,1,0:T(8,128)(2,1)S(1)}, u32[]{:S(2)}, u32[]{:S(2)}) %all-to-all-start.5) | async-done | bytes 1572896 | tf_op jit(solution)/shard_map/all_to_all | solution.py:15
  222.1 3.8 %fusion.7 = f32[512,384]{1,0:T(8,128)} fusion(bf16[16,8,16,384]{3,2,1,0:T(8,128)(2,1)S(1)} %all-to-all-done.5, bf16[8,16,16,512]{3,2,0,1:T(8,128)(2,1)} %all-gather.8.cloned.1.call-done), kind=kOutput, calls=%fused_computation.10 | convolution fusion | flops 805306368 | bytes 4456448 | tf_op jit(solution)/shard_map/dot_general | solution.py:586
  (103 shorter events, 30.8 us)
Async XLA Ops:
  7.2 32.7 %all-gather.10.cloned.1.call-start = ((), (), s32[]{:S(2)}) async-start(), calls=%async_computation.7 | async-start | bytes 3538944 | tf_op jit(solution)/shard_map/all_gather | solution.py:510
  9.2 102.2 %all-gather.12.cloned.1.call-start = ((), (), s32[]{:S(2)}) async-start(), calls=%async_computation.8 | async-start | bytes 1671168 | tf_op jit(solution)/shard_map/all_gather | solution.py:523
  10.3 11.0 %copy-start.14 = (s32[16]{0:T(128)S(1)}, s32[16]{0:T(128)}, u32[]{:S(2)}) copy-start(s32[16]{0:T(128)} %param.21) | copy-start | bytes 196
  10.3 13.7 %copy-start.1 = (bf16[256,512]{1,0:T(8,128)(2,1)S(1)}, bf16[256,512]{1,0:T(8,128)(2,1)}, u32[]{:S(2)}) copy-start(bf16[256,512]{1,0:T(8,128)(2,1)} %left.3) | copy-start | bytes 786436
  13.9 17.5 %collective-permute-start = (bf16[4,64,512]{2,1,0:T(8,128)(2,1)S(1)}, bf16[4,64,512]{2,1,0:T(8,128)(2,1)S(1)}, u32[]{:S(2)}, u32[]{:S(2)}) collective-permute-start(bf16[4,64,512]{2,1,0:T(8,128)(2,1)S(1)} %get-tuple-element.49), channel_id=1, source_target_pairs={{0,4},{1,5},{2,6},{3,7},{4,8},{5,9},{6,10},{7,11},{8,12},{9,13},{1... | collective-permute-start | bytes 786440 | tf_op jit(solution)/shard_map/ppermute | solution.py:42
  15.6 15.8 %collective-permute-start.1 = (bf16[4,64,512]{2,1,0:T(8,128)(2,1)S(1)}, bf16[4,64,512]{2,1,0:T(8,128)(2,1)S(1)}, u32[]{:S(2)}, u32[]{:S(2)}) collective-permute-start(bf16[4,64,512]{2,1,0:T(8,128)(2,1)S(1)} %get-tuple-element.50), channel_id=1, source_target_pairs={{0,12},{1,13},{2,14},{3,15},{4,0},{5,1},{6,2},{7,3},{8,4},{9,5},{1... | collective-permute-start | bytes 786440 | tf_op jit(solution)/shard_map/ppermute | solution.py:42
  17.2 14.2 %collective-permute-start.2 = (bf16[4,64,512]{2,1,0:T(8,128)(2,1)S(1)}, bf16[4,64,512]{2,1,0:T(8,128)(2,1)S(1)}, u32[]{:S(2)}, u32[]{:S(2)}) collective-permute-start(bf16[4,64,512]{2,1,0:T(8,128)(2,1)S(1)} %get-tuple-element.53), channel_id=1, source_target_pairs={{0,1},{1,2},{2,3},{3,0},{4,5},{5,6},{6,7},{7,4},{8,9},{9,10},{10,1... | collective-permute-start | bytes 786440 | tf_op jit(solution)/shard_map/ppermute | solution.py:42
  19.2 12.2 %collective-permute-start.3 = (bf16[4,64,512]{2,1,0:T(8,128)(2,1)S(1)}, bf16[4,64,512]{2,1,0:T(8,128)(2,1)S(1)}, u32[]{:S(2)}, u32[]{:S(2)}) collective-permute-start(bf16[4,64,512]{2,1,0:T(8,128)(2,1)S(1)} %get-tuple-element.54), channel_id=1, source_target_pairs={{0,3},{1,0},{2,1},{3,2},{4,7},{5,4},{6,5},{7,6},{8,11},{9,8},{10,9... | collective-permute-start | bytes 786440 | tf_op jit(solution)/shard_map/ppermute | solution.py:42
  33.3 14.4 %collective-permute-start.4 = (bf16[4,128,512]{2,1,0:T(8,128)(2,1)}, bf16[4,128,512]{2,1,0:T(8,128)(2,1)S(1)}, u32[]{:S(2)}, u32[]{:S(2)}) collective-permute-start(bf16[4,128,512]{2,1,0:T(8,128)(2,1)} %get-tuple-element.55), channel_id=1, source_target_pairs={{0,4},{1,5},{2,6},{3,7},{4,8},{5,9},{6,10},{7,11},{8,12},{9,13},{1... | collective-permute-start | bytes 1572872 | tf_op jit(solution)/shard_map/ppermute | solution.py:42
  33.6 14.0 %collective-permute-start.5 = (bf16[4,128,512]{2,1,0:T(8,128)(2,1)}, bf16[4,128,512]{2,1,0:T(8,128)(2,1)S(1)}, u32[]{:S(2)}, u32[]{:S(2)}) collective-permute-start(bf16[4,128,512]{2,1,0:T(8,128)(2,1)} %get-tuple-element.56), channel_id=1, source_target_pairs={{0,12},{1,13},{2,14},{3,15},{4,0},{5,1},{6,2},{7,3},{8,4},{9,5},{1... | collective-permute-start | bytes 1572872 | tf_op jit(solution)/shard_map/ppermute | solution.py:42
  36.5 13.8 %collective-permute-start.6 = (bf16[4,128,512]{2,1,0:T(8,128)(2,1)}, bf16[4,128,512]{2,1,0:T(8,128)(2,1)S(1)}, u32[]{:S(2)}, u32[]{:S(2)}) collective-permute-start(bf16[4,128,512]{2,1,0:T(8,128)(2,1)} %get-tuple-element.58), channel_id=1, source_target_pairs={{0,1},{1,2},{2,3},{3,0},{4,5},{5,6},{6,7},{7,4},{8,9},{9,10},{10,1... | collective-permute-start | bytes 1572872 | tf_op jit(solution)/shard_map/ppermute | solution.py:42
  36.5 13.8 %collective-permute-start.7 = (bf16[4,128,512]{2,1,0:T(8,128)(2,1)}, bf16[4,128,512]{2,1,0:T(8,128)(2,1)}, u32[]{:S(2)}, u32[]{:S(2)}) collective-permute-start(bf16[4,128,512]{2,1,0:T(8,128)(2,1)} %get-tuple-element.59), channel_id=1, source_target_pairs={{0,3},{1,0},{2,1},{3,2},{4,7},{5,4},{6,5},{7,6},{8,11},{9,8},{10,9... | collective-permute-start | bytes 1572872 | tf_op jit(solution)/shard_map/ppermute | solution.py:42
  44.2 6.1 %copy-start.11 = (bf16[1,8,1,3072]{3,2,1,0:T(2,128)(2,1)}, bf16[1,8,1,3072]{3,2,1,0:T(2,128)(2,1)S(1)}, u32[]{:S(2)}) copy-start(bf16[1,8,1,3072]{3,2,1,0:T(2,128)(2,1)S(1)} %get-tuple-element.93) | copy-start | bytes 147460
  44.3 13.9 %copy-start.2 = (bf16[2,8,3072]{2,1,0:T(8,128)(2,1)}, bf16[2,8,3072]{2,1,0:T(8,128)(2,1)S(1)}, u32[]{:S(2)}) copy-start(bf16[2,8,3072]{2,1,0:T(8,128)(2,1)S(1)} %pad_maximum_fusion.2.refs_7_) | copy-start | bytes 294916
  50.3 17.9 %copy-start.13 = (f32[512]{0:T(512)S(1)}, f32[512]{0:T(512)}, u32[]{:S(2)}) copy-start(f32[512]{0:T(512)} %param.18) | copy-start | bytes 6148
  53.7 14.5 %copy-start.10 = (bf16[256,512]{1,0:T(8,128)(2,1)S(1)}, bf16[256,512]{1,0:T(8,128)(2,1)}, u32[]{:S(2)}) copy-start(bf16[256,512]{1,0:T(8,128)(2,1)} %param.17) | copy-start | bytes 786436
  53.7 7.7 %collective-permute-start.8 = (bf16[128,512]{1,0:T(8,128)(2,1)}, bf16[128,512]{1,0:T(8,128)(2,1)S(1)}, u32[]{:S(2)}, u32[]{:S(2)}) collective-permute-start(bf16[128,512]{1,0:T(8,128)(2,1)} %get-tuple-element.61), channel_id=1, source_target_pairs={{0,1},{1,2},{2,3},{3,0},{4,5},{5,6},{6,7},{7,4},{8,9},{9,10},{10,1... | collective-permute-start | bytes 393224 | tf_op jit(solution)/shard_map/ppermute | solution.py:42
  53.9 9.0 %collective-permute-start.9 = (bf16[128,512]{1,0:T(8,128)(2,1)}, bf16[128,512]{1,0:T(8,128)(2,1)S(1)}, u32[]{:S(2)}, u32[]{:S(2)}) collective-permute-start(bf16[128,512]{1,0:T(8,128)(2,1)} %get-tuple-element.62), channel_id=1, source_target_pairs={{0,2},{1,3},{2,0},{3,1},{4,6},{5,7},{6,4},{7,5},{8,10},{9,11},{10,... | collective-permute-start | bytes 393224 | tf_op jit(solution)/shard_map/ppermute | solution.py:42
  58.2 5.2 %collective-permute-start.10 = (bf16[128,512]{1,0:T(8,128)(2,1)}, bf16[128,512]{1,0:T(8,128)(2,1)S(1)}, u32[]{:S(2)}, u32[]{:S(2)}) collective-permute-start(bf16[128,512]{1,0:T(8,128)(2,1)} %get-tuple-element.63), channel_id=1, source_target_pairs={{0,3},{1,0},{2,1},{3,2},{4,7},{5,4},{6,5},{7,6},{8,11},{9,8},{10,9... | collective-permute-start | bytes 393224 | tf_op jit(solution)/shard_map/ppermute | solution.py:42
  58.3 10.1 %copy-start.15 = (bf16[512,3072]{1,0:T(8,128)(2,1)S(1)}, bf16[512,3072]{1,0:T(8,128)(2,1)}, u32[]{:S(2)}) copy-start(bf16[512,3072]{1,0:T(8,128)(2,1)} %param.19) | copy-start | bytes 9437188
  59.4 7.9 %collective-permute-start.11 = (bf16[128,512]{1,0:T(8,128)(2,1)}, bf16[128,512]{1,0:T(8,128)(2,1)S(1)}, u32[]{:S(2)}, u32[]{:S(2)}) collective-permute-start(bf16[128,512]{1,0:T(8,128)(2,1)} %copy-done.6), channel_id=1, source_target_pairs={{0,4},{1,5},{2,6},{3,7},{4,8},{5,9},{6,10},{7,11},{8,12},{9,13},{1... | collective-permute-start | bytes 393224 | tf_op jit(solution)/shard_map/ppermute | solution.py:42
  59.5 7.8 %collective-permute-start.12 = (bf16[128,512]{1,0:T(8,128)(2,1)}, bf16[128,512]{1,0:T(8,128)(2,1)S(1)}, u32[]{:S(2)}, u32[]{:S(2)}) collective-permute-start(bf16[128,512]{1,0:T(8,128)(2,1)} %copy-done.5), channel_id=1, source_target_pairs={{0,8},{1,9},{2,10},{3,11},{4,12},{5,13},{6,14},{7,15},{8,0},{9,1},... | collective-permute-start | bytes 393224 | tf_op jit(solution)/shard_map/ppermute | solution.py:42
  61.4 6.7 %collective-permute-start.13 = (bf16[128,512]{1,0:T(8,128)(2,1)S(1)}, bf16[128,512]{1,0:T(8,128)(2,1)S(1)}, u32[]{:S(2)}, u32[]{:S(2)}) collective-permute-start(bf16[128,512]{1,0:T(8,128)(2,1)S(1)} %get-tuple-element.67), channel_id=1, source_target_pairs={{0,12},{1,13},{2,14},{3,15},{4,0},{5,1},{6,2},{7,3},{8,4},{9,5},{1... | collective-permute-start | bytes 393224 | tf_op jit(solution)/shard_map/ppermute | solution.py:42
  70.9 26.0 %copy-start.4 = (s32[256]{0:T(256)S(1)}, s32[256]{0:T(256)}, u32[]{:S(2)}) copy-start(s32[256]{0:T(256)} %param.20) | copy-start | bytes 3076
  70.9 26.0 %all-to-all-start = ((bf16[16,144,384]{2,1,0:T(8,128)(2,1)}), bf16[16,144,384]{2,1,0:T(8,128)(2,1)S(1)}, u32[]{:S(2)}, u32[]{:S(2)}) async-start(bf16[16,144,384]{2,1,0:T(8,128)(2,1)} %bitcast.24), calls=%async_computation | async-start | bytes 3538944 | tf_op jit(solution)/shard_map/all_to_all | solution.py:15
  99.2 24.8 %all-to-all-start.1 = ((bf16[16,128,384]{2,1,0:T(8,128)(2,1)}), bf16[16,128,384]{2,1,0:T(8,128)(2,1)S(1)}, u32[]{:S(2)}, u32[]{:S(2)}) async-start(bf16[16,128,384]{2,1,0:T(8,128)(2,1)} %get-tuple-element.68), calls=%async_computation.1 | async-start | bytes 3145728 | tf_op jit(solution)/shard_map/all_to_all | solution.py:15
  134.5 22.7 %all-to-all-start.2 = ((bf16[16,16,3072]{2,1,0:T(8,128)(2,1)}), bf16[16,16,3072]{2,1,0:T(8,128)(2,1)S(1)}, u32[]{:S(2)}, u32[]{:S(2)}) async-start(bf16[16,16,3072]{2,1,0:T(8,128)(2,1)} %get-tuple-element.72.order), calls=%async_computation.2 | async-start | bytes 3145728 | tf_op jit(solution)/shard_map/all_to_all | solution.py:15
  138.3 71.8 %all-gather.14.cloned.1.call-start = ((), (), s32[]{:S(2)}) async-start(), calls=%async_computation.9 | async-start | bytes 1769472 | tf_op jit(solution)/shard_map/all_gather | solution.py:593
  158.1 24.8 %copy-start.3 = (f32[3072]{0:T(1024)S(1)}, f32[3072]{0:T(1024)}, u32[]{:S(2)}) copy-start(f32[3072]{0:T(1024)} %param.24) | copy-start | bytes 36868
  158.2 56.1 %all-gather.8.cloned.1.call-start = ((), (), s32[]{:S(2)}) async-start(), calls=%async_computation.6 | async-start | bytes 2359296 | tf_op jit(solution)/shard_map/all_gather | solution.py:557
  158.7 24.2 %all-to-all-start.3 = ((bf16[16,16,3072]{2,1,0:T(8,128)(2,1)}), bf16[16,16,3072]{2,1,0:T(8,128)(2,1)S(1)}, u32[]{:S(2)}, u32[]{:S(2)}) async-start(bf16[16,16,3072]{2,1,0:T(8,128)(2,1)} %bitcast.43), calls=%async_computation.3 | async-start | bytes 3145728 | tf_op jit(solution)/shard_map/all_to_all | solution.py:15
  194.5 27.7 %all-to-all-start.5 = ((bf16[16,8,16,384]{3,2,1,0:T(8,128)(2,1)}), bf16[16,8,16,384]{3,2,1,0:T(8,128)(2,1)S(1)}, u32[]{:S(2)}, u32[]{:S(2)}) async-start(bf16[16,8,16,384]{3,2,1,0:T(8,128)(2,1)} %shard_map.149), calls=%async_computation.5 | async-start | bytes 3145728 | tf_op jit(solution)/shard_map/all_to_all | solution.py:15
  (7 other events, 13.3 us)
Sparse Core Ops, SparseCore 0:
  9.7 30.1 all-gather.9
  58.4 53.0 all-gather.11
  158.3 22.2 all-gather.13
  182.1 25.0 all-gather.7

commit v11 on v7

--- a/solution.py
+++ b/solution.py
@@ -13,6 +13,10 @@
 
 def exchange(pieces, axis):
     return lax.all_to_all(pieces, axis, split_axis=0, concat_axis=0, tiled=True)
+
+
+def take(array, starts, sizes):
+    return lax.dynamic_slice(array, starts, sizes, allow_negative_indices=False)
 
 
 def three_parts(value):
@@ -495,7 +499,7 @@
 
     ids = jnp.arange(block_owner.shape[0], dtype=jnp.int32)
     my_ids = dp * blocks + jnp.arange(blocks, dtype=jnp.int32)
-    my_owner = lax.dynamic_slice_in_dim(block_owner, dp * blocks, blocks)
+    my_owner = take(block_owner, (dp * blocks,), (blocks,))
     my_slot = jnp.sum(
         (block_owner[None, :] == my_owner[:, None]) & (ids[None, :] < my_ids[:, None]),
         axis=1,
@@ -507,7 +511,7 @@
         picked = []
         for k in range(blocks):
             at = (my_owner[k], 0, my_slot[k], 0)
-            piece = lax.dynamic_slice(everyone, at, (1, rows, 1, student_width))
+            piece = take(everyone, at, (1, rows, 1, student_width))
             picked.append(piece.reshape(rows, student_width))
         return jnp.stack(picked)
 
@@ -559,16 +563,18 @@
     dn, output = lax.optimization_barrier((dn, output))
     dn = exchange(dn.reshape(n_mp, mine_rows, student_width), "mp")
     here = mp * mine_rows
-    state_rows = lax.dynamic_slice_in_dim(
-        state.reshape(blocks, BLK, student_width), mp * rows, rows, 1
+    state_rows = take(
+        state.reshape(blocks, BLK, student_width),
+        (0, mp * rows, 0),
+        (blocks, rows, student_width),
     )
     out_rows = home(output, state_rows.reshape(mine_rows, student_width))
     dproj = slope(
         dn,
-        lax.dynamic_slice(
+        take(
             dy, ((mp % groups) * blocks, mp // groups, 0, 0), (blocks, 1, rows, student_width)
         ).reshape(mine_rows, student_width),
-        lax.dynamic_slice_in_dim(state, here, mine_rows, 0),
+        take(state, (here, 0), (mine_rows, student_width)),
         student_gain,
         n_dp,
         out_rows,
@@ -590,7 +596,7 @@
         chosen = mine & (ranks == slot)
         index = jnp.sum(jnp.where(chosen, ids, 0))
         at = (index // blocks, (index % blocks) * rows, 0)
-        piece = lax.dynamic_slice(back, at, (1, rows, student_width))[0]
+        piece = take(back, at, (1, rows, student_width))[0]
         picks.append(jnp.where(jnp.any(chosen), piece, jnp.zeros((), half)))
     student_out = jnp.stack(picks, axis=1)
     return (student_out[None], adapter_grad)

time: 229 us -> 234 us (1.022)
  between operations: 31.7 us -> 24.4 us
  waiting for transfers between devices: 79.1 us -> 85.8 us
  local copies, waits for them, and re-layouts: 11.1 us -> 16.1 us
    all_to_all x5, waiting for transfers between devices: 63.3 us -> 72.6 us  [exchange(): return lax.all_to_all(pieces, axis, split_axis=0, concat_axis=0, tiled=True)]
    ppermute x14, waiting for transfers between devices: 15.1 us -> 12.5 us  [step(): return lax.ppermute(value, 'mp', pairs)]
    dynamic_slice x3, local copies, waits for them, and re-layouts: 1.81 us -> 4.27 us  [take(): return lax.dynamic_slice(array, starts, sizes, allow_negative_indices=False)]
    another operation x1, local copies, waits for them, and re-layouts: 0.84 us -> 3.29 us  [fetch(): return jnp.stack(picked)]
  transfers between devices with their start and end apart: 24 -> 24, of which waited for: 12 -> 12; matrix products, arithmetic and copies ran while one was open for 9% -> 11% of each run, Pallas kernels for 14% -> 14%
where the time goes in v11:
time: 234 us; the launch traced here: 233 us
  waiting for transfers between devices  85.8 us (37%)
  starting transfers between devices  45.5 us (19%)
  Pallas kernels  32.6 us (14%)
  between operations  24.4 us (10%)
  local copies, waits for them, and re-layouts  16.1 us (7%)
  blocking collectives  10.3 us (4%)
  matrix products  10 us (4%)
  other arithmetic  8 us (3%)
    all_to_all x5, waiting for transfers between devices, exchange(): return lax.all_to_all(pieces, axis, split_axis=0, concat_axis=0, tiled=True)  72.6 us
    all_to_all x5, starting transfers between devices, exchange(): return lax.all_to_all(pieces, axis, split_axis=0, concat_axis=0, tiled=True)  23.8 us
    ppermute x14, starting transfers between devices, step(): return lax.ppermute(value, 'mp', pairs)  21.6 us
    ppermute x14, waiting for transfers between devices, step(): return lax.ppermute(value, 'mp', pairs)  12.5 us
    pallas_call x2, Pallas kernels, terms(): pl.pallas_call(kernel, in_specs=[scalars, whole, pl.BlockSpec(memory_spac...  10.9 us
    all_to_all x1, blocking collectives, exchange(): return lax.all_to_all(pieces, axis, split_axis=0, concat_axis=0, tiled=True)  10.3 us
    pallas_call x1, Pallas kernels, forward(): pl.pallas_call(forward_kernel, in_specs=[whole, whole, pl.BlockSpec(memor...  9.54 us
    unnamed x29, local copies, waits for them, and re-layouts  5.45 us
  transfers between devices with their start and end apart: 24, of which 12 were waited for; matrix products, arithmetic and copies ran while one was open for 11% of the time, Pallas kernels for 14%

profile of v11, /device:TPU:0, one launch (start us, length us, event | category | flops | bytes accessed | tf_op | source)
XLA Modules:
  0.0 232.8 jit_solution(17500297260412330390)
XLA Ops:
  10.0 3.6 %shard_map.141 = (bf16[4,64,512]{2,1,0:T(8,128)(2,1)S(1)}, bf16[4,64,512]{2,1,0:T(8,128)(2,1)S(1)}, bf16[4,64,512]{2,1,0:T(8,128)(2,1)S(1)}, bf16[4,64,512]{2,1,0:T(8,128)(2,1)S(1)}) custom-call(s32[2]{0:T(128)S(1)} %pad_add_fusion.1.place, bf16[256,512]{1,0:T(8,128)(2,1)S(1)} %copy-done, bf16[512,8192]{1,0:T(8,128)(2,1)} %right.3), custom_call_target="tpu_custom_call" | custom-call | flops 536870912 | bytes 4194304 | tf_op jit(solution)/shard_map/pallas_call | solution.py:135
  16.9 2.0 collective-permute-start.2
  18.9 2.1 collective-permute-start.3
  23.3 7.3 %shard_map.140 = (bf16[4,128,512]{2,1,0:T(8,128)(2,1)S(1)}, bf16[4,128,512]{2,1,0:T(8,128)(2,1)S(1)}, bf16[4,128,512]{2,1,0:T(8,128)(2,1)S(1)}, bf16[4,128,512]{...) custom-call(s32[2]{0:T(128)S(1)} %pad_add_fusion.1.place, ...), custom_call_target="tpu_custom_call" | custom-call | flops 2147483648 | bytes 8388608 | tf_op jit(solution)/shard_map/pallas_call | solution.py:135
  30.7 1.9 shard_map.142
  32.9 2.9 %collective-permute-start.5 = (bf16[4,128,512]{2,1,0:T(8,128)(2,1)}, bf16[4,128,512]{2,1,0:T(8,128)(2,1)S(1)}, u32[]{:S(2)}, u32[]{:S(2)}) collective-permute-start(bf16[4,128,512]{2,1,0:T(8,128)(2,1)} %get-tuple-element.56), channel_id=1, source_target_pairs={{0,12},{1,13},{2,14},{3,15},{4,0},{5,1},{6,2},{7,3},{8,4},{9,5},{1... | collective-permute-start | bytes 1572872 | tf_op jit(solution)/shard_map/ppermute | solution.py:42
  35.8 3.2 %collective-permute-start.7 = (bf16[4,128,512]{2,1,0:T(8,128)(2,1)}, bf16[4,128,512]{2,1,0:T(8,128)(2,1)S(1)}, u32[]{:S(2)}, u32[]{:S(2)}) collective-permute-start(bf16[4,128,512]{2,1,0:T(8,128)(2,1)} %get-tuple-element.59), channel_id=1, source_target_pairs={{0,3},{1,0},{2,1},{3,2},{4,7},{5,4},{6,5},{7,6},{8,11},{9,8},{10,9... | collective-permute-start | bytes 1572872 | tf_op jit(solution)/shard_map/ppermute | solution.py:42
  39.0 3.3 %constant_dynamic-slice_fusion.2 = (bf16[1,8,1,3072]{3,1,2,0:T(8,128)(2,1)S(1)}, bf16[1,8,1,3072]{3,1,2,0:T(8,128)(2,1)S(1)}) fusion(bf16[8,8,4,3072]{3,1,2,0:T(8,128)(2,1)} %all-gather.10.cloned.1.call-done, s32[]{:T(128)} %bitcast, s32[]{:T(128)} %bitcast.1, s32[]{:T(128)} %bitcast.3, s32[]{:T(128)} %bitcast.4), kind=kLoop, calls=%fused_computation.50 | loop fusion | bytes 196624 | tf_op jit(solution)/shard_map/dynamic_slice | solution.py:19
  42.3 4.6 %collective-permute-done.4.refs_1_ = bf16[4,128,512]{2,1,0:T(8,128)(2,1)S(1)} collective-permute-done((bf16[4,128,512]{2,1,0:T(8,128)(2,1)}, bf16[4,128,512]{2,1,0:T(8,128)(2,1)S(1)}, u32[]{:S(2)}, u32[]{:S(2)}) %collective-permute-start.4) | collective-permute-done | bytes 524320 | tf_op jit(solution)/shard_map/ppermute | solution.py:42
  46.9 2.7 %collective-permute-done.6.refs_4_ = bf16[4,128,512]{2,1,0:T(8,128)(2,1)S(1)} collective-permute-done((bf16[4,128,512]{2,1,0:T(8,128)(2,1)}, bf16[4,128,512]{2,1,0:T(8,128)(2,1)S(1)}, u32[]{:S(2)}, u32[]{:S(2)}) %collective-permute-start.6) | collective-permute-done | bytes 524320 | tf_op jit(solution)/shard_map/ppermute | solution.py:42
  50.7 4.3 %collective-permute-start.9 = (bf16[128,512]{1,0:T(8,128)(2,1)S(1)}, bf16[128,512]{1,0:T(8,128)(2,1)S(1)}, u32[]{:S(2)}, u32[]{:S(2)}) collective-permute-start(bf16[128,512]{1,0:T(8,128)(2,1)S(1)} %get-tuple-element.62), channel_id=1, source_target_pairs={{0,2},{1,3},{2,0},{3,1},{4,6},{5,7},{6,4},{7,5},{8,10},{9,11},{10,... | collective-permute-start | bytes 393224 | tf_op jit(solution)/shard_map/ppermute | solution.py:42
  55.1 1.9 collective-permute-start.12
  60.1 2.5 %collective-permute-done.11 = bf16[128,512]{1,0:T(8,128)(2,1)S(1)} collective-permute-done((bf16[128,512]{1,0:T(8,128)(2,1)S(1)}, bf16[128,512]{1,0:T(8,128)(2,1)S(1)}, u32[]{:S(2)}, u32[]{:S(2)}) %collective-permute-start.11) | collective-permute-done | bytes 131104 | tf_op jit(solution)/shard_map/ppermute | solution.py:42
  66.3 5.4 %all-to-all-start = ((bf16[16,144,384]{2,1,0:T(8,128)(2,1)}), bf16[16,144,384]{2,1,0:T(8,128)(2,1)S(1)}, u32[]{:S(2)}, u32[]{:S(2)}) async-start(bf16[16,144,384]{2,1,0:T(8,128)(2,1)} %bitcast.21), calls=%async_computation | async-start | bytes 3538944 | tf_op jit(solution)/shard_map/all_to_all | solution.py:15
  71.8 3.3 %dynamic-slice_bitcast_fusion.3 = (bf16[1,8,3072]{2,1,0:T(8,128)(2,1)S(1)}, bf16[1,8,3072]{2,1,0:T(8,128)(2,1)S(1)}) fusion(bf16[8,8,4,3072]{3,1,2,0:T(8,128)(2,1)} %all-gather.8.cloned.1.call-done, s32[]{:T(128)} %bitcast, s32[]{:T(128)} %bitcast.1, s32[]{:T(128)} %bitcast.3, s32[]{:T(128)} %bitcast.4), kind=kLoop, calls=%fused_computation.33 | loop fusion | bytes 196624 | tf_op jit(solution)/shard_map/stack;reshape | solution.py:516
  75.9 16.4 %all-to-all-done.message = bf16[16,144,384]{2,1,0:T(8,128)(2,1)S(1)} async-done(((bf16[16,144,384]{2,1,0:T(8,128)(2,1)}), bf16[16,144,384]{2,1,0:T(8,128)(2,1)S(1)}, u32[]{:S(2)}, u32[]{:S(2)}) %all-to-all-start) | async-done | bytes 1769504 | tf_op jit(solution)/shard_map/all_to_all | solution.py:15
  92.3 2.3 shard_map.144
  94.6 5.0 %all-to-all-start.1 = ((bf16[16,128,384]{2,1,0:T(8,128)(2,1)}), bf16[16,128,384]{2,1,0:T(8,128)(2,1)S(1)}, u32[]{:S(2)}, u32[]{:S(2)}) async-start(bf16[16,128,384]{2,1,0:T(8,128)(2,1)} %get-tuple-element.68), calls=%async_computation.1 | async-start | bytes 3145728 | tf_op jit(solution)/shard_map/all_to_all | solution.py:15
  100.7 18.8 %all-to-all-done.1.pieces = bf16[16,128,384]{2,1,0:T(8,128)(2,1)S(1)} async-done(((bf16[16,128,384]{2,1,0:T(8,128)(2,1)}), bf16[16,128,384]{2,1,0:T(8,128)(2,1)S(1)}, u32[]{:S(2)}, u32[]{:S(2)}) %all-to-all-start.1) | async-done | bytes 1572896 | tf_op jit(solution)/shard_map/all_to_all | solution.py:15
  120.7 9.5 %shard_map.145 = (bf16[256,3072]{1,0:T(8,128)(2,1)}, f32[256,512]{1,0:T(8,128)}, f32[256,512]{1,0:T(8,128)}, bf16[16,16,3072]{2,1,0:T(8,128)(2,1)}) custom-call(bf16[16,128,384]{2,1,0:T(8,128)(2,1)} %copy-done.6, f32[1,3072]{1,0:T(1,128)} %bitcast.84, bf16[2,128,512]{2,1,0:T(8,128)(2,1)} %fusion.10.order, bf16[3072,512]{1,0:T(8,128)(2,1)} %gate_hbm.1, ...), custom_call_target="tpu_custom_call" | custom-call | flops 2415919104 | bytes 17301504 | tf_op jit(solution)/shard_map/pallas_call | solution.py:413
  130.3 5.9 %all-to-all-start.2 = ((bf16[16,16,3072]{2,1,0:T(8,128)(2,1)}), bf16[16,16,3072]{2,1,0:T(8,128)(2,1)S(1)}, u32[]{:S(2)}, u32[]{:S(2)}) async-start(bf16[16,16,3072]{2,1,0:T(8,128)(2,1)} %get-tuple-element.72.order), calls=%async_computation.2 | async-start | bytes 3145728 | tf_op jit(solution)/shard_map/all_to_all | solution.py:15
  136.2 4.6 %shard_map.146 = (bf16[256,512]{1,0:T(8,128)(2,1)}, bf16[256,512]{1,0:T(8,128)(2,1)}) custom-call(bf16[256,3072]{1,0:T(8,128)(2,1)} %bitcast.90, bf16[3072,512]{1,0:T(8,128)(2,1)} %down.1, f32[256,512]{1,0:T(8,128)} %get-tuple-element.70.gate, f32[256,512]{1,0:T(8,128)} %get-tuple-element.71.up, bf16[16,16,3072]{2,1,0:T(8,128)(2,1)} %get-tuple-element.72.order), custom_call_target="tpu_custom_call" | custom-call | flops 805306368 | bytes 6815744 | tf_op jit(solution)/shard_map/pallas_call | solution.py:218
  141.8 2.1 fusion.30
  143.9 2.2 fusion
  146.2 10.4 %all-to-all-done.2.terms = bf16[16,16,3072]{2,1,0:T(8,128)(2,1)S(1)} async-done(((bf16[16,16,3072]{2,1,0:T(8,128)(2,1)}), bf16[16,16,3072]{2,1,0:T(8,128)(2,1)S(1)}, u32[]{:S(2)}, u32[]{:S(2)}) %all-to-all-start.2) | async-done | bytes 1572896 | tf_op jit(solution)/shard_map/all_to_all | solution.py:15
  158.1 3.7 %all-to-all-start.3 = ((bf16[16,16,3072]{2,1,0:T(8,128)(2,1)}), bf16[16,16,3072]{2,1,0:T(8,128)(2,1)S(1)}, u32[]{:S(2)}, u32[]{:S(2)}) async-start(bf16[16,16,3072]{2,1,0:T(8,128)(2,1)} %bitcast.38), calls=%async_computation.3 | async-start | bytes 3145728 | tf_op jit(solution)/shard_map/all_to_all | solution.py:15
  163.6 19.4 %all-to-all-done.3.terms = bf16[16,16,3072]{2,1,0:T(8,128)(2,1)S(1)} async-done(((bf16[16,16,3072]{2,1,0:T(8,128)(2,1)}), bf16[16,16,3072]{2,1,0:T(8,128)(2,1)S(1)}, u32[]{:S(2)}, u32[]{:S(2)}) %all-to-all-start.3) | async-done | bytes 1572896 | tf_op jit(solution)/shard_map/all_to_all | solution.py:15
  183.3 10.3 %all_to_all.30.piece = bf16[8,16,384]{2,1,0:T(8,128)(2,1)S(1)} all-to-all(bf16[8,16,384]{2,1,0:T(8,128)(2,1)S(1)} %shard_map.148), channel_id=1, replica_groups=mesh['dp'=8,'mp'=16] {'dp'}, dimensions={0} | all-to-all | bytes 196608 | tf_op jit(solution)/shard_map/all_to_all | solution.py:15
  194.9 3.8 %all-to-all-start.5 = ((bf16[16,8,16,384]{3,2,1,0:T(8,128)(2,1)}), bf16[16,8,16,384]{3,2,1,0:T(8,128)(2,1)S(1)}, u32[]{:S(2)}, u32[]{:S(2)}) async-start(bf16[16,8,16,384]{3,2,1,0:T(8,128)(2,1)} %shard_map.149), calls=%async_computation.5 | async-start | bytes 3145728 | tf_op jit(solution)/shard_map/all_to_all | solution.py:15
  210.6 3.3 %select_bitcast_fusion.3 = (bf16[8,1,3072]{2,0,1:T(8,128)(2,1)S(1)}, bf16[8,1,3072]{2,0,1:T(8,128)(2,1)S(1)}, bf16[8,1,3072]{2,0,1:T(8,128)(2,1)S(1)}, bf16[8,1,3072]{2,0,1:T(8,128)(2,1)S(1)}) fusion(bf16[8,32,3072]{2,1,0:T(8,128)(2,1)} %bitcast.99, s32[]{:T(128)S(6)} %select_n.131, s32[]{:T(128)S(6)} %mul.54, pred[]{:T(512)} %get-tuple-element.84, ...), kind=kLoop, calls=%fused_computation.31 | loop fusion | flops 98304 | bytes 393252 | tf_op jit(solution)/shard_map/jit(_where)/select_n | solution.py:600
  214.8 7.7 %all-to-all-done.5 = bf16[16,8,16,384]{3,2,1,0:T(8,128)(2,1)S(1)} async-done(((bf16[16,8,16,384]{3,2,1,0:T(8,128)(2,1)}), bf16[16,8,16,384]{3,2,1,0:T(8,128)(2,1)S(1)}, u32[]{:S(2)}, u32[]{:S(2)}) %all-to-all-start.5) | async-done | bytes 1572896 | tf_op jit(solution)/shard_map/all_to_all | solution.py:15
  222.5 3.8 %fusion.7 = f32[512,384]{1,0:T(8,128)} fusion(bf16[16,8,16,384]{3,2,1,0:T(8,128)(2,1)S(1)} %all-to-all-done.5, bf16[8,16,16,512]{3,2,0,1:T(8,128)(2,1)} %all-gather.12.cloned.1.call-done), kind=kOutput, calls=%fused_computation.10 | convolution fusion | flops 805306368 | bytes 4456448 | tf_op jit(solution)/shard_map/dot_general | solution.py:583
  (96 shorter events, 28.2 us)
Async XLA Ops:
  7.2 31.9 %all-gather.10.cloned.1.call-start = ((), (), s32[]{:S(2)}) async-start(), calls=%async_computation.7 | async-start | bytes 1769472 | tf_op jit(solution)/shard_map/all_gather | solution.py:510
  8.9 62.9 %all-gather.8.cloned.1.call-start = ((), (), s32[]{:S(2)}) async-start(), calls=%async_computation.6 | async-start | bytes 1769472 | tf_op jit(solution)/shard_map/all_gather | solution.py:510
  10.0 11.0 %copy-start.9 = (bf16[1,8,4,3072]{3,2,1,0:T(4,128)(2,1)S(1)}, bf16[1,8,4,3072]{3,2,1,0:T(4,128)(2,1)}, u32[]{:S(2)}) copy-start(bf16[1,8,4,3072]{3,2,1,0:T(4,128)(2,1)} %param.23) | copy-start | bytes 589828
  10.0 11.8 %copy-start.11 = (s32[16]{0:T(128)S(1)}, s32[16]{0:T(128)}, u32[]{:S(2)}) copy-start(s32[16]{0:T(128)} %param.21) | copy-start | bytes 196
  10.0 13.3 %copy-start.1 = (bf16[256,512]{1,0:T(8,128)(2,1)S(1)}, bf16[256,512]{1,0:T(8,128)(2,1)}, u32[]{:S(2)}) copy-start(bf16[256,512]{1,0:T(8,128)(2,1)} %left.3) | copy-start | bytes 786436
  13.6 17.1 %collective-permute-start = (bf16[4,64,512]{2,1,0:T(8,128)(2,1)S(1)}, bf16[4,64,512]{2,1,0:T(8,128)(2,1)S(1)}, u32[]{:S(2)}, u32[]{:S(2)}) collective-permute-start(bf16[4,64,512]{2,1,0:T(8,128)(2,1)S(1)} %get-tuple-element.49), channel_id=1, source_target_pairs={{0,4},{1,5},{2,6},{3,7},{4,8},{5,9},{6,10},{7,11},{8,12},{9,13},{1... | collective-permute-start | bytes 786440 | tf_op jit(solution)/shard_map/ppermute | solution.py:42
  15.3 15.3 %collective-permute-start.1 = (bf16[4,64,512]{2,1,0:T(8,128)(2,1)S(1)}, bf16[4,64,512]{2,1,0:T(8,128)(2,1)S(1)}, u32[]{:S(2)}, u32[]{:S(2)}) collective-permute-start(bf16[4,64,512]{2,1,0:T(8,128)(2,1)S(1)} %get-tuple-element.50), channel_id=1, source_target_pairs={{0,12},{1,13},{2,14},{3,15},{4,0},{5,1},{6,2},{7,3},{8,4},{9,5},{1... | collective-permute-start | bytes 786440 | tf_op jit(solution)/shard_map/ppermute | solution.py:42
  16.9 13.8 %collective-permute-start.2 = (bf16[4,64,512]{2,1,0:T(8,128)(2,1)S(1)}, bf16[4,64,512]{2,1,0:T(8,128)(2,1)S(1)}, u32[]{:S(2)}, u32[]{:S(2)}) collective-permute-start(bf16[4,64,512]{2,1,0:T(8,128)(2,1)S(1)} %get-tuple-element.53), channel_id=1, source_target_pairs={{0,1},{1,2},{2,3},{3,0},{4,5},{5,6},{6,7},{7,4},{8,9},{9,10},{10,1... | collective-permute-start | bytes 786440 | tf_op jit(solution)/shard_map/ppermute | solution.py:42
  18.9 11.8 %collective-permute-start.3 = (bf16[4,64,512]{2,1,0:T(8,128)(2,1)S(1)}, bf16[4,64,512]{2,1,0:T(8,128)(2,1)S(1)}, u32[]{:S(2)}, u32[]{:S(2)}) collective-permute-start(bf16[4,64,512]{2,1,0:T(8,128)(2,1)S(1)} %get-tuple-element.54), channel_id=1, source_target_pairs={{0,3},{1,0},{2,1},{3,2},{4,7},{5,4},{6,5},{7,6},{8,11},{9,8},{10,9... | collective-permute-start | bytes 786440 | tf_op jit(solution)/shard_map/ppermute | solution.py:42
  32.6 14.4 %collective-permute-start.4 = (bf16[4,128,512]{2,1,0:T(8,128)(2,1)}, bf16[4,128,512]{2,1,0:T(8,128)(2,1)S(1)}, u32[]{:S(2)}, u32[]{:S(2)}) collective-permute-start(bf16[4,128,512]{2,1,0:T(8,128)(2,1)} %get-tuple-element.55), channel_id=1, source_target_pairs={{0,4},{1,5},{2,6},{3,7},{4,8},{5,9},{6,10},{7,11},{8,12},{9,13},{1... | collective-permute-start | bytes 1572872 | tf_op jit(solution)/shard_map/ppermute | solution.py:42
  32.9 14.0 %collective-permute-start.5 = (bf16[4,128,512]{2,1,0:T(8,128)(2,1)}, bf16[4,128,512]{2,1,0:T(8,128)(2,1)S(1)}, u32[]{:S(2)}, u32[]{:S(2)}) collective-permute-start(bf16[4,128,512]{2,1,0:T(8,128)(2,1)} %get-tuple-element.56), channel_id=1, source_target_pairs={{0,12},{1,13},{2,14},{3,15},{4,0},{5,1},{6,2},{7,3},{8,4},{9,5},{1... | collective-permute-start | bytes 1572872 | tf_op jit(solution)/shard_map/ppermute | solution.py:42
  35.8 13.8 %collective-permute-start.6 = (bf16[4,128,512]{2,1,0:T(8,128)(2,1)}, bf16[4,128,512]{2,1,0:T(8,128)(2,1)S(1)}, u32[]{:S(2)}, u32[]{:S(2)}) collective-permute-start(bf16[4,128,512]{2,1,0:T(8,128)(2,1)} %get-tuple-element.58), channel_id=1, source_target_pairs={{0,1},{1,2},{2,3},{3,0},{4,5},{5,6},{6,7},{7,4},{8,9},{9,10},{10,1... | collective-permute-start | bytes 1572872 | tf_op jit(solution)/shard_map/ppermute | solution.py:42
  35.8 13.8 %collective-permute-start.7 = (bf16[4,128,512]{2,1,0:T(8,128)(2,1)}, bf16[4,128,512]{2,1,0:T(8,128)(2,1)S(1)}, u32[]{:S(2)}, u32[]{:S(2)}) collective-permute-start(bf16[4,128,512]{2,1,0:T(8,128)(2,1)} %get-tuple-element.59), channel_id=1, source_target_pairs={{0,3},{1,0},{2,1},{3,2},{4,7},{5,4},{6,5},{7,6},{8,11},{9,8},{10,9... | collective-permute-start | bytes 1572872 | tf_op jit(solution)/shard_map/ppermute | solution.py:42
  49.6 14.2 %copy-start.12 = (bf16[512,3072]{1,0:T(8,128)(2,1)S(1)}, bf16[512,3072]{1,0:T(8,128)(2,1)}, u32[]{:S(2)}) copy-start(bf16[512,3072]{1,0:T(8,128)(2,1)} %param.19) | copy-start | bytes 9437188
  50.5 13.1 %copy-start.7 = (bf16[256,512]{1,0:T(8,128)(2,1)S(1)}, bf16[256,512]{1,0:T(8,128)(2,1)}, u32[]{:S(2)}) copy-start(bf16[256,512]{1,0:T(8,128)(2,1)} %param.17) | copy-start | bytes 786436
  50.6 13.1 %copy-start.10 = (f32[512]{0:T(512)S(1)}, f32[512]{0:T(512)}, u32[]{:S(2)}) copy-start(f32[512]{0:T(512)} %param.18) | copy-start | bytes 6148
  50.6 6.6 %collective-permute-start.8 = (bf16[128,512]{1,0:T(8,128)(2,1)S(1)}, bf16[128,512]{1,0:T(8,128)(2,1)S(1)}, u32[]{:S(2)}, u32[]{:S(2)}) collective-permute-start(bf16[128,512]{1,0:T(8,128)(2,1)S(1)} %get-tuple-element.61), channel_id=1, source_target_pairs={{0,1},{1,2},{2,3},{3,0},{4,5},{5,6},{6,7},{7,4},{8,9},{9,10},{10,1... | collective-permute-start | bytes 393224 | tf_op jit(solution)/shard_map/ppermute | solution.py:42
  50.7 8.7 %collective-permute-start.9 = (bf16[128,512]{1,0:T(8,128)(2,1)S(1)}, bf16[128,512]{1,0:T(8,128)(2,1)S(1)}, u32[]{:S(2)}, u32[]{:S(2)}) collective-permute-start(bf16[128,512]{1,0:T(8,128)(2,1)S(1)} %get-tuple-element.62), channel_id=1, source_target_pairs={{0,2},{1,3},{2,0},{3,1},{4,6},{5,7},{6,4},{7,5},{8,10},{9,11},{10,... | collective-permute-start | bytes 393224 | tf_op jit(solution)/shard_map/ppermute | solution.py:42
  55.1 5.0 %collective-permute-start.10 = (bf16[128,512]{1,0:T(8,128)(2,1)S(1)}, bf16[128,512]{1,0:T(8,128)(2,1)S(1)}, u32[]{:S(2)}, u32[]{:S(2)}) collective-permute-start(bf16[128,512]{1,0:T(8,128)(2,1)S(1)} %get-tuple-element.63), channel_id=1, source_target_pairs={{0,3},{1,0},{2,1},{3,2},{4,7},{5,4},{6,5},{7,6},{8,11},{9,8},{10,9... | collective-permute-start | bytes 393224 | tf_op jit(solution)/shard_map/ppermute | solution.py:42
  55.1 7.6 %collective-permute-start.11 = (bf16[128,512]{1,0:T(8,128)(2,1)S(1)}, bf16[128,512]{1,0:T(8,128)(2,1)S(1)}, u32[]{:S(2)}, u32[]{:S(2)}) collective-permute-start(bf16[128,512]{1,0:T(8,128)(2,1)S(1)} %get-tuple-element.65), channel_id=1, source_target_pairs={{0,4},{1,5},{2,6},{3,7},{4,8},{5,9},{6,10},{7,11},{8,12},{9,13},{1... | collective-permute-start | bytes 393224 | tf_op jit(solution)/shard_map/ppermute | solution.py:42
  55.1 7.6 %collective-permute-start.12 = (bf16[128,512]{1,0:T(8,128)(2,1)S(1)}, bf16[128,512]{1,0:T(8,128)(2,1)S(1)}, u32[]{:S(2)}, u32[]{:S(2)}) collective-permute-start(bf16[128,512]{1,0:T(8,128)(2,1)S(1)} %get-tuple-element.66), channel_id=1, source_target_pairs={{0,8},{1,9},{2,10},{3,11},{4,12},{5,13},{6,14},{7,15},{8,0},{9,1},... | collective-permute-start | bytes 393224 | tf_op jit(solution)/shard_map/ppermute | solution.py:42
  57.2 6.3 %collective-permute-start.13 = (bf16[128,512]{1,0:T(8,128)(2,1)S(1)}, bf16[128,512]{1,0:T(8,128)(2,1)S(1)}, u32[]{:S(2)}, u32[]{:S(2)}) collective-permute-start(bf16[128,512]{1,0:T(8,128)(2,1)S(1)} %get-tuple-element.67), channel_id=1, source_target_pairs={{0,12},{1,13},{2,14},{3,15},{4,0},{5,1},{6,2},{7,3},{8,4},{9,5},{1... | collective-permute-start | bytes 393224 | tf_op jit(solution)/shard_map/ppermute | solution.py:42
  66.3 26.0 %copy-start.3 = (s32[256]{0:T(256)S(1)}, s32[256]{0:T(256)}, u32[]{:S(2)}) copy-start(s32[256]{0:T(256)} %param.20) | copy-start | bytes 3076
  66.3 26.0 %all-to-all-start = ((bf16[16,144,384]{2,1,0:T(8,128)(2,1)}), bf16[16,144,384]{2,1,0:T(8,128)(2,1)S(1)}, u32[]{:S(2)}, u32[]{:S(2)}) async-start(bf16[16,144,384]{2,1,0:T(8,128)(2,1)} %bitcast.21), calls=%async_computation | async-start | bytes 3538944 | tf_op jit(solution)/shard_map/all_to_all | solution.py:15
  71.8 64.4 %all-gather.14.cloned.1.call-start = ((), (), s32[]{:S(2)}) async-start(), calls=%async_computation.9 | async-start | bytes 1671168 | tf_op jit(solution)/shard_map/all_gather | solution.py:520
  94.6 25.0 %all-to-all-start.1 = ((bf16[16,128,384]{2,1,0:T(8,128)(2,1)}), bf16[16,128,384]{2,1,0:T(8,128)(2,1)S(1)}, u32[]{:S(2)}, u32[]{:S(2)}) async-start(bf16[16,128,384]{2,1,0:T(8,128)(2,1)} %get-tuple-element.68), calls=%async_computation.1 | async-start | bytes 3145728 | tf_op jit(solution)/shard_map/all_to_all | solution.py:15
  130.3 26.3 %all-to-all-start.2 = ((bf16[16,16,3072]{2,1,0:T(8,128)(2,1)}), bf16[16,16,3072]{2,1,0:T(8,128)(2,1)S(1)}, u32[]{:S(2)}, u32[]{:S(2)}) async-start(bf16[16,16,3072]{2,1,0:T(8,128)(2,1)} %get-tuple-element.72.order), calls=%async_computation.2 | async-start | bytes 3145728 | tf_op jit(solution)/shard_map/all_to_all | solution.py:15
  136.1 74.5 %all-gather.16.cloned.1.call-start = ((), (), s32[]{:S(2)}) async-start(), calls=%async_computation.10 | async-start | bytes 1769472 | tf_op jit(solution)/shard_map/all_gather | solution.py:590
  157.5 57.4 %all-gather.12.cloned.1.call-start = ((), (), s32[]{:S(2)}) async-start(), calls=%async_computation.8 | async-start | bytes 2359296 | tf_op jit(solution)/shard_map/all_gather | solution.py:554
  158.0 24.9 %copy-start.2 = (f32[3072]{0:T(1024)S(1)}, f32[3072]{0:T(1024)}, u32[]{:S(2)}) copy-start(f32[3072]{0:T(1024)} %param.24) | copy-start | bytes 36868
  158.1 24.9 %all-to-all-start.3 = ((bf16[16,16,3072]{2,1,0:T(8,128)(2,1)}), bf16[16,16,3072]{2,1,0:T(8,128)(2,1)S(1)}, u32[]{:S(2)}, u32[]{:S(2)}) async-start(bf16[16,16,3072]{2,1,0:T(8,128)(2,1)} %bitcast.38), calls=%async_computation.3 | async-start | bytes 3145728 | tf_op jit(solution)/shard_map/all_to_all | solution.py:15
  194.9 27.6 %all-to-all-start.5 = ((bf16[16,8,16,384]{3,2,1,0:T(8,128)(2,1)}), bf16[16,8,16,384]{3,2,1,0:T(8,128)(2,1)S(1)}, u32[]{:S(2)}, u32[]{:S(2)}) async-start(bf16[16,8,16,384]{3,2,1,0:T(8,128)(2,1)} %shard_map.149), calls=%async_computation.5 | async-start | bytes 3145728 | tf_op jit(solution)/shard_map/all_to_all | solution.py:15
  (5 other events, 12.0 us)
Sparse Core Ops, SparseCore 0:
  10.3 26.9 all-gather.9
  38.9 24.4 all-gather.7
  75.9 52.5 all-gather.13
  157.6 21.8 all-gather.15
  181.0 25.0 all-gather.11

commit v12 on v11

--- a/solution.py
+++ b/solution.py
@@ -31,6 +31,10 @@
 
 
 SIDE = 4
+
+
+def partner(value):
+    return lax.ppermute(value, "dp", [(d, d ^ 1) for d in range(lax.axis_size("dp"))])
 
 
 def step(value, along_y, along_z):
@@ -291,7 +295,7 @@
         sh[pl.ds(source * rows, rows), :] = tail[:rows]
         squares = squares + tail[rows:]
     tokens = token_slot.shape[1]
-    squares = jnp.sum(squares, axis=0, keepdims=True)[:, :tokens]
+    squares = jnp.sum(squares[:3], axis=0, keepdims=True)[:, :tokens]
     inverse[...] = lax.rsqrt(squares / place[1].astype(full) + epsilon)
     slots = jnp.where(place[0] == 0, token_slot[:, :BLK], token_slot[:, BLK:])
     scale = jnp.where(place[0] == 0, inverse[:, :BLK], inverse[:, BLK:])
@@ -341,9 +345,9 @@
 
 
 def forward_kernel(
-    pieces, gain, order, gate_hbm, up_hbm, down_hbm, state, gate, up, out, normed, act, held, sems
+    pieces, gain, order, other, gate_hbm, up_hbm, down_hbm, state, gate, up, out, normed, act, held, sems
 ):
-    del order
+    del order, other
     parts = 3
     part = gate_hbm.shape[0] // parts
 
@@ -405,14 +409,14 @@
             out[to, :, at] = jnp.concatenate([first, second], axis=0).astype(half)
 
 
-def forward(pieces, gain, gate_w, up_w, down_w, order):
+def forward(pieces, gain, gate_w, up_w, down_w, order, other):
     width, hidden = gate_w.shape
     n_mp = pieces.shape[0]
     rows = 2 * BLK
     whole = pl.BlockSpec(memory_space=pltpu.VMEM)
     return pl.pallas_call(
         forward_kernel,
-        in_specs=[whole, whole, pl.BlockSpec(memory_space=pl.ANY)]
+        in_specs=[whole, whole] + [pl.BlockSpec(memory_space=pl.ANY)] * 2
         + [pl.BlockSpec(memory_space=pltpu.HBM)] * 3,
         out_specs=[whole] * 4,
         out_shape=[
@@ -433,7 +437,7 @@
             bytes_accessed=6 * width * hidden + 10 * rows * width,
             transcendentals=rows * hidden,
         ),
-    )(pieces, gain[None], order, gate_w, up_w, down_w)
+    )(pieces, gain[None], order, other, gate_w, up_w, down_w)
 
 
 def slope_kernel(terms, dy, state, gain, order, out):
@@ -531,7 +535,10 @@
         preferred_element_type=full,
     ).astype(half)
     sh_parts = jnp.swapaxes(sh_rows.reshape(blocks, rows, groups, cols), 1, 2)
-    sq_parts = jnp.zeros((8, cols), half).at[:3, :tokens].set(three_parts(squares))
+    sq_parts = three_parts(squares)
+    sq_parts = jnp.pad(
+        jnp.concatenate([sq_parts, partner(sq_parts)], axis=0), ((0, 2), (0, cols - tokens))
+    )
     message = jnp.concatenate(
         [
             parts,
@@ -555,7 +562,7 @@
     pooled_all = jnp.swapaxes(pooled_all, 0, 1).reshape(n_dp * tokens, width_here)
 
     state, gate, up, output = forward(
-        states, student_gain, gate_weight, up_weight, down_weight, pooled
+        states, student_gain, gate_weight, up_weight, down_weight, pooled, partner(states[0, :8, :128])
     )
     grad_gate, grad_up = backward(dy.reshape(tokens, student_width), down_weight, gate, up, output)
     dn = (times_rows(grad_gate, gate_weight) + times_rows(grad_up, up_weight)).astype(half)

time: 234 us -> 250 us (1.068)
  waiting for transfers between devices: 85.8 us -> 106 us
  starting transfers between devices: 45.5 us -> 43 us
    all_to_all x5, waiting for transfers between devices: 72.6 us -> 92.5 us  [exchange(): return lax.all_to_all(pieces, axis, split_axis=0, concat_axis=0, tiled=True)]
    all_to_all x5, starting transfers between devices: 23.8 us -> 21.2 us  [exchange(): return lax.all_to_all(pieces, axis, split_axis=0, concat_axis=0, tiled=True)]
    unnamed x29 -> x31, local copies, waits for them, and re-layouts: 5.45 us -> 4.83 us
  transfers between devices with their start and end apart: 24 -> 26, of which waited for: 12 -> 13; matrix products, arithmetic and copies ran while one was open for 11% -> 11% of each run, Pallas kernels for 14% -> 13%
where the time goes in v12:
time: 250 us; the launch traced here: 249 us
  waiting for transfers between devices  106 us (42%)
  starting transfers between devices  43 us (17%)
  Pallas kernels  32.5 us (13%)
  between operations  23.9 us (10%)
  local copies, waits for them, and re-layouts  15.6 us (6%)
  matrix products  10.3 us (4%)
  blocking collectives  9.76 us (4%)
  other arithmetic  8.26 us (3%)
    all_to_all x5, waiting for transfers between devices, exchange(): return lax.all_to_all(pieces, axis, split_axis=0, concat_axis=0, tiled=True)  92.5 us
    ppermute x14, starting transfers between devices, step(): return lax.ppermute(value, 'mp', pairs)  21.6 us
    all_to_all x5, starting transfers between devices, exchange(): return lax.all_to_all(pieces, axis, split_axis=0, concat_axis=0, tiled=True)  21.2 us
    ppermute x14, waiting for transfers between devices, step(): return lax.ppermute(value, 'mp', pairs)  12.5 us
    pallas_call x2, Pallas kernels, terms(): pl.pallas_call(kernel, in_specs=[scalars, whole, pl.BlockSpec(memory_spac...  10.9 us
    all_to_all x1, blocking collectives, exchange(): return lax.all_to_all(pieces, axis, split_axis=0, concat_axis=0, tiled=True)  9.76 us
    pallas_call x1, Pallas kernels, forward(): pl.pallas_call(forward_kernel, in_specs=[whole, whole] + [pl.BlockSpec(me...  9.44 us
  transfers between devices with their start and end apart: 26, of which 13 were waited for; matrix products, arithmetic and copies ran while one was open for 11% of the time, Pallas kernels for 13%

profile of v12, /device:TPU:0, one launch (start us, length us, event | category | flops | bytes accessed | tf_op | source)
XLA Modules:
  0.0 249.1 jit_solution(18345537489069011140)
XLA Ops:
  10.0 3.6 %shard_map.141 = (bf16[4,64,512]{2,1,0:T(8,128)(2,1)S(1)}, bf16[4,64,512]{2,1,0:T(8,128)(2,1)S(1)}, bf16[4,64,512]{2,1,0:T(8,128)(2,1)S(1)}, bf16[4,64,512]{2,1,0:T(8,128)(2,1)S(1)}) custom-call(s32[2]{0:T(128)S(1)} %pad_add_fusion.1.place, bf16[256,512]{1,0:T(8,128)(2,1)S(1)} %copy-done, bf16[512,8192]{1,0:T(8,128)(2,1)} %right.3), custom_call_target="tpu_custom_call" | custom-call | flops 536870912 | bytes 4194304 | tf_op jit(solution)/shard_map/pallas_call | solution.py:139
  16.9 2.0 collective-permute-start.2
  18.9 2.1 collective-permute-start.3
  23.3 7.3 %shard_map.140 = (bf16[4,128,512]{2,1,0:T(8,128)(2,1)S(1)}, bf16[4,128,512]{2,1,0:T(8,128)(2,1)S(1)}, bf16[4,128,512]{2,1,0:T(8,128)(2,1)S(1)}, bf16[4,128,512]{...) custom-call(s32[2]{0:T(128)S(1)} %pad_add_fusion.1.place, ...), custom_call_target="tpu_custom_call" | custom-call | flops 2147483648 | bytes 8388608 | tf_op jit(solution)/shard_map/pallas_call | solution.py:139
  30.7 1.9 shard_map.142
  32.9 2.9 %collective-permute-start.5 = (bf16[4,128,512]{2,1,0:T(8,128)(2,1)}, bf16[4,128,512]{2,1,0:T(8,128)(2,1)S(1)}, u32[]{:S(2)}, u32[]{:S(2)}) collective-permute-start(bf16[4,128,512]{2,1,0:T(8,128)(2,1)} %get-tuple-element.44), channel_id=1, source_target_pairs={{0,12},{1,13},{2,14},{3,15},{4,0},{5,1},{6,2},{7,3},{8,4},{9,5},{1... | collective-permute-start | bytes 1572872 | tf_op jit(solution)/shard_map/ppermute | solution.py:46
  35.8 3.2 %collective-permute-start.7 = (bf16[4,128,512]{2,1,0:T(8,128)(2,1)}, bf16[4,128,512]{2,1,0:T(8,128)(2,1)S(1)}, u32[]{:S(2)}, u32[]{:S(2)}) collective-permute-start(bf16[4,128,512]{2,1,0:T(8,128)(2,1)} %get-tuple-element.47), channel_id=1, source_target_pairs={{0,3},{1,0},{2,1},{3,2},{4,7},{5,4},{6,5},{7,6},{8,11},{9,8},{10,9... | collective-permute-start | bytes 1572872 | tf_op jit(solution)/shard_map/ppermute | solution.py:46
  39.0 3.3 %constant_dynamic-slice_fusion.2 = (bf16[1,8,1,3072]{3,1,2,0:T(8,128)(2,1)S(1)}, bf16[1,8,1,3072]{3,1,2,0:T(8,128)(2,1)S(1)}) fusion(bf16[8,8,4,3072]{3,1,2,0:T(8,128)(2,1)} %all-gather.10.cloned.1.call-done, s32[]{:T(128)} %bitcast, s32[]{:T(128)} %bitcast.1, s32[]{:T(128)} %bitcast.3, s32[]{:T(128)} %bitcast.4), kind=kLoop, calls=%fused_computation.53 | loop fusion | bytes 196624 | tf_op jit(solution)/shard_map/dynamic_slice | solution.py:19
  42.4 4.5 %collective-permute-done.4.refs_1_ = bf16[4,128,512]{2,1,0:T(8,128)(2,1)S(1)} collective-permute-done((bf16[4,128,512]{2,1,0:T(8,128)(2,1)}, bf16[4,128,512]{2,1,0:T(8,128)(2,1)S(1)}, u32[]{:S(2)}, u32[]{:S(2)}) %collective-permute-start.4) | collective-permute-done | bytes 524320 | tf_op jit(solution)/shard_map/ppermute | solution.py:46
  46.9 2.7 %collective-permute-done.6.refs_4_ = bf16[4,128,512]{2,1,0:T(8,128)(2,1)S(1)} collective-permute-done((bf16[4,128,512]{2,1,0:T(8,128)(2,1)}, bf16[4,128,512]{2,1,0:T(8,128)(2,1)S(1)}, u32[]{:S(2)}, u32[]{:S(2)}) %collective-permute-start.6) | collective-permute-done | bytes 524320 | tf_op jit(solution)/shard_map/ppermute | solution.py:46
  50.7 4.4 %collective-permute-start.9 = (bf16[128,512]{1,0:T(8,128)(2,1)S(1)}, bf16[128,512]{1,0:T(8,128)(2,1)S(1)}, u32[]{:S(2)}, u32[]{:S(2)}) collective-permute-start(bf16[128,512]{1,0:T(8,128)(2,1)S(1)} %get-tuple-element.50), channel_id=1, source_target_pairs={{0,2},{1,3},{2,0},{3,1},{4,6},{5,7},{6,4},{7,5},{8,10},{9,11},{10,... | collective-permute-start | bytes 393224 | tf_op jit(solution)/shard_map/ppermute | solution.py:46
  55.1 1.9 collective-permute-start.12
  60.1 2.5 %collective-permute-done.11 = bf16[128,512]{1,0:T(8,128)(2,1)S(1)} collective-permute-done((bf16[128,512]{1,0:T(8,128)(2,1)S(1)}, bf16[128,512]{1,0:T(8,128)(2,1)S(1)}, u32[]{:S(2)}, u32[]{:S(2)}) %collective-permute-start.11) | collective-permute-done | bytes 131104 | tf_op jit(solution)/shard_map/ppermute | solution.py:46
  66.5 5.5 %all-to-all-start = ((bf16[16,144,384]{2,1,0:T(8,128)(2,1)}), bf16[16,144,384]{2,1,0:T(8,128)(2,1)S(1)}, u32[]{:S(2)}, u32[]{:S(2)}) async-start(bf16[16,144,384]{2,1,0:T(8,128)(2,1)} %bitcast.21), calls=%async_computation | async-start | bytes 3538944 | tf_op jit(solution)/shard_map/all_to_all | solution.py:15
  72.1 3.4 %dynamic-slice_bitcast_fusion.3 = (bf16[1,8,3072]{2,1,0:T(8,128)(2,1)S(1)}, bf16[1,8,3072]{2,1,0:T(8,128)(2,1)S(1)}) fusion(bf16[8,8,4,3072]{3,1,2,0:T(8,128)(2,1)} %all-gather.8.cloned.1.call-done, s32[]{:T(128)} %bitcast, s32[]{:T(128)} %bitcast.1, s32[]{:T(128)} %bitcast.3, s32[]{:T(128)} %bitcast.4), kind=kLoop, calls=%fused_computation.33 | loop fusion | bytes 196624 | tf_op jit(solution)/shard_map/stack;reshape | solution.py:520
  76.2 23.5 %all-to-all-done.message = bf16[16,144,384]{2,1,0:T(8,128)(2,1)S(1)} async-done(((bf16[16,144,384]{2,1,0:T(8,128)(2,1)}), bf16[16,144,384]{2,1,0:T(8,128)(2,1)S(1)}, u32[]{:S(2)}, u32[]{:S(2)}) %all-to-all-start) | async-done | bytes 1769504 | tf_op jit(solution)/shard_map/all_to_all | solution.py:15
  99.7 2.3 shard_map.144
  102.0 4.0 %all-to-all-start.1 = ((bf16[16,128,384]{2,1,0:T(8,128)(2,1)}), bf16[16,128,384]{2,1,0:T(8,128)(2,1)S(1)}, u32[]{:S(2)}, u32[]{:S(2)}) async-start(bf16[16,128,384]{2,1,0:T(8,128)(2,1)} %get-tuple-element.56), calls=%async_computation.1 | async-start | bytes 3145728 | tf_op jit(solution)/shard_map/all_to_all | solution.py:15
  106.2 25.8 %all-to-all-done.1.pieces = bf16[16,128,384]{2,1,0:T(8,128)(2,1)S(1)} async-done(((bf16[16,128,384]{2,1,0:T(8,128)(2,1)}), bf16[16,128,384]{2,1,0:T(8,128)(2,1)S(1)}, u32[]{:S(2)}, u32[]{:S(2)}) %all-to-all-start.1) | async-done | bytes 1572896 | tf_op jit(solution)/shard_map/all_to_all | solution.py:15
  133.8 9.4 %shard_map.145 = (bf16[256,3072]{1,0:T(8,128)(2,1)}, f32[256,512]{1,0:T(8,128)}, f32[256,512]{1,0:T(8,128)}, bf16[16,16,3072]{2,1,0:T(8,128)(2,1)}) custom-call(bf16[16,128,384]{2,1,0:T(8,128)(2,1)} %copy-done.6, f32[1,3072]{1,0:T(1,128)} %bitcast.86, bf16[2,128,512]{2,1,0:T(8,128)(2,1)} %fusion.10.order, bf16[8,128]{1,0:T(8,128)(2,1)} %copy-done.11, ...), custom_call_target="tpu_custom_call" | custom-call | flops 2415919104 | bytes 17301504 | tf_op jit(solution)/shard_map/pallas_call | solution.py:417
  143.2 4.3 %all-to-all-start.2 = ((bf16[16,16,3072]{2,1,0:T(8,128)(2,1)}), bf16[16,16,3072]{2,1,0:T(8,128)(2,1)S(1)}, u32[]{:S(2)}, u32[]{:S(2)}) async-start(bf16[16,16,3072]{2,1,0:T(8,128)(2,1)} %get-tuple-element.60.order), calls=%async_computation.2 | async-start | bytes 3145728 | tf_op jit(solution)/shard_map/all_to_all | solution.py:15
  147.6 4.6 %shard_map.146 = (bf16[256,512]{1,0:T(8,128)(2,1)}, bf16[256,512]{1,0:T(8,128)(2,1)}) custom-call(bf16[256,3072]{1,0:T(8,128)(2,1)} %bitcast.92, bf16[3072,512]{1,0:T(8,128)(2,1)} %down.1, f32[256,512]{1,0:T(8,128)} %get-tuple-element.58.gate, f32[256,512]{1,0:T(8,128)} %get-tuple-element.59.up, bf16[16,16,3072]{2,1,0:T(8,128)(2,1)} %get-tuple-element.60.order), custom_call_target="tpu_custom_call" | custom-call | flops 805306368 | bytes 6815744 | tf_op jit(solution)/shard_map/pallas_call | solution.py:222
  153.2 2.1 fusion.33
  155.3 2.3 fusion
  157.6 14.6 %all-to-all-done.2.terms = bf16[16,16,3072]{2,1,0:T(8,128)(2,1)S(1)} async-done(((bf16[16,16,3072]{2,1,0:T(8,128)(2,1)}), bf16[16,16,3072]{2,1,0:T(8,128)(2,1)S(1)}, u32[]{:S(2)}, u32[]{:S(2)}) %all-to-all-start.2) | async-done | bytes 1572896 | tf_op jit(solution)/shard_map/all_to_all | solution.py:15
  173.6 3.7 %all-to-all-start.3 = ((bf16[16,16,3072]{2,1,0:T(8,128)(2,1)}), bf16[16,16,3072]{2,1,0:T(8,128)(2,1)S(1)}, u32[]{:S(2)}, u32[]{:S(2)}) async-start(bf16[16,16,3072]{2,1,0:T(8,128)(2,1)} %bitcast.39), calls=%async_computation.3 | async-start | bytes 3145728 | tf_op jit(solution)/shard_map/all_to_all | solution.py:15
  179.2 20.6 %all-to-all-done.3.terms = bf16[16,16,3072]{2,1,0:T(8,128)(2,1)S(1)} async-done(((bf16[16,16,3072]{2,1,0:T(8,128)(2,1)}), bf16[16,16,3072]{2,1,0:T(8,128)(2,1)S(1)}, u32[]{:S(2)}, u32[]{:S(2)}) %all-to-all-start.3) | async-done | bytes 1572896 | tf_op jit(solution)/shard_map/all_to_all | solution.py:15
  200.1 9.8 %all_to_all.30.piece = bf16[8,16,384]{2,1,0:T(8,128)(2,1)S(1)} all-to-all(bf16[8,16,384]{2,1,0:T(8,128)(2,1)S(1)} %shard_map.148), channel_id=1, replica_groups=mesh['dp'=8,'mp'=16] {'dp'}, dimensions={0} | all-to-all | bytes 196608 | tf_op jit(solution)/shard_map/all_to_all | solution.py:15
  211.2 3.7 %all-to-all-start.5 = ((bf16[16,8,16,384]{3,2,1,0:T(8,128)(2,1)}), bf16[16,8,16,384]{3,2,1,0:T(8,128)(2,1)S(1)}, u32[]{:S(2)}, u32[]{:S(2)}) async-start(bf16[16,8,16,384]{3,2,1,0:T(8,128)(2,1)} %shard_map.149), calls=%async_computation.5 | async-start | bytes 3145728 | tf_op jit(solution)/shard_map/all_to_all | solution.py:15
  226.3 3.6 %select_bitcast_fusion.3 = (bf16[8,1,3072]{2,0,1:T(8,128)(2,1)S(1)}, bf16[8,1,3072]{2,0,1:T(8,128)(2,1)S(1)}, bf16[8,1,3072]{2,0,1:T(8,128)(2,1)S(1)}, bf16[8,1,3072]{2,0,1:T(8,128)(2,1)S(1)}) fusion(bf16[8,32,3072]{2,1,0:T(8,128)(2,1)} %bitcast.101, s32[]{:T(128)S(6)} %select_n.131, s32[]{:T(128)S(6)} %mul.54, pred[]{:T(512)} %get-tuple-element.72, ...), kind=kLoop, calls=%fused_computation.31 | loop fusion | flops 98304 | bytes 393252 | tf_op jit(solution)/shard_map/jit(_where)/select_n | solution.py:607
  230.8 8.1 %all-to-all-done.5 = bf16[16,8,16,384]{3,2,1,0:T(8,128)(2,1)S(1)} async-done(((bf16[16,8,16,384]{3,2,1,0:T(8,128)(2,1)}), bf16[16,8,16,384]{3,2,1,0:T(8,128)(2,1)S(1)}, u32[]{:S(2)}, u32[]{:S(2)}) %all-to-all-start.5) | async-done | bytes 1572896 | tf_op jit(solution)/shard_map/all_to_all | solution.py:15
  238.9 3.8 %fusion.7 = f32[512,384]{1,0:T(8,128)} fusion(bf16[16,8,16,384]{3,2,1,0:T(8,128)(2,1)S(1)} %all-to-all-done.5, bf16[8,16,16,512]{3,2,0,1:T(8,128)(2,1)} %all-gather.12.cloned.1.call-done), kind=kOutput, calls=%fused_computation.10 | convolution fusion | flops 805306368 | bytes 4456448 | tf_op jit(solution)/shard_map/dot_general | solution.py:590
  (104 shorter events, 28.0 us)
Async XLA Ops:
  7.2 31.9 %all-gather.10.cloned.1.call-start = ((), (), s32[]{:S(2)}) async-start(), calls=%async_computation.7 | async-start | bytes 1769472 | tf_op jit(solution)/shard_map/all_gather | solution.py:514
  8.9 63.2 %all-gather.8.cloned.1.call-start = ((), (), s32[]{:S(2)}) async-start(), calls=%async_computation.6 | async-start | bytes 1769472 | tf_op jit(solution)/shard_map/all_gather | solution.py:514
  10.0 13.3 %copy-start.1 = (bf16[256,512]{1,0:T(8,128)(2,1)S(1)}, bf16[256,512]{1,0:T(8,128)(2,1)}, u32[]{:S(2)}) copy-start(bf16[256,512]{1,0:T(8,128)(2,1)} %left.3) | copy-start | bytes 786436
  13.6 17.1 %collective-permute-start = (bf16[4,64,512]{2,1,0:T(8,128)(2,1)S(1)}, bf16[4,64,512]{2,1,0:T(8,128)(2,1)S(1)}, u32[]{:S(2)}, u32[]{:S(2)}) collective-permute-start(bf16[4,64,512]{2,1,0:T(8,128)(2,1)S(1)} %get-tuple-element.37), channel_id=1, source_target_pairs={{0,4},{1,5},{2,6},{3,7},{4,8},{5,9},{6,10},{7,11},{8,12},{9,13},{1... | collective-permute-start | bytes 786440 | tf_op jit(solution)/shard_map/ppermute | solution.py:46
  15.3 15.4 %collective-permute-start.1 = (bf16[4,64,512]{2,1,0:T(8,128)(2,1)S(1)}, bf16[4,64,512]{2,1,0:T(8,128)(2,1)S(1)}, u32[]{:S(2)}, u32[]{:S(2)}) collective-permute-start(bf16[4,64,512]{2,1,0:T(8,128)(2,1)S(1)} %get-tuple-element.38), channel_id=1, source_target_pairs={{0,12},{1,13},{2,14},{3,15},{4,0},{5,1},{6,2},{7,3},{8,4},{9,5},{1... | collective-permute-start | bytes 786440 | tf_op jit(solution)/shard_map/ppermute | solution.py:46
  16.9 13.8 %collective-permute-start.2 = (bf16[4,64,512]{2,1,0:T(8,128)(2,1)S(1)}, bf16[4,64,512]{2,1,0:T(8,128)(2,1)S(1)}, u32[]{:S(2)}, u32[]{:S(2)}) collective-permute-start(bf16[4,64,512]{2,1,0:T(8,128)(2,1)S(1)} %get-tuple-element.41), channel_id=1, source_target_pairs={{0,1},{1,2},{2,3},{3,0},{4,5},{5,6},{6,7},{7,4},{8,9},{9,10},{10,1... | collective-permute-start | bytes 786440 | tf_op jit(solution)/shard_map/ppermute | solution.py:46
  18.9 11.8 %collective-permute-start.3 = (bf16[4,64,512]{2,1,0:T(8,128)(2,1)S(1)}, bf16[4,64,512]{2,1,0:T(8,128)(2,1)S(1)}, u32[]{:S(2)}, u32[]{:S(2)}) collective-permute-start(bf16[4,64,512]{2,1,0:T(8,128)(2,1)S(1)} %get-tuple-element.42), channel_id=1, source_target_pairs={{0,3},{1,0},{2,1},{3,2},{4,7},{5,4},{6,5},{7,6},{8,11},{9,8},{10,9... | collective-permute-start | bytes 786440 | tf_op jit(solution)/shard_map/ppermute | solution.py:46
  32.5 14.4 %collective-permute-start.4 = (bf16[4,128,512]{2,1,0:T(8,128)(2,1)}, bf16[4,128,512]{2,1,0:T(8,128)(2,1)S(1)}, u32[]{:S(2)}, u32[]{:S(2)}) collective-permute-start(bf16[4,128,512]{2,1,0:T(8,128)(2,1)} %get-tuple-element.43), channel_id=1, source_target_pairs={{0,4},{1,5},{2,6},{3,7},{4,8},{5,9},{6,10},{7,11},{8,12},{9,13},{1... | collective-permute-start | bytes 1572872 | tf_op jit(solution)/shard_map/ppermute | solution.py:46
  32.9 14.0 %collective-permute-start.5 = (bf16[4,128,512]{2,1,0:T(8,128)(2,1)}, bf16[4,128,512]{2,1,0:T(8,128)(2,1)S(1)}, u32[]{:S(2)}, u32[]{:S(2)}) collective-permute-start(bf16[4,128,512]{2,1,0:T(8,128)(2,1)} %get-tuple-element.44), channel_id=1, source_target_pairs={{0,12},{1,13},{2,14},{3,15},{4,0},{5,1},{6,2},{7,3},{8,4},{9,5},{1... | collective-permute-start | bytes 1572872 | tf_op jit(solution)/shard_map/ppermute | solution.py:46
  35.8 13.8 %collective-permute-start.6 = (bf16[4,128,512]{2,1,0:T(8,128)(2,1)}, bf16[4,128,512]{2,1,0:T(8,128)(2,1)S(1)}, u32[]{:S(2)}, u32[]{:S(2)}) collective-permute-start(bf16[4,128,512]{2,1,0:T(8,128)(2,1)} %get-tuple-element.46), channel_id=1, source_target_pairs={{0,1},{1,2},{2,3},{3,0},{4,5},{5,6},{6,7},{7,4},{8,9},{9,10},{10,1... | collective-permute-start | bytes 1572872 | tf_op jit(solution)/shard_map/ppermute | solution.py:46
  35.8 13.8 %collective-permute-start.7 = (bf16[4,128,512]{2,1,0:T(8,128)(2,1)}, bf16[4,128,512]{2,1,0:T(8,128)(2,1)S(1)}, u32[]{:S(2)}, u32[]{:S(2)}) collective-permute-start(bf16[4,128,512]{2,1,0:T(8,128)(2,1)} %get-tuple-element.47), channel_id=1, source_target_pairs={{0,3},{1,0},{2,1},{3,2},{4,7},{5,4},{6,5},{7,6},{8,11},{9,8},{10,9... | collective-permute-start | bytes 1572872 | tf_op jit(solution)/shard_map/ppermute | solution.py:46
  49.6 14.3 %copy-start.13 = (bf16[512,3072]{1,0:T(8,128)(2,1)S(1)}, bf16[512,3072]{1,0:T(8,128)(2,1)}, u32[]{:S(2)}) copy-start(bf16[512,3072]{1,0:T(8,128)(2,1)} %param.17) | copy-start | bytes 9437188
  50.5 13.1 %copy-start.7 = (bf16[256,512]{1,0:T(8,128)(2,1)S(1)}, bf16[256,512]{1,0:T(8,128)(2,1)}, u32[]{:S(2)}) copy-start(bf16[256,512]{1,0:T(8,128)(2,1)} %param.15) | copy-start | bytes 786436
  50.5 13.1 %copy-start.10 = (f32[512]{0:T(512)S(1)}, f32[512]{0:T(512)}, u32[]{:S(2)}) copy-start(f32[512]{0:T(512)} %param.16) | copy-start | bytes 6148
  50.6 6.6 %collective-permute-start.8 = (bf16[128,512]{1,0:T(8,128)(2,1)S(1)}, bf16[128,512]{1,0:T(8,128)(2,1)S(1)}, u32[]{:S(2)}, u32[]{:S(2)}) collective-permute-start(bf16[128,512]{1,0:T(8,128)(2,1)S(1)} %get-tuple-element.49), channel_id=1, source_target_pairs={{0,1},{1,2},{2,3},{3,0},{4,5},{5,6},{6,7},{7,4},{8,9},{9,10},{10,1... | collective-permute-start | bytes 393224 | tf_op jit(solution)/shard_map/ppermute | solution.py:46
  50.7 8.7 %collective-permute-start.9 = (bf16[128,512]{1,0:T(8,128)(2,1)S(1)}, bf16[128,512]{1,0:T(8,128)(2,1)S(1)}, u32[]{:S(2)}, u32[]{:S(2)}) collective-permute-start(bf16[128,512]{1,0:T(8,128)(2,1)S(1)} %get-tuple-element.50), channel_id=1, source_target_pairs={{0,2},{1,3},{2,0},{3,1},{4,6},{5,7},{6,4},{7,5},{8,10},{9,11},{10,... | collective-permute-start | bytes 393224 | tf_op jit(solution)/shard_map/ppermute | solution.py:46
  55.0 5.0 %collective-permute-start.10 = (bf16[128,512]{1,0:T(8,128)(2,1)S(1)}, bf16[128,512]{1,0:T(8,128)(2,1)S(1)}, u32[]{:S(2)}, u32[]{:S(2)}) collective-permute-start(bf16[128,512]{1,0:T(8,128)(2,1)S(1)} %get-tuple-element.51), channel_id=1, source_target_pairs={{0,3},{1,0},{2,1},{3,2},{4,7},{5,4},{6,5},{7,6},{8,11},{9,8},{10,9... | collective-permute-start | bytes 393224 | tf_op jit(solution)/shard_map/ppermute | solution.py:46
  55.0 7.6 %collective-permute-start.11 = (bf16[128,512]{1,0:T(8,128)(2,1)S(1)}, bf16[128,512]{1,0:T(8,128)(2,1)S(1)}, u32[]{:S(2)}, u32[]{:S(2)}) collective-permute-start(bf16[128,512]{1,0:T(8,128)(2,1)S(1)} %get-tuple-element.53), channel_id=1, source_target_pairs={{0,4},{1,5},{2,6},{3,7},{4,8},{5,9},{6,10},{7,11},{8,12},{9,13},{1... | collective-permute-start | bytes 393224 | tf_op jit(solution)/shard_map/ppermute | solution.py:46
  55.1 7.6 %collective-permute-start.12 = (bf16[128,512]{1,0:T(8,128)(2,1)S(1)}, bf16[128,512]{1,0:T(8,128)(2,1)S(1)}, u32[]{:S(2)}, u32[]{:S(2)}) collective-permute-start(bf16[128,512]{1,0:T(8,128)(2,1)S(1)} %get-tuple-element.54), channel_id=1, source_target_pairs={{0,8},{1,9},{2,10},{3,11},{4,12},{5,13},{6,14},{7,15},{8,0},{9,1},... | collective-permute-start | bytes 393224 | tf_op jit(solution)/shard_map/ppermute | solution.py:46
  57.2 6.3 %collective-permute-start.13 = (bf16[128,512]{1,0:T(8,128)(2,1)S(1)}, bf16[128,512]{1,0:T(8,128)(2,1)S(1)}, u32[]{:S(2)}, u32[]{:S(2)}) collective-permute-start(bf16[128,512]{1,0:T(8,128)(2,1)S(1)} %get-tuple-element.55), channel_id=1, source_target_pairs={{0,12},{1,13},{2,14},{3,15},{4,0},{5,1},{6,2},{7,3},{8,4},{9,5},{1... | collective-permute-start | bytes 393224 | tf_op jit(solution)/shard_map/ppermute | solution.py:46
  63.8 1.2 collective-permute-start.14
  66.5 33.1 %copy-start.3 = (s32[256]{0:T(256)S(1)}, s32[256]{0:T(256)}, u32[]{:S(2)}) copy-start(s32[256]{0:T(256)} %param.18) | copy-start | bytes 3076
  66.5 33.1 %all-to-all-start = ((bf16[16,144,384]{2,1,0:T(8,128)(2,1)}), bf16[16,144,384]{2,1,0:T(8,128)(2,1)S(1)}, u32[]{:S(2)}, u32[]{:S(2)}) async-start(bf16[16,144,384]{2,1,0:T(8,128)(2,1)} %bitcast.21), calls=%async_computation | async-start | bytes 3538944 | tf_op jit(solution)/shard_map/all_to_all | solution.py:15
  72.0 75.6 %all-gather.14.cloned.1.call-start = ((), (), s32[]{:S(2)}) async-start(), calls=%async_computation.9 | async-start | bytes 1671168 | tf_op jit(solution)/shard_map/all_gather | solution.py:524
  102.0 30.1 %all-to-all-start.1 = ((bf16[16,128,384]{2,1,0:T(8,128)(2,1)}), bf16[16,128,384]{2,1,0:T(8,128)(2,1)S(1)}, u32[]{:S(2)}, u32[]{:S(2)}) async-start(bf16[16,128,384]{2,1,0:T(8,128)(2,1)} %get-tuple-element.56), calls=%async_computation.1 | async-start | bytes 3145728 | tf_op jit(solution)/shard_map/all_to_all | solution.py:15
  132.0 1.2 collective-permute-start.15
  143.2 28.9 %all-to-all-start.2 = ((bf16[16,16,3072]{2,1,0:T(8,128)(2,1)}), bf16[16,16,3072]{2,1,0:T(8,128)(2,1)S(1)}, u32[]{:S(2)}, u32[]{:S(2)}) async-start(bf16[16,16,3072]{2,1,0:T(8,128)(2,1)} %get-tuple-element.60.order), calls=%async_computation.2 | async-start | bytes 3145728 | tf_op jit(solution)/shard_map/all_to_all | solution.py:15
  147.5 78.8 %all-gather.16.cloned.1.call-start = ((), (), s32[]{:S(2)}) async-start(), calls=%async_computation.10 | async-start | bytes 1769472 | tf_op jit(solution)/shard_map/all_gather | solution.py:597
  173.0 57.7 %all-gather.12.cloned.1.call-start = ((), (), s32[]{:S(2)}) async-start(), calls=%async_computation.8 | async-start | bytes 2359296 | tf_op jit(solution)/shard_map/all_gather | solution.py:561
  173.6 26.2 %copy-start.2 = (f32[3072]{0:T(1024)S(1)}, f32[3072]{0:T(1024)}, u32[]{:S(2)}) copy-start(f32[3072]{0:T(1024)} %param.22) | copy-start | bytes 36868
  173.6 26.1 %all-to-all-start.3 = ((bf16[16,16,3072]{2,1,0:T(8,128)(2,1)}), bf16[16,16,3072]{2,1,0:T(8,128)(2,1)S(1)}, u32[]{:S(2)}, u32[]{:S(2)}) async-start(bf16[16,16,3072]{2,1,0:T(8,128)(2,1)} %bitcast.39), calls=%async_computation.3 | async-start | bytes 3145728 | tf_op jit(solution)/shard_map/all_to_all | solution.py:15
  211.2 27.7 %all-to-all-start.5 = ((bf16[16,8,16,384]{3,2,1,0:T(8,128)(2,1)}), bf16[16,8,16,384]{3,2,1,0:T(8,128)(2,1)S(1)}, u32[]{:S(2)}, u32[]{:S(2)}) async-start(bf16[16,8,16,384]{3,2,1,0:T(8,128)(2,1)} %shard_map.149), calls=%async_computation.5 | async-start | bytes 3145728 | tf_op jit(solution)/shard_map/all_to_all | solution.py:15
  (8 other events, 35.4 us)
Sparse Core Ops, SparseCore 0:
  10.3 26.9 all-gather.9
  38.9 24.6 all-gather.7
  76.2 57.5 all-gather.13
  173.2 22.3 all-gather.15
  197.1 25.1 all-gather.11

commit v13 on v10

--- a/solution.py
+++ b/solution.py
@@ -341,9 +341,9 @@
 
 
 def forward_kernel(
-    pieces, gain, order, other, gate_hbm, up_hbm, down_hbm, state, gate, up, out, normed, act, held, sems
+    pieces, gain, order, gate_hbm, up_hbm, down_hbm, state, gate, up, out, normed, act, held, sems
 ):
-    del order, other
+    del order
     parts = 3
     part = gate_hbm.shape[0] // parts
 
@@ -405,14 +405,14 @@
             out[to, :, at] = jnp.concatenate([first, second], axis=0).astype(half)
 
 
-def forward(pieces, gain, gate_w, up_w, down_w, order, other):
+def forward(pieces, gain, gate_w, up_w, down_w, order):
     width, hidden = gate_w.shape
     n_mp = pieces.shape[0]
     rows = 2 * BLK
     whole = pl.BlockSpec(memory_space=pltpu.VMEM)
     return pl.pallas_call(
         forward_kernel,
-        in_specs=[whole, whole] + [pl.BlockSpec(memory_space=pl.ANY)] * 2
+        in_specs=[whole, whole, pl.BlockSpec(memory_space=pl.ANY)]
         + [pl.BlockSpec(memory_space=pltpu.HBM)] * 3,
         out_specs=[whole] * 4,
         out_shape=[
@@ -433,7 +433,7 @@
             bytes_accessed=6 * width * hidden + 10 * rows * width,
             transcendentals=rows * hidden,
         ),
-    )(pieces, gain[None], order, other, gate_w, up_w, down_w)
+    )(pieces, gain[None], order, gate_w, up_w, down_w)
 
 
 def slope_kernel(terms, dy, state, gain, order, out):
@@ -558,7 +558,7 @@
     pooled_all = jnp.swapaxes(pooled_all, 0, 1).reshape(n_dp * tokens, width_here)
 
     state, gate, up, output = forward(
-        states, student_gain, gate_weight, up_weight, down_weight, pooled, dy[0, 0, :, :128]
+        states, student_gain, gate_weight, up_weight, down_weight, pooled
     )
     grad_gate, grad_up = backward(dy.reshape(tokens, student_width), down_weight, gate, up, output)
     dn = (times_rows(grad_gate, gate_weight) + times_rows(grad_up, up_weight)).astype(half)

time: 234 us -> 223 us (0.953)
  waiting for transfers between devices: 82.7 us -> 76.8 us
  local copies, waits for them, and re-layouts: 15.1 us -> 11.4 us
    all_gather x1, waiting for transfers between devices: 3.89 us -> 0.02 us  [on_device(): dy = lax.all_gather(dy_rows, 'mp', axis=0, tiled=False)]
    all_to_all x5, waiting for transfers between devices: 66.8 us -> 64.3 us  [exchange(): return lax.all_to_all(pieces, axis, split_axis=0, concat_axis=0, tiled=True)]
    unnamed x37 -> x31, local copies, waits for them, and re-layouts: 5.46 us -> 3.1 us
  transfers between devices with their start and end apart: 23 -> 23, of which waited for: 12 -> 12; matrix products, arithmetic and copies ran while one was open for 11% -> 9% of each run, Pallas kernels for 9% -> 14%
where the time goes in v13:
time: 223 us; the launch traced here: 222 us
  waiting for transfers between devices  76.8 us (34%)
  starting transfers between devices  46.1 us (21%)
  Pallas kernels  33.1 us (15%)
  between operations  24.9 us (11%)
  local copies, waits for them, and re-layouts  11.4 us (5%)
  matrix products  10.1 us (5%)
  blocking collectives  9.95 us (4%)
  other arithmetic  9.57 us (4%)
    all_to_all x5, waiting for transfers between devices, exchange(): return lax.all_to_all(pieces, axis, split_axis=0, concat_axis=0, tiled=True)  64.3 us
    all_to_all x5, starting transfers between devices, exchange(): return lax.all_to_all(pieces, axis, split_axis=0, concat_axis=0, tiled=True)  23.9 us
    ppermute x14, starting transfers between devices, step(): return lax.ppermute(value, 'mp', pairs)  22 us
    ppermute x14, waiting for transfers between devices, step(): return lax.ppermute(value, 'mp', pairs)  10.9 us
    pallas_call x2, Pallas kernels, terms(): pl.pallas_call(kernel, in_specs=[scalars, whole, pl.BlockSpec(memory_spac...  10.9 us
    all_to_all x1, blocking collectives, exchange(): return lax.all_to_all(pieces, axis, split_axis=0, concat_axis=0, tiled=True)  9.95 us
    pallas_call x1, Pallas kernels, forward(): pl.pallas_call(forward_kernel, in_specs=[whole, whole, pl.BlockSpec(memor...  9.5 us
    dynamic_slice x3, local copies, waits for them, and re-layouts, take(): return lax.dynamic_slice(array, starts, sizes, allow_negative_indices=False)  5.2 us
  transfers between devices with their start and end apart: 23, of which 12 were waited for; matrix products, arithmetic and copies ran while one was open for 9% of the time, Pallas kernels for 14%

profile of v13, /device:TPU:0, one launch (start us, length us, event | category | flops | bytes accessed | tf_op | source)
XLA Modules:
  0.0 221.9 jit_solution(9980835969736078056)
XLA Ops:
  7.2 2.0 pad_maximum_fusion.1
  10.3 3.6 %shard_map.141 = (bf16[4,64,512]{2,1,0:T(8,128)(2,1)S(1)}, bf16[4,64,512]{2,1,0:T(8,128)(2,1)S(1)}, bf16[4,64,512]{2,1,0:T(8,128)(2,1)S(1)}, bf16[4,64,512]{2,1,0:T(8,128)(2,1)S(1)}) custom-call(s32[2]{0:T(128)S(1)} %pad_add_fusion.1.place, bf16[256,512]{1,0:T(8,128)(2,1)S(1)} %copy-done, bf16[512,8192]{1,0:T(8,128)(2,1)} %right.3), custom_call_target="tpu_custom_call" | custom-call | flops 536870912 | bytes 4194304 | tf_op jit(solution)/shard_map/pallas_call | solution.py:135
  17.1 2.0 collective-permute-start.2
  19.1 2.1 collective-permute-start.3
  23.9 7.3 %shard_map.140 = (bf16[4,128,512]{2,1,0:T(8,128)(2,1)S(1)}, bf16[4,128,512]{2,1,0:T(8,128)(2,1)S(1)}, bf16[4,128,512]{2,1,0:T(8,128)(2,1)S(1)}, bf16[4,128,512]{...) custom-call(s32[2]{0:T(128)S(1)} %pad_add_fusion.1.place, ...), custom_call_target="tpu_custom_call" | custom-call | flops 2147483648 | bytes 8388608 | tf_op jit(solution)/shard_map/pallas_call | solution.py:135
  31.2 1.9 shard_map.142
  33.5 2.9 %collective-permute-start.5 = (bf16[4,128,512]{2,1,0:T(8,128)(2,1)}, bf16[4,128,512]{2,1,0:T(8,128)(2,1)S(1)}, u32[]{:S(2)}, u32[]{:S(2)}) collective-permute-start(bf16[4,128,512]{2,1,0:T(8,128)(2,1)} %get-tuple-element.56), channel_id=1, source_target_pairs={{0,12},{1,13},{2,14},{3,15},{4,0},{5,1},{6,2},{7,3},{8,4},{9,5},{1... | collective-permute-start | bytes 1572872 | tf_op jit(solution)/shard_map/ppermute | solution.py:42
  36.3 3.2 %collective-permute-start.7 = (bf16[4,128,512]{2,1,0:T(8,128)(2,1)}, bf16[4,128,512]{2,1,0:T(8,128)(2,1)}, u32[]{:S(2)}, u32[]{:S(2)}) collective-permute-start(bf16[4,128,512]{2,1,0:T(8,128)(2,1)} %get-tuple-element.59), channel_id=1, source_target_pairs={{0,3},{1,0},{2,1},{3,2},{4,7},{5,4},{6,5},{7,6},{8,11},{9,8},{10,9... | collective-permute-start | bytes 1572872 | tf_op jit(solution)/shard_map/ppermute | solution.py:42
  39.9 4.2 %constant_dynamic-slice_fusion.2 = (bf16[1,8,1,3072]{3,2,1,0:T(2,128)(2,1)S(1)}, bf16[1,8,1,3072]{3,2,1,0:T(2,128)(2,1)S(1)}, bf16[1,8,1,3072]{3,2,1,0:T(2,128)(2,1)S(1)}, bf16[1,8,1,3072]{3,2,1,0:T(2,128)(2,1)S(1)}) fusion(bf16[8,8,8,3072]{3,2,1,0:T(8,128)(2,1)} %bitcast.110, s32[]{:T(128)} %bitcast.3, s32[]{:T(128)} %bitcast.4, s32[]{:T(128)} %bitcast.6, ...), kind=kLoop, calls=%fused_computation.51 | loop fusion | bytes 393240 | tf_op jit(solution)/shard_map/dynamic_slice | solution.py:19
  44.3 3.2 %collective-permute-done.4.refs_1_ = bf16[4,128,512]{2,1,0:T(8,128)(2,1)S(1)} collective-permute-done((bf16[4,128,512]{2,1,0:T(8,128)(2,1)}, bf16[4,128,512]{2,1,0:T(8,128)(2,1)S(1)}, u32[]{:S(2)}, u32[]{:S(2)}) %collective-permute-start.4) | collective-permute-done | bytes 524320 | tf_op jit(solution)/shard_map/ppermute | solution.py:42
  47.5 2.7 %collective-permute-done.6.refs_4_ = bf16[4,128,512]{2,1,0:T(8,128)(2,1)S(1)} collective-permute-done((bf16[4,128,512]{2,1,0:T(8,128)(2,1)}, bf16[4,128,512]{2,1,0:T(8,128)(2,1)S(1)}, u32[]{:S(2)}, u32[]{:S(2)}) %collective-permute-start.6) | collective-permute-done | bytes 524320 | tf_op jit(solution)/shard_map/ppermute | solution.py:42
  51.9 4.3 %collective-permute-start.9 = (bf16[128,512]{1,0:T(8,128)(2,1)S(1)}, bf16[128,512]{1,0:T(8,128)(2,1)S(1)}, u32[]{:S(2)}, u32[]{:S(2)}) collective-permute-start(bf16[128,512]{1,0:T(8,128)(2,1)S(1)} %get-tuple-element.62), channel_id=1, source_target_pairs={{0,2},{1,3},{2,0},{3,1},{4,6},{5,7},{6,4},{7,5},{8,10},{9,11},{10,... | collective-permute-start | bytes 393224 | tf_op jit(solution)/shard_map/ppermute | solution.py:42
  56.5 1.9 collective-permute-start.12
  61.3 2.7 %collective-permute-done.11 = bf16[128,512]{1,0:T(8,128)(2,1)S(1)} collective-permute-done((bf16[128,512]{1,0:T(8,128)(2,1)S(1)}, bf16[128,512]{1,0:T(8,128)(2,1)S(1)}, u32[]{:S(2)}, u32[]{:S(2)}) %collective-permute-start.11) | collective-permute-done | bytes 131104 | tf_op jit(solution)/shard_map/ppermute | solution.py:42
  67.7 5.5 %all-to-all-start = ((bf16[16,144,384]{2,1,0:T(8,128)(2,1)}), bf16[16,144,384]{2,1,0:T(8,128)(2,1)S(1)}, u32[]{:S(2)}, u32[]{:S(2)}) async-start(bf16[16,144,384]{2,1,0:T(8,128)(2,1)} %bitcast.24), calls=%async_computation | async-start | bytes 3538944 | tf_op jit(solution)/shard_map/all_to_all | solution.py:15
  74.0 19.2 %all-to-all-done.message = bf16[16,144,384]{2,1,0:T(8,128)(2,1)S(1)} async-done(((bf16[16,144,384]{2,1,0:T(8,128)(2,1)}), bf16[16,144,384]{2,1,0:T(8,128)(2,1)S(1)}, u32[]{:S(2)}, u32[]{:S(2)}) %all-to-all-start) | async-done | bytes 1769504 | tf_op jit(solution)/shard_map/all_to_all | solution.py:15
  93.2 2.3 %shard_map.144 = (bf16[16,128,384]{2,1,0:T(8,128)(2,1)}, f32[1,256]{1,0:T(1,128)S(1)}) custom-call(s32[2]{0:T(128)S(1)} %pad_add_fusion.place, bf16[16,144,384]{2,1,0:T(8,128)(2,1)S(1)} %all-to-all-done.message, s32[1,256]{1,0:T(1,128)S(1)} %bitcast.95), custom_call_target="tpu_custom_call" | custom-call | flops 5308416 | bytes 3538944 | tf_op jit(solution)/shard_map/pallas_call | solution.py:322
  95.5 5.2 %all-to-all-start.1 = ((bf16[16,128,384]{2,1,0:T(8,128)(2,1)}), bf16[16,128,384]{2,1,0:T(8,128)(2,1)S(1)}, u32[]{:S(2)}, u32[]{:S(2)}) async-start(bf16[16,128,384]{2,1,0:T(8,128)(2,1)} %get-tuple-element.68), calls=%async_computation.1 | async-start | bytes 3145728 | tf_op jit(solution)/shard_map/all_to_all | solution.py:15
  101.9 16.3 %all-to-all-done.1.pieces = bf16[16,128,384]{2,1,0:T(8,128)(2,1)S(1)} async-done(((bf16[16,128,384]{2,1,0:T(8,128)(2,1)}), bf16[16,128,384]{2,1,0:T(8,128)(2,1)S(1)}, u32[]{:S(2)}, u32[]{:S(2)}) %all-to-all-start.1) | async-done | bytes 1572896 | tf_op jit(solution)/shard_map/all_to_all | solution.py:15
  119.3 9.5 %shard_map.145 = (bf16[256,3072]{1,0:T(8,128)(2,1)}, f32[256,512]{1,0:T(8,128)}, f32[256,512]{1,0:T(8,128)}, bf16[16,16,3072]{2,1,0:T(8,128)(2,1)}) custom-call(bf16[16,128,384]{2,1,0:T(8,128)(2,1)} %copy-done.7, f32[1,3072]{1,0:T(1,128)} %bitcast.93, bf16[2,128,512]{2,1,0:T(8,128)(2,1)} %fusion.10.order, bf16[3072,512]{1,0:T(8,128)(2,1)} %gate_hbm.1, ...), custom_call_target="tpu_custom_call" | custom-call | flops 2415919104 | bytes 17301504 | tf_op jit(solution)/shard_map/pallas_call | solution.py:413
  128.8 5.8 %all-to-all-start.2 = ((bf16[16,16,3072]{2,1,0:T(8,128)(2,1)}), bf16[16,16,3072]{2,1,0:T(8,128)(2,1)S(1)}, u32[]{:S(2)}, u32[]{:S(2)}) async-start(bf16[16,16,3072]{2,1,0:T(8,128)(2,1)} %get-tuple-element.72.order), calls=%async_computation.2 | async-start | bytes 3145728 | tf_op jit(solution)/shard_map/all_to_all | solution.py:15
  134.7 4.6 %shard_map.146 = (bf16[256,512]{1,0:T(8,128)(2,1)}, bf16[256,512]{1,0:T(8,128)(2,1)}) custom-call(bf16[256,3072]{1,0:T(8,128)(2,1)} %bitcast.99, bf16[3072,512]{1,0:T(8,128)(2,1)} %down.1, f32[256,512]{1,0:T(8,128)} %get-tuple-element.70.gate, f32[256,512]{1,0:T(8,128)} %get-tuple-element.71.up, bf16[16,16,3072]{2,1,0:T(8,128)(2,1)} %get-tuple-element.72.order), custom_call_target="tpu_custom_call" | custom-call | flops 805306368 | bytes 6815744 | tf_op jit(solution)/shard_map/pallas_call | solution.py:218
  140.3 2.1 fusion.30
  142.4 2.3 %fusion = bf16[256,3072]{1,0:T(8,128)(2,1)} fusion(f32[256,3072]{1,0:T(8,128)S(1)} %fusion.30, bf16[256,512]{1,0:T(8,128)(2,1)S(1)} %copy-done.9, bf16[3072,512]{1,0:T(8,128)(2,1)S(1)} %copy-done.6), kind=kOutput, calls=%fused_computation.1 | convolution fusion | flops 806879232 | bytes 8126464 | tf_op jit(solution)/shard_map/dot_general | solution.py:30
  144.7 6.3 %all-to-all-done.2.terms = bf16[16,16,3072]{2,1,0:T(8,128)(2,1)S(1)} async-done(((bf16[16,16,3072]{2,1,0:T(8,128)(2,1)}), bf16[16,16,3072]{2,1,0:T(8,128)(2,1)S(1)}, u32[]{:S(2)}, u32[]{:S(2)}) %all-to-all-start.2) | async-done | bytes 1572896 | tf_op jit(solution)/shard_map/all_to_all | solution.py:15
  152.5 3.7 %all-to-all-start.3 = ((bf16[16,16,3072]{2,1,0:T(8,128)(2,1)}), bf16[16,16,3072]{2,1,0:T(8,128)(2,1)S(1)}, u32[]{:S(2)}, u32[]{:S(2)}) async-start(bf16[16,16,3072]{2,1,0:T(8,128)(2,1)} %bitcast.41), calls=%async_computation.3 | async-start | bytes 3145728 | tf_op jit(solution)/shard_map/all_to_all | solution.py:15
  158.0 14.3 %all-to-all-done.3.terms = bf16[16,16,3072]{2,1,0:T(8,128)(2,1)S(1)} async-done(((bf16[16,16,3072]{2,1,0:T(8,128)(2,1)}), bf16[16,16,3072]{2,1,0:T(8,128)(2,1)S(1)}, u32[]{:S(2)}, u32[]{:S(2)}) %all-to-all-start.3) | async-done | bytes 1572896 | tf_op jit(solution)/shard_map/all_to_all | solution.py:15
  172.7 9.9 %all_to_all.30.piece = bf16[8,16,384]{2,1,0:T(8,128)(2,1)S(1)} all-to-all(bf16[8,16,384]{2,1,0:T(8,128)(2,1)S(1)} %shard_map.148), channel_id=1, replica_groups=mesh['dp'=8,'mp'=16] {'dp'}, dimensions={0} | all-to-all | bytes 196608 | tf_op jit(solution)/shard_map/all_to_all | solution.py:15
  183.9 3.7 %all-to-all-start.5 = ((bf16[16,8,16,384]{3,2,1,0:T(8,128)(2,1)}), bf16[16,8,16,384]{3,2,1,0:T(8,128)(2,1)S(1)}, u32[]{:S(2)}, u32[]{:S(2)}) async-start(bf16[16,8,16,384]{3,2,1,0:T(8,128)(2,1)} %shard_map.149), calls=%async_computation.5 | async-start | bytes 3145728 | tf_op jit(solution)/shard_map/all_to_all | solution.py:15
  198.9 3.5 %select_bitcast_fusion.3 = (bf16[8,1,3072]{2,0,1:T(8,128)(2,1)S(1)}, bf16[8,1,3072]{2,0,1:T(8,128)(2,1)S(1)}, bf16[8,1,3072]{2,0,1:T(8,128)(2,1)S(1)}, bf16[8,1,3072]{2,0,1:T(8,128)(2,1)S(1)}) fusion(bf16[8,32,3072]{2,1,0:T(8,128)(2,1)} %bitcast.111, s32[]{:T(128)S(6)} %select_n.131, s32[]{:T(128)S(6)} %mul.54, pred[]{:T(512)} %get-tuple-element.84, ...), kind=kLoop, calls=%fused_computation.34 | loop fusion | flops 98304 | bytes 393252 | tf_op jit(solution)/shard_map/jit(_where)/select_n | solution.py:603
  203.4 8.3 %all-to-all-done.5 = bf16[16,8,16,384]{3,2,1,0:T(8,128)(2,1)S(1)} async-done(((bf16[16,8,16,384]{3,2,1,0:T(8,128)(2,1)}), bf16[16,8,16,384]{3,2,1,0:T(8,128)(2,1)S(1)}, u32[]{:S(2)}, u32[]{:S(2)}) %all-to-all-start.5) | async-done | bytes 1572896 | tf_op jit(solution)/shard_map/all_to_all | solution.py:15
  211.6 3.8 %fusion.7 = f32[512,384]{1,0:T(8,128)} fusion(bf16[16,8,16,384]{3,2,1,0:T(8,128)(2,1)S(1)} %all-to-all-done.5, bf16[8,16,16,512]{3,2,0,1:T(8,128)(2,1)} %all-gather.8.cloned.1.call-done), kind=kOutput, calls=%fused_computation.10 | convolution fusion | flops 805306368 | bytes 4456448 | tf_op jit(solution)/shard_map/dot_general | solution.py:586
  (96 shorter events, 26.8 us)
Async XLA Ops:
  7.2 32.7 %all-gather.10.cloned.1.call-start = ((), (), s32[]{:S(2)}) async-start(), calls=%async_computation.7 | async-start | bytes 3538944 | tf_op jit(solution)/shard_map/all_gather | solution.py:510
  10.3 11.0 %copy-start.11 = (s32[16]{0:T(128)S(1)}, s32[16]{0:T(128)}, u32[]{:S(2)}) copy-start(s32[16]{0:T(128)} %param.21) | copy-start | bytes 196
  10.3 13.7 %copy-start.1 = (bf16[256,512]{1,0:T(8,128)(2,1)S(1)}, bf16[256,512]{1,0:T(8,128)(2,1)}, u32[]{:S(2)}) copy-start(bf16[256,512]{1,0:T(8,128)(2,1)} %left.3) | copy-start | bytes 786436
  13.8 17.4 %collective-permute-start = (bf16[4,64,512]{2,1,0:T(8,128)(2,1)S(1)}, bf16[4,64,512]{2,1,0:T(8,128)(2,1)S(1)}, u32[]{:S(2)}, u32[]{:S(2)}) collective-permute-start(bf16[4,64,512]{2,1,0:T(8,128)(2,1)S(1)} %get-tuple-element.49), channel_id=1, source_target_pairs={{0,4},{1,5},{2,6},{3,7},{4,8},{5,9},{6,10},{7,11},{8,12},{9,13},{1... | collective-permute-start | bytes 786440 | tf_op jit(solution)/shard_map/ppermute | solution.py:42
  15.6 15.7 %collective-permute-start.1 = (bf16[4,64,512]{2,1,0:T(8,128)(2,1)S(1)}, bf16[4,64,512]{2,1,0:T(8,128)(2,1)S(1)}, u32[]{:S(2)}, u32[]{:S(2)}) collective-permute-start(bf16[4,64,512]{2,1,0:T(8,128)(2,1)S(1)} %get-tuple-element.50), channel_id=1, source_target_pairs={{0,12},{1,13},{2,14},{3,15},{4,0},{5,1},{6,2},{7,3},{8,4},{9,5},{1... | collective-permute-start | bytes 786440 | tf_op jit(solution)/shard_map/ppermute | solution.py:42
  17.1 14.1 %collective-permute-start.2 = (bf16[4,64,512]{2,1,0:T(8,128)(2,1)S(1)}, bf16[4,64,512]{2,1,0:T(8,128)(2,1)S(1)}, u32[]{:S(2)}, u32[]{:S(2)}) collective-permute-start(bf16[4,64,512]{2,1,0:T(8,128)(2,1)S(1)} %get-tuple-element.53), channel_id=1, source_target_pairs={{0,1},{1,2},{2,3},{3,0},{4,5},{5,6},{6,7},{7,4},{8,9},{9,10},{10,1... | collective-permute-start | bytes 786440 | tf_op jit(solution)/shard_map/ppermute | solution.py:42
  19.1 12.1 %collective-permute-start.3 = (bf16[4,64,512]{2,1,0:T(8,128)(2,1)S(1)}, bf16[4,64,512]{2,1,0:T(8,128)(2,1)S(1)}, u32[]{:S(2)}, u32[]{:S(2)}) collective-permute-start(bf16[4,64,512]{2,1,0:T(8,128)(2,1)S(1)} %get-tuple-element.54), channel_id=1, source_target_pairs={{0,3},{1,0},{2,1},{3,2},{4,7},{5,4},{6,5},{7,6},{8,11},{9,8},{10,9... | collective-permute-start | bytes 786440 | tf_op jit(solution)/shard_map/ppermute | solution.py:42
  33.1 14.4 %collective-permute-start.4 = (bf16[4,128,512]{2,1,0:T(8,128)(2,1)}, bf16[4,128,512]{2,1,0:T(8,128)(2,1)S(1)}, u32[]{:S(2)}, u32[]{:S(2)}) collective-permute-start(bf16[4,128,512]{2,1,0:T(8,128)(2,1)} %get-tuple-element.55), channel_id=1, source_target_pairs={{0,4},{1,5},{2,6},{3,7},{4,8},{5,9},{6,10},{7,11},{8,12},{9,13},{1... | collective-permute-start | bytes 1572872 | tf_op jit(solution)/shard_map/ppermute | solution.py:42
  33.5 14.0 %collective-permute-start.5 = (bf16[4,128,512]{2,1,0:T(8,128)(2,1)}, bf16[4,128,512]{2,1,0:T(8,128)(2,1)S(1)}, u32[]{:S(2)}, u32[]{:S(2)}) collective-permute-start(bf16[4,128,512]{2,1,0:T(8,128)(2,1)} %get-tuple-element.56), channel_id=1, source_target_pairs={{0,12},{1,13},{2,14},{3,15},{4,0},{5,1},{6,2},{7,3},{8,4},{9,5},{1... | collective-permute-start | bytes 1572872 | tf_op jit(solution)/shard_map/ppermute | solution.py:42
  36.3 13.8 %collective-permute-start.6 = (bf16[4,128,512]{2,1,0:T(8,128)(2,1)}, bf16[4,128,512]{2,1,0:T(8,128)(2,1)S(1)}, u32[]{:S(2)}, u32[]{:S(2)}) collective-permute-start(bf16[4,128,512]{2,1,0:T(8,128)(2,1)} %get-tuple-element.58), channel_id=1, source_target_pairs={{0,1},{1,2},{2,3},{3,0},{4,5},{5,6},{6,7},{7,4},{8,9},{9,10},{10,1... | collective-permute-start | bytes 1572872 | tf_op jit(solution)/shard_map/ppermute | solution.py:42
  36.3 13.8 %collective-permute-start.7 = (bf16[4,128,512]{2,1,0:T(8,128)(2,1)}, bf16[4,128,512]{2,1,0:T(8,128)(2,1)}, u32[]{:S(2)}, u32[]{:S(2)}) collective-permute-start(bf16[4,128,512]{2,1,0:T(8,128)(2,1)} %get-tuple-element.59), channel_id=1, source_target_pairs={{0,3},{1,0},{2,1},{3,2},{4,7},{5,4},{6,5},{7,6},{8,11},{9,8},{10,9... | collective-permute-start | bytes 1572872 | tf_op jit(solution)/shard_map/ppermute | solution.py:42
  44.3 17.0 %copy-start.2 = (bf16[2,8,3072]{2,1,0:T(8,128)(2,1)}, bf16[2,8,3072]{2,1,0:T(8,128)(2,1)S(1)}, u32[]{:S(2)}) copy-start(bf16[2,8,3072]{2,1,0:T(8,128)(2,1)S(1)} %pad_maximum_fusion.2.refs_7_) | copy-start | bytes 294916
  50.2 14.8 %copy-start.8 = (bf16[256,512]{1,0:T(8,128)(2,1)S(1)}, bf16[256,512]{1,0:T(8,128)(2,1)}, u32[]{:S(2)}) copy-start(bf16[256,512]{1,0:T(8,128)(2,1)} %param.17) | copy-start | bytes 786436
  50.2 14.8 %copy-start.10 = (f32[512]{0:T(512)S(1)}, f32[512]{0:T(512)}, u32[]{:S(2)}) copy-start(f32[512]{0:T(512)} %param.18) | copy-start | bytes 6148
  51.6 13.6 %copy-start.12 = (bf16[512,3072]{1,0:T(8,128)(2,1)S(1)}, bf16[512,3072]{1,0:T(8,128)(2,1)}, u32[]{:S(2)}) copy-start(bf16[512,3072]{1,0:T(8,128)(2,1)} %param.19) | copy-start | bytes 9437188
  51.7 6.7 %collective-permute-start.8 = (bf16[128,512]{1,0:T(8,128)(2,1)S(1)}, bf16[128,512]{1,0:T(8,128)(2,1)S(1)}, u32[]{:S(2)}, u32[]{:S(2)}) collective-permute-start(bf16[128,512]{1,0:T(8,128)(2,1)S(1)} %get-tuple-element.61), channel_id=1, source_target_pairs={{0,1},{1,2},{2,3},{3,0},{4,5},{5,6},{6,7},{7,4},{8,9},{9,10},{10,1... | collective-permute-start | bytes 393224 | tf_op jit(solution)/shard_map/ppermute | solution.py:42
  51.9 8.7 %collective-permute-start.9 = (bf16[128,512]{1,0:T(8,128)(2,1)S(1)}, bf16[128,512]{1,0:T(8,128)(2,1)S(1)}, u32[]{:S(2)}, u32[]{:S(2)}) collective-permute-start(bf16[128,512]{1,0:T(8,128)(2,1)S(1)} %get-tuple-element.62), channel_id=1, source_target_pairs={{0,2},{1,3},{2,0},{3,1},{4,6},{5,7},{6,4},{7,5},{8,10},{9,11},{10,... | collective-permute-start | bytes 393224 | tf_op jit(solution)/shard_map/ppermute | solution.py:42
  56.2 5.0 %collective-permute-start.10 = (bf16[128,512]{1,0:T(8,128)(2,1)S(1)}, bf16[128,512]{1,0:T(8,128)(2,1)S(1)}, u32[]{:S(2)}, u32[]{:S(2)}) collective-permute-start(bf16[128,512]{1,0:T(8,128)(2,1)S(1)} %get-tuple-element.63), channel_id=1, source_target_pairs={{0,3},{1,0},{2,1},{3,2},{4,7},{5,4},{6,5},{7,6},{8,11},{9,8},{10,9... | collective-permute-start | bytes 393224 | tf_op jit(solution)/shard_map/ppermute | solution.py:42
  56.4 7.7 %collective-permute-start.11 = (bf16[128,512]{1,0:T(8,128)(2,1)S(1)}, bf16[128,512]{1,0:T(8,128)(2,1)S(1)}, u32[]{:S(2)}, u32[]{:S(2)}) collective-permute-start(bf16[128,512]{1,0:T(8,128)(2,1)S(1)} %get-tuple-element.65), channel_id=1, source_target_pairs={{0,4},{1,5},{2,6},{3,7},{4,8},{5,9},{6,10},{7,11},{8,12},{9,13},{1... | collective-permute-start | bytes 393224 | tf_op jit(solution)/shard_map/ppermute | solution.py:42
  56.5 7.6 %collective-permute-start.12 = (bf16[128,512]{1,0:T(8,128)(2,1)S(1)}, bf16[128,512]{1,0:T(8,128)(2,1)S(1)}, u32[]{:S(2)}, u32[]{:S(2)}) collective-permute-start(bf16[128,512]{1,0:T(8,128)(2,1)S(1)} %get-tuple-element.66), channel_id=1, source_target_pairs={{0,8},{1,9},{2,10},{3,11},{4,12},{5,13},{6,14},{7,15},{8,0},{9,1},... | collective-permute-start | bytes 393224 | tf_op jit(solution)/shard_map/ppermute | solution.py:42
  58.4 6.5 %collective-permute-start.13 = (bf16[128,512]{1,0:T(8,128)(2,1)S(1)}, bf16[128,512]{1,0:T(8,128)(2,1)S(1)}, u32[]{:S(2)}, u32[]{:S(2)}) collective-permute-start(bf16[128,512]{1,0:T(8,128)(2,1)S(1)} %get-tuple-element.67), channel_id=1, source_target_pairs={{0,12},{1,13},{2,14},{3,15},{4,0},{5,1},{6,2},{7,3},{8,4},{9,5},{1... | collective-permute-start | bytes 393224 | tf_op jit(solution)/shard_map/ppermute | solution.py:42
  67.7 25.5 %copy-start.4 = (s32[256]{0:T(256)S(1)}, s32[256]{0:T(256)}, u32[]{:S(2)}) copy-start(s32[256]{0:T(256)} %param.20) | copy-start | bytes 3076
  67.7 25.5 %all-to-all-start = ((bf16[16,144,384]{2,1,0:T(8,128)(2,1)}), bf16[16,144,384]{2,1,0:T(8,128)(2,1)S(1)}, u32[]{:S(2)}, u32[]{:S(2)}) async-start(bf16[16,144,384]{2,1,0:T(8,128)(2,1)} %bitcast.24), calls=%async_computation | async-start | bytes 3538944 | tf_op jit(solution)/shard_map/all_to_all | solution.py:15
  73.2 61.6 %all-gather.12.cloned.1.call-start = ((), (), s32[]{:S(2)}) async-start(), calls=%async_computation.8 | async-start | bytes 1671168 | tf_op jit(solution)/shard_map/all_gather | solution.py:523
  95.5 22.7 %all-to-all-start.1 = ((bf16[16,128,384]{2,1,0:T(8,128)(2,1)}), bf16[16,128,384]{2,1,0:T(8,128)(2,1)S(1)}, u32[]{:S(2)}, u32[]{:S(2)}) async-start(bf16[16,128,384]{2,1,0:T(8,128)(2,1)} %get-tuple-element.68), calls=%async_computation.1 | async-start | bytes 3145728 | tf_op jit(solution)/shard_map/all_to_all | solution.py:15
  128.8 22.1 %all-to-all-start.2 = ((bf16[16,16,3072]{2,1,0:T(8,128)(2,1)}), bf16[16,16,3072]{2,1,0:T(8,128)(2,1)S(1)}, u32[]{:S(2)}, u32[]{:S(2)}) async-start(bf16[16,16,3072]{2,1,0:T(8,128)(2,1)} %get-tuple-element.72.order), calls=%async_computation.2 | async-start | bytes 3145728 | tf_op jit(solution)/shard_map/all_to_all | solution.py:15
  134.6 64.3 %all-gather.14.cloned.1.call-start = ((), (), s32[]{:S(2)}) async-start(), calls=%async_computation.9 | async-start | bytes 1769472 | tf_op jit(solution)/shard_map/all_gather | solution.py:593
  134.7 5.6 %copy-start.5 = (bf16[3072,512]{1,0:T(8,128)(2,1)S(1)}, bf16[3072,512]{1,0:T(8,128)(2,1)}, u32[]{:S(2)}) copy-start(bf16[3072,512]{1,0:T(8,128)(2,1)} %gate_hbm.1) | copy-start | bytes 9437188
  151.9 20.4 %copy-start.3 = (f32[3072]{0:T(1024)S(1)}, f32[3072]{0:T(1024)}, u32[]{:S(2)}) copy-start(f32[3072]{0:T(1024)} %param.24) | copy-start | bytes 36868
  151.9 51.5 %all-gather.8.cloned.1.call-start = ((), (), s32[]{:S(2)}) async-start(), calls=%async_computation.6 | async-start | bytes 2359296 | tf_op jit(solution)/shard_map/all_gather | solution.py:557
  152.5 19.8 %all-to-all-start.3 = ((bf16[16,16,3072]{2,1,0:T(8,128)(2,1)}), bf16[16,16,3072]{2,1,0:T(8,128)(2,1)S(1)}, u32[]{:S(2)}, u32[]{:S(2)}) async-start(bf16[16,16,3072]{2,1,0:T(8,128)(2,1)} %bitcast.41), calls=%async_computation.3 | async-start | bytes 3145728 | tf_op jit(solution)/shard_map/all_to_all | solution.py:15
  183.9 27.8 %all-to-all-start.5 = ((bf16[16,8,16,384]{3,2,1,0:T(8,128)(2,1)}), bf16[16,8,16,384]{3,2,1,0:T(8,128)(2,1)S(1)}, u32[]{:S(2)}, u32[]{:S(2)}) async-start(bf16[16,8,16,384]{3,2,1,0:T(8,128)(2,1)} %shard_map.149), calls=%async_computation.5 | async-start | bytes 3145728 | tf_op jit(solution)/shard_map/all_to_all | solution.py:15
  (4 other events, 6.4 us)
Sparse Core Ops, SparseCore 0:
  9.7 30.1 all-gather.9
  76.8 50.3 all-gather.11
  152.0 22.0 all-gather.13
  175.7 25.0 all-gather.7

commit v14 on v13

--- a/solution.py
+++ b/solution.py
@@ -107,7 +107,7 @@
 
 
 def gather_kernel(place, *refs):
-    ins, outs = refs[:6], refs[8:]
+    ins, outs = refs[:6], refs[7:]
     for block in (0, 1):
         kept, from_down, from_up = ins[3 * block : 3 * block + 3]
         here = place[1 - block]
@@ -168,7 +168,7 @@
     from_down1, from_up1 = step(up1, 0, 1), step(down1, 0, -1)
     sums = pl.pallas_call(
         gather_kernel,
-        in_specs=[scalars] + [whole] * 6 + [anywhere] * 2,
+        in_specs=[scalars] + [whole] * 6 + [anywhere],
         out_specs=[whole] * (2 * SIDE),
         out_shape=[
             jax.ShapeDtypeStruct((BLK, width), half if distance else full)
@@ -523,7 +523,7 @@
     dy = lax.all_gather(dy_rows, "mp", axis=0, tiled=False)
 
     hidden = residual.astype(full) + jnp.concatenate(
-        [total(v) for v in teacher_terms(attention, out_proj, mp, (sh_rows, dy_rows))], axis=0
+        [total(v) for v in teacher_terms(attention, out_proj, mp, (sh_rows,))], axis=0
     )
     squares = jnp.sum(hidden * hidden, axis=1)
     gained_hidden = hidden * final_gain

time: 223 us -> 222 us (level)
  transfers between devices with their start and end apart: 23 -> 23, of which waited for: 12 -> 13; matrix products, arithmetic and copies ran while one was open for 9% -> 10% of each run, Pallas kernels for 14% -> 14%
where the time goes in v14:
time: 222 us; the launch traced here: 221 us
  waiting for transfers between devices  75.3 us (34%)
  starting transfers between devices  45.6 us (21%)
  Pallas kernels  32.6 us (15%)
  between operations  25.6 us (12%)
  local copies, waits for them, and re-layouts  12.2 us (5%)
  other arithmetic  10.1 us (5%)
  matrix products  10 us (5%)
  blocking collectives  9.86 us (4%)
    all_to_all x5, waiting for transfers between devices, exchange(): return lax.all_to_all(pieces, axis, split_axis=0, concat_axis=0, tiled=True)  64.1 us
    all_to_all x5, starting transfers between devices, exchange(): return lax.all_to_all(pieces, axis, split_axis=0, concat_axis=0, tiled=True)  23.8 us
    ppermute x14, starting transfers between devices, step(): return lax.ppermute(value, 'mp', pairs)  21.6 us
    pallas_call x2, Pallas kernels, terms(): pl.pallas_call(kernel, in_specs=[scalars, whole, pl.BlockSpec(memory_spac...  10.9 us
    ppermute x14, waiting for transfers between devices, step(): return lax.ppermute(value, 'mp', pairs)  10.5 us
    all_to_all x1, blocking collectives, exchange(): return lax.all_to_all(pieces, axis, split_axis=0, concat_axis=0, tiled=True)  9.86 us
    pallas_call x1, Pallas kernels, forward(): pl.pallas_call(forward_kernel, in_specs=[whole, whole, pl.BlockSpec(memor...  9.52 us
    dynamic_slice x3, local copies, waits for them, and re-layouts, take(): return lax.dynamic_slice(array, starts, sizes, allow_negative_indices=False)  6.05 us
  transfers between devices with their start and end apart: 23, of which 13 were waited for; matrix products, arithmetic and copies ran while one was open for 10% of the time, Pallas kernels for 14%

profile of v14, /device:TPU:0, one launch (start us, length us, event | category | flops | bytes accessed | tf_op | source)
XLA Modules:
  0.0 221.3 jit_solution(11403164168901164878)
XLA Ops:
  7.2 2.0 pad_maximum_fusion.1
  10.3 3.6 %shard_map.141 = (bf16[4,64,512]{2,1,0:T(8,128)(2,1)S(1)}, bf16[4,64,512]{2,1,0:T(8,128)(2,1)S(1)}, bf16[4,64,512]{2,1,0:T(8,128)(2,1)S(1)}, bf16[4,64,512]{2,1,0:T(8,128)(2,1)S(1)}) custom-call(s32[2]{0:T(128)S(1)} %pad_add_fusion.1.place, bf16[256,512]{1,0:T(8,128)(2,1)S(1)} %copy-done, bf16[512,8192]{1,0:T(8,128)(2,1)} %right.3), custom_call_target="tpu_custom_call" | custom-call | flops 536870912 | bytes 4194304 | tf_op jit(solution)/shard_map/pallas_call | solution.py:135
  17.1 2.0 collective-permute-start.2
  19.1 2.1 collective-permute-start.3
  24.1 7.3 %shard_map.140 = (bf16[4,128,512]{2,1,0:T(8,128)(2,1)S(1)}, bf16[4,128,512]{2,1,0:T(8,128)(2,1)S(1)}, bf16[4,128,512]{2,1,0:T(8,128)(2,1)S(1)}, bf16[4,128,512]{...) custom-call(s32[2]{0:T(128)S(1)} %pad_add_fusion.1.place, ...), custom_call_target="tpu_custom_call" | custom-call | flops 2147483648 | bytes 8388608 | tf_op jit(solution)/shard_map/pallas_call | solution.py:135
  31.5 1.9 shard_map.142
  33.7 2.9 %collective-permute-start.5 = (bf16[4,128,512]{2,1,0:T(8,128)(2,1)}, bf16[4,128,512]{2,1,0:T(8,128)(2,1)S(1)}, u32[]{:S(2)}, u32[]{:S(2)}) collective-permute-start(bf16[4,128,512]{2,1,0:T(8,128)(2,1)} %get-tuple-element.56), channel_id=1, source_target_pairs={{0,12},{1,13},{2,14},{3,15},{4,0},{5,1},{6,2},{7,3},{8,4},{9,5},{1... | collective-permute-start | bytes 1572872 | tf_op jit(solution)/shard_map/ppermute | solution.py:42
  36.6 3.2 %collective-permute-start.7 = (bf16[4,128,512]{2,1,0:T(8,128)(2,1)}, bf16[4,128,512]{2,1,0:T(8,128)(2,1)S(1)}, u32[]{:S(2)}, u32[]{:S(2)}) collective-permute-start(bf16[4,128,512]{2,1,0:T(8,128)(2,1)} %get-tuple-element.59), channel_id=1, source_target_pairs={{0,3},{1,0},{2,1},{3,2},{4,7},{5,4},{6,5},{7,6},{8,11},{9,8},{10,9... | collective-permute-start | bytes 1572872 | tf_op jit(solution)/shard_map/ppermute | solution.py:42
  39.9 5.1 %fusion.28 = (bf16[8,3072]{1,0:T(8,128)(2,1)S(1)}, bf16[1,8,1,3072]{3,2,1,0:T(2,128)(2,1)S(1)}, bf16[8,3072]{1,0:T(8,128)(2,1)S(1)}, bf16[1,8,1,3072]{3,2,1,0:T(...) fusion(bf16[8,8,8,3072]{3,2,1,0:T(8,128)(2,1)} %bitcast.104, s32[]{:T(128)} %bitcast.3, ...), kind=kLoop, calls=%fused_computation.80 | loop fusion | bytes 491544 | tf_op jit(solution)/shard_map/dynamic_slice | solution.py:19
  45.1 2.7 %collective-permute-done.4.refs_1_ = bf16[4,128,512]{2,1,0:T(8,128)(2,1)S(1)} collective-permute-done((bf16[4,128,512]{2,1,0:T(8,128)(2,1)}, bf16[4,128,512]{2,1,0:T(8,128)(2,1)S(1)}, u32[]{:S(2)}, u32[]{:S(2)}) %collective-permute-start.4) | collective-permute-done | bytes 524320 | tf_op jit(solution)/shard_map/ppermute | solution.py:42
  47.7 2.7 %collective-permute-done.6.refs_4_ = bf16[4,128,512]{2,1,0:T(8,128)(2,1)S(1)} collective-permute-done((bf16[4,128,512]{2,1,0:T(8,128)(2,1)}, bf16[4,128,512]{2,1,0:T(8,128)(2,1)S(1)}, u32[]{:S(2)}, u32[]{:S(2)}) %collective-permute-start.6) | collective-permute-done | bytes 524320 | tf_op jit(solution)/shard_map/ppermute | solution.py:42
  51.5 4.3 %collective-permute-start.9 = (bf16[128,512]{1,0:T(8,128)(2,1)S(1)}, bf16[128,512]{1,0:T(8,128)(2,1)S(1)}, u32[]{:S(2)}, u32[]{:S(2)}) collective-permute-start(bf16[128,512]{1,0:T(8,128)(2,1)S(1)} %get-tuple-element.62), channel_id=1, source_target_pairs={{0,2},{1,3},{2,0},{3,1},{4,6},{5,7},{6,4},{7,5},{8,10},{9,11},{10,... | collective-permute-start | bytes 393224 | tf_op jit(solution)/shard_map/ppermute | solution.py:42
  55.8 2.0 collective-permute-start.12
  60.8 2.6 %collective-permute-done.11 = bf16[128,512]{1,0:T(8,128)(2,1)S(1)} collective-permute-done((bf16[128,512]{1,0:T(8,128)(2,1)S(1)}, bf16[128,512]{1,0:T(8,128)(2,1)S(1)}, u32[]{:S(2)}, u32[]{:S(2)}) %collective-permute-start.11) | collective-permute-done | bytes 131104 | tf_op jit(solution)/shard_map/ppermute | solution.py:42
  67.0 5.5 %all-to-all-start = ((bf16[16,144,384]{2,1,0:T(8,128)(2,1)}), bf16[16,144,384]{2,1,0:T(8,128)(2,1)S(1)}, u32[]{:S(2)}, u32[]{:S(2)}) async-start(bf16[16,144,384]{2,1,0:T(8,128)(2,1)} %bitcast.18), calls=%async_computation | async-start | bytes 3538944 | tf_op jit(solution)/shard_map/all_to_all | solution.py:15
  73.4 19.2 %all-to-all-done.message = bf16[16,144,384]{2,1,0:T(8,128)(2,1)S(1)} async-done(((bf16[16,144,384]{2,1,0:T(8,128)(2,1)}), bf16[16,144,384]{2,1,0:T(8,128)(2,1)S(1)}, u32[]{:S(2)}, u32[]{:S(2)}) %all-to-all-start) | async-done | bytes 1769504 | tf_op jit(solution)/shard_map/all_to_all | solution.py:15
  92.6 2.3 %shard_map.144 = (bf16[16,128,384]{2,1,0:T(8,128)(2,1)}, f32[1,256]{1,0:T(1,128)S(1)}) custom-call(s32[2]{0:T(128)S(1)} %pad_add_fusion.place, bf16[16,144,384]{2,1,0:T(8,128)(2,1)S(1)} %all-to-all-done.message, s32[1,256]{1,0:T(1,128)S(1)} %bitcast.91), custom_call_target="tpu_custom_call" | custom-call | flops 5308416 | bytes 3538944 | tf_op jit(solution)/shard_map/pallas_call | solution.py:322
  94.9 5.1 %all-to-all-start.1 = ((bf16[16,128,384]{2,1,0:T(8,128)(2,1)}), bf16[16,128,384]{2,1,0:T(8,128)(2,1)S(1)}, u32[]{:S(2)}, u32[]{:S(2)}) async-start(bf16[16,128,384]{2,1,0:T(8,128)(2,1)} %get-tuple-element.68), calls=%async_computation.1 | async-start | bytes 3145728 | tf_op jit(solution)/shard_map/all_to_all | solution.py:15
  101.2 16.4 %all-to-all-done.1.pieces = bf16[16,128,384]{2,1,0:T(8,128)(2,1)S(1)} async-done(((bf16[16,128,384]{2,1,0:T(8,128)(2,1)}), bf16[16,128,384]{2,1,0:T(8,128)(2,1)S(1)}, u32[]{:S(2)}, u32[]{:S(2)}) %all-to-all-start.1) | async-done | bytes 1572896 | tf_op jit(solution)/shard_map/all_to_all | solution.py:15
  118.7 9.5 %shard_map.145 = (bf16[256,3072]{1,0:T(8,128)(2,1)}, f32[256,512]{1,0:T(8,128)}, f32[256,512]{1,0:T(8,128)}, bf16[16,16,3072]{2,1,0:T(8,128)(2,1)}) custom-call(bf16[16,128,384]{2,1,0:T(8,128)(2,1)} %copy-done.6, f32[1,3072]{1,0:T(1,128)} %bitcast.89, bf16[2,128,512]{2,1,0:T(8,128)(2,1)} %fusion.10.order, bf16[3072,512]{1,0:T(8,128)(2,1)} %gate_hbm.1, ...), custom_call_target="tpu_custom_call" | custom-call | flops 2415919104 | bytes 17301504 | tf_op jit(solution)/shard_map/pallas_call | solution.py:413
  128.3 5.8 %all-to-all-start.2 = ((bf16[16,16,3072]{2,1,0:T(8,128)(2,1)}), bf16[16,16,3072]{2,1,0:T(8,128)(2,1)S(1)}, u32[]{:S(2)}, u32[]{:S(2)}) async-start(bf16[16,16,3072]{2,1,0:T(8,128)(2,1)} %get-tuple-element.72.order), calls=%async_computation.2 | async-start | bytes 3145728 | tf_op jit(solution)/shard_map/all_to_all | solution.py:15
  134.2 4.6 %shard_map.146 = (bf16[256,512]{1,0:T(8,128)(2,1)}, bf16[256,512]{1,0:T(8,128)(2,1)}) custom-call(bf16[256,3072]{1,0:T(8,128)(2,1)} %bitcast.95, bf16[3072,512]{1,0:T(8,128)(2,1)} %down.1, f32[256,512]{1,0:T(8,128)} %get-tuple-element.70.gate, f32[256,512]{1,0:T(8,128)} %get-tuple-element.71.up, bf16[16,16,3072]{2,1,0:T(8,128)(2,1)} %get-tuple-element.72.order), custom_call_target="tpu_custom_call" | custom-call | flops 805306368 | bytes 6815744 | tf_op jit(solution)/shard_map/pallas_call | solution.py:218
  139.8 2.1 fusion.32
  141.9 2.2 %fusion = bf16[256,3072]{1,0:T(8,128)(2,1)} fusion(f32[256,3072]{1,0:T(8,128)S(1)} %fusion.32, bf16[256,512]{1,0:T(8,128)(2,1)S(1)} %copy-done.9, bf16[3072,512]{1,0:T(8,128)(2,1)S(1)} %copy-done.5), kind=kOutput, calls=%fused_computation.1 | convolution fusion | flops 806879232 | bytes 8126464 | tf_op jit(solution)/shard_map/dot_general | solution.py:30
  144.1 6.3 %all-to-all-done.2.terms = bf16[16,16,3072]{2,1,0:T(8,128)(2,1)S(1)} async-done(((bf16[16,16,3072]{2,1,0:T(8,128)(2,1)}), bf16[16,16,3072]{2,1,0:T(8,128)(2,1)S(1)}, u32[]{:S(2)}, u32[]{:S(2)}) %all-to-all-start.2) | async-done | bytes 1572896 | tf_op jit(solution)/shard_map/all_to_all | solution.py:15
  151.9 3.7 %all-to-all-start.3 = ((bf16[16,16,3072]{2,1,0:T(8,128)(2,1)}), bf16[16,16,3072]{2,1,0:T(8,128)(2,1)S(1)}, u32[]{:S(2)}, u32[]{:S(2)}) async-start(bf16[16,16,3072]{2,1,0:T(8,128)(2,1)} %bitcast.35), calls=%async_computation.3 | async-start | bytes 3145728 | tf_op jit(solution)/shard_map/all_to_all | solution.py:15
  157.5 14.3 %all-to-all-done.3.terms = bf16[16,16,3072]{2,1,0:T(8,128)(2,1)S(1)} async-done(((bf16[16,16,3072]{2,1,0:T(8,128)(2,1)}), bf16[16,16,3072]{2,1,0:T(8,128)(2,1)S(1)}, u32[]{:S(2)}, u32[]{:S(2)}) %all-to-all-start.3) | async-done | bytes 1572896 | tf_op jit(solution)/shard_map/all_to_all | solution.py:15
  172.1 9.9 %all_to_all.30.piece = bf16[8,16,384]{2,1,0:T(8,128)(2,1)S(1)} all-to-all(bf16[8,16,384]{2,1,0:T(8,128)(2,1)S(1)} %shard_map.148), channel_id=1, replica_groups=mesh['dp'=8,'mp'=16] {'dp'}, dimensions={0} | all-to-all | bytes 196608 | tf_op jit(solution)/shard_map/all_to_all | solution.py:15
  183.3 3.7 %all-to-all-start.5 = ((bf16[16,8,16,384]{3,2,1,0:T(8,128)(2,1)}), bf16[16,8,16,384]{3,2,1,0:T(8,128)(2,1)S(1)}, u32[]{:S(2)}, u32[]{:S(2)}) async-start(bf16[16,8,16,384]{3,2,1,0:T(8,128)(2,1)} %shard_map.149), calls=%async_computation.5 | async-start | bytes 3145728 | tf_op jit(solution)/shard_map/all_to_all | solution.py:15
  198.8 3.4 %select_bitcast_fusion.3 = (bf16[8,1,3072]{2,0,1:T(8,128)(2,1)S(1)}, bf16[8,1,3072]{2,0,1:T(8,128)(2,1)S(1)}, bf16[8,1,3072]{2,0,1:T(8,128)(2,1)S(1)}, bf16[8,1,3072]{2,0,1:T(8,128)(2,1)S(1)}) fusion(bf16[8,32,3072]{2,1,0:T(8,128)(2,1)} %bitcast.105, s32[]{:T(128)S(6)} %select_n.131, s32[]{:T(128)S(6)} %mul.54, pred[]{:T(512)} %get-tuple-element.88, ...), kind=kLoop, calls=%fused_computation.36 | loop fusion | flops 98304 | bytes 393252 | tf_op jit(solution)/shard_map/jit(_where)/select_n | solution.py:603
  203.1 7.9 %all-to-all-done.5 = bf16[16,8,16,384]{3,2,1,0:T(8,128)(2,1)S(1)} async-done(((bf16[16,8,16,384]{3,2,1,0:T(8,128)(2,1)}), bf16[16,8,16,384]{3,2,1,0:T(8,128)(2,1)S(1)}, u32[]{:S(2)}, u32[]{:S(2)}) %all-to-all-start.5) | async-done | bytes 1572896 | tf_op jit(solution)/shard_map/all_to_all | solution.py:15
  211.0 3.8 %fusion.7 = f32[512,384]{1,0:T(8,128)} fusion(bf16[16,8,16,384]{3,2,1,0:T(8,128)(2,1)S(1)} %all-to-all-done.5, bf16[8,16,16,512]{3,2,0,1:T(8,128)(2,1)} %all-gather.8.cloned.1.call-done), kind=kOutput, calls=%fused_computation.10 | convolution fusion | flops 805306368 | bytes 4456448 | tf_op jit(solution)/shard_map/dot_general | solution.py:586
  (93 shorter events, 25.8 us)
Async XLA Ops:
  7.2 32.7 %all-gather.10.cloned.1.call-start = ((), (), s32[]{:S(2)}) async-start(), calls=%async_computation.7 | async-start | bytes 3538944 | tf_op jit(solution)/shard_map/all_gather | solution.py:510
  10.3 11.0 %copy-start.11 = (s32[16]{0:T(128)S(1)}, s32[16]{0:T(128)}, u32[]{:S(2)}) copy-start(s32[16]{0:T(128)} %param.21) | copy-start | bytes 196
  10.3 13.9 %copy-start.1 = (bf16[256,512]{1,0:T(8,128)(2,1)S(1)}, bf16[256,512]{1,0:T(8,128)(2,1)}, u32[]{:S(2)}) copy-start(bf16[256,512]{1,0:T(8,128)(2,1)} %left.3) | copy-start | bytes 786436
  13.8 17.6 %collective-permute-start = (bf16[4,64,512]{2,1,0:T(8,128)(2,1)S(1)}, bf16[4,64,512]{2,1,0:T(8,128)(2,1)S(1)}, u32[]{:S(2)}, u32[]{:S(2)}) collective-permute-start(bf16[4,64,512]{2,1,0:T(8,128)(2,1)S(1)} %get-tuple-element.49), channel_id=1, source_target_pairs={{0,4},{1,5},{2,6},{3,7},{4,8},{5,9},{6,10},{7,11},{8,12},{9,13},{1... | collective-permute-start | bytes 786440 | tf_op jit(solution)/shard_map/ppermute | solution.py:42
  15.6 15.9 %collective-permute-start.1 = (bf16[4,64,512]{2,1,0:T(8,128)(2,1)S(1)}, bf16[4,64,512]{2,1,0:T(8,128)(2,1)S(1)}, u32[]{:S(2)}, u32[]{:S(2)}) collective-permute-start(bf16[4,64,512]{2,1,0:T(8,128)(2,1)S(1)} %get-tuple-element.50), channel_id=1, source_target_pairs={{0,12},{1,13},{2,14},{3,15},{4,0},{5,1},{6,2},{7,3},{8,4},{9,5},{1... | collective-permute-start | bytes 786440 | tf_op jit(solution)/shard_map/ppermute | solution.py:42
  17.1 14.3 %collective-permute-start.2 = (bf16[4,64,512]{2,1,0:T(8,128)(2,1)S(1)}, bf16[4,64,512]{2,1,0:T(8,128)(2,1)S(1)}, u32[]{:S(2)}, u32[]{:S(2)}) collective-permute-start(bf16[4,64,512]{2,1,0:T(8,128)(2,1)S(1)} %get-tuple-element.53), channel_id=1, source_target_pairs={{0,1},{1,2},{2,3},{3,0},{4,5},{5,6},{6,7},{7,4},{8,9},{9,10},{10,1... | collective-permute-start | bytes 786440 | tf_op jit(solution)/shard_map/ppermute | solution.py:42
  19.1 12.3 %collective-permute-start.3 = (bf16[4,64,512]{2,1,0:T(8,128)(2,1)S(1)}, bf16[4,64,512]{2,1,0:T(8,128)(2,1)S(1)}, u32[]{:S(2)}, u32[]{:S(2)}) collective-permute-start(bf16[4,64,512]{2,1,0:T(8,128)(2,1)S(1)} %get-tuple-element.54), channel_id=1, source_target_pairs={{0,3},{1,0},{2,1},{3,2},{4,7},{5,4},{6,5},{7,6},{8,11},{9,8},{10,9... | collective-permute-start | bytes 786440 | tf_op jit(solution)/shard_map/ppermute | solution.py:42
  33.3 14.4 %collective-permute-start.4 = (bf16[4,128,512]{2,1,0:T(8,128)(2,1)}, bf16[4,128,512]{2,1,0:T(8,128)(2,1)S(1)}, u32[]{:S(2)}, u32[]{:S(2)}) collective-permute-start(bf16[4,128,512]{2,1,0:T(8,128)(2,1)} %get-tuple-element.55), channel_id=1, source_target_pairs={{0,4},{1,5},{2,6},{3,7},{4,8},{5,9},{6,10},{7,11},{8,12},{9,13},{1... | collective-permute-start | bytes 1572872 | tf_op jit(solution)/shard_map/ppermute | solution.py:42
  33.7 14.0 %collective-permute-start.5 = (bf16[4,128,512]{2,1,0:T(8,128)(2,1)}, bf16[4,128,512]{2,1,0:T(8,128)(2,1)S(1)}, u32[]{:S(2)}, u32[]{:S(2)}) collective-permute-start(bf16[4,128,512]{2,1,0:T(8,128)(2,1)} %get-tuple-element.56), channel_id=1, source_target_pairs={{0,12},{1,13},{2,14},{3,15},{4,0},{5,1},{6,2},{7,3},{8,4},{9,5},{1... | collective-permute-start | bytes 1572872 | tf_op jit(solution)/shard_map/ppermute | solution.py:42
  36.6 13.8 %collective-permute-start.6 = (bf16[4,128,512]{2,1,0:T(8,128)(2,1)}, bf16[4,128,512]{2,1,0:T(8,128)(2,1)S(1)}, u32[]{:S(2)}, u32[]{:S(2)}) collective-permute-start(bf16[4,128,512]{2,1,0:T(8,128)(2,1)} %get-tuple-element.58), channel_id=1, source_target_pairs={{0,1},{1,2},{2,3},{3,0},{4,5},{5,6},{6,7},{7,4},{8,9},{9,10},{10,1... | collective-permute-start | bytes 1572872 | tf_op jit(solution)/shard_map/ppermute | solution.py:42
  36.6 13.8 %collective-permute-start.7 = (bf16[4,128,512]{2,1,0:T(8,128)(2,1)}, bf16[4,128,512]{2,1,0:T(8,128)(2,1)S(1)}, u32[]{:S(2)}, u32[]{:S(2)}) collective-permute-start(bf16[4,128,512]{2,1,0:T(8,128)(2,1)} %get-tuple-element.59), channel_id=1, source_target_pairs={{0,3},{1,0},{2,1},{3,2},{4,7},{5,4},{6,5},{7,6},{8,11},{9,8},{10,9... | collective-permute-start | bytes 1572872 | tf_op jit(solution)/shard_map/ppermute | solution.py:42
  50.4 14.0 %copy-start.7 = (bf16[256,512]{1,0:T(8,128)(2,1)S(1)}, bf16[256,512]{1,0:T(8,128)(2,1)}, u32[]{:S(2)}) copy-start(bf16[256,512]{1,0:T(8,128)(2,1)} %param.17) | copy-start | bytes 786436
  50.4 14.0 %copy-start.10 = (f32[512]{0:T(512)S(1)}, f32[512]{0:T(512)}, u32[]{:S(2)}) copy-start(f32[512]{0:T(512)} %param.18) | copy-start | bytes 6148
  50.4 14.2 %copy-start.12 = (bf16[512,3072]{1,0:T(8,128)(2,1)S(1)}, bf16[512,3072]{1,0:T(8,128)(2,1)}, u32[]{:S(2)}) copy-start(bf16[512,3072]{1,0:T(8,128)(2,1)} %param.19) | copy-start | bytes 9437188
  51.3 6.6 %collective-permute-start.8 = (bf16[128,512]{1,0:T(8,128)(2,1)S(1)}, bf16[128,512]{1,0:T(8,128)(2,1)S(1)}, u32[]{:S(2)}, u32[]{:S(2)}) collective-permute-start(bf16[128,512]{1,0:T(8,128)(2,1)S(1)} %get-tuple-element.61), channel_id=1, source_target_pairs={{0,1},{1,2},{2,3},{3,0},{4,5},{5,6},{6,7},{7,4},{8,9},{9,10},{10,1... | collective-permute-start | bytes 393224 | tf_op jit(solution)/shard_map/ppermute | solution.py:42
  51.5 8.6 %collective-permute-start.9 = (bf16[128,512]{1,0:T(8,128)(2,1)S(1)}, bf16[128,512]{1,0:T(8,128)(2,1)S(1)}, u32[]{:S(2)}, u32[]{:S(2)}) collective-permute-start(bf16[128,512]{1,0:T(8,128)(2,1)S(1)} %get-tuple-element.62), channel_id=1, source_target_pairs={{0,2},{1,3},{2,0},{3,1},{4,6},{5,7},{6,4},{7,5},{8,10},{9,11},{10,... | collective-permute-start | bytes 393224 | tf_op jit(solution)/shard_map/ppermute | solution.py:42
  55.8 5.0 %collective-permute-start.10 = (bf16[128,512]{1,0:T(8,128)(2,1)S(1)}, bf16[128,512]{1,0:T(8,128)(2,1)S(1)}, u32[]{:S(2)}, u32[]{:S(2)}) collective-permute-start(bf16[128,512]{1,0:T(8,128)(2,1)S(1)} %get-tuple-element.63), channel_id=1, source_target_pairs={{0,3},{1,0},{2,1},{3,2},{4,7},{5,4},{6,5},{7,6},{8,11},{9,8},{10,9... | collective-permute-start | bytes 393224 | tf_op jit(solution)/shard_map/ppermute | solution.py:42
  55.8 7.6 %collective-permute-start.11 = (bf16[128,512]{1,0:T(8,128)(2,1)S(1)}, bf16[128,512]{1,0:T(8,128)(2,1)S(1)}, u32[]{:S(2)}, u32[]{:S(2)}) collective-permute-start(bf16[128,512]{1,0:T(8,128)(2,1)S(1)} %get-tuple-element.65), channel_id=1, source_target_pairs={{0,4},{1,5},{2,6},{3,7},{4,8},{5,9},{6,10},{7,11},{8,12},{9,13},{1... | collective-permute-start | bytes 393224 | tf_op jit(solution)/shard_map/ppermute | solution.py:42
  55.8 7.6 %collective-permute-start.12 = (bf16[128,512]{1,0:T(8,128)(2,1)S(1)}, bf16[128,512]{1,0:T(8,128)(2,1)S(1)}, u32[]{:S(2)}, u32[]{:S(2)}) collective-permute-start(bf16[128,512]{1,0:T(8,128)(2,1)S(1)} %get-tuple-element.66), channel_id=1, source_target_pairs={{0,8},{1,9},{2,10},{3,11},{4,12},{5,13},{6,14},{7,15},{8,0},{9,1},... | collective-permute-start | bytes 393224 | tf_op jit(solution)/shard_map/ppermute | solution.py:42
  57.9 6.3 %collective-permute-start.13 = (bf16[128,512]{1,0:T(8,128)(2,1)S(1)}, bf16[128,512]{1,0:T(8,128)(2,1)S(1)}, u32[]{:S(2)}, u32[]{:S(2)}) collective-permute-start(bf16[128,512]{1,0:T(8,128)(2,1)S(1)} %get-tuple-element.67), channel_id=1, source_target_pairs={{0,12},{1,13},{2,14},{3,15},{4,0},{5,1},{6,2},{7,3},{8,4},{9,5},{1... | collective-permute-start | bytes 393224 | tf_op jit(solution)/shard_map/ppermute | solution.py:42
  67.0 5.5 %copy-start.8 = (bf16[1,8,1,3072]{3,2,1,0:T(2,128)(2,1)S(1)}, bf16[1,8,1,3072]{3,2,1,0:T(2,128)(2,1)}, u32[]{:S(2)}) copy-start(bf16[1,8,1,3072]{3,2,1,0:T(2,128)(2,1)} %get-tuple-element.104) | copy-start | bytes 147460
  67.0 25.6 %copy-start.3 = (s32[256]{0:T(256)S(1)}, s32[256]{0:T(256)}, u32[]{:S(2)}) copy-start(s32[256]{0:T(256)} %param.20) | copy-start | bytes 3076
  67.0 25.6 %all-to-all-start = ((bf16[16,144,384]{2,1,0:T(8,128)(2,1)}), bf16[16,144,384]{2,1,0:T(8,128)(2,1)S(1)}, u32[]{:S(2)}, u32[]{:S(2)}) async-start(bf16[16,144,384]{2,1,0:T(8,128)(2,1)} %bitcast.18), calls=%async_computation | async-start | bytes 3538944 | tf_op jit(solution)/shard_map/all_to_all | solution.py:15
  72.5 61.6 %all-gather.12.cloned.1.call-start = ((), (), s32[]{:S(2)}) async-start(), calls=%async_computation.8 | async-start | bytes 1671168 | tf_op jit(solution)/shard_map/all_gather | solution.py:523
  94.9 22.7 %all-to-all-start.1 = ((bf16[16,128,384]{2,1,0:T(8,128)(2,1)}), bf16[16,128,384]{2,1,0:T(8,128)(2,1)S(1)}, u32[]{:S(2)}, u32[]{:S(2)}) async-start(bf16[16,128,384]{2,1,0:T(8,128)(2,1)} %get-tuple-element.68), calls=%async_computation.1 | async-start | bytes 3145728 | tf_op jit(solution)/shard_map/all_to_all | solution.py:15
  128.3 22.2 %all-to-all-start.2 = ((bf16[16,16,3072]{2,1,0:T(8,128)(2,1)}), bf16[16,16,3072]{2,1,0:T(8,128)(2,1)S(1)}, u32[]{:S(2)}, u32[]{:S(2)}) async-start(bf16[16,16,3072]{2,1,0:T(8,128)(2,1)} %get-tuple-element.72.order), calls=%async_computation.2 | async-start | bytes 3145728 | tf_op jit(solution)/shard_map/all_to_all | solution.py:15
  134.1 64.7 %all-gather.14.cloned.1.call-start = ((), (), s32[]{:S(2)}) async-start(), calls=%async_computation.9 | async-start | bytes 1769472 | tf_op jit(solution)/shard_map/all_gather | solution.py:593
  134.2 5.6 %copy-start.4 = (bf16[3072,512]{1,0:T(8,128)(2,1)S(1)}, bf16[3072,512]{1,0:T(8,128)(2,1)}, u32[]{:S(2)}) copy-start(bf16[3072,512]{1,0:T(8,128)(2,1)} %gate_hbm.1) | copy-start | bytes 9437188
  151.3 20.4 %copy-start.2 = (f32[3072]{0:T(1024)S(1)}, f32[3072]{0:T(1024)}, u32[]{:S(2)}) copy-start(f32[3072]{0:T(1024)} %param.24) | copy-start | bytes 36868
  151.3 51.8 %all-gather.8.cloned.1.call-start = ((), (), s32[]{:S(2)}) async-start(), calls=%async_computation.6 | async-start | bytes 2359296 | tf_op jit(solution)/shard_map/all_gather | solution.py:557
  151.9 19.8 %all-to-all-start.3 = ((bf16[16,16,3072]{2,1,0:T(8,128)(2,1)}), bf16[16,16,3072]{2,1,0:T(8,128)(2,1)S(1)}, u32[]{:S(2)}, u32[]{:S(2)}) async-start(bf16[16,16,3072]{2,1,0:T(8,128)(2,1)} %bitcast.35), calls=%async_computation.3 | async-start | bytes 3145728 | tf_op jit(solution)/shard_map/all_to_all | solution.py:15
  183.3 27.8 %all-to-all-start.5 = ((bf16[16,8,16,384]{3,2,1,0:T(8,128)(2,1)}), bf16[16,8,16,384]{3,2,1,0:T(8,128)(2,1)S(1)}, u32[]{:S(2)}, u32[]{:S(2)}) async-start(bf16[16,8,16,384]{3,2,1,0:T(8,128)(2,1)} %shard_map.149), calls=%async_computation.5 | async-start | bytes 3145728 | tf_op jit(solution)/shard_map/all_to_all | solution.py:15
  (4 other events, 6.4 us)
Sparse Core Ops, SparseCore 0:
  9.7 30.1 all-gather.9
  76.1 50.4 all-gather.11
  151.5 22.0 all-gather.13
  175.1 25.0 all-gather.7
